TPU v7x, 32 devices: a whole 2x2x4 slice. The times are simulated.
32 devices in a mesh: dp: 8 (over z, y), mp: 4 (over x, core).
Axes of the slice: x: 2, y: 2, z: 4, core: 2. Of those that a mesh axis runs over, the one named last changes fastest.
Arguments:
- texts: bfloat16 [192, 128, 1024], P('dp')
- w_qkv: bfloat16 [1024, 3072], P(None, 'mp'), may hold values from -0.1875 to 0.1875
- w_out: bfloat16 [1024, 1024], P('mp'), may hold values from -0.75 to 0.75
- w_self: bfloat16 [1024, 1024], P('mp'), may hold values from -0.1875 to 0.1875
- w_neigh: bfloat16 [1024, 1024], P('mp'), may hold values from -0.1875 to 0.1875
- neighbours: int32 [192, 16], P('dp'), may hold values from -1 to 191, as said below
- cotangent: bfloat16 [192, 1024], P('dp', 'mp'), may hold values from -6 to 6
Outputs:
- mixed: bfloat16 [192, 1024], P('dp', 'mp')
- node_grad: bfloat16 [192, 1024], P('dp', 'mp')
- grad_w_self: float32 [1024, 1024], P('mp')
- grad_w_neigh: float32 [1024, 1024], P('mp')
- grad_w_out: float32 [1024, 1024], P('mp')
Inputs may be any that keep to these rules, and one draw needn't show every extreme that they name: `neighbours`: A node id j lives with index j // 24 of dp. In the rows of one dp device (aligned blocks of 24 rows) at most 48 entries fall in any one owner's id range, and some owner gets exactly 48; entries are -1 or ids below 192. Some targets have every slot -1.
All inputs are finite; a program needn't handle non-finite values.
Results may differ from a plain program's by a relative error of at most 0.029.
The roundings to bfloat16 on the way count: a program that leaves them out, or rounds other values in their place, can miss the bound.
Values may be sent and summed in bfloat16 or wider, within the bound.
No kernel may reach another device: no remote copies, remote signals or barrier semaphores. Data moves between devices by JAX's collectives and lax.ppermute only.
A program may use at most 64 MiB of HBM per device.

v0:
```python
import jax
import jax.numpy as jnp
from jax import lax
from jax.sharding import PartitionSpec as P

HD = 64


def per_device(texts, w_qkv, w_out, w_self, w_neigh, neighbours, cotangent):
    node_dev, seq_len, width = texts.shape
    fan = neighbours.shape[1]
    cols = w_self.shape[0]
    heads_here = w_qkv.shape[1] // (3 * HD)
    groups = lax.axis_size("dp")
    slots = node_dev * fan
    limit = slots // groups
    factor = 1.0 / jnp.sqrt(jnp.float32(node_dev * groups))
    qkv = jnp.einsum("nld,de->nle", texts, w_qkv, preferred_element_type=jnp.float32).astype(
        jnp.bfloat16
    )
    qkv = qkv.reshape(node_dev, seq_len, heads_here, 3, HD)
    scores = jnp.einsum(
        "nqhd,nkhd->nhqk",
        qkv[:, :, :, 0, :],
        qkv[:, :, :, 1, :],
        preferred_element_type=jnp.float32,
    )
    probs = jax.nn.softmax(scores / jnp.sqrt(jnp.float32(HD)), axis=-1).astype(jnp.bfloat16)
    context = jnp.einsum(
        "nhqk,nkhd->nhd", probs, qkv[:, :, :, 2, :], preferred_element_type=jnp.float32
    )
    pooled = (
        (context / jnp.float32(seq_len)).reshape(node_dev, heads_here * HD).astype(jnp.bfloat16)
    )
    partial_embed = jnp.dot(pooled, w_out, preferred_element_type=jnp.float32)
    token_mean = jnp.mean(texts.astype(jnp.float32), axis=1)
    embed = (token_mean + lax.psum(partial_embed, "mp")).astype(jnp.bfloat16)
    start_col = lax.axis_index("mp") * cols
    embed_cols = lax.dynamic_slice_in_dim(embed, start_col, cols, 1)
    valid = neighbours >= 0
    cnt = jnp.maximum(jnp.sum(valid, axis=1).astype(jnp.float32), 1.0)
    flat_ids = neighbours.reshape(slots)
    flat_valid = flat_ids >= 0
    owner = jnp.where(flat_valid, flat_ids // node_dev, 0)
    local = jnp.where(flat_valid, flat_ids % node_dev, 0)
    owner_hot = ((owner[:, None] == jnp.arange(groups)[None, :]) & flat_valid[:, None]).astype(
        jnp.int32
    )
    before = jnp.cumsum(owner_hot, axis=0) - owner_hot
    rank = jnp.sum(before * owner_hot, axis=1)
    position = jnp.where(flat_valid, owner * limit + rank, slots)
    wanted = (
        jnp.full((slots,), -1, jnp.int32)
        .at[position]
        .set(local, mode="drop")
        .reshape(groups, limit)
    )
    asked = lax.all_to_all(wanted, "dp", split_axis=0, concat_axis=0, tiled=True).reshape(slots)
    select = (asked[:, None] == jnp.arange(node_dev)[None, :]).astype(jnp.bfloat16)
    sending = jnp.dot(select, embed_cols, preferred_element_type=jnp.float32).astype(jnp.bfloat16)
    arrived = lax.all_to_all(
        sending.reshape(groups, limit, cols), "dp", split_axis=0, concat_axis=0, tiled=True
    ).reshape(slots, cols)
    gather_hot = jnp.sum(
        position.reshape(node_dev, fan)[:, :, None] == jnp.arange(slots)[None, None, :], axis=1
    ).astype(jnp.bfloat16)
    agg = (jnp.dot(gather_hot, arrived, preferred_element_type=jnp.float32) / cnt[:, None]).astype(
        jnp.bfloat16
    )
    partial_z = jnp.dot(embed_cols, w_self, preferred_element_type=jnp.float32) + jnp.dot(
        agg, w_neigh, preferred_element_type=jnp.float32
    )
    z_cols = lax.psum_scatter(partial_z, "mp", scatter_dimension=1, tiled=True)
    mixed = jax.nn.gelu(z_cols).astype(jnp.bfloat16)
    _, pullback = jax.vjp(jax.nn.gelu, z_cols)
    dz_cols = pullback(cotangent.astype(jnp.float32))[0].astype(jnp.bfloat16)
    dz_full = lax.all_gather(dz_cols, "mp", axis=1, tiled=True)
    d_agg = lax.dot_general(
        dz_full, w_neigh, (((1,), (1,)), ((), ())), preferred_element_type=jnp.float32
    )
    msg = (d_agg / cnt[:, None]).astype(jnp.bfloat16)
    self_term = lax.dot_general(
        dz_full, w_self, (((1,), (1,)), ((), ())), preferred_element_type=jnp.float32
    )
    slot_msgs = lax.dot_general(
        gather_hot, msg, (((0,), (0,)), ((), ())), preferred_element_type=jnp.float32
    ).astype(jnp.bfloat16)
    returned = lax.all_to_all(
        slot_msgs.reshape(groups, limit, cols), "dp", split_axis=0, concat_axis=0, tiled=True
    ).reshape(slots, cols)
    neighbour_sum = lax.dot_general(
        select, returned, (((0,), (0,)), ((), ())), preferred_element_type=jnp.float32
    )
    node_grad = (self_term + neighbour_sum).astype(jnp.bfloat16)
    grad_full = lax.all_gather(node_grad, "mp", axis=1, tiled=True)
    local_self = lax.dot_general(
        embed_cols, dz_full, (((0,), (0,)), ((), ())), preferred_element_type=jnp.float32
    )
    local_neigh = lax.dot_general(
        agg, dz_full, (((0,), (0,)), ((), ())), preferred_element_type=jnp.float32
    )
    local_out = lax.dot_general(
        pooled, grad_full, (((0,), (0,)), ((), ())), preferred_element_type=jnp.float32
    )
    sum_self, sum_neigh, sum_out = lax.psum((local_self, local_neigh, local_out), "dp")
    return (mixed, node_grad, sum_self * factor, sum_neigh * factor, sum_out * factor)


def solution(mesh):
    return jax.shard_map(
        per_device,
        mesh=mesh,
        in_specs=(
            P("dp", None, None),
            P(None, "mp"),
            P("mp", None),
            P("mp", None),
            P("mp", None),
            P("dp", None),
            P("dp", "mp"),
        ),
        out_specs=(P("dp", "mp"), P("dp", "mp"), P("mp", None), P("mp", None), P("mp", None)),
        check_vma=False,
    )
```

profile of v0, /device:TPU:0, one launch (start us, length us, event | category | flops | bytes accessed | tf_op | source)
XLA Modules:
  0.0 277.4 jit_solution(17649135358498554399)
XLA Ops:
  7.2 1.4 copy-done
  8.6 9.5 %convolution_convert_fusion = bf16[24,128,768]{2,1,0:T(8,128)(2,1)} fusion(bf16[24,128,1024]{2,1,0:T(8,128)(2,1)} %param.7, bf16[1024,768]{1,0:T(8,128)(2,1)S(1)} %copy-done), kind=kOutput, calls=%fused_computation.10 | convolution fusion | flops 4834197504 | bytes 12582912 | tf_op jit(solution)/shard_map/nld,de->nle/dot_general | solution.py:18
  18.0 6.7 %copy.22 = bf16[24,128,768]{1,2,0:T(8,128)(2,1)} copy(bf16[24,128,768]{2,1,0:T(8,128)(2,1)} %convolution_convert_fusion) | data formatting | bytes 9437184 | tf_op jit(solution)/shard_map/convert_element_type | solution.py:18
  24.8 5.6 %fusion.7 = f32[24,4,128,128]{2,3,1,0:T(8,128)} fusion(bf16[24,128,4,3,64]{1,4,3,2,0:T(8,128)(2,1)} %bitcast.56), kind=kOutput, calls=%fused_computation.14 | convolution fusion | flops 201326592 | bytes 9437184 | tf_op jit(solution)/shard_map/nqhd,nkhd->nhqk/dot_general | solution.py:22
  30.4 6.8 %convert_reduce_fusion.1 = f32[24,4,128]{2,1,0:T(4,128)S(1)} fusion(f32[24,4,128,128]{2,3,1,0:T(8,128)} %fusion.7), kind=kOutput, calls=%fused_computation.4 | output fusion | flops 11022590 | bytes 6340608 | tf_op jit(solution)/shard_map/div | solution.py:28
  37.2 2.4 fusion.6
  39.8 0.8 fusion.47
  41.6 0.9 reduce-window.6
  43.0 2.9 %scatter_custom_fusion = s32[384]{0:T(512)S(1)} fusion(s32[384]{0:T(512)S(1)} %fusion.40, s32[384]{0:T(512)S(1)} %get-tuple-element.18, s32[]{:T(128)} %constant.30.clone.1), kind=kCustom, calls=%fused_computation.86 | custom fusion | bytes 1540 | tf_op jit(solution)/shard_map/scatter | solution.py:55
  45.9 0.7 all_to_all.12
  46.6 7.3 %all-to-all-start = ((s32[8,1,48]{2,1,0:T(1,128)}), s32[8,1,48]{2,1,0:T(1,128)S(1)}, u32[]{:S(2)}, u32[]{:S(2)}) async-start(s32[8,1,48]{2,1,0:T(1,128)} %all_to_all.12), calls=%async_computation | async-start | bytes 8192 | tf_op jit(solution)/shard_map/all_to_all | solution.py:58
  53.9 4.3 %convert_reduce_fusion = f32[24,1024]{1,0:T(8,128)S(1)} fusion(bf16[24,128,1024]{2,1,0:T(8,128)(2,1)} %param.7), kind=kLoop, calls=%fused_computation.3 | loop fusion | flops 6266880 | bytes 6389760 | tf_op jit(solution)/shard_map/reduce_sum | solution.py:36
  58.3 1.9 all-to-all-done
  61.5 13.2 %all-reduce.4.cloned.1.call-done = f32[24,1024]{1,0:T(8,128)} async-done(((f32[24,1024]{1,0:T(8,128)}), f32[24,1024]{1,0:T(8,128)}) %all-reduce.4.cloned.1.call-update) | async-done | bytes 98320 | tf_op jit(solution)/shard_map/psum | solution.py:37
  74.8 0.7 fusion.24
  75.5 0.9 convolution_convert_fusion.1
  76.5 5.5 %all-to-all-start.1 = ((bf16[8,48,256]{2,1,0:T(8,128)(2,1)}), bf16[8,48,256]{2,1,0:T(8,128)(2,1)S(1)}, u32[]{:S(2)}, u32[]{:S(2)}) async-start(bf16[8,48,256]{2,1,0:T(8,128)(2,1)} %bitcast.11), calls=%async_computation.1 | async-start | bytes 393216 | tf_op jit(solution)/shard_map/all_to_all | solution.py:61
  82.4 7.3 %all-to-all-done.1 = bf16[8,48,256]{2,1,0:T(8,128)(2,1)S(1)} async-done(((bf16[8,48,256]{2,1,0:T(8,128)(2,1)}), bf16[8,48,256]{2,1,0:T(8,128)(2,1)S(1)}, u32[]{:S(2)}, u32[]{:S(2)}) %all-to-all-start.1) | async-done | bytes 196640 | tf_op jit(solution)/shard_map/all_to_all | solution.py:61
  89.9 0.8 convolution_add_fusion
  90.8 16.8 %reduce-scatter.2.cloned.1.call-done = f32[24,256]{1,0:T(8,128)} async-done(((f32[24,1024]{1,0:T(8,128)}), f32[24,256]{1,0:T(8,128)}) %reduce-scatter.2.cloned.1.call-update) | async-done | bytes 24592 | tf_op jit(solution)/shard_map/reduce_scatter | solution.py:73
  107.6 1.4 fusion.16
  108.9 5.2 %all_gather.6 = bf16[24,1024]{1,0:T(8,128)(2,1)S(1)} all-gather(bf16[24,256]{1,0:T(8,128)(2,1)S(1)} %get-tuple-element.12), channel_id=1, replica_groups=mesh['dp'=8,'mp'=4] {'mp'}, dimensions={1}, use_global_device_ids=true | all-gather | bytes 61440 | tf_op jit(solution)/shard_map/all_gather | solution.py:77
  114.1 1.2 convolution_convert_fusion.2
  115.4 1.3 fusion.50
  116.6 5.5 %all-to-all-start.2 = ((bf16[8,48,256]{2,1,0:T(8,128)(2,1)}), bf16[8,48,256]{2,1,0:T(8,128)(2,1)S(1)}, u32[]{:S(2)}, u32[]{:S(2)}) async-start(bf16[8,48,256]{2,1,0:T(8,128)(2,1)} %bitcast.13), calls=%async_computation.3 | async-start | bytes 393216 | tf_op jit(solution)/shard_map/all_to_all | solution.py:88
  122.4 1.3 fusion.51
  123.8 6.9 %all-to-all-done.2 = bf16[8,48,256]{2,1,0:T(8,128)(2,1)S(1)} async-done(((bf16[8,48,256]{2,1,0:T(8,128)(2,1)}), bf16[8,48,256]{2,1,0:T(8,128)(2,1)S(1)}, u32[]{:S(2)}, u32[]{:S(2)}) %all-to-all-start.2) | async-done | bytes 196640 | tf_op jit(solution)/shard_map/all_to_all | solution.py:88
  130.9 5.2 %all_gather.7 = bf16[24,1024]{1,0:T(8,128)(2,1)S(1)} all-gather(bf16[24,256]{1,0:T(8,128)(2,1)S(1)} %fusion.10), channel_id=1, replica_groups=mesh['dp'=8,'mp'=4] {'mp'}, dimensions={1}, use_global_device_ids=true | all-gather | bytes 61440 | tf_op jit(solution)/shard_map/all_gather | solution.py:95
  136.2 1.3 fusion.52
  137.5 127.8 %all-reduce.6.cloned.1.call-done = (f32[256,1024]{1,0:T(8,128)}, f32[256,1024]{1,0:T(8,128)}, f32[256,1024]{1,0:T(8,128)}) async-done(((f32[256,1024]{1,0:T(8,128)}, f32[256,1024]{1,0:T(8,128)}, f32[256,1024]{1,0:T(8,128)}), (f32[256,1024]{1,0:T(8,128)}, f32[256,1024]{1,0:T(8,128)}, f32[256,1024]{1,0:T(8,128)})) %all-reduce.6.cloned.1.call-update) | async-done | bytes 3145744 | tf_op jit(solution)/shard_map/psum | solution.py:105
  265.3 2.3 broadcast_multiply_fusion.2
  267.6 3.2 %broadcast_multiply_fusion = (f32[256,1024]{1,0:T(8,128)}, f32[256,1024]{1,0:T(8,128)}) fusion(f32[256,1024]{1,0:T(8,128)} %get-tuple-element.7, f32[256,1024]{1,0:T(8,128)} %get-tuple-element.6), kind=kLoop, calls=%fused_computation.28 | loop fusion | flops 524288 | bytes 4194304 | tf_op jit(solution)/shard_map/mul | solution.py:106
  (52 shorter events, 4.2 us)
Async XLA Ops:
  7.2 1.4 copy-start
  7.2 67.6 %all-reduce.4.cloned.1.call-start = ((), (), s32[]{:S(2)}) async-start(), calls=%async_computation.4 | async-start | bytes 196608 | tf_op jit(solution)/shard_map/psum | solution.py:37
  30.4 9.4 %copy-start.3 = (bf16[256,1024]{1,0:T(8,128)(2,1)S(1)}, bf16[256,1024]{1,0:T(8,128)(2,1)}, u32[]{:S(2)}) copy-start(bf16[256,1024]{1,0:T(8,128)(2,1)} %param.9) | copy-start | bytes 1572868
  30.4 10.3 %copy-start.6 = (s32[24,16]{0,1:T(8,128)S(1)}, s32[24,16]{0,1:T(8,128)}, u32[]{:S(2)}) copy-start(s32[24,16]{0,1:T(8,128)} %param.12) | copy-start | bytes 4612
  37.2 45.0 %copy-start.1 = (bf16[256,1024]{1,0:T(8,128)(2,1)S(1)}, bf16[256,1024]{1,0:T(8,128)(2,1)}, u32[]{:S(2)}) copy-start(bf16[256,1024]{1,0:T(8,128)(2,1)} %param.10) | copy-start | bytes 1572868
  37.2 52.7 %copy-start.2 = (bf16[256,1024]{1,0:T(8,128)(2,1)S(1)}, bf16[256,1024]{1,0:T(8,128)(2,1)}, u32[]{:S(2)}) copy-start(bf16[256,1024]{1,0:T(8,128)(2,1)} %param.11) | copy-start | bytes 1572868
  37.2 70.3 %copy-start.5 = (bf16[24,256]{1,0:T(8,128)(2,1)S(1)}, bf16[24,256]{1,0:T(8,128)(2,1)}, u32[]{:S(2)}) copy-start(bf16[24,256]{1,0:T(8,128)(2,1)} %param.13) | copy-start | bytes 36868
  46.6 13.7 %all-to-all-start = ((s32[8,1,48]{2,1,0:T(1,128)}), s32[8,1,48]{2,1,0:T(1,128)S(1)}, u32[]{:S(2)}, u32[]{:S(2)}) async-start(s32[8,1,48]{2,1,0:T(1,128)} %all_to_all.12), calls=%async_computation | async-start | bytes 8192 | tf_op jit(solution)/shard_map/all_to_all | solution.py:58
  76.5 13.3 %all-to-all-start.1 = ((bf16[8,48,256]{2,1,0:T(8,128)(2,1)}), bf16[8,48,256]{2,1,0:T(8,128)(2,1)S(1)}, u32[]{:S(2)}, u32[]{:S(2)}) async-start(bf16[8,48,256]{2,1,0:T(8,128)(2,1)} %bitcast.11), calls=%async_computation.1 | async-start | bytes 393216 | tf_op jit(solution)/shard_map/all_to_all | solution.py:61
  82.0 25.6 %reduce-scatter.2.cloned.1.call-start = ((), (), s32[]{:S(2)}) async-start(), calls=%async_computation.5 | async-start | bytes 122880 | tf_op jit(solution)/shard_map/reduce_scatter | solution.py:73
  116.6 14.0 %all-to-all-start.2 = ((bf16[8,48,256]{2,1,0:T(8,128)(2,1)}), bf16[8,48,256]{2,1,0:T(8,128)(2,1)S(1)}, u32[]{:S(2)}, u32[]{:S(2)}) async-start(bf16[8,48,256]{2,1,0:T(8,128)(2,1)} %bitcast.13), calls=%async_computation.3 | async-start | bytes 393216 | tf_op jit(solution)/shard_map/all_to_all | solution.py:88
  122.2 143.1 %all-reduce.6.cloned.1.call-start = ((), (), s32[]{:S(2)}) async-start(), calls=%async_computation.6 | async-start | bytes 6291456 | tf_op jit(solution)/shard_map/psum | solution.py:105
  130.9 140.0 %copy-start.4 = (bf16[24,256]{1,0:T(8,128)(2,1)}, bf16[24,256]{1,0:T(8,128)(2,1)S(1)}, u32[]{:S(2)}) copy-start(bf16[24,256]{1,0:T(8,128)(2,1)S(1)} %fusion.10) | copy-start | bytes 36868
Sparse Core Ops, SparseCore 0:
  40.7 33.9 all-reduce.3
  90.9 16.6 reduce-scatter.1
  137.6 127.6 all-reduce.5
where the time goes:
time: 278 us; the launch traced here: 277 us
  waiting for transfers between devices  174 us (63%)
  matrix products  26 us (9%)
  other arithmetic  20.9 us (8%)
  starting transfers between devices  18.4 us (7%)
  between operations  13.9 us (5%)
  local copies, waits for them, and re-layouts  13.6 us (5%)
  blocking collectives  10.4 us (4%)
    psum x1, waiting for transfers between devices, per_device(): lax.psum((local_self, local_neigh, local_out), 'dp')  128 us
    reduce_scatter x1, waiting for transfers between devices, per_device(): z_cols = lax.psum_scatter(partial_z, 'mp', scatter_dimension=1, tiled=True)  16.8 us
    psum x1, waiting for transfers between devices, per_device(): embed = (token_mean + lax.psum(partial_embed, 'mp')).astype(jnp.bfloat16)  13.2 us
    dot_general x1, matrix products, per_device(): jnp.einsum('nld,de->nle', texts, w_qkv, preferred_element_type=jnp.float32)  9.47 us
    all_to_all x1, waiting for transfers between devices, per_device(): lax.all_to_all(sending.reshape(groups, limit, cols), 'dp', split_axis=0,...  7.33 us
    all_to_all x1, starting transfers between devices, per_device(): lax.all_to_all(wanted, 'dp', split_axis=0, concat_axis=0, tiled=True)  7.28 us
    all_to_all x1, waiting for transfers between devices, per_device(): lax.all_to_all(slot_msgs.reshape(groups, limit, cols), 'dp', split_axis=0...  6.85 us
    div x1, other arithmetic, per_device(): jax.nn.softmax(scores / jnp.sqrt(jnp.float32(HD)), axis=-1)  6.81 us
  transfers between devices with their start and end apart: 6, of which 6 were waited for; matrix products, arithmetic and copies ran while one was open for 5% of the time, Pallas kernels for 0%

commit v1 on v0

v1 whole, which is shorter than its diff:
```python
import jax
import jax.numpy as jnp
from jax import lax
from jax.sharding import PartitionSpec as P

HD = 64
BF = jnp.bfloat16
F32 = jnp.float32


def attention(texts, w_qkv):
    node_dev, seq_len, width = texts.shape
    heads_here = w_qkv.shape[1] // (3 * HD)
    qkv = jnp.einsum("nld,de->nle", texts, w_qkv, preferred_element_type=F32).astype(BF)
    qkv = qkv.reshape(node_dev, seq_len, heads_here, 3, HD)
    scores = jnp.einsum(
        "nqhd,nkhd->nhqk", qkv[:, :, :, 0, :], qkv[:, :, :, 1, :], preferred_element_type=F32
    )
    probs = jax.nn.softmax(scores / jnp.sqrt(jnp.float32(HD)), axis=-1).astype(BF)
    context = jnp.einsum("nhqk,nkhd->nhd", probs, qkv[:, :, :, 2, :], preferred_element_type=F32)
    return (context / jnp.float32(seq_len)).reshape(node_dev, heads_here * HD).astype(BF)


def gather_all(block):
    whole = lax.all_gather(block, ("dp", "mp"), axis=0, tiled=False)
    dp, mp = lax.axis_size("dp"), lax.axis_size("mp")
    rows, cols = block.shape
    whole = whole.reshape(dp, mp, rows, cols).transpose(0, 2, 1, 3)
    return whole.reshape(dp * rows, mp * cols)


def dot_t(a, b):
    return lax.dot_general(a, b, (((1,), (1,)), ((), ())), preferred_element_type=F32)


def t_dot(a, b):
    return lax.dot_general(a, b, (((0,), (0,)), ((), ())), preferred_element_type=F32)


def per_device(texts, w_qkv, w_out, w_self, w_neigh, neighbours, cotangent):
    node_dev, seq_len, width = texts.shape
    cols = w_self.shape[0]
    nodes = node_dev * lax.axis_size("dp")
    factor = 1.0 / jnp.sqrt(jnp.float32(nodes))
    row0 = lax.axis_index("dp") * node_dev
    col0 = lax.axis_index("mp") * cols

    def own_cols(a):
        return lax.dynamic_slice_in_dim(a, col0, cols, 1)

    w_out = lax.all_gather(w_out, "mp", axis=0, tiled=True)
    w_self = lax.all_gather(w_self, "mp", axis=0, tiled=True)
    w_neigh = lax.all_gather(w_neigh, "mp", axis=0, tiled=True)
    ids = lax.all_gather(neighbours, "dp", axis=0, tiled=True)
    cot = gather_all(cotangent)
    my_texts = lax.dynamic_slice_in_dim(texts, col0, cols, 2)
    token_mean = gather_all(jnp.mean(my_texts.astype(F32), axis=1))

    pooled = gather_all(attention(texts, w_qkv))
    embed = (token_mean + jnp.dot(pooled, w_out, preferred_element_type=F32)).astype(BF)
    cnt = jnp.maximum(jnp.sum(ids >= 0, axis=1).astype(F32), 1.0)[:, None]
    counts = jnp.sum(ids[:, :, None] == jnp.arange(nodes)[None, None, :], axis=1).astype(BF)
    agg = (jnp.dot(counts, embed, preferred_element_type=F32) / cnt).astype(BF)
    z = jnp.dot(embed, w_self, preferred_element_type=F32) + jnp.dot(
        agg, w_neigh, preferred_element_type=F32
    )
    out, pullback = jax.vjp(jax.nn.gelu, z)
    mixed = out.astype(BF)
    dz = pullback(cot.astype(F32))[0].astype(BF)
    msg = (dot_t(dz, w_neigh) / cnt).astype(BF)
    node_grad = (dot_t(dz, w_self) + t_dot(counts, msg)).astype(BF)
    grads = [
        t_dot(own_cols(left), right) * factor
        for left, right in ((embed, dz), (agg, dz), (pooled, node_grad))
    ]
    own = [
        lax.dynamic_slice(a, (row0, col0), (node_dev, cols)) for a in (mixed, node_grad)
    ]
    return (*own, *grads)


def solution(mesh):
    return jax.shard_map(
        per_device,
        mesh=mesh,
        in_specs=(
            P("dp", None, None),
            P(None, "mp"),
            P("mp", None),
            P("mp", None),
            P("mp", None),
            P("dp", None),
            P("dp", "mp"),
        ),
        out_specs=(P("dp", "mp"), P("dp", "mp"), P("mp", None), P("mp", None), P("mp", None)),
        check_vma=False,
    )
```

time: 278 us -> 225 us (0.81)
  waiting for transfers between devices: 174 us -> 2.1 us
  blocking collectives: 10.4 us -> 153 us
  starting transfers between devices: 18.4 us -> 0.11 us
  other arithmetic: 20.9 us -> 11 us
  matrix products: 26 us -> 34.7 us
  local copies, waits for them, and re-layouts: 13.6 us -> 9.48 us
    all_gather x2 -> x4, blocking collectives: 10.4 us -> 153 us  [the longest x3 123 us: gather_all(): whole = lax.all_gather(block, ('dp', 'mp'), axis=0, tiled=False)]
    psum x2 -> x0, waiting for transfers between devices: 141 us -> none  [the longest x1 128 us: per_device(): lax.psum((local_self, local_neigh, local_out), 'dp')]
    all_to_all x3 -> x0, starting transfers between devices: 18.3 us -> none  [the longest x1 7.28 us: per_device(): lax.all_to_all(wanted, 'dp', split_axis=0, concat_axis=0, tiled=True)]
    reduce_scatter x1 -> x0, waiting for transfers between devices: 16.8 us -> none  [per_device(): z_cols = lax.psum_scatter(partial_z, 'mp', scatter_dimension=1, tiled=True)]
    all_to_all x3 -> x0, waiting for transfers between devices: 16.1 us -> none  [the longest x1 7.33 us: per_device(): lax.all_to_all(sending.reshape(groups, limit, cols), 'dp', split_axis=0,...]
    dot_general x14 -> x12, matrix products: 26 us -> 34.7 us  [the longest x1 9.49 us: attention(): jnp.einsum('nld,de->nle', texts, w_qkv, preferred_element_type=F32)]
    mul x2 -> x0, other arithmetic: 5.58 us -> none  [the longest x1 3.23 us: per_device(): sum_out * factor]
    scatter x1 -> x0, local copies, waits for them, and re-layouts: 2.91 us -> none  [per_device(): wanted = jnp.full((slots,), -1, jnp.int32).at[position].set(local, mode='...]
  transfers between devices with their start and end apart: 6 -> 3, of which waited for: 6 -> 0; matrix products, arithmetic and copies ran while one was open for 5% -> 18% of each run, Pallas kernels for 0% -> 0%
where the time goes in v1:
time: 225 us
  blocking collectives  153 us (68%)
  matrix products  34.7 us (15%)
  between operations  13.9 us (6%)
  other arithmetic  11 us (5%)
  local copies, waits for them, and re-layouts  9.48 us (4%)
    all_gather x3, blocking collectives, gather_all(): whole = lax.all_gather(block, ('dp', 'mp'), axis=0, tiled=False)  123 us
    all_gather x1, blocking collectives, per_device(): ids = lax.all_gather(neighbours, 'dp', axis=0, tiled=True)  30.5 us
    dot_general x1, matrix products, attention(): jnp.einsum('nld,de->nle', texts, w_qkv, preferred_element_type=F32)  9.49 us
    div x1, other arithmetic, attention(): jax.nn.softmax(scores / jnp.sqrt(jnp.float32(HD)), axis=-1).astype(BF)  6.81 us
    convert_element_type x1, local copies, waits for them, and re-layouts, attention(): jnp.einsum('nld,de->nle', texts, w_qkv, preferred_element_type=F32)  6.7 us
    dot_general x4, matrix products, t_dot(): lax.dot_general(a, b, (((0,), (0,)), ((), ())), preferred_element_type=F32)  6.65 us
    dot_general x1, matrix products, attention(): jnp.einsum('nqhd,nkhd->nhqk', qkv[:, :, :, 0, :], qkv[:, :, :, 1, :], pre...  5.61 us
  transfers between devices with their start and end apart: 3, of which 0 were waited for; matrix products, arithmetic and copies ran while one was open for 18% of the time, Pallas kernels for 0%

profile of v1, /device:TPU:0, one launch (start us, length us, event | category | flops | bytes accessed | tf_op | source)
XLA Modules:
  0.0 224.5 jit_solution(1241683172798168443)
XLA Ops:
  7.2 0.7 all-gather.7.cloned.1.call-update
  8.0 0.7 all-gather.9.cloned.1.call-update
  8.7 0.7 all-gather.11.cloned.1.call-update
  9.4 1.7 convert_reduce_fusion.2
  11.1 9.5 %convolution_convert_fusion = bf16[24,128,768]{2,1,0:T(8,128)(2,1)} fusion(bf16[24,128,1024]{2,1,0:T(8,128)(2,1)} %param.7, bf16[1024,768]{1,0:T(8,128)(2,1)S(1)} %copy-done), kind=kOutput, calls=%fused_computation.11 | convolution fusion | flops 4834197504 | bytes 12582912 | tf_op jit(solution)/shard_map/nld,de->nle/dot_general | solution.py:14
  20.6 6.7 %copy.39 = bf16[24,128,768]{1,2,0:T(8,128)(2,1)} copy(bf16[24,128,768]{2,1,0:T(8,128)(2,1)} %convolution_convert_fusion) | data formatting | bytes 9437184 | tf_op jit(solution)/shard_map/convert_element_type | solution.py:14
  27.3 5.6 %fusion.7 = f32[24,4,128,128]{2,3,1,0:T(8,128)} fusion(bf16[24,128,4,3,64]{1,4,3,2,0:T(8,128)(2,1)} %bitcast.59), kind=kOutput, calls=%fused_computation.15 | convolution fusion | flops 201326592 | bytes 9437184 | tf_op jit(solution)/shard_map/nqhd,nkhd->nhqk/dot_general | solution.py:16
  32.9 45.8 %all-gather = f32[768,256]{1,0:T(8,128)S(1)} all-gather(f32[24,256]{1,0:T(8,128)S(1)} %broadcast_multiply_fusion), channel_id=2, replica_groups=mesh['dp'=8,'mp'=4] {'dp','mp'}, dimensions={0}, use_global_device_ids=true | all-gather | bytes 811008 | tf_op jit(solution)/shard_map/all_gather | solution.py:25
  78.7 0.3 copy.38
  79.0 0.1 copy.50
  79.1 6.8 %convert_reduce_fusion = f32[24,4,128]{2,1,0:T(4,128)S(1)} fusion(f32[24,4,128,128]{2,3,1,0:T(8,128)} %fusion.7), kind=kOutput, calls=%fused_computation.2 | output fusion | flops 11022590 | bytes 6340608 | tf_op jit(solution)/shard_map/div | solution.py:19
  86.0 2.3 %fusion.6 = f32[24,4,1,64]{3,2,1,0:T(1,128)S(1)} fusion(f32[24,4,128,1]{2,3,1,0:T(1,128)S(1)} %bitcast.73, bf16[24,128,4,3,64]{1,4,3,2,0:T(8,128)(2,1)} %bitcast.60), kind=kOutput, calls=%fused_computation.13 | convolution fusion | flops 1572864 | bytes 1646592 | tf_op jit(solution)/shard_map/nhqk,nkhd->nhd/dot_general | solution.py:20
  88.3 0.1 convert_element_type.76
  88.4 37.7 %all_gather.27 = bf16[32,24,256]{2,1,0:T(8,128)(2,1)S(1)} all-gather(bf16[1,24,256]{2,1,0:T(8,128)(2,1)S(1)} %convert_element_type.76), channel_id=1, replica_groups=mesh['dp'=8,'mp'=4] {'dp','mp'}, dimensions={0}, use_global_device_ids=true | all-gather | bytes 405504 | tf_op jit(solution)/shard_map/all_gather | solution.py:25
  126.1 0.2 copy.42
  126.4 30.5 %all-gather.2 = s32[8,24,16]{1,2,0:T(8,128)S(1)} all-gather(s32[1,24,16]{1,2,0:T(8,128)S(1)} %bitcast.72), channel_id=1, replica_groups=mesh['dp'=8,'mp'=4] {'dp'}, dimensions={0}, use_global_device_ids=true | all-gather | bytes 13824 | tf_op jit(solution)/shard_map/all_gather | solution.py:54
  157.0 0.1 copy.44
  157.1 39.2 %all-gather.1 = bf16[768,256]{1,0:T(8,128)(2,1)S(1)} all-gather(bf16[24,256]{1,0:T(8,128)(2,1)S(1)} %copy-done.3), channel_id=3, replica_groups=mesh['dp'=8,'mp'=4] {'dp','mp'}, dimensions={0}, use_global_device_ids=true | all-gather | bytes 405504 | tf_op jit(solution)/shard_map/all_gather | solution.py:25
  196.3 0.2 copy.45
  196.5 1.0 copy.52
  197.5 1.1 convert_reduce_fusion.1
  198.7 2.2 fusion.9
  200.9 0.3 fusion.10
  201.2 3.1 %fusion.33 = f32[192,1024]{1,0:T(8,128)} fusion(bf16[192,1024]{1,0:T(8,128)(2,1)S(1)} %fusion.9, bf16[1024,1024]{1,0:T(8,128)(2,1)} %all-gather.9.cloned.1.call-done), kind=kOutput, calls=%fused_computation.56 | convolution fusion | flops 402653184 | bytes 3276800 | tf_op jit(solution)/shard_map/dot_general | solution.py:64
  204.3 4.2 %fusion.19 = (bf16[192,1024]{1,0:T(8,128)(2,1)S(1)}, f32[192,1024]{1,0:T(8,128)}, f32[192,1024]{1,0:T(8,128)}) fusion(f32[192,1024]{1,0:T(8,128)} %bitcast.70, f32[192,1024]{1,0:T(8,128)} %fusion.33, bf16[192,1024]{1,0:T(8,128)(2,1)S(1)} %fusion.10, bf16[1024,1024]{1,0:T(8,128)(2,1)} %all-gather.11.cloned.1.call-done), kind=kOutput, calls=%fused_computation.38 | convolution fusion | flops 406781952 | bytes 6029312 | tf_op jit(solution)/shard_map/dot_general | solution.py:64
  208.5 1.3 convolution_multiply_fusion.1
  209.8 1.3 convolution_multiply_fusion.2
  211.1 0.9 fusion.34
  212.0 2.7 %fusion.12 = bf16[192,1024]{1,0:T(8,128)(2,1)S(1)} fusion(f32[192,1024]{1,0:T(8,128)S(1)} %fusion.34, bf16[192,1024]{1,0:T(8,128)(2,1)S(1)} %get-tuple-element.5, bf16[1024,1024]{1,0:T(8,128)(2,1)} %all-gather.11.cloned.1.call-done, f32[192]{0:T(256)S(1)} %convert_maximum_fusion, s32[192,192]{1,0:T(8,128)} %copy-done.2), kind=kOutput, calls=%fused_computation.29 | convolution fusion | flops 478973952 | bytes 3818240 | tf_op jit(solution)/shard_map/dot_general | solution.py:37
  214.7 1.3 convolution_multiply_fusion
  216.0 0.6 dynamic_slice.20
  216.6 1.4 fusion.26
  (23 shorter events, 0.4 us)
Async XLA Ops:
  7.2 3.9 %copy-start = (bf16[1024,768]{1,0:T(8,128)(2,1)S(1)}, bf16[1024,768]{1,0:T(8,128)(2,1)}, u32[]{:S(2)}) copy-start(bf16[1024,768]{1,0:T(8,128)(2,1)} %param.8) | copy-start | bytes 4718596
  7.2 191.5 %all-gather.7.cloned.1.call-start = ((), (), s32[]{:S(2)}) async-start(), calls=%async_computation | async-start | bytes 2621440 | tf_op jit(solution)/shard_map/all_gather | solution.py:51
  7.9 193.3 %all-gather.9.cloned.1.call-start = ((), (), s32[]{:S(2)}) async-start(), calls=%async_computation.1 | async-start | bytes 2621440 | tf_op jit(solution)/shard_map/all_gather | solution.py:52
  8.7 195.6 %all-gather.11.cloned.1.call-start = ((), (), s32[]{:S(2)}) async-start(), calls=%async_computation.2 | async-start | bytes 2621440 | tf_op jit(solution)/shard_map/all_gather | solution.py:53
  85.9 40.4 %copy-start.4 = (s32[24,16]{0,1:T(8,128)S(1)}, s32[24,16]{0,1:T(8,128)}, u32[]{:S(2)}) copy-start(s32[24,16]{0,1:T(8,128)} %param.12) | copy-start | bytes 4612
  85.9 71.1 %copy-start.3 = (bf16[24,256]{1,0:T(8,128)(2,1)S(1)}, bf16[24,256]{1,0:T(8,128)(2,1)}, u32[]{:S(2)}) copy-start(bf16[24,256]{1,0:T(8,128)(2,1)} %param.13) | copy-start | bytes 36868
  198.6 2.5 %copy-start.2 = (s32[192,192]{1,0:T(8,128)}, s32[192,192]{1,0:T(8,128)S(1)}, u32[]{:S(2)}) copy-start(s32[192,192]{1,0:T(8,128)S(1)} %convert_reduce_fusion.1) | copy-start | bytes 442372
  208.5 2.6 %copy-start.1 = (bf16[1024,1024]{1,0:T(8,128)(2,1)S(1)}, bf16[1024,1024]{1,0:T(8,128)(2,1)}, u32[]{:S(2)}) copy-start(bf16[1024,1024]{1,0:T(8,128)(2,1)} %all-gather.9.cloned.1.call-done) | copy-start | bytes 6291460
Sparse Core Ops, SparseCore 0:
  9.6 25.2 all-gather.6
  36.5 25.9 all-gather.8
  64.0 22.8 all-gather.10

commit v2 on v1

--- a/solution.py
+++ b/solution.py
@@ -21,12 +21,48 @@
     return (context / jnp.float32(seq_len)).reshape(node_dev, heads_here * HD).astype(BF)
 
 
+def hop(x, axis, bit):
+    size = lax.axis_size(axis)
+    return lax.ppermute(x, axis, [(i, i ^ bit) for i in range(size)])
+
+
+def gather_dp(block):
+    size = lax.axis_size("dp")
+    if size > 8:
+        return lax.all_gather(block, "dp", axis=0, tiled=True)
+    parts = jnp.stack([block] + [hop(block, "dp", i) for i in range(1, size)])
+    parts = parts[jnp.arange(size) ^ lax.axis_index("dp")]
+    return parts.reshape(size * block.shape[0], block.shape[1])
+
+
+def gather_mp(block):
+    across = hop(block, "mp", 2)
+    here = hop(block, "mp", 1)
+    there = hop(across, "mp", 1)
+    parts = jnp.stack([block, here, across, there])
+    return parts[jnp.arange(4) ^ lax.axis_index("mp")]
+
+
 def gather_all(block):
-    whole = lax.all_gather(block, ("dp", "mp"), axis=0, tiled=False)
-    dp, mp = lax.axis_size("dp"), lax.axis_size("mp")
-    rows, cols = block.shape
-    whole = whole.reshape(dp, mp, rows, cols).transpose(0, 2, 1, 3)
-    return whole.reshape(dp * rows, mp * cols)
+    return jnp.concatenate(list(gather_mp(gather_dp(block))), axis=1)
+
+
+def gather_weight(w):
+    rows = w.shape[0] // 2
+    side = lax.axis_index("dp") % 2
+    first = hop(lax.dynamic_slice_in_dim(w, side * rows, rows, 0), "mp", 2)
+    second = hop(first, "dp", 1)
+    across = [first, second]
+    here = hop(w, "mp", 1)
+    there = [hop(a, "mp", 1) for a in across]
+
+    def order(pair):
+        low = jnp.where(side == 0, pair[0], pair[1])
+        high = jnp.where(side == 0, pair[1], pair[0])
+        return jnp.concatenate([low, high])
+
+    parts = jnp.stack([w, here, order(across), order(there)])
+    return parts[jnp.arange(4) ^ lax.axis_index("mp")].reshape(4 * w.shape[0], w.shape[1])
 
 
 def dot_t(a, b):
@@ -48,10 +84,10 @@
     def own_cols(a):
         return lax.dynamic_slice_in_dim(a, col0, cols, 1)
 
-    w_out = lax.all_gather(w_out, "mp", axis=0, tiled=True)
-    w_self = lax.all_gather(w_self, "mp", axis=0, tiled=True)
-    w_neigh = lax.all_gather(w_neigh, "mp", axis=0, tiled=True)
-    ids = lax.all_gather(neighbours, "dp", axis=0, tiled=True)
+    w_out = gather_weight(w_out)
+    w_self = gather_weight(w_self)
+    w_neigh = gather_weight(w_neigh)
+    ids = gather_dp(neighbours)
     cot = gather_all(cotangent)
     my_texts = lax.dynamic_slice_in_dim(texts, col0, cols, 2)
     token_mean = gather_all(jnp.mean(my_texts.astype(F32), axis=1))

time: 225 us -> 216 us (0.960)
  blocking collectives: 153 us -> 0 us
  waiting for transfers between devices: 2.1 us -> 73.6 us
  starting transfers between devices: 0.11 us -> 49.4 us
  local copies, waits for them, and re-layouts: 9.48 us -> 29.8 us
  other arithmetic: 11 us -> 28.6 us
  between operations: 13.9 us -> 1.28 us
  matrix products: 34.7 us -> 31.9 us
    all_gather x4 -> x0, blocking collectives: 153 us -> none  [the longest x3 123 us: gather_all(): whole = lax.all_gather(block, ('dp', 'mp'), axis=0, tiled=False)]
    ppermute x0 -> x52, waiting for transfers between devices: none -> 73.6 us  [hop(): return lax.ppermute(x, axis, [(i, i ^ bit) for i in range(size)])]
    ppermute x0 -> x52, starting transfers between devices: none -> 49.4 us  [hop(): return lax.ppermute(x, axis, [(i, i ^ bit) for i in range(size)])]
    gather x0 -> x10, local copies, waits for them, and re-layouts: none -> 14.9 us  [the longest x3 10.9 us: gather_weight(): parts[jnp.arange(4) ^ lax.axis_index('mp')]]
    another operation x0 -> x9, other arithmetic: none -> 10.6 us  [the longest x6 8.53 us: gather_weight(): parts = jnp.stack([w, here, order(across), order(there)])]
    select_n x0 -> x8, other arithmetic: none -> 5.44 us  [the longest x6 5.43 us: order(): low = jnp.where(side == 0, pair[0], pair[1])]
    dot_general x1, matrix products: 4.21 us -> 0.58 us  [per_device(): jnp.dot(agg, w_neigh, preferred_element_type=F32)]
    dynamic_slice x0 -> x3, local copies, waits for them, and re-layouts: none -> 2.68 us  [gather_weight(): first = hop(lax.dynamic_slice_in_dim(w, side * rows, rows, 0), 'mp', 2)]
  transfers between devices with their start and end apart: 3 -> 52, of which waited for: 0 -> 22; matrix products, arithmetic and copies ran while one was open for 18% -> 16% of each run, Pallas kernels for 0% -> 0%
where the time goes in v2:
time: 216 us; the launch traced here: 215 us
  waiting for transfers between devices  73.6 us (34%)
  starting transfers between devices  49.4 us (23%)
  matrix products  31.9 us (15%)
  local copies, waits for them, and re-layouts  29.8 us (14%)
  other arithmetic  28.6 us (13%)
    ppermute x52, waiting for transfers between devices, hop(): return lax.ppermute(x, axis, [(i, i ^ bit) for i in range(size)])  73.6 us
    ppermute x52, starting transfers between devices, hop(): return lax.ppermute(x, axis, [(i, i ^ bit) for i in range(size)])  49.4 us
    gather x3, local copies, waits for them, and re-layouts, gather_weight(): parts[jnp.arange(4) ^ lax.axis_index('mp')]  10.9 us
    dot_general x1, matrix products, attention(): jnp.einsum('nld,de->nle', texts, w_qkv, preferred_element_type=F32)  9.43 us
    another operation x6, other arithmetic, gather_weight(): parts = jnp.stack([w, here, order(across), order(there)])  8.53 us
    dot_general x4, matrix products, t_dot(): lax.dot_general(a, b, (((0,), (0,)), ((), ())), preferred_element_type=F32)  8.3 us
    div x1, other arithmetic, attention(): jax.nn.softmax(scores / jnp.sqrt(jnp.float32(HD)), axis=-1).astype(BF)  6.77 us
    convert_element_type x1, local copies, waits for them, and re-layouts, attention(): jnp.einsum('nld,de->nle', texts, w_qkv, preferred_element_type=F32)  6.64 us
  transfers between devices with their start and end apart: 52, of which 22 were waited for; matrix products, arithmetic and copies ran while one was open for 16% of the time, Pallas kernels for 0%

profile of v2, /device:TPU:0, one launch (start us, length us, event | category | flops | bytes accessed | tf_op | source)
XLA Modules:
  0.0 214.5 jit_solution(14820748810014610939)
XLA Ops:
  2.0 9.4 %convolution_convert_fusion = bf16[24,128,768]{2,1,0:T(8,128)(2,1)} fusion(bf16[24,128,1024]{2,1,0:T(8,128)(2,1)} %param.7, bf16[1024,768]{1,0:T(8,128)(2,1)S(1)} %copy-done), kind=kOutput, calls=%fused_computation.21 | convolution fusion | flops 4834197504 | bytes 12582912 | tf_op jit(solution)/shard_map/nld,de->nle/dot_general | solution.py:14
  11.5 6.6 %copy.19 = bf16[24,128,768]{1,2,0:T(8,128)(2,1)} copy(bf16[24,128,768]{2,1,0:T(8,128)(2,1)} %convolution_convert_fusion) | data formatting | bytes 9437184 | tf_op jit(solution)/shard_map/convert_element_type | solution.py:14
  18.1 5.6 %fusion.7 = f32[24,4,128,128]{2,3,1,0:T(8,128)} fusion(bf16[24,128,4,3,64]{1,4,3,2,0:T(8,128)(2,1)} %bitcast.164), kind=kOutput, calls=%fused_computation.28 | convolution fusion | flops 201326592 | bytes 9437184 | tf_op jit(solution)/shard_map/nqhd,nkhd->nhqk/dot_general | solution.py:16
  23.7 6.8 %convert_reduce_fusion = f32[24,4,128]{2,1,0:T(4,128)S(1)} fusion(f32[24,4,128,128]{2,3,1,0:T(8,128)} %fusion.7), kind=kOutput, calls=%fused_computation.12 | output fusion | flops 11022590 | bytes 6340608 | tf_op jit(solution)/shard_map/div | solution.py:19
  30.5 2.4 %fusion.6 = f32[24,4,1,64]{3,2,1,0:T(1,128)S(1)} fusion(f32[24,4,128,1]{2,3,1,0:T(1,128)S(1)} %bitcast.188, bf16[24,128,4,3,64]{1,4,3,2,0:T(8,128)(2,1)} %bitcast.165), kind=kOutput, calls=%fused_computation.26 | convolution fusion | flops 1572864 | bytes 1646592 | tf_op jit(solution)/shard_map/nhqk,nkhd->nhd/dot_general | solution.py:20
  33.0 3.0 %collective-permute-start.10 = (bf16[24,256]{1,0:T(8,128)(2,1)S(1)}, bf16[24,256]{1,0:T(8,128)(2,1)S(1)}, u32[]{:S(2)}, u32[]{:S(2)}) collective-permute-start(bf16[24,256]{1,0:T(8,128)(2,1)S(1)} %convert_element_type.73), channel_id=1, source_target_pairs={{0,4},{4,0},{8,12},{12,8},{16,20},{20,16},{24,28},{28,24},{1,5},{5... | collective-permute-start | bytes 36872 | tf_op jit(solution)/shard_map/ppermute | solution.py:26
  37.6 3.0 %collective-permute-start.13 = (bf16[24,256]{1,0:T(8,128)(2,1)S(1)}, bf16[24,256]{1,0:T(8,128)(2,1)S(1)}, u32[]{:S(2)}, u32[]{:S(2)}) collective-permute-start(bf16[24,256]{1,0:T(8,128)(2,1)S(1)} %convert_element_type.73), channel_id=1, source_target_pairs={{0,16},{4,20},{8,24},{12,28},{16,0},{20,4},{24,8},{28,12},{1,17},{... | collective-permute-start | bytes 36872 | tf_op jit(solution)/shard_map/ppermute | solution.py:26
  51.9 3.0 %collective-permute-done.32 = s32[24,16]{0,1:T(8,128)S(1)} collective-permute-done((s32[24,16]{0,1:T(8,128)S(1)}, s32[24,16]{0,1:T(8,128)S(1)}, u32[]{:S(2)}, u32[]{:S(2)}) %collective-permute-start.32) | collective-permute-done | bytes 1568 | tf_op jit(solution)/shard_map/ppermute | solution.py:26
  55.3 4.2 %collective-permute-done.33 = s32[24,16]{0,1:T(8,128)S(1)} collective-permute-done((s32[24,16]{0,1:T(8,128)S(1)}, s32[24,16]{0,1:T(8,128)S(1)}, u32[]{:S(2)}, u32[]{:S(2)}) %collective-permute-start.33) | collective-permute-done | bytes 1568 | tf_op jit(solution)/shard_map/ppermute | solution.py:26
  59.5 5.4 %collective-permute-done.34 = s32[24,16]{0,1:T(8,128)S(1)} collective-permute-done((s32[24,16]{0,1:T(8,128)S(1)}, s32[24,16]{0,1:T(8,128)S(1)}, u32[]{:S(2)}, u32[]{:S(2)}) %collective-permute-start.34) | collective-permute-done | bytes 1568 | tf_op jit(solution)/shard_map/ppermute | solution.py:26
  66.3 4.1 %collective-permute-done.35 = s32[24,16]{0,1:T(8,128)S(1)} collective-permute-done((s32[24,16]{0,1:T(8,128)S(1)}, s32[24,16]{0,1:T(8,128)S(1)}, u32[]{:S(2)}, u32[]{:S(2)}) %collective-permute-start.35) | collective-permute-done | bytes 1568 | tf_op jit(solution)/shard_map/ppermute | solution.py:26
  71.7 5.1 %collective-permute-done.36 = s32[24,16]{0,1:T(8,128)S(1)} collective-permute-done((s32[24,16]{0,1:T(8,128)S(1)}, s32[24,16]{0,1:T(8,128)S(1)}, u32[]{:S(2)}, u32[]{:S(2)}) %collective-permute-start.36) | collective-permute-done | bytes 1568 | tf_op jit(solution)/shard_map/ppermute | solution.py:26
  89.3 3.2 %collective-permute-done.42 = bf16[24,256]{1,0:T(8,128)(2,1)S(1)} collective-permute-done((bf16[24,256]{1,0:T(8,128)(2,1)S(1)}, bf16[24,256]{1,0:T(8,128)(2,1)S(1)}, u32[]{:S(2)}, u32[]{:S(2)}) %collective-permute-start.42) | collective-permute-done | bytes 12320 | tf_op jit(solution)/shard_map/ppermute | solution.py:26
  92.6 3.6 %collective-permute-done.43 = bf16[24,256]{1,0:T(8,128)(2,1)S(1)} collective-permute-done((bf16[24,256]{1,0:T(8,128)(2,1)S(1)}, bf16[24,256]{1,0:T(8,128)(2,1)S(1)}, u32[]{:S(2)}, u32[]{:S(2)}) %collective-permute-start.43) | collective-permute-done | bytes 12320 | tf_op jit(solution)/shard_map/ppermute | solution.py:26
  97.1 3.7 %collective-permute-done.44 = bf16[24,256]{1,0:T(8,128)(2,1)S(1)} collective-permute-done((bf16[24,256]{1,0:T(8,128)(2,1)S(1)}, bf16[24,256]{1,0:T(8,128)(2,1)S(1)}, u32[]{:S(2)}, u32[]{:S(2)}) %collective-permute-start.44) | collective-permute-done | bytes 12320 | tf_op jit(solution)/shard_map/ppermute | solution.py:26
  101.6 3.7 %collective-permute-done.45 = bf16[24,256]{1,0:T(8,128)(2,1)S(1)} collective-permute-done((bf16[24,256]{1,0:T(8,128)(2,1)S(1)}, bf16[24,256]{1,0:T(8,128)(2,1)S(1)}, u32[]{:S(2)}, u32[]{:S(2)}) %collective-permute-start.45) | collective-permute-done | bytes 12320 | tf_op jit(solution)/shard_map/ppermute | solution.py:26
  107.2 3.8 %collective-permute-done.46 = bf16[24,256]{1,0:T(8,128)(2,1)S(1)} collective-permute-done((bf16[24,256]{1,0:T(8,128)(2,1)S(1)}, bf16[24,256]{1,0:T(8,128)(2,1)S(1)}, u32[]{:S(2)}, u32[]{:S(2)}) %collective-permute-start.46) | collective-permute-done | bytes 12320 | tf_op jit(solution)/shard_map/ppermute | solution.py:26
  112.3 4.2 %collective-permute-done.47 = bf16[24,256]{1,0:T(8,128)(2,1)S(1)} collective-permute-done((bf16[24,256]{1,0:T(8,128)(2,1)S(1)}, bf16[24,256]{1,0:T(8,128)(2,1)S(1)}, u32[]{:S(2)}, u32[]{:S(2)}) %collective-permute-start.47) | collective-permute-done | bytes 12320 | tf_op jit(solution)/shard_map/ppermute | solution.py:26
  117.7 5.1 %collective-permute-done.48 = bf16[24,256]{1,0:T(8,128)(2,1)S(1)} collective-permute-done((bf16[24,256]{1,0:T(8,128)(2,1)S(1)}, bf16[24,256]{1,0:T(8,128)(2,1)S(1)}, u32[]{:S(2)}, u32[]{:S(2)}) %collective-permute-start.48) | collective-permute-done | bytes 12320 | tf_op jit(solution)/shard_map/ppermute | solution.py:26
  125.4 2.3 %collective-permute-start.6 = (f32[24,256]{1,0:T(8,128)S(1)}, f32[24,256]{1,0:T(8,128)S(1)}, u32[]{:S(2)}, u32[]{:S(2)}) collective-permute-start(f32[24,256]{1,0:T(8,128)S(1)} %broadcast_multiply_fusion), channel_id=1, source_target_pairs={{0,28},{4,24},{8,20},{12,16},{16,12},{20,8},{24,4},{28,0},{1,29},{... | collective-permute-start | bytes 73736 | tf_op jit(solution)/shard_map/ppermute | solution.py:26
  133.4 5.6 %collective-permute-done.18 = bf16[192,256]{1,0:T(8,128)(2,1)S(1)} collective-permute-done((bf16[192,256]{1,0:T(8,128)(2,1)S(1)}, bf16[192,256]{1,0:T(8,128)(2,1)S(1)}, u32[]{:S(2)}, u32[]{:S(2)}) %collective-permute-start.18) | collective-permute-done | bytes 98336 | tf_op jit(solution)/shard_map/ppermute | solution.py:26
  148.8 2.4 %collective-permute-start.26 = (bf16[128,1024]{1,0:T(8,128)(2,1)}, bf16[128,1024]{1,0:T(8,128)(2,1)}, u32[]{:S(2)}, u32[]{:S(2)}) collective-permute-start(bf16[128,1024]{1,0:T(8,128)(2,1)} %constant_dynamic-slice_fusion.1), channel_id=1, source_target_pairs={{0,2},{1,3},{2,0},{3,1},{4,6},{5,7},{6,4},{7,5},{8,10},{9,11},{10,... | collective-permute-start | bytes 786440 | tf_op jit(solution)/shard_map/ppermute | solution.py:26
  158.5 4.2 %collective-permute-done.22 = bf16[128,1024]{1,0:T(8,128)(2,1)} collective-permute-done((bf16[128,1024]{1,0:T(8,128)(2,1)}, bf16[128,1024]{1,0:T(8,128)(2,1)}, u32[]{:S(2)}, u32[]{:S(2)}) %collective-permute-start.22) | collective-permute-done | bytes 262176 | tf_op jit(solution)/shard_map/ppermute | solution.py:26
  165.4 2.9 %collective-permute-done.39 = bf16[128,1024]{1,0:T(8,128)(2,1)} collective-permute-done((bf16[128,1024]{1,0:T(8,128)(2,1)}, bf16[128,1024]{1,0:T(8,128)(2,1)}, u32[]{:S(2)}, u32[]{:S(2)}) %collective-permute-start.39) | collective-permute-done | bytes 262176 | tf_op jit(solution)/shard_map/ppermute | solution.py:26
  169.3 3.0 %collective-permute-done.27 = bf16[128,1024]{1,0:T(8,128)(2,1)S(1)} collective-permute-done((bf16[128,1024]{1,0:T(8,128)(2,1)}, bf16[128,1024]{1,0:T(8,128)(2,1)S(1)}, u32[]{:S(2)}, u32[]{:S(2)}) %collective-permute-start.27) | collective-permute-done | bytes 262176 | tf_op jit(solution)/shard_map/ppermute | solution.py:26
  174.7 2.8 %pad_maximum_fusion = bf16[4,256,1024]{2,1,0:T(8,128)(2,1)} fusion(bf16[1,256,1024]{2,1,0:T(8,128)(2,1)S(1)} %get-tuple-element.33, bf16[1,256,1024]{2,1,0:T(8,128)(2,1)S(1)} %get-tuple-element.32, bf16[1,256,1024]{2,1,0:T(8,128)(2,1)} %bitcast.45, bf16[1,256,1024]{2,1,0:T(8,128)(2,1)} %bitcast.44), kind=kLoop, calls=%fused_computation.22 | loop fusion | flops 3145728 | bytes 4194304 | tf_op jit(solution)/shard_map/stack | solution.py:64
  177.5 3.6 %gather_fusion.4 = bf16[4,256,1024]{2,1,0:T(8,128)(2,1)} fusion(bf16[4,256,1024]{2,1,0:T(8,128)(2,1)} %pad_maximum_fusion, s32[1024]{0:T(1024)S(1)} %pad_clamp_fusion), kind=kCustom, calls=%fused_computation.4 | custom fusion | bytes 4194320 | tf_op jit(solution)/shard_map/gather | solution.py:65
  182.4 2.8 %pad_maximum_fusion.2 = bf16[4,256,1024]{2,1,0:T(8,128)(2,1)} fusion(bf16[1,256,1024]{2,1,0:T(8,128)(2,1)S(1)} %get-tuple-element.35, bf16[1,256,1024]{2,1,0:T(8,128)(2,1)S(1)} %get-tuple-element.34, bf16[1,256,1024]{2,1,0:T(8,128)(2,1)} %bitcast.64, bf16[1,256,1024]{2,1,0:T(8,128)(2,1)} %bitcast.63), kind=kLoop, calls=%fused_computation.24 | loop fusion | flops 3145728 | bytes 4194304 | tf_op jit(solution)/shard_map/stack | solution.py:64
  185.2 3.6 %gather_fusion.7 = bf16[4,256,1024]{2,1,0:T(8,128)(2,1)} fusion(bf16[4,256,1024]{2,1,0:T(8,128)(2,1)} %pad_maximum_fusion.2, s32[1024]{0:T(1024)S(1)} %pad_clamp_fusion), kind=kCustom, calls=%fused_computation.7 | custom fusion | bytes 4194320 | tf_op jit(solution)/shard_map/gather | solution.py:65
  190.0 2.7 %pad_maximum_fusion.1 = bf16[4,256,1024]{2,1,0:T(8,128)(2,1)} fusion(bf16[1,256,1024]{2,1,0:T(8,128)(2,1)S(1)} %get-tuple-element.37, bf16[1,256,1024]{2,1,0:T(8,128)(2,1)S(1)} %get-tuple-element.36, bf16[1,256,1024]{2,1,0:T(8,128)(2,1)} %bitcast.50, bf16[1,256,1024]{2,1,0:T(8,128)(2,1)S(1)} %bitcast.171), kind=kLoop, calls=%fused_computation.23 | loop fusion | flops 3145728 | bytes 4194304 | tf_op jit(solution)/shard_map/stack | solution.py:64
  192.7 3.7 %gather_fusion.5 = bf16[4,256,1024]{2,1,0:T(8,128)(2,1)} fusion(bf16[4,256,1024]{2,1,0:T(8,128)(2,1)} %pad_maximum_fusion.1, s32[1024]{0:T(1024)S(1)} %pad_clamp_fusion), kind=kCustom, calls=%fused_computation.5 | custom fusion | bytes 4194320 | tf_op jit(solution)/shard_map/gather | solution.py:65
  203.4 2.6 %fusion.13 = f32[192,1024]{1,0:T(8,128)S(1)} fusion(bf16[192,1024]{1,0:T(8,128)(2,1)S(1)} %get-tuple-element.5, bf16[1024,1024]{1,0:T(8,128)(2,1)} %bitcast.168, f32[192]{0:T(256)S(1)} %max.17, s32[192,192]{1,0:T(8,128)S(1)} %copy-done.15), kind=kOutput, calls=%fused_computation.43 | convolution fusion | flops 478580736 | bytes 3425024 | tf_op jit(solution)/shard_map/dot_general | solution.py:73
  (212 shorter events, 85.0 us)
Async XLA Ops:
  33.0 46.3 %collective-permute-start.10 = (bf16[24,256]{1,0:T(8,128)(2,1)S(1)}, bf16[24,256]{1,0:T(8,128)(2,1)S(1)}, u32[]{:S(2)}, u32[]{:S(2)}) collective-permute-start(bf16[24,256]{1,0:T(8,128)(2,1)S(1)} %convert_element_type.73), channel_id=1, source_target_pairs={{0,4},{4,0},{8,12},{12,8},{16,20},{20,16},{24,28},{28,24},{1,5},{5... | collective-permute-start | bytes 36872 | tf_op jit(solution)/shard_map/ppermute | solution.py:26
  36.0 44.9 %collective-permute-start.11 = (bf16[24,256]{1,0:T(8,128)(2,1)S(1)}, bf16[24,256]{1,0:T(8,128)(2,1)S(1)}, u32[]{:S(2)}, u32[]{:S(2)}) collective-permute-start(bf16[24,256]{1,0:T(8,128)(2,1)S(1)} %convert_element_type.73), channel_id=1, source_target_pairs={{0,8},{4,12},{8,0},{12,4},{16,24},{20,28},{24,16},{28,20},{1,9},{5... | collective-permute-start | bytes 36872 | tf_op jit(solution)/shard_map/ppermute | solution.py:26
  37.6 45.6 %collective-permute-start.12 = (bf16[24,256]{1,0:T(8,128)(2,1)S(1)}, bf16[24,256]{1,0:T(8,128)(2,1)S(1)}, u32[]{:S(2)}, u32[]{:S(2)}) collective-permute-start(bf16[24,256]{1,0:T(8,128)(2,1)S(1)} %convert_element_type.73), channel_id=1, source_target_pairs={{0,12},{4,8},{8,4},{12,0},{16,28},{20,24},{24,20},{28,16},{1,13},{... | collective-permute-start | bytes 36872 | tf_op jit(solution)/shard_map/ppermute | solution.py:26
  37.6 47.1 %collective-permute-start.13 = (bf16[24,256]{1,0:T(8,128)(2,1)S(1)}, bf16[24,256]{1,0:T(8,128)(2,1)S(1)}, u32[]{:S(2)}, u32[]{:S(2)}) collective-permute-start(bf16[24,256]{1,0:T(8,128)(2,1)S(1)} %convert_element_type.73), channel_id=1, source_target_pairs={{0,16},{4,20},{8,24},{12,28},{16,0},{20,4},{24,8},{28,12},{1,17},{... | collective-permute-start | bytes 36872 | tf_op jit(solution)/shard_map/ppermute | solution.py:26
  76.7 8.1 %collective-permute-start.14 = (bf16[24,256]{1,0:T(8,128)(2,1)S(1)}, bf16[24,256]{1,0:T(8,128)(2,1)S(1)}, u32[]{:S(2)}, u32[]{:S(2)}) collective-permute-start(bf16[24,256]{1,0:T(8,128)(2,1)S(1)} %convert_element_type.73), channel_id=1, source_target_pairs={{0,20},{4,16},{8,28},{12,24},{16,4},{20,0},{24,12},{28,8},{1,21},{... | collective-permute-start | bytes 36872 | tf_op jit(solution)/shard_map/ppermute | solution.py:26
  79.3 7.4 %collective-permute-start.15 = (bf16[24,256]{1,0:T(8,128)(2,1)S(1)}, bf16[24,256]{1,0:T(8,128)(2,1)S(1)}, u32[]{:S(2)}, u32[]{:S(2)}) collective-permute-start(bf16[24,256]{1,0:T(8,128)(2,1)S(1)} %convert_element_type.73), channel_id=1, source_target_pairs={{0,24},{4,28},{8,16},{12,20},{16,8},{20,12},{24,0},{28,4},{1,25},{... | collective-permute-start | bytes 36872 | tf_op jit(solution)/shard_map/ppermute | solution.py:26
  80.9 7.9 %collective-permute-start.16 = (bf16[24,256]{1,0:T(8,128)(2,1)S(1)}, bf16[24,256]{1,0:T(8,128)(2,1)S(1)}, u32[]{:S(2)}, u32[]{:S(2)}) collective-permute-start(bf16[24,256]{1,0:T(8,128)(2,1)S(1)} %convert_element_type.73), channel_id=1, source_target_pairs={{0,28},{4,24},{8,20},{12,16},{16,12},{20,8},{24,4},{28,0},{1,29},{... | collective-permute-start | bytes 36872 | tf_op jit(solution)/shard_map/ppermute | solution.py:26
  83.2 40.8 %collective-permute-start = (f32[24,256]{1,0:T(8,128)S(1)}, f32[24,256]{1,0:T(8,128)S(1)}, u32[]{:S(2)}, u32[]{:S(2)}) collective-permute-start(f32[24,256]{1,0:T(8,128)S(1)} %broadcast_multiply_fusion), channel_id=1, source_target_pairs={{0,4},{4,0},{8,12},{12,8},{16,20},{20,16},{24,28},{28,24},{1,5},{5... | collective-permute-start | bytes 73736 | tf_op jit(solution)/shard_map/ppermute | solution.py:26
  84.7 40.7 %collective-permute-start.1 = (f32[24,256]{1,0:T(8,128)S(1)}, f32[24,256]{1,0:T(8,128)S(1)}, u32[]{:S(2)}, u32[]{:S(2)}) collective-permute-start(f32[24,256]{1,0:T(8,128)S(1)} %broadcast_multiply_fusion), channel_id=1, source_target_pairs={{0,8},{4,12},{8,0},{12,4},{16,24},{20,28},{24,16},{28,20},{1,9},{5... | collective-permute-start | bytes 73736 | tf_op jit(solution)/shard_map/ppermute | solution.py:26
  84.9 42.9 %collective-permute-start.2 = (f32[24,256]{1,0:T(8,128)S(1)}, f32[24,256]{1,0:T(8,128)S(1)}, u32[]{:S(2)}, u32[]{:S(2)}) collective-permute-start(f32[24,256]{1,0:T(8,128)S(1)} %broadcast_multiply_fusion), channel_id=1, source_target_pairs={{0,12},{4,8},{8,4},{12,0},{16,28},{20,24},{24,20},{28,16},{1,13},{... | collective-permute-start | bytes 73736 | tf_op jit(solution)/shard_map/ppermute | solution.py:26
  86.7 41.1 %collective-permute-start.3 = (f32[24,256]{1,0:T(8,128)S(1)}, f32[24,256]{1,0:T(8,128)S(1)}, u32[]{:S(2)}, u32[]{:S(2)}) collective-permute-start(f32[24,256]{1,0:T(8,128)S(1)} %broadcast_multiply_fusion), channel_id=1, source_target_pairs={{0,16},{4,20},{8,24},{12,28},{16,0},{20,4},{24,8},{28,12},{1,17},{... | collective-permute-start | bytes 73736 | tf_op jit(solution)/shard_map/ppermute | solution.py:26
  122.9 6.5 %collective-permute-start.4 = (f32[24,256]{1,0:T(8,128)S(1)}, f32[24,256]{1,0:T(8,128)S(1)}, u32[]{:S(2)}, u32[]{:S(2)}) collective-permute-start(f32[24,256]{1,0:T(8,128)S(1)} %broadcast_multiply_fusion), channel_id=1, source_target_pairs={{0,20},{4,16},{8,28},{12,24},{16,4},{20,0},{24,12},{28,8},{1,21},{... | collective-permute-start | bytes 73736 | tf_op jit(solution)/shard_map/ppermute | solution.py:26
  125.4 6.5 %collective-permute-start.6 = (f32[24,256]{1,0:T(8,128)S(1)}, f32[24,256]{1,0:T(8,128)S(1)}, u32[]{:S(2)}, u32[]{:S(2)}) collective-permute-start(f32[24,256]{1,0:T(8,128)S(1)} %broadcast_multiply_fusion), channel_id=1, source_target_pairs={{0,28},{4,24},{8,20},{12,16},{16,12},{20,8},{24,4},{28,0},{1,29},{... | collective-permute-start | bytes 73736 | tf_op jit(solution)/shard_map/ppermute | solution.py:26
  127.7 46.5 %collective-permute-start.20 = (bf16[256,1024]{1,0:T(8,128)(2,1)}, bf16[256,1024]{1,0:T(8,128)(2,1)}, u32[]{:S(2)}, u32[]{:S(2)}) collective-permute-start(bf16[256,1024]{1,0:T(8,128)(2,1)} %param.9), channel_id=1, source_target_pairs={{0,1},{1,0},{2,3},{3,2},{4,5},{5,4},{6,7},{7,6},{8,9},{9,8},{10,11... | collective-permute-start | bytes 1572872 | tf_op jit(solution)/shard_map/ppermute | solution.py:26
  127.8 21.0 %collective-permute-start.21 = (bf16[128,1024]{1,0:T(8,128)(2,1)S(1)}, bf16[128,1024]{1,0:T(8,128)(2,1)}, u32[]{:S(2)}, u32[]{:S(2)}) collective-permute-start(bf16[128,1024]{1,0:T(8,128)(2,1)S(1)} %constant_dynamic-slice_fusion.2), channel_id=1, source_target_pairs={{0,2},{1,3},{2,0},{3,1},{4,6},{5,7},{6,4},{7,5},{8,10},{9,11},{10,... | collective-permute-start | bytes 786440 | tf_op jit(solution)/shard_map/ppermute | solution.py:26
  129.3 9.7 %collective-permute-start.18 = (bf16[192,256]{1,0:T(8,128)(2,1)S(1)}, bf16[192,256]{1,0:T(8,128)(2,1)S(1)}, u32[]{:S(2)}, u32[]{:S(2)}) collective-permute-start(bf16[192,256]{1,0:T(8,128)(2,1)S(1)} %bitcast.178), channel_id=1, source_target_pairs={{0,2},{1,3},{2,0},{3,1},{4,6},{5,7},{6,4},{7,5},{8,10},{9,11},{10,... | collective-permute-start | bytes 294920 | tf_op jit(solution)/shard_map/ppermute | solution.py:26
  130.0 9.6 %collective-permute-start.17 = (bf16[192,256]{1,0:T(8,128)(2,1)S(1)}, bf16[192,256]{1,0:T(8,128)(2,1)S(1)}, u32[]{:S(2)}, u32[]{:S(2)}) collective-permute-start(bf16[192,256]{1,0:T(8,128)(2,1)S(1)} %bitcast.179), channel_id=1, source_target_pairs={{0,1},{1,0},{2,3},{3,2},{4,5},{5,4},{6,7},{7,6},{8,9},{9,8},{10,11... | collective-permute-start | bytes 294920 | tf_op jit(solution)/shard_map/ppermute | solution.py:26
  131.9 8.8 %collective-permute-start.50 = (bf16[192,256]{1,0:T(8,128)(2,1)S(1)}, bf16[192,256]{1,0:T(8,128)(2,1)S(1)}, u32[]{:S(2)}, u32[]{:S(2)}) collective-permute-start(bf16[192,256]{1,0:T(8,128)(2,1)S(1)} %bitcast.175), channel_id=1, source_target_pairs={{0,2},{1,3},{2,0},{3,1},{4,6},{5,7},{6,4},{7,5},{8,10},{9,11},{10,... | collective-permute-start | bytes 294920 | tf_op jit(solution)/shard_map/ppermute | solution.py:26
  140.7 6.8 %collective-permute-start.8 = (f32[192,256]{1,0:T(8,128)S(1)}, f32[192,256]{1,0:T(8,128)}, u32[]{:S(2)}, u32[]{:S(2)}) collective-permute-start(f32[192,256]{1,0:T(8,128)S(1)} %bitcast.172), channel_id=1, source_target_pairs={{0,2},{1,3},{2,0},{3,1},{4,6},{5,7},{6,4},{7,5},{8,10},{9,11},{10,... | collective-permute-start | bytes 589832 | tf_op jit(solution)/shard_map/ppermute | solution.py:26
  143.7 9.4 %collective-permute-start.38 = (bf16[128,1024]{1,0:T(8,128)(2,1)S(1)}, bf16[128,1024]{1,0:T(8,128)(2,1)}, u32[]{:S(2)}, u32[]{:S(2)}) collective-permute-start(bf16[128,1024]{1,0:T(8,128)(2,1)S(1)} %constant_dynamic-slice_fusion), channel_id=1, source_target_pairs={{0,2},{1,3},{2,0},{3,1},{4,6},{5,7},{6,4},{7,5},{8,10},{9,11},{10,... | collective-permute-start | bytes 786440 | tf_op jit(solution)/shard_map/ppermute | solution.py:26
  147.5 7.3 %collective-permute-start.9 = (f32[192,256]{1,0:T(8,128)}, f32[192,256]{1,0:T(8,128)S(1)}, u32[]{:S(2)}, u32[]{:S(2)}) collective-permute-start(f32[192,256]{1,0:T(8,128)} %collective-permute-done.8), channel_id=1, source_target_pairs={{0,1},{1,0},{2,3},{3,2},{4,5},{5,4},{6,7},{7,6},{8,9},{9,8},{10,11... | collective-permute-start | bytes 589832 | tf_op jit(solution)/shard_map/ppermute | solution.py:26
  148.3 34.1 %collective-permute-start.37 = (bf16[256,1024]{1,0:T(8,128)(2,1)}, bf16[256,1024]{1,0:T(8,128)(2,1)}, u32[]{:S(2)}, u32[]{:S(2)}) collective-permute-start(bf16[256,1024]{1,0:T(8,128)(2,1)} %param.11), channel_id=1, source_target_pairs={{0,1},{1,0},{2,3},{3,2},{4,5},{5,4},{6,7},{7,6},{8,9},{9,8},{10,11... | collective-permute-start | bytes 1572872 | tf_op jit(solution)/shard_map/ppermute | solution.py:26
  148.8 9.7 %collective-permute-start.26 = (bf16[128,1024]{1,0:T(8,128)(2,1)}, bf16[128,1024]{1,0:T(8,128)(2,1)}, u32[]{:S(2)}, u32[]{:S(2)}) collective-permute-start(bf16[128,1024]{1,0:T(8,128)(2,1)} %constant_dynamic-slice_fusion.1), channel_id=1, source_target_pairs={{0,2},{1,3},{2,0},{3,1},{4,6},{5,7},{6,4},{7,5},{8,10},{9,11},{10,... | collective-permute-start | bytes 786440 | tf_op jit(solution)/shard_map/ppermute | solution.py:26
  153.1 9.5 %collective-permute-start.22 = (bf16[128,1024]{1,0:T(8,128)(2,1)}, bf16[128,1024]{1,0:T(8,128)(2,1)}, u32[]{:S(2)}, u32[]{:S(2)}) collective-permute-start(bf16[128,1024]{1,0:T(8,128)(2,1)} %collective-permute-done.21), channel_id=1, source_target_pairs={{0,4},{4,0},{8,12},{12,8},{16,20},{20,16},{24,28},{28,24},{1,5},{5... | collective-permute-start | bytes 786440 | tf_op jit(solution)/shard_map/ppermute | solution.py:26
  154.8 13.5 %collective-permute-start.39 = (bf16[128,1024]{1,0:T(8,128)(2,1)}, bf16[128,1024]{1,0:T(8,128)(2,1)}, u32[]{:S(2)}, u32[]{:S(2)}) collective-permute-start(bf16[128,1024]{1,0:T(8,128)(2,1)} %collective-permute-done.38), channel_id=1, source_target_pairs={{0,4},{4,0},{8,12},{12,8},{16,20},{20,16},{24,28},{28,24},{1,5},{5... | collective-permute-start | bytes 786440 | tf_op jit(solution)/shard_map/ppermute | solution.py:26
  158.5 15.0 %collective-permute-start.23 = (bf16[128,1024]{1,0:T(8,128)(2,1)}, bf16[128,1024]{1,0:T(8,128)(2,1)S(1)}, u32[]{:S(2)}, u32[]{:S(2)}) collective-permute-start(bf16[128,1024]{1,0:T(8,128)(2,1)} %collective-permute-done.21), channel_id=1, source_target_pairs={{0,1},{1,0},{2,3},{3,2},{4,5},{5,4},{6,7},{7,6},{8,9},{9,8},{10,11... | collective-permute-start | bytes 786440 | tf_op jit(solution)/shard_map/ppermute | solution.py:26
  162.7 9.7 %collective-permute-start.27 = (bf16[128,1024]{1,0:T(8,128)(2,1)}, bf16[128,1024]{1,0:T(8,128)(2,1)S(1)}, u32[]{:S(2)}, u32[]{:S(2)}) collective-permute-start(bf16[128,1024]{1,0:T(8,128)(2,1)} %collective-permute-done.26), channel_id=1, source_target_pairs={{0,4},{4,0},{8,12},{12,8},{16,20},{20,16},{24,28},{28,24},{1,5},{5... | collective-permute-start | bytes 786440 | tf_op jit(solution)/shard_map/ppermute | solution.py:26
  172.4 17.6 %collective-permute-start.25 = (bf16[256,1024]{1,0:T(8,128)(2,1)S(1)}, bf16[256,1024]{1,0:T(8,128)(2,1)}, u32[]{:S(2)}, u32[]{:S(2)}) collective-permute-start(bf16[256,1024]{1,0:T(8,128)(2,1)S(1)} %copy-done.5), channel_id=1, source_target_pairs={{0,1},{1,0},{2,3},{3,2},{4,5},{5,4},{6,7},{7,6},{8,9},{9,8},{10,11... | collective-permute-start | bytes 1572872 | tf_op jit(solution)/shard_map/ppermute | solution.py:26
  173.5 7.6 %collective-permute-start.40 = (bf16[128,1024]{1,0:T(8,128)(2,1)}, bf16[128,1024]{1,0:T(8,128)(2,1)}, u32[]{:S(2)}, u32[]{:S(2)}) collective-permute-start(bf16[128,1024]{1,0:T(8,128)(2,1)} %collective-permute-done.38), channel_id=1, source_target_pairs={{0,1},{1,0},{2,3},{3,2},{4,5},{5,4},{6,7},{7,6},{8,9},{9,8},{10,11... | collective-permute-start | bytes 786440 | tf_op jit(solution)/shard_map/ppermute | solution.py:26
  174.0 7.2 %collective-permute-start.41 = (bf16[128,1024]{1,0:T(8,128)(2,1)}, bf16[128,1024]{1,0:T(8,128)(2,1)}, u32[]{:S(2)}, u32[]{:S(2)}) collective-permute-start(bf16[128,1024]{1,0:T(8,128)(2,1)} %collective-permute-done.39), channel_id=1, source_target_pairs={{0,1},{1,0},{2,3},{3,2},{4,5},{5,4},{6,7},{7,6},{8,9},{9,8},{10,11... | collective-permute-start | bytes 786440 | tf_op jit(solution)/shard_map/ppermute | solution.py:26
  174.2 14.6 %collective-permute-start.28 = (bf16[128,1024]{1,0:T(8,128)(2,1)}, bf16[128,1024]{1,0:T(8,128)(2,1)}, u32[]{:S(2)}, u32[]{:S(2)}) collective-permute-start(bf16[128,1024]{1,0:T(8,128)(2,1)} %collective-permute-done.26), channel_id=1, source_target_pairs={{0,1},{1,0},{2,3},{3,2},{4,5},{5,4},{6,7},{7,6},{8,9},{9,8},{10,11... | collective-permute-start | bytes 786440 | tf_op jit(solution)/shard_map/ppermute | solution.py:26
  181.1 7.7 %collective-permute-start.29 = (bf16[128,1024]{1,0:T(8,128)(2,1)}, bf16[128,1024]{1,0:T(8,128)(2,1)}, u32[]{:S(2)}, u32[]{:S(2)}) collective-permute-start(bf16[128,1024]{1,0:T(8,128)(2,1)} %copy-done.10), channel_id=1, source_target_pairs={{0,1},{1,0},{2,3},{3,2},{4,5},{5,4},{6,7},{7,6},{8,9},{9,8},{10,11... | collective-permute-start | bytes 786440 | tf_op jit(solution)/shard_map/ppermute | solution.py:26
  (43 other events, 204.4 us)

commit v3 on v1

v3 whole, which is shorter than its diff:
```python
import functools

import jax
import jax.numpy as jnp
from jax import lax
from jax.experimental import pallas as pl
from jax.experimental.pallas import tpu as pltpu
from jax.sharding import PartitionSpec as P

HD = 64
BF = jnp.bfloat16
F32 = jnp.float32
NODES_STEP = 3
WIDE_LIMIT = 256
IDS_COLS = 128
MIB = 1 << 20


def dot_t(a, b):
    return lax.dot_general(a, b, (((1,), (1,)), ((), ())), preferred_element_type=F32)


def t_dot(a, b):
    return lax.dot_general(a, b, (((0,), (0,)), ((), ())), preferred_element_type=F32)


def dot(a, b):
    return jnp.dot(a, b, preferred_element_type=F32)


def attention_kernel(heads, place_ref, x_ref, w_ref, cot_ref, ids_ref, out_ref, wp, acc_p, acc_m):
    step = pl.program_id(0)
    nodes, seq, width = x_ref.shape
    cols = heads * HD

    @pl.when(step == 0)
    def _():
        for part in range(3):
            for h in range(0, heads, 2):
                a = h * 3 * HD + part * HD
                b = a + 3 * HD
                wp[:, part * cols + h * HD : part * cols + (h + 2) * HD] = jnp.concatenate(
                    [w_ref[:, a : a + HD], w_ref[:, b : b + HD]], axis=1
                )

    own = pl.ds(pl.multiple_of(place_ref[0] * cols, 128), cols)
    qkv = dot(x_ref[...].reshape(nodes * seq, width), wp[...]).astype(BF)
    lane = lax.broadcasted_iota(jnp.int32, (seq, cols), 1) // HD
    row = lax.broadcasted_iota(jnp.int32, (heads * seq, cols), 0) // seq
    column = lax.broadcasted_iota(jnp.int32, (heads * seq, cols), 1) // HD
    ones = (row == column).astype(F32).astype(BF)
    zero = jnp.zeros((seq, cols), BF)
    for n in range(nodes):
        at = slice(n * seq, (n + 1) * seq)
        q, k, v = (qkv[at, i * cols : (i + 1) * cols] for i in range(3))
        spread = jnp.concatenate([jnp.where(lane == h, q, zero) for h in range(heads)], axis=0)
        s = dot_t(k, spread)
        e = jnp.exp((s - jnp.max(s, axis=0, keepdims=True)) * (HD**-0.5))
        p = (e * (1.0 / jnp.sum(e, axis=0, keepdims=True))).astype(BF)
        weight = dot(p, ones)
        context = jnp.sum(weight * v.astype(F32), axis=0, keepdims=True)
        acc_p[pl.ds(step * nodes + n, 1), :] = context * (1.0 / seq)
        mean = jnp.sum(x_ref[n, :, own].astype(F32), axis=0, keepdims=True)
        acc_m[pl.ds(step * nodes + n, 1), :] = mean * (1.0 / seq)

    @pl.when(step == pl.num_programs(0) - 1)
    def _():
        out_ref[:, :cols] = acc_p[...].astype(BF)
        out_ref[:, cols : 2 * cols] = cot_ref[...]
        out_ref[:, 2 * cols : 3 * cols] = acc_m[...].astype(BF)
        out_ref[:, 3 * cols :] = ids_ref[...]


def attention(place, texts, w_qkv, cotangent, ids):
    node_dev, seq, width = texts.shape
    cols = w_qkv.shape[1] // 3
    heads = cols // HD
    tokens = node_dev * seq
    return pl.pallas_call(
        functools.partial(attention_kernel, heads),
        out_shape=jax.ShapeDtypeStruct((node_dev, 3 * cols + IDS_COLS), BF),
        grid_spec=pltpu.PrefetchScalarGridSpec(
            num_scalar_prefetch=1,
            grid=(node_dev // NODES_STEP,),
            in_specs=[
                pl.BlockSpec((NODES_STEP, seq, width), lambda i, _: (i, 0, 0)),
                pl.BlockSpec((width, 3 * cols), lambda i, _: (0, 0)),
                pl.BlockSpec((node_dev, cols), lambda i, _: (0, 0)),
                pl.BlockSpec((node_dev, IDS_COLS), lambda i, _: (0, 0)),
            ],
            out_specs=pl.BlockSpec((node_dev, 3 * cols + IDS_COLS), lambda i, _: (0, 0)),
            scratch_shapes=[
                pltpu.VMEM((width, 3 * cols), BF),
                pltpu.VMEM((node_dev, cols), F32),
                pltpu.VMEM((node_dev, cols), F32),
            ],
        ),
        compiler_params=pltpu.CompilerParams(vmem_limit_bytes=40 * MIB),
        cost_estimate=pl.CostEstimate(
            flops=2 * tokens * width * 3 * cols + 8 * tokens * seq * cols,
            bytes_accessed=2 * tokens * width + 6 * width * cols,
            transcendentals=tokens * seq * heads,
        ),
    )(place, texts, w_qkv, cotangent, ids)


def gelu_parts(z):
    root = 0.7978845608028654
    cube = 0.044715
    t = jnp.tanh(root * (z + cube * (z * z * z)))
    half = 0.5 * (1.0 + t)
    slope = half + 0.5 * z * (1.0 - t * t) * (root * (1.0 + 3.0 * cube * (z * z)))
    return z * half, slope


def graph_kernel(
    place_ref, got_ref, *refs
):
    blocks, (mixed_ref, grad_ref, g_self, g_neigh, g_out), scratch = refs[:6], refs[6:11], refs[11:]
    w, pooled, embed, agg, dz, node_grad, wide, sem = scratch
    mp, dp = place_ref[0], place_ref[1]
    rows, cols = g_self.shape[0], g_self.shape[0]
    groups, node_dev = got_ref.shape[1], got_ref.shape[2]
    nodes = groups * node_dev
    parts = got_ref.shape[0]
    width = parts * cols
    own = pl.ds(pl.multiple_of(mp * cols, 128), cols)

    copies = []
    for k in range(3):
        pair = [pltpu.make_async_copy(blocks[k], w.at[k, mp], sem.at[k, 0])]
        for r in range(1, parts):
            pair.append(
                pltpu.make_async_copy(
                    blocks[2 + r].at[pl.ds(k * rows, rows)], w.at[k, mp ^ r], sem.at[k, r]
                )
            )
        copies.append(pair)
    for pair in copies:
        for c in pair:
            c.start()

    def part(m, i, size=cols):
        return got_ref[m, :, :, i : i + size].astype(F32).reshape(nodes, size)

    for m in range(parts):
        pooled[:, m * cols : (m + 1) * cols] = part(m, 0).astype(BF)

    packed = part(0, 3 * cols, IDS_COLS)
    fan = IDS_COLS // 8
    ids = packed[:, :fan] * 16.0 + packed[:, fan : 2 * fan] - 1.0
    cnt = jnp.maximum(jnp.sum((ids >= 0.0).astype(F32), axis=1, keepdims=True), 1.0)
    every = lax.broadcasted_iota(jnp.int32, (nodes, nodes), 1).astype(F32)
    counts = jnp.zeros((nodes, nodes), F32)
    for s in range(fan):
        counts += (ids[:, s : s + 1] == every).astype(F32)
    counts_t = counts.T.astype(BF)
    counts = counts.astype(BF)

    def whole(k):
        return w[k].reshape(width, width)

    for c in copies[0]:
        c.wait()
    sums = dot(pooled[...], whole(0))
    for m in range(parts):
        at = slice(m * cols, (m + 1) * cols)
        embed[:, at] = (part(m, 2 * cols) + sums[:, at]).astype(BF)
    agg[...] = (dot(counts, embed[...]) / cnt).astype(BF)
    for c in copies[1] + copies[2]:
        c.wait()
    z = dot(embed[...], whole(1)) + dot(agg[...], whole(2))
    mixed, slope = gelu_parts(z)
    wide[...] = mixed.reshape(groups, node_dev, width)
    mixed_ref[...] = wide[dp, :, own].astype(BF)
    for m in range(parts):
        at = slice(m * cols, (m + 1) * cols)
        dz[:, at] = (part(m, cols) * slope[:, at]).astype(BF)
    msg = (dot_t(dz[...], whole(2)) / cnt).astype(BF)
    total = dot_t(dz[...], whole(1)) + dot(counts_t, msg)
    node_grad[...] = total.astype(BF)
    wide[...] = total.reshape(groups, node_dev, width)
    grad_ref[...] = wide[dp, :, own].astype(BF)
    factor = 1.0 / jnp.sqrt(jnp.float32(nodes))
    g_self[...] = t_dot(embed[:, own], dz[...]) * factor
    g_neigh[...] = t_dot(agg[:, own], dz[...]) * factor
    g_out[...] = t_dot(pooled[:, own], node_grad[...]) * factor


def graph(place, got, weights, moved):
    parts, groups, node_dev, _ = got.shape
    cols, width = weights[0].shape
    nodes = groups * node_dev
    vmem = pl.BlockSpec(memory_space=pltpu.VMEM)
    slab = jax.ShapeDtypeStruct((node_dev, cols), BF)
    big = jax.ShapeDtypeStruct((cols, width), F32)
    return pl.pallas_call(
        graph_kernel,
        out_shape=(slab, slab, big, big, big),
        in_specs=[pl.BlockSpec(memory_space=pltpu.SMEM), vmem] + [pl.BlockSpec(memory_space=pl.ANY)] * 6,
        out_specs=(vmem,) * 5,
        scratch_shapes=[
            pltpu.VMEM((3, parts, cols, width), BF),
            pltpu.VMEM((nodes, width), BF),
            pltpu.VMEM((nodes, width), BF),
            pltpu.VMEM((nodes, width), BF),
            pltpu.VMEM((nodes, width), BF),
            pltpu.VMEM((nodes, width), BF),
            pltpu.VMEM((groups, node_dev, width), F32),
            pltpu.SemaphoreType.DMA((3, parts)),
        ],
        compiler_params=pltpu.CompilerParams(vmem_limit_bytes=48 * MIB),
        cost_estimate=pl.CostEstimate(
            flops=2 * nodes * width * width * 6, bytes_accessed=10 * MIB, transcendentals=nodes * width
        ),
    )(place, got, *weights, *moved)


def graph_wide(place, got, weights, moved):
    mp, dp = place[0], place[1]
    parts, groups, node_dev, _ = got.shape
    cols, width = weights[0].shape
    nodes = groups * node_dev
    order = jnp.arange(parts) ^ mp
    blocks = jnp.stack([jnp.concatenate(weights), *moved])[order].reshape(parts, 3, cols, width)
    w_out, w_self, w_neigh = (blocks[:, k].reshape(width, width) for k in range(3))

    def part(i):
        return got[..., i * cols : (i + 1) * cols].reshape(parts, nodes, cols).transpose(1, 0, 2).reshape(nodes, width)

    pooled = part(0)
    packed = got[0, :, :, 3 * cols :].reshape(nodes, IDS_COLS).astype(jnp.int32)
    fan = IDS_COLS // 8
    ids = packed[:, :fan] * 16 + packed[:, fan : 2 * fan] - 1
    cnt = jnp.maximum(jnp.sum(ids >= 0, axis=1).astype(F32), 1.0)[:, None]
    counts = jnp.sum(ids[:, :, None] == jnp.arange(nodes)[None, None, :], axis=1).astype(BF)
    embed = (part(2).astype(F32) + dot(pooled, w_out)).astype(BF)
    agg = (dot(counts, embed) / cnt).astype(BF)
    mixed, slope = gelu_parts(dot(embed, w_self) + dot(agg, w_neigh))
    dz = (part(1).astype(F32) * slope).astype(BF)
    msg = (dot_t(dz, w_neigh) / cnt).astype(BF)
    node_grad = (dot_t(dz, w_self) + t_dot(counts, msg)).astype(BF)
    factor = 1.0 / jnp.sqrt(jnp.float32(nodes))
    grads = [
        t_dot(lax.dynamic_slice_in_dim(a, mp * cols, cols, 1), b) * factor
        for a, b in ((embed, dz), (agg, dz), (pooled, node_grad))
    ]
    own = [
        lax.dynamic_slice(a, (dp * node_dev, mp * cols), (node_dev, cols)).astype(BF)
        for a in (mixed, node_grad)
    ]
    return (*own, *grads)


def hop(x, axis, bit):
    return lax.ppermute(x, axis, [(i, i ^ bit) for i in range(lax.axis_size(axis))])


def per_device(texts, w_qkv, w_out, w_self, w_neigh, neighbours, cotangent):
    node_dev = texts.shape[0]
    nodes = node_dev * lax.axis_size("dp")
    place = jnp.stack([lax.axis_index("mp"), lax.axis_index("dp")]).astype(jnp.int32)
    weights = (w_out, w_self, w_neigh)
    stacked = jnp.concatenate(weights)
    across = hop(stacked, "mp", 2)
    here = hop(stacked, "mp", 1)
    there = hop(across, "mp", 1)

    shifted = neighbours + 1
    fan = neighbours.shape[1]
    ids = jnp.concatenate([shifted // 16, shifted % 16], axis=1).astype(BF)
    ids = jnp.pad(ids, ((0, 0), (0, IDS_COLS - 2 * fan)))
    sent = attention(place, texts, w_qkv, cotangent, ids)
    got = lax.all_gather(sent, "dp", axis=0, tiled=False)
    got = lax.all_gather(got, "mp", axis=0, tiled=False)
    body = graph if nodes <= WIDE_LIMIT else graph_wide
    return body(place, got, weights, (here, across, there))


def solution(mesh):
    return jax.shard_map(
        per_device,
        mesh=mesh,
        in_specs=(
            P("dp", None, None),
            P(None, "mp"),
            P("mp", None),
            P("mp", None),
            P("mp", None),
            P("dp", None),
            P("dp", "mp"),
        ),
        out_specs=(P("dp", "mp"), P("dp", "mp"), P("mp", None), P("mp", None), P("mp", None)),
        check_vma=False,
    )
```

time: 225 us -> 99.9 us (0.44)
  blocking collectives: 153 us -> 33.2 us
  matrix products: 34.7 us -> 0 us
  Pallas kernels: 0 us -> 21.4 us
  waiting for transfers between devices: 2.1 us -> 18.2 us
  other arithmetic: 11 us -> 0.17 us
  starting transfers between devices: 0.11 us -> 3.54 us
    all_gather x4 -> x1, blocking collectives: 153 us -> 33.2 us  [per_device(): got = lax.all_gather(sent, 'dp', axis=0, tiled=False)]
    dot_general x12 -> x0, matrix products: 34.7 us -> none  [the longest x1 9.49 us: attention(): jnp.einsum('nld,de->nle', texts, w_qkv, preferred_element_type=F32)]
    pallas_call x0 -> x2, Pallas kernels: none -> 21.4 us  [the longest x1 13.9 us: attention(): pl.pallas_call(functools.partial(attention_kernel, heads), out_shape=jax....]
    all_gather x3 -> x1, waiting for transfers between devices: 0.04 us -> 13.7 us  [per_device(): got = lax.all_gather(got, 'mp', axis=0, tiled=False)]
    convert_element_type x3 -> x0, local copies, waits for them, and re-layouts: 6.95 us -> none  [the longest x1 6.7 us: attention(): jnp.einsum('nld,de->nle', texts, w_qkv, preferred_element_type=F32)]
    div x2 -> x0, other arithmetic: 6.81 us -> none  [the longest x1 6.81 us: attention(): jax.nn.softmax(scores / jnp.sqrt(jnp.float32(HD)), axis=-1).astype(BF)]
    unnamed x15 -> x19, local copies, waits for them, and re-layouts: 1.44 us -> 8.09 us
    ppermute x0 -> x3, waiting for transfers between devices: none -> 4.47 us  [hop(): lax.ppermute(x, axis, [(i, i ^ bit) for i in range(lax.axis_size(axis))])]
  transfers between devices with their start and end apart: 3 -> 4, of which waited for: 0 -> 2; matrix products, arithmetic and copies ran while one was open for 18% -> 0% of each run, Pallas kernels for 0% -> 14%
where the time goes in v3:
time: 99.9 us; the launch traced here: 99.6 us
  blocking collectives  33.2 us (33%)
  Pallas kernels  21.4 us (21%)
  waiting for transfers between devices  18.2 us (18%)
  between operations  14.1 us (14%)
  local copies, waits for them, and re-layouts  8.93 us (9%)
  starting transfers between devices  3.54 us (4%)
    all_gather x1, blocking collectives, per_device(): got = lax.all_gather(sent, 'dp', axis=0, tiled=False)  33.2 us
    pallas_call x1, Pallas kernels, attention(): pl.pallas_call(functools.partial(attention_kernel, heads), out_shape=jax....  13.9 us
    all_gather x1, waiting for transfers between devices, per_device(): got = lax.all_gather(got, 'mp', axis=0, tiled=False)  13.7 us
    unnamed x19, local copies, waits for them, and re-layouts  8.09 us
    pallas_call x1, Pallas kernels, graph(): pl.pallas_call(graph_kernel, out_shape=(slab, slab, big, big, big), in_sp...  7.52 us
    ppermute x3, waiting for transfers between devices, hop(): lax.ppermute(x, axis, [(i, i ^ bit) for i in range(lax.axis_size(axis))])  4.47 us
    ppermute x3, starting transfers between devices, hop(): lax.ppermute(x, axis, [(i, i ^ bit) for i in range(lax.axis_size(axis))])  3.5 us
  transfers between devices with their start and end apart: 4, of which 2 were waited for; matrix products, arithmetic and copies ran while one was open for 0% of the time, Pallas kernels for 14%

profile of v3, /device:TPU:0, one launch (start us, length us, event | category | flops | bytes accessed | tf_op | source)
XLA Modules:
  0.0 99.6 jit_solution(3096063587366131870)
XLA Ops:
  7.2 0.0 copy-start.2
  7.2 0.0 copy-start.7
  7.2 0.0 copy-start.6
  7.2 0.0 copy-start.4
  7.2 0.0 all-gather.4.cloned.1.call-start
  7.3 2.0 %constant_dynamic-update-slice_fusion.2 = bf16[768,1024]{1,0:T(8,128)(2,1)} fusion(bf16[256,1024]{1,0:T(8,128)(2,1)} %refs_0_.1), kind=kLoop, calls=%fused_computation.15 | loop fusion | bytes 1048576
  9.3 1.9 %constant_dynamic-update-slice_fusion.1 = bf16[768,1024]{1,0:T(8,128)(2,1)} fusion(bf16[768,1024]{1,0:T(8,128)(2,1)} %constant_dynamic-update-slice_fusion.2, bf16[256,1024]{1,0:T(8,128)(2,1)} %refs_1_.1), kind=kLoop, calls=%fused_computation.14 | loop fusion | bytes 1048576
  11.1 0.0 copy-done.2
  11.1 0.8 constant_dynamic-update-slice_fusion
  12.0 2.9 %collective-permute-start.1 = (bf16[768,1024]{1,0:T(8,128)(2,1)}, bf16[768,1024]{1,0:T(8,128)(2,1)}, u32[]{:S(2)}, u32[]{:S(2)}) collective-permute-start(bf16[768,1024]{1,0:T(8,128)(2,1)} %constant_dynamic-update-slice_fusion), channel_id=1, source_target_pairs={{0,2},{1,3},{2,0},{3,1},{4,6},{5,7},{6,4},{7,5},{8,10},{9,11},{10,... | collective-permute-start | bytes 4718600 | tf_op jit(solution)/shard_map/ppermute | solution.py:256
  14.9 0.0 copy-done.7
  14.9 0.1 copy.13
  15.0 0.1 pad_add_fusion.place_ref
  15.1 0.1 fusion.6.ids_ref
  15.2 0.0 copy-done.6
  15.2 0.0 copy-done.4
  15.2 0.0 copy-start.3
  15.2 2.8 %copy-done.3 = bf16[24,128,1024]{2,1,0:T(8,128)(2,1)S(1)} copy-done((bf16[24,128,1024]{2,1,0:T(8,128)(2,1)S(1)}, bf16[24,128,1024]{2,1,0:T(8,128)(2,1)}, u32[]{:S(2)}) %copy-start.3) | copy-done | bytes 6291480
  18.0 0.0 copy-start
  18.0 13.9 %shard_map.110 = bf16[24,896]{1,0:T(8,128)(2,1)S(1)} custom-call(s32[2]{0:T(128)S(1)} %pad_add_fusion.place_ref, bf16[24,128,1024]{2,1,0:T(8,128)(2,1)S(1)} %copy-done.3, bf16[1024,768]{1,0:T(8,128)(2,1)S(1)} %copy-done.4, bf16[24,256]{1,0:T(8,128)(2,1)S(1)} %copy-done.6, bf16[24,128]{1,0:T(8,128)(2,1)S(1)} %fusion.6.ids_ref), custom_call_target="tpu_custom_call" | custom-call | flops 5637144576 | bytes 7864320 | tf_op jit(solution)/shard_map/pallas_call | solution.py:79
  31.9 33.2 %all-gather = bf16[192,896]{1,0:T(8,128)(2,1)} all-gather(bf16[24,896]{1,0:T(8,128)(2,1)S(1)} %shard_map.110), channel_id=2, replica_groups=mesh['dp'=8,'mp'=4] {'dp'}, dimensions={0}, use_global_device_ids=true | all-gather | bytes 387072 | tf_op jit(solution)/shard_map/all_gather | solution.py:274
  65.1 0.0 all-gather.4.cloned.1.call-update
  65.1 0.1 collective-permute-start
  65.2 0.0 collective-permute-done.1.refs_4_
  65.2 0.5 collective-permute-start.2
  65.7 4.5 %collective-permute-done.refs_3_ = bf16[768,1024]{1,0:T(8,128)(2,1)S(1)} collective-permute-done((bf16[768,1024]{1,0:T(8,128)(2,1)}, bf16[768,1024]{1,0:T(8,128)(2,1)S(1)}, u32[]{:S(2)}, u32[]{:S(2)}) %collective-permute-start) | collective-permute-done | bytes 1572896 | tf_op jit(solution)/shard_map/ppermute | solution.py:256
  70.2 13.7 %all-gather.4.cloned.1.call-done = bf16[32,24,896]{2,1,0:T(8,128)(2,1)} async-done(((bf16[8,24,896]{2,1,0:T(8,128)(2,1)}), bf16[32,24,896]{2,1,0:T(8,128)(2,1)}) %all-gather.4.cloned.1.call-update) | async-done | bytes 1376272 | tf_op jit(solution)/shard_map/all_gather | solution.py:275
  83.9 0.0 collective-permute-done.2.refs_5_
  83.9 0.0 copy-done
  83.9 0.0 copy-done.1
  83.9 1.3 %copy-done.5 = bf16[32,24,896]{2,1,0:T(8,128)(2,1)S(1)} copy-done((bf16[32,24,896]{2,1,0:T(8,128)(2,1)S(1)}, bf16[32,24,896]{2,1,0:T(8,128)(2,1)}, u32[]{:S(2)}) %copy-start.5) | copy-done | bytes 1376280
  85.2 7.5 %shard_map.111 = (bf16[24,256]{1,0:T(8,128)(2,1)}, bf16[24,256]{1,0:T(8,128)(2,1)}, f32[256,1024]{1,0:T(8,128)}, f32[256,1024]{1,0:T(8,128)}, f32[256,1024]{1,0:T(8,128)}) custom-call(s32[2]{0:T(128)S(1)} %pad_add_fusion.place_ref, bf16[4,8,24,896]{3,2,1,0:T(8,128)(2,1)S(1)} %bitcast.4, bf16[256,1024]{1,0:T(8,128)(2,1)S(1)} %copy-done, ...), custom_call_target="tpu_custom_call" | custom-call | flops 2415919104 | bytes 10485760 | tf_op jit(solution)/shard_map/pallas_call | solution.py:197
  (3 shorter events, 0.0 us)
Async XLA Ops:
  7.2 4.0 %copy-start.2 = (bf16[256,1024]{1,0:T(8,128)(2,1)S(1)}, bf16[256,1024]{1,0:T(8,128)(2,1)}, u32[]{:S(2)}) copy-start(bf16[256,1024]{1,0:T(8,128)(2,1)} %refs_2_.1) | copy-start | bytes 1572868
  7.2 7.7 %copy-start.7 = (s32[24,16]{0,1:T(8,128)S(1)}, s32[24,16]{0,1:T(8,128)}, u32[]{:S(2)}) copy-start(s32[24,16]{0,1:T(8,128)} %param.12) | copy-start | bytes 4612
  7.2 8.0 %copy-start.6 = (bf16[24,256]{1,0:T(8,128)(2,1)S(1)}, bf16[24,256]{1,0:T(8,128)(2,1)}, u32[]{:S(2)}) copy-start(bf16[24,256]{1,0:T(8,128)(2,1)} %cot_ref.1) | copy-start | bytes 36868
  7.2 8.0 %copy-start.4 = (bf16[1024,768]{1,0:T(8,128)(2,1)S(1)}, bf16[1024,768]{1,0:T(8,128)(2,1)}, u32[]{:S(2)}) copy-start(bf16[1024,768]{1,0:T(8,128)(2,1)} %w_ref.1) | copy-start | bytes 4718596
  7.2 76.7 %all-gather.4.cloned.1.call-start = ((), (), s32[]{:S(2)}) async-start(), calls=%async_computation | async-start | bytes 1720320 | tf_op jit(solution)/shard_map/all_gather | solution.py:275
  12.0 53.2 %collective-permute-start.1 = (bf16[768,1024]{1,0:T(8,128)(2,1)}, bf16[768,1024]{1,0:T(8,128)(2,1)}, u32[]{:S(2)}, u32[]{:S(2)}) collective-permute-start(bf16[768,1024]{1,0:T(8,128)(2,1)} %constant_dynamic-update-slice_fusion), channel_id=1, source_target_pairs={{0,2},{1,3},{2,0},{3,1},{4,6},{5,7},{6,4},{7,5},{8,10},{9,11},{10,... | collective-permute-start | bytes 4718600 | tf_op jit(solution)/shard_map/ppermute | solution.py:256
  15.2 2.8 %copy-start.3 = (bf16[24,128,1024]{2,1,0:T(8,128)(2,1)S(1)}, bf16[24,128,1024]{2,1,0:T(8,128)(2,1)}, u32[]{:S(2)}) copy-start(bf16[24,128,1024]{2,1,0:T(8,128)(2,1)} %x_ref.1) | copy-start | bytes 18874372
  18.0 65.9 %copy-start = (bf16[256,1024]{1,0:T(8,128)(2,1)S(1)}, bf16[256,1024]{1,0:T(8,128)(2,1)}, u32[]{:S(2)}) copy-start(bf16[256,1024]{1,0:T(8,128)(2,1)} %refs_0_.1) | copy-start | bytes 1572868
  18.0 65.9 %copy-start.1 = (bf16[256,1024]{1,0:T(8,128)(2,1)S(1)}, bf16[256,1024]{1,0:T(8,128)(2,1)}, u32[]{:S(2)}) copy-start(bf16[256,1024]{1,0:T(8,128)(2,1)} %refs_1_.1) | copy-start | bytes 1572868
  65.1 5.0 %collective-permute-start = (bf16[768,1024]{1,0:T(8,128)(2,1)}, bf16[768,1024]{1,0:T(8,128)(2,1)S(1)}, u32[]{:S(2)}, u32[]{:S(2)}) collective-permute-start(bf16[768,1024]{1,0:T(8,128)(2,1)} %constant_dynamic-update-slice_fusion), channel_id=1, source_target_pairs={{0,1},{1,0},{2,3},{3,2},{4,5},{5,4},{6,7},{7,6},{8,9},{9,8},{10,11... | collective-permute-start | bytes 4718600 | tf_op jit(solution)/shard_map/ppermute | solution.py:256
  65.2 18.7 %collective-permute-start.2 = (bf16[768,1024]{1,0:T(8,128)(2,1)}, bf16[768,1024]{1,0:T(8,128)(2,1)}, u32[]{:S(2)}, u32[]{:S(2)}) collective-permute-start(bf16[768,1024]{1,0:T(8,128)(2,1)} %collective-permute-done.1.refs_4_), channel_id=1, source_target_pairs={{0,1},{1,0},{2,3},{3,2},{4,5},{5,4},{6,7},{7,6},{8,9},{9,8},{10,11... | collective-permute-start | bytes 4718600 | tf_op jit(solution)/shard_map/ppermute | solution.py:256
  83.9 1.3 %copy-start.5 = (bf16[32,24,896]{2,1,0:T(8,128)(2,1)S(1)}, bf16[32,24,896]{2,1,0:T(8,128)(2,1)}, u32[]{:S(2)}) copy-start(bf16[32,24,896]{2,1,0:T(8,128)(2,1)} %all-gather.4.cloned.1.call-done) | copy-start | bytes 4128772
Sparse Core Ops, SparseCore 0:
  65.2 18.5 all-gather.3

commit v4 on v3

--- a/solution.py
+++ b/solution.py
@@ -95,7 +95,7 @@
                 pltpu.VMEM((node_dev, cols), F32),
             ],
         ),
-        compiler_params=pltpu.CompilerParams(vmem_limit_bytes=40 * MIB),
+        compiler_params=pltpu.CompilerParams(vmem_limit_bytes=60 * MIB),
         cost_estimate=pl.CostEstimate(
             flops=2 * tokens * width * 3 * cols + 8 * tokens * seq * cols,
             bytes_accessed=2 * tokens * width + 6 * width * cols,
@@ -120,9 +120,8 @@
     w, pooled, embed, agg, dz, node_grad, wide, sem = scratch
     mp, dp = place_ref[0], place_ref[1]
     rows, cols = g_self.shape[0], g_self.shape[0]
-    groups, node_dev = got_ref.shape[1], got_ref.shape[2]
+    groups, parts, node_dev, _ = got_ref.shape
     nodes = groups * node_dev
-    parts = got_ref.shape[0]
     width = parts * cols
     own = pl.ds(pl.multiple_of(mp * cols, 128), cols)
 
@@ -141,7 +140,7 @@
             c.start()
 
     def part(m, i, size=cols):
-        return got_ref[m, :, :, i : i + size].astype(F32).reshape(nodes, size)
+        return got_ref[:, m, :, i : i + size].astype(F32).reshape(nodes, size)
 
     for m in range(parts):
         pooled[:, m * cols : (m + 1) * cols] = part(m, 0).astype(BF)
@@ -188,7 +187,7 @@
 
 
 def graph(place, got, weights, moved):
-    parts, groups, node_dev, _ = got.shape
+    groups, parts, node_dev, _ = got.shape
     cols, width = weights[0].shape
     nodes = groups * node_dev
     vmem = pl.BlockSpec(memory_space=pltpu.VMEM)
@@ -209,7 +208,7 @@
             pltpu.VMEM((groups, node_dev, width), F32),
             pltpu.SemaphoreType.DMA((3, parts)),
         ],
-        compiler_params=pltpu.CompilerParams(vmem_limit_bytes=48 * MIB),
+        compiler_params=pltpu.CompilerParams(vmem_limit_bytes=60 * MIB),
         cost_estimate=pl.CostEstimate(
             flops=2 * nodes * width * width * 6, bytes_accessed=10 * MIB, transcendentals=nodes * width
         ),
@@ -218,7 +217,7 @@
 
 def graph_wide(place, got, weights, moved):
     mp, dp = place[0], place[1]
-    parts, groups, node_dev, _ = got.shape
+    groups, parts, node_dev, _ = got.shape
     cols, width = weights[0].shape
     nodes = groups * node_dev
     order = jnp.arange(parts) ^ mp
@@ -226,10 +225,11 @@
     w_out, w_self, w_neigh = (blocks[:, k].reshape(width, width) for k in range(3))
 
     def part(i):
-        return got[..., i * cols : (i + 1) * cols].reshape(parts, nodes, cols).transpose(1, 0, 2).reshape(nodes, width)
+        block = got[..., i * cols : (i + 1) * cols].transpose(0, 2, 1, 3)
+        return block.reshape(nodes, width)
 
     pooled = part(0)
-    packed = got[0, :, :, 3 * cols :].reshape(nodes, IDS_COLS).astype(jnp.int32)
+    packed = got[:, 0, :, 3 * cols :].reshape(nodes, IDS_COLS).astype(jnp.int32)
     fan = IDS_COLS // 8
     ids = packed[:, :fan] * 16 + packed[:, fan : 2 * fan] - 1
     cnt = jnp.maximum(jnp.sum(ids >= 0, axis=1).astype(F32), 1.0)[:, None]
@@ -252,6 +252,31 @@
     return (*own, *grads)
 
 
+def stack_kernel(a, b, c, out, sem):
+    rows = a.shape[0]
+    copies = [
+        pltpu.make_async_copy(ref, out.at[pl.ds(k * rows, rows)], sem.at[k])
+        for k, ref in enumerate((a, b, c))
+    ]
+    for copy in copies:
+        copy.start()
+    for copy in copies:
+        copy.wait()
+
+
+def stack(weights):
+    rows, width = weights[0].shape
+    anywhere = pl.BlockSpec(memory_space=pl.ANY)
+    return pl.pallas_call(
+        stack_kernel,
+        out_shape=jax.ShapeDtypeStruct((3 * rows, width), BF),
+        in_specs=[anywhere] * 3,
+        out_specs=anywhere,
+        scratch_shapes=[pltpu.SemaphoreType.DMA((3,))],
+        compiler_params=pltpu.CompilerParams(vmem_limit_bytes=60 * MIB),
+    )(*weights)
+
+
 def hop(x, axis, bit):
     return lax.ppermute(x, axis, [(i, i ^ bit) for i in range(lax.axis_size(axis))])
 
@@ -261,7 +286,7 @@
     nodes = node_dev * lax.axis_size("dp")
     place = jnp.stack([lax.axis_index("mp"), lax.axis_index("dp")]).astype(jnp.int32)
     weights = (w_out, w_self, w_neigh)
-    stacked = jnp.concatenate(weights)
+    stacked = stack(weights)
     across = hop(stacked, "mp", 2)
     here = hop(stacked, "mp", 1)
     there = hop(across, "mp", 1)
@@ -271,8 +296,8 @@
     ids = jnp.concatenate([shifted // 16, shifted % 16], axis=1).astype(BF)
     ids = jnp.pad(ids, ((0, 0), (0, IDS_COLS - 2 * fan)))
     sent = attention(place, texts, w_qkv, cotangent, ids)
-    got = lax.all_gather(sent, "dp", axis=0, tiled=False)
-    got = lax.all_gather(got, "mp", axis=0, tiled=False)
+    got = lax.all_gather(sent, ("dp", "mp"), axis=0, tiled=False)
+    got = got.reshape(lax.axis_size("dp"), lax.axis_size("mp"), *sent.shape)
     body = graph if nodes <= WIDE_LIMIT else graph_wide
     return body(place, got, weights, (here, across, there))
 

time: 99.9 us -> 148 us (1.48)
  Pallas kernels: 21.4 us -> 74.3 us
  waiting for transfers between devices: 18.2 us -> 55 us
  blocking collectives: 33.2 us -> 0 us
  local copies, waits for them, and re-layouts: 8.93 us -> 0.08 us
    pallas_call x0 -> x1, Pallas kernels: none -> 48.8 us  [stack(): pl.pallas_call(stack_kernel, out_shape=jax.ShapeDtypeStruct((3 * rows, wi...]
    all_gather x1 -> x0, blocking collectives: 33.2 us -> none  [per_device(): got = lax.all_gather(sent, 'dp', axis=0, tiled=False)]
    all_gather x1, waiting for transfers between devices: 13.7 us -> 38.1 us  [per_device(): got = lax.all_gather(sent, ('dp', 'mp'), axis=0, tiled=False)]
    ppermute x3, waiting for transfers between devices: 4.47 us -> 16.9 us  [hop(): lax.ppermute(x, axis, [(i, i ^ bit) for i in range(lax.axis_size(axis))])]
    unnamed x19 -> x7, local copies, waits for them, and re-layouts: 8.09 us -> 0.08 us
    pallas_call x1, Pallas kernels: 13.9 us -> 16.5 us  [attention(): pl.pallas_call(functools.partial(attention_kernel, heads), out_shape=jax....]
    pallas_call x1, Pallas kernels: 7.52 us -> 9.03 us  [graph(): pl.pallas_call(graph_kernel, out_shape=(slab, slab, big, big, big), in_sp...]
  transfers between devices with their start and end apart: 4 -> 4, of which waited for: 2 -> 2; matrix products, arithmetic and copies ran while one was open for 0% -> 1% of each run, Pallas kernels for 14% -> 11%
where the time goes in v4:
time: 148 us
  Pallas kernels  74.3 us (50%)
  waiting for transfers between devices  55 us (37%)
  between operations  14.1 us (10%)
  starting transfers between devices  3.12 us (2%)
    pallas_call x1, Pallas kernels, stack(): pl.pallas_call(stack_kernel, out_shape=jax.ShapeDtypeStruct((3 * rows, wi...  48.8 us
    all_gather x1, waiting for transfers between devices, per_device(): got = lax.all_gather(sent, ('dp', 'mp'), axis=0, tiled=False)  38.1 us
    ppermute x3, waiting for transfers between devices, hop(): lax.ppermute(x, axis, [(i, i ^ bit) for i in range(lax.axis_size(axis))])  16.9 us
    pallas_call x1, Pallas kernels, attention(): pl.pallas_call(functools.partial(attention_kernel, heads), out_shape=jax....  16.5 us
    pallas_call x1, Pallas kernels, graph(): pl.pallas_call(graph_kernel, out_shape=(slab, slab, big, big, big), in_sp...  9.03 us
    ppermute x3, starting transfers between devices, hop(): lax.ppermute(x, axis, [(i, i ^ bit) for i in range(lax.axis_size(axis))])  3.08 us
  transfers between devices with their start and end apart: 4, of which 2 were waited for; matrix products, arithmetic and copies ran while one was open for 1% of the time, Pallas kernels for 11%

profile of v4, /device:TPU:0, one launch (start us, length us, event | category | flops | bytes accessed | tf_op | source)
XLA Modules:
  0.0 148.0 jit_solution(10698607370875576734)
XLA Ops:
  7.2 0.0 copy-start.1
  7.2 0.0 all-gather.3.cloned.1.call-start
  7.2 48.8 %shard_map.111 = bf16[768,1024]{1,0:T(8,128)(2,1)} custom-call(bf16[256,1024]{1,0:T(8,128)(2,1)} %refs_0_.1, bf16[256,1024]{1,0:T(8,128)(2,1)} %refs_1_.1, bf16[256,1024]{1,0:T(8,128)(2,1)} %refs_2_.1), custom_call_target="tpu_custom_call" | custom-call | tf_op jit(solution)/shard_map/pallas_call | solution.py:270
  56.0 3.0 %collective-permute-start.1 = (bf16[768,1024]{1,0:T(8,128)(2,1)}, bf16[768,1024]{1,0:T(8,128)(2,1)S(1)}, u32[]{:S(2)}, u32[]{:S(2)}) collective-permute-start(bf16[768,1024]{1,0:T(8,128)(2,1)} %shard_map.111), channel_id=1, source_target_pairs={{0,2},{1,3},{2,0},{3,1},{4,6},{5,7},{6,4},{7,5},{8,10},{9,11},{10,... | collective-permute-start | bytes 4718600 | tf_op jit(solution)/shard_map/ppermute | solution.py:281
  59.0 0.0 copy-done.1
  59.0 0.1 copy.12
  59.1 0.6 pad_add_fusion.place_ref
  59.7 0.7 fusion.6.ids_ref
  60.4 0.0 copy-start
  60.4 16.5 %shard_map.110 = bf16[24,896]{1,0:T(8,128)(2,1)} custom-call(s32[2]{0:T(128)} %pad_add_fusion.place_ref, bf16[24,128,1024]{2,1,0:T(8,128)(2,1)} %x_ref.1, bf16[1024,768]{1,0:T(8,128)(2,1)} %w_ref.1, bf16[24,256]{1,0:T(8,128)(2,1)} %cot_ref.1, bf16[24,128]{1,0:T(8,128)(2,1)} %fusion.6.ids_ref), custom_call_target="tpu_custom_call" | custom-call | flops 5637144576 | bytes 7864320 | tf_op jit(solution)/shard_map/pallas_call | solution.py:79
  76.9 0.0 all-gather.3.cloned.1.call-update
  77.0 0.0 copy-done
  77.0 0.1 collective-permute-start
  77.0 16.9 %collective-permute-done.1.refs_4_ = bf16[768,1024]{1,0:T(8,128)(2,1)S(1)} collective-permute-done((bf16[768,1024]{1,0:T(8,128)(2,1)}, bf16[768,1024]{1,0:T(8,128)(2,1)S(1)}, u32[]{:S(2)}, u32[]{:S(2)}) %collective-permute-start.1) | collective-permute-done | bytes 1572896 | tf_op jit(solution)/shard_map/ppermute | solution.py:281
  93.9 0.0 copy-start.2
  93.9 0.0 collective-permute-start.2
  93.9 0.0 collective-permute-done.refs_3_
  93.9 38.1 %all-gather.3.cloned.1.call-done = bf16[768,896]{1,0:T(8,128)(2,1)} async-done(((bf16[24,896]{1,0:T(8,128)(2,1)}), bf16[768,896]{1,0:T(8,128)(2,1)}) %all-gather.3.cloned.1.call-update) | async-done | bytes 1376272 | tf_op jit(solution)/shard_map/all_gather | solution.py:299
  132.1 0.0 collective-permute-done.2.refs_5_
  132.1 0.0 copy-done.2
  132.1 9.0 %shard_map.112 = (bf16[24,256]{1,0:T(8,128)(2,1)}, bf16[24,256]{1,0:T(8,128)(2,1)}, f32[256,1024]{1,0:T(8,128)}, f32[256,1024]{1,0:T(8,128)}, f32[256,1024]{1,0:T(8,128)}) custom-call(s32[2]{0:T(128)} %pad_add_fusion.place_ref, bf16[8,4,24,896]{3,2,1,0:T(8,128)(2,1)} %bitcast.3, bf16[256,1024]{1,0:T(8,128)(2,1)} %refs_0_.1, bf16[256,1024]{1,0:T(8,128)(2,1)} %refs_1_.1, ...), custom_call_target="tpu_custom_call" | custom-call | flops 2415919104 | bytes 10485760 | tf_op jit(solution)/shard_map/pallas_call | solution.py:196
  (1 shorter events, 0.0 us)
Async XLA Ops:
  7.2 51.8 %copy-start.1 = (s32[24,16]{0,1:T(8,128)S(1)}, s32[24,16]{0,1:T(8,128)}, u32[]{:S(2)}) copy-start(s32[24,16]{0,1:T(8,128)} %param.12) | copy-start | bytes 4612
  7.2 124.9 %all-gather.3.cloned.1.call-start = ((), (), s32[]{:S(2)}) async-start(), calls=%async_computation | async-start | bytes 1419264 | tf_op jit(solution)/shard_map/all_gather | solution.py:299
  56.0 37.9 %collective-permute-start.1 = (bf16[768,1024]{1,0:T(8,128)(2,1)}, bf16[768,1024]{1,0:T(8,128)(2,1)S(1)}, u32[]{:S(2)}, u32[]{:S(2)}) collective-permute-start(bf16[768,1024]{1,0:T(8,128)(2,1)} %shard_map.111), channel_id=1, source_target_pairs={{0,2},{1,3},{2,0},{3,1},{4,6},{5,7},{6,4},{7,5},{8,10},{9,11},{10,... | collective-permute-start | bytes 4718600 | tf_op jit(solution)/shard_map/ppermute | solution.py:281
  60.4 16.6 %copy-start = (bf16[768,1024]{1,0:T(8,128)(2,1)S(1)}, bf16[768,1024]{1,0:T(8,128)(2,1)}, u32[]{:S(2)}) copy-start(bf16[768,1024]{1,0:T(8,128)(2,1)} %shard_map.111) | copy-start | bytes 4718596
  77.0 17.0 %collective-permute-start = (bf16[768,1024]{1,0:T(8,128)(2,1)S(1)}, bf16[768,1024]{1,0:T(8,128)(2,1)}, u32[]{:S(2)}, u32[]{:S(2)}) collective-permute-start(bf16[768,1024]{1,0:T(8,128)(2,1)S(1)} %copy-done), channel_id=1, source_target_pairs={{0,1},{1,0},{2,3},{3,2},{4,5},{5,4},{6,7},{7,6},{8,9},{9,8},{10,11... | collective-permute-start | bytes 4718600 | tf_op jit(solution)/shard_map/ppermute | solution.py:281
  93.9 38.1 %copy-start.2 = (bf16[768,1024]{1,0:T(8,128)(2,1)}, bf16[768,1024]{1,0:T(8,128)(2,1)S(1)}, u32[]{:S(2)}) copy-start(bf16[768,1024]{1,0:T(8,128)(2,1)S(1)} %collective-permute-done.1.refs_4_) | copy-start | bytes 4718596
  93.9 38.1 %collective-permute-start.2 = (bf16[768,1024]{1,0:T(8,128)(2,1)S(1)}, bf16[768,1024]{1,0:T(8,128)(2,1)}, u32[]{:S(2)}, u32[]{:S(2)}) collective-permute-start(bf16[768,1024]{1,0:T(8,128)(2,1)S(1)} %collective-permute-done.1.refs_4_), channel_id=1, source_target_pairs={{0,1},{1,0},{2,3},{3,2},{4,5},{5,4},{6,7},{7,6},{8,9},{9,8},{10,11... | collective-permute-start | bytes 4718600 | tf_op jit(solution)/shard_map/ppermute | solution.py:281
Sparse Core Ops, SparseCore 0:
  77.1 54.9 all-gather.2

commit v5 on v4

--- a/solution.py
+++ b/solution.py
@@ -113,18 +113,21 @@
     return z * half, slope
 
 
-def graph_kernel(
-    place_ref, got_ref, *refs
-):
-    blocks, (mixed_ref, grad_ref, g_self, g_neigh, g_out), scratch = refs[:6], refs[6:11], refs[11:]
-    w, pooled, embed, agg, dz, node_grad, wide, sem = scratch
-    mp, dp = place_ref[0], place_ref[1]
-    rows, cols = g_self.shape[0], g_self.shape[0]
-    groups, parts, node_dev, _ = got_ref.shape
+def graph_kernel(place_ref, names_ref, *refs):
+    parts = 4
+    got, blocks, refs = refs[:parts], refs[parts : parts + 6], refs[parts + 6 :]
+    (mixed_ref, grad_ref, g_self, g_neigh, g_out), scratch = refs[:5], refs[5:]
+    w, pooled, embed, agg, dz, node_grad, mean, cot, sem = scratch
+    mp = place_ref[0]
+    groups, node_dev, _ = got[0].shape
     nodes = groups * node_dev
+    rows = cols = g_self.shape[0]
     width = parts * cols
-    own = pl.ds(pl.multiple_of(mp * cols, 128), cols)
-
+
+    def place(r):
+        return pl.ds(pl.multiple_of((mp ^ r) * cols, 128), cols)
+
+    own = place(0)
     copies = []
     for k in range(3):
         pair = [pltpu.make_async_copy(blocks[k], w.at[k, mp], sem.at[k, 0])]
@@ -139,20 +142,22 @@
         for c in pair:
             c.start()
 
-    def part(m, i, size=cols):
-        return got_ref[:, m, :, i : i + size].astype(F32).reshape(nodes, size)
-
-    for m in range(parts):
-        pooled[:, m * cols : (m + 1) * cols] = part(m, 0).astype(BF)
+    def part(r, i, size=cols):
+        return got[r][:, :, i : i + size].astype(F32).reshape(nodes, size)
+
+    for r in range(parts):
+        pooled[:, place(r)] = part(r, 0).astype(BF)
+        cot[:, place(r)] = part(r, cols)
+        mean[:, place(r)] = part(r, 2 * cols)
 
     packed = part(0, 3 * cols, IDS_COLS)
     fan = IDS_COLS // 8
     ids = packed[:, :fan] * 16.0 + packed[:, fan : 2 * fan] - 1.0
     cnt = jnp.maximum(jnp.sum((ids >= 0.0).astype(F32), axis=1, keepdims=True), 1.0)
-    every = lax.broadcasted_iota(jnp.int32, (nodes, nodes), 1).astype(F32)
+    names = names_ref[...]
     counts = jnp.zeros((nodes, nodes), F32)
     for s in range(fan):
-        counts += (ids[:, s : s + 1] == every).astype(F32)
+        counts += (ids[:, s : s + 1] == names).astype(F32)
     counts_t = counts.T.astype(BF)
     counts = counts.astype(BF)
 
@@ -161,33 +166,29 @@
 
     for c in copies[0]:
         c.wait()
-    sums = dot(pooled[...], whole(0))
-    for m in range(parts):
-        at = slice(m * cols, (m + 1) * cols)
-        embed[:, at] = (part(m, 2 * cols) + sums[:, at]).astype(BF)
+    embed[...] = (mean[...] + dot(pooled[...], whole(0))).astype(BF)
     agg[...] = (dot(counts, embed[...]) / cnt).astype(BF)
     for c in copies[1] + copies[2]:
         c.wait()
     z = dot(embed[...], whole(1)) + dot(agg[...], whole(2))
     mixed, slope = gelu_parts(z)
-    wide[...] = mixed.reshape(groups, node_dev, width)
-    mixed_ref[...] = wide[dp, :, own].astype(BF)
-    for m in range(parts):
-        at = slice(m * cols, (m + 1) * cols)
-        dz[:, at] = (part(m, cols) * slope[:, at]).astype(BF)
+    mean[:node_dev, :] = mixed[:node_dev, :]
+    mixed_ref[...] = mean[:node_dev, own].astype(BF)
+    dz[...] = (cot[...] * slope).astype(BF)
     msg = (dot_t(dz[...], whole(2)) / cnt).astype(BF)
     total = dot_t(dz[...], whole(1)) + dot(counts_t, msg)
     node_grad[...] = total.astype(BF)
-    wide[...] = total.reshape(groups, node_dev, width)
-    grad_ref[...] = wide[dp, :, own].astype(BF)
+    cot[:node_dev, :] = total[:node_dev, :]
+    grad_ref[...] = cot[:node_dev, own].astype(BF)
     factor = 1.0 / jnp.sqrt(jnp.float32(nodes))
     g_self[...] = t_dot(embed[:, own], dz[...]) * factor
     g_neigh[...] = t_dot(agg[:, own], dz[...]) * factor
     g_out[...] = t_dot(pooled[:, own], node_grad[...]) * factor
 
 
-def graph(place, got, weights, moved):
-    groups, parts, node_dev, _ = got.shape
+def graph(place, names, got, weights, moved):
+    parts = len(got)
+    groups, node_dev, _ = got[0].shape
     cols, width = weights[0].shape
     nodes = groups * node_dev
     vmem = pl.BlockSpec(memory_space=pltpu.VMEM)
@@ -196,7 +197,9 @@
     return pl.pallas_call(
         graph_kernel,
         out_shape=(slab, slab, big, big, big),
-        in_specs=[pl.BlockSpec(memory_space=pltpu.SMEM), vmem] + [pl.BlockSpec(memory_space=pl.ANY)] * 6,
+        in_specs=[pl.BlockSpec(memory_space=pltpu.SMEM)]
+        + [vmem] * (1 + parts)
+        + [pl.BlockSpec(memory_space=pl.ANY)] * 6,
         out_specs=(vmem,) * 5,
         scratch_shapes=[
             pltpu.VMEM((3, parts, cols, width), BF),
@@ -205,19 +208,21 @@
             pltpu.VMEM((nodes, width), BF),
             pltpu.VMEM((nodes, width), BF),
             pltpu.VMEM((nodes, width), BF),
-            pltpu.VMEM((groups, node_dev, width), F32),
+            pltpu.VMEM((nodes, width), F32),
+            pltpu.VMEM((nodes, width), F32),
             pltpu.SemaphoreType.DMA((3, parts)),
         ],
-        compiler_params=pltpu.CompilerParams(vmem_limit_bytes=60 * MIB),
+        compiler_params=pltpu.CompilerParams(vmem_limit_bytes=36 * MIB),
         cost_estimate=pl.CostEstimate(
             flops=2 * nodes * width * width * 6, bytes_accessed=10 * MIB, transcendentals=nodes * width
         ),
-    )(place, got, *weights, *moved)
-
-
-def graph_wide(place, got, weights, moved):
-    mp, dp = place[0], place[1]
-    groups, parts, node_dev, _ = got.shape
+    )(place, names, *got, *weights, *moved)
+
+
+def graph_wide(place, names, got, weights, moved):
+    mp = place[0]
+    parts = len(got)
+    groups, node_dev, _ = got[0].shape
     cols, width = weights[0].shape
     nodes = groups * node_dev
     order = jnp.arange(parts) ^ mp
@@ -225,15 +230,16 @@
     w_out, w_self, w_neigh = (blocks[:, k].reshape(width, width) for k in range(3))
 
     def part(i):
-        block = got[..., i * cols : (i + 1) * cols].transpose(0, 2, 1, 3)
-        return block.reshape(nodes, width)
+        block = jnp.stack([g[:, :, i * cols : (i + 1) * cols] for g in got])[order]
+        return block.transpose(1, 2, 0, 3).reshape(nodes, width)
 
     pooled = part(0)
-    packed = got[:, 0, :, 3 * cols :].reshape(nodes, IDS_COLS).astype(jnp.int32)
+    packed = got[0][:, :, 3 * cols :].reshape(nodes, IDS_COLS).astype(jnp.int32)
     fan = IDS_COLS // 8
     ids = packed[:, :fan] * 16 + packed[:, fan : 2 * fan] - 1
     cnt = jnp.maximum(jnp.sum(ids >= 0, axis=1).astype(F32), 1.0)[:, None]
-    counts = jnp.sum(ids[:, :, None] == jnp.arange(nodes)[None, None, :], axis=1).astype(BF)
+    names = names.astype(jnp.int32)[:, None, :]
+    counts = jnp.sum(ids[:, :, None] == names, axis=1).astype(BF)
     embed = (part(2).astype(F32) + dot(pooled, w_out)).astype(BF)
     agg = (dot(counts, embed) / cnt).astype(BF)
     mixed, slope = gelu_parts(dot(embed, w_self) + dot(agg, w_neigh))
@@ -241,15 +247,12 @@
     msg = (dot_t(dz, w_neigh) / cnt).astype(BF)
     node_grad = (dot_t(dz, w_self) + t_dot(counts, msg)).astype(BF)
     factor = 1.0 / jnp.sqrt(jnp.float32(nodes))
-    grads = [
-        t_dot(lax.dynamic_slice_in_dim(a, mp * cols, cols, 1), b) * factor
-        for a, b in ((embed, dz), (agg, dz), (pooled, node_grad))
-    ]
-    own = [
-        lax.dynamic_slice(a, (dp * node_dev, mp * cols), (node_dev, cols)).astype(BF)
-        for a in (mixed, node_grad)
-    ]
-    return (*own, *grads)
+
+    def own(a):
+        return lax.dynamic_slice_in_dim(a, mp * cols, cols, 1)
+
+    grads = [t_dot(own(a), b) * factor for a, b in ((embed, dz), (agg, dz), (pooled, node_grad))]
+    return (own(mixed[:node_dev]).astype(BF), own(node_grad[:node_dev]), *grads)
 
 
 def stack_kernel(a, b, c, out, sem):
@@ -266,12 +269,11 @@
 
 def stack(weights):
     rows, width = weights[0].shape
-    anywhere = pl.BlockSpec(memory_space=pl.ANY)
     return pl.pallas_call(
         stack_kernel,
         out_shape=jax.ShapeDtypeStruct((3 * rows, width), BF),
-        in_specs=[anywhere] * 3,
-        out_specs=anywhere,
+        in_specs=[pl.BlockSpec(memory_space=pltpu.VMEM)] * 3,
+        out_specs=pl.BlockSpec(memory_space=pl.ANY),
         scratch_shapes=[pltpu.SemaphoreType.DMA((3,))],
         compiler_params=pltpu.CompilerParams(vmem_limit_bytes=60 * MIB),
     )(*weights)
@@ -289,17 +291,27 @@
     stacked = stack(weights)
     across = hop(stacked, "mp", 2)
     here = hop(stacked, "mp", 1)
-    there = hop(across, "mp", 1)
 
     shifted = neighbours + 1
     fan = neighbours.shape[1]
     ids = jnp.concatenate([shifted // 16, shifted % 16], axis=1).astype(BF)
     ids = jnp.pad(ids, ((0, 0), (0, IDS_COLS - 2 * fan)))
-    sent = attention(place, texts, w_qkv, cotangent, ids)
-    got = lax.all_gather(sent, ("dp", "mp"), axis=0, tiled=False)
-    got = got.reshape(lax.axis_size("dp"), lax.axis_size("mp"), *sent.shape)
+    sent = attention(place, texts, w_qkv, cotangent, ids)[None]
+
+    order, bit = [0], lax.axis_size("dp") // 2
+    while bit:
+        sent = jnp.concatenate([sent, hop(sent, "dp", bit)])
+        order = order + [i ^ bit for i in order]
+        bit //= 2
+    owners = jnp.array(order, jnp.int32) ^ lax.axis_index("dp")
+    names = owners[:, None] * node_dev + jnp.arange(node_dev)[None, :]
+    names = names.reshape(1, nodes).astype(F32)
+    across, sent = lax.optimization_barrier((across, sent))
+    there = hop(across, "mp", 1)
+    got_across = hop(sent, "mp", 2)
+    got = (sent, hop(sent, "mp", 1), got_across, hop(got_across, "mp", 1))
     body = graph if nodes <= WIDE_LIMIT else graph_wide
-    return body(place, got, weights, (here, across, there))
+    return body(place, names, got, weights, (here, across, there))
 
 
 def solution(mesh):

time: 148 us -> 63 us (0.43)
  Pallas kernels: 74.3 us -> 27.2 us
  waiting for transfers between devices: 55 us -> 21 us
  between operations: 14.1 us -> 0.73 us
  starting transfers between devices: 3.12 us -> 9.74 us
  other arithmetic: 1.31 us -> 3.78 us
    pallas_call x1, Pallas kernels: 48.8 us -> 2.55 us  [stack(): pl.pallas_call(stack_kernel, out_shape=jax.ShapeDtypeStruct((3 * rows, wi...]
    all_gather x1 -> x0, waiting for transfers between devices: 38.1 us -> none  [per_device(): got = lax.all_gather(sent, ('dp', 'mp'), axis=0, tiled=False)]
    ppermute x3 -> x9, starting transfers between devices: 3.08 us -> 9.74 us  [hop(): lax.ppermute(x, axis, [(i, i ^ bit) for i in range(lax.axis_size(axis))])]
    ppermute x3 -> x9, waiting for transfers between devices: 16.9 us -> 21 us  [hop(): lax.ppermute(x, axis, [(i, i ^ bit) for i in range(lax.axis_size(axis))])]
    concatenate x0 -> x3, other arithmetic: none -> 2.43 us  [per_device(): sent = jnp.concatenate([sent, hop(sent, 'dp', bit)])]
  transfers between devices with their start and end apart: 4 -> 9, of which waited for: 2 -> 5; matrix products, arithmetic and copies ran while one was open for 1% -> 6% of each run, Pallas kernels for 11% -> 26%
where the time goes in v5:
time: 63 us; the launch traced here: 62.6 us
  Pallas kernels  27.2 us (43%)
  waiting for transfers between devices  21 us (33%)
  starting transfers between devices  9.74 us (15%)
  other arithmetic  3.78 us (6%)
  between operations  0.73 us (1%)
    ppermute x9, waiting for transfers between devices, hop(): lax.ppermute(x, axis, [(i, i ^ bit) for i in range(lax.axis_size(axis))])  21 us
    pallas_call x1, Pallas kernels, attention(): pl.pallas_call(functools.partial(attention_kernel, heads), out_shape=jax....  16.5 us
    ppermute x9, starting transfers between devices, hop(): lax.ppermute(x, axis, [(i, i ^ bit) for i in range(lax.axis_size(axis))])  9.74 us
    pallas_call x1, Pallas kernels, graph(): pl.pallas_call(graph_kernel, out_shape=(slab, slab, big, big, big), in_sp...  8.12 us
    pallas_call x1, Pallas kernels, stack(): pl.pallas_call(stack_kernel, out_shape=jax.ShapeDtypeStruct((3 * rows, wi...  2.55 us
    concatenate x3, other arithmetic, per_device(): sent = jnp.concatenate([sent, hop(sent, 'dp', bit)])  2.43 us
  transfers between devices with their start and end apart: 9, of which 5 were waited for; matrix products, arithmetic and copies ran while one was open for 6% of the time, Pallas kernels for 26%

profile of v5, /device:TPU:0, one launch (start us, length us, event | category | flops | bytes accessed | tf_op | source)
XLA Modules:
  0.0 62.6 jit_solution(8540272750652405866)
XLA Ops:
  0.6 2.6 %shard_map.119 = bf16[768,1024]{1,0:T(8,128)(2,1)} custom-call(bf16[256,1024]{1,0:T(8,128)(2,1)} %refs_4_.1, bf16[256,1024]{1,0:T(8,128)(2,1)} %refs_5_.1, bf16[256,1024]{1,0:T(8,128)(2,1)} %refs_6_.1), custom_call_target="tpu_custom_call" | custom-call | tf_op jit(solution)/shard_map/pallas_call | solution.py:272
  3.2 3.0 %collective-permute-start = (bf16[768,1024]{1,0:T(8,128)(2,1)}, bf16[768,1024]{1,0:T(8,128)(2,1)S(1)}, u32[]{:S(2)}, u32[]{:S(2)}) collective-permute-start(bf16[768,1024]{1,0:T(8,128)(2,1)} %shard_map.119), channel_id=1, source_target_pairs={{0,2},{1,3},{2,0},{3,1},{4,6},{5,7},{6,4},{7,5},{8,10},{9,11},{10,... | collective-permute-start | bytes 4718600 | tf_op jit(solution)/shard_map/ppermute | solution.py:283
  6.2 0.6 pad_add_fusion.place_ref
  6.8 0.1 copy.13
  6.9 0.7 %fusion.6.ids_ref = bf16[24,128]{1,0:T(8,128)(2,1)} fusion(bf16[24,16]{1,0:T(8,128)(2,1)S(1)} %get-tuple-element.10, bf16[24,16]{1,0:T(8,128)(2,1)S(1)} %get-tuple-element.9), kind=kLoop, calls=%fused_computation.17 | loop fusion | flops 21504 | bytes 7680 | tf_op jit(solution)/shard_map/concatenate | solution.py:297
  7.6 0.0 copy-start.3
  7.6 16.5 %shard_map.120 = bf16[24,896]{1,0:T(8,128)(2,1)} custom-call(s32[2]{0:T(128)} %pad_add_fusion.place_ref, bf16[24,128,1024]{2,1,0:T(8,128)(2,1)} %x_ref.1, bf16[1024,768]{1,0:T(8,128)(2,1)} %w_ref.1, bf16[24,256]{1,0:T(8,128)(2,1)} %cot_ref.1, bf16[24,128]{1,0:T(8,128)(2,1)} %fusion.6.ids_ref), custom_call_target="tpu_custom_call" | custom-call | flops 5637144576 | bytes 7864320 | tf_op jit(solution)/shard_map/pallas_call | solution.py:79
  24.1 2.6 %collective-permute-start.1 = (bf16[1,24,896]{2,1,0:T(8,128)(2,1)}, bf16[1,24,896]{2,1,0:T(8,128)(2,1)S(1)}, u32[]{:S(2)}, u32[]{:S(2)}) collective-permute-start(bf16[1,24,896]{2,1,0:T(8,128)(2,1)} %bitcast.3), channel_id=1, source_target_pairs={{0,16},{4,20},{8,24},{12,28},{16,0},{20,4},{24,8},{28,12},{1,17},{... | collective-permute-start | bytes 129032 | tf_op jit(solution)/shard_map/ppermute | solution.py:283
  26.7 2.6 %collective-permute-done.1 = bf16[1,24,896]{2,1,0:T(8,128)(2,1)S(1)} collective-permute-done((bf16[1,24,896]{2,1,0:T(8,128)(2,1)}, bf16[1,24,896]{2,1,0:T(8,128)(2,1)S(1)}, u32[]{:S(2)}, u32[]{:S(2)}) %collective-permute-start.1) | collective-permute-done | bytes 43040 | tf_op jit(solution)/shard_map/ppermute | solution.py:283
  29.3 0.8 %pad_maximum_fusion.2 = bf16[2,24,896]{2,1,0:T(8,128)(2,1)S(1)} fusion(bf16[1,24,896]{2,1,0:T(8,128)(2,1)S(1)} %collective-permute-done.1, bf16[1,24,896]{2,1,0:T(8,128)(2,1)} %bitcast.4), kind=kLoop, calls=%fused_computation.2 | loop fusion | flops 43008 | bytes 172032 | tf_op jit(solution)/shard_map/concatenate | solution.py:303
  30.1 1.6 %collective-permute-start.2 = (bf16[2,24,896]{2,1,0:T(8,128)(2,1)S(1)}, bf16[2,24,896]{2,1,0:T(8,128)(2,1)S(1)}, u32[]{:S(2)}, u32[]{:S(2)}) collective-permute-start(bf16[2,24,896]{2,1,0:T(8,128)(2,1)S(1)} %pad_maximum_fusion.2), channel_id=1, source_target_pairs={{0,8},{4,12},{8,0},{12,4},{16,24},{20,28},{24,16},{28,20},{1,9},{5... | collective-permute-start | bytes 258056 | tf_op jit(solution)/shard_map/ppermute | solution.py:283
  31.7 3.0 %collective-permute-done.2 = bf16[2,24,896]{2,1,0:T(8,128)(2,1)S(1)} collective-permute-done((bf16[2,24,896]{2,1,0:T(8,128)(2,1)S(1)}, bf16[2,24,896]{2,1,0:T(8,128)(2,1)S(1)}, u32[]{:S(2)}, u32[]{:S(2)}) %collective-permute-start.2) | collective-permute-done | bytes 86048 | tf_op jit(solution)/shard_map/ppermute | solution.py:283
  34.7 0.8 %pad_maximum_fusion.1 = bf16[4,24,896]{2,1,0:T(8,128)(2,1)S(1)} fusion(bf16[2,24,896]{2,1,0:T(8,128)(2,1)S(1)} %collective-permute-done.2, bf16[1,24,896]{2,1,0:T(8,128)(2,1)S(1)} %collective-permute-done.1, bf16[1,24,896]{2,1,0:T(8,128)(2,1)} %bitcast.5), kind=kLoop, calls=%fused_computation.1 | loop fusion | flops 172032 | bytes 344064 | tf_op jit(solution)/shard_map/concatenate | solution.py:303
  35.5 1.6 %collective-permute-start.3 = (bf16[4,24,896]{2,1,0:T(8,128)(2,1)S(1)}, bf16[4,24,896]{2,1,0:T(8,128)(2,1)S(1)}, u32[]{:S(2)}, u32[]{:S(2)}) collective-permute-start(bf16[4,24,896]{2,1,0:T(8,128)(2,1)S(1)} %pad_maximum_fusion.1), channel_id=1, source_target_pairs={{0,4},{4,0},{8,12},{12,8},{16,20},{20,16},{24,28},{28,24},{1,5},{5... | collective-permute-start | bytes 516104 | tf_op jit(solution)/shard_map/ppermute | solution.py:283
  37.1 0.0 collective-permute-start.7
  37.1 3.9 %collective-permute-done.3 = bf16[4,24,896]{2,1,0:T(8,128)(2,1)S(1)} collective-permute-done((bf16[4,24,896]{2,1,0:T(8,128)(2,1)S(1)}, bf16[4,24,896]{2,1,0:T(8,128)(2,1)S(1)}, u32[]{:S(2)}, u32[]{:S(2)}) %collective-permute-start.3) | collective-permute-done | bytes 172064 | tf_op jit(solution)/shard_map/ppermute | solution.py:283
  41.0 0.8 %pad_maximum_fusion.refs_0_ = bf16[8,24,896]{2,1,0:T(8,128)(2,1)S(1)} fusion(bf16[4,24,896]{2,1,0:T(8,128)(2,1)S(1)} %collective-permute-done.3, bf16[2,24,896]{2,1,0:T(8,128)(2,1)S(1)} %collective-permute-done.2, bf16[1,24,896]{2,1,0:T(8,128)(2,1)S(1)} %collective-permute-done.1, bf16[1,24,896]{2,1,0:T(8,128)(2,1)} %bitcast.6), kind=kLoop, calls=%fused_computation | loop fusion | flops 516096 | bytes 688128 | tf_op jit(solution)/shard_map/concatenate | solution.py:303
  41.8 0.0 collective-permute-done.refs_8_
  41.8 0.1 collective-permute-start.8
  41.9 0.7 %collective-permute-start.5 = (bf16[8,24,896]{2,1,0:T(8,128)(2,1)S(1)}, bf16[8,24,896]{2,1,0:T(8,128)(2,1)}, u32[]{:S(2)}, u32[]{:S(2)}) collective-permute-start(bf16[8,24,896]{2,1,0:T(8,128)(2,1)S(1)} %pad_maximum_fusion.refs_0_), channel_id=1, source_target_pairs={{0,2},{1,3},{2,0},{3,1},{4,6},{5,7},{6,4},{7,5},{8,10},{9,11},{10,... | collective-permute-start | bytes 1032200 | tf_op jit(solution)/shard_map/ppermute | solution.py:283
  42.6 0.2 collective-permute-start.4
  42.8 9.7 %collective-permute-done.5.refs_2_ = bf16[8,24,896]{2,1,0:T(8,128)(2,1)} collective-permute-done((bf16[8,24,896]{2,1,0:T(8,128)(2,1)S(1)}, bf16[8,24,896]{2,1,0:T(8,128)(2,1)}, u32[]{:S(2)}, u32[]{:S(2)}) %collective-permute-start.5) | collective-permute-done | bytes 344096 | tf_op jit(solution)/shard_map/ppermute | solution.py:283
  52.5 0.0 collective-permute-start.6
  52.5 0.0 copy-done.5
  52.5 0.1 add_convert_fusion
  52.5 0.1 convert_element_type.9.names_ref
  52.6 0.0 collective-permute-done.7.refs_7_
  52.6 0.0 collective-permute-done.4.refs_1_
  52.6 1.8 %collective-permute-done.6.refs_3_ = bf16[8,24,896]{2,1,0:T(8,128)(2,1)} collective-permute-done((bf16[8,24,896]{2,1,0:T(8,128)(2,1)}, bf16[8,24,896]{2,1,0:T(8,128)(2,1)}, u32[]{:S(2)}, u32[]{:S(2)}) %collective-permute-start.6) | collective-permute-done | bytes 344096 | tf_op jit(solution)/shard_map/ppermute | solution.py:283
  54.5 0.0 collective-permute-done.8.refs_9_
  54.5 0.0 copy-done.2
  54.5 8.1 %shard_map.121 = (bf16[24,256]{1,0:T(8,128)(2,1)}, bf16[24,256]{1,0:T(8,128)(2,1)}, f32[256,1024]{1,0:T(8,128)}, f32[256,1024]{1,0:T(8,128)}, f32[256,1024]{1,0:T(8,128)}) custom-call(s32[2]{0:T(128)S(1)} %copy-done.3, f32[1,192]{1,0:T(1,128)S(1)} %convert_element_type.9.names_ref, bf16[8,24,896]{2,1,0:T(8,128)(2,1)S(1)} %pad_maximum_fusion.refs_0_, ...), custom_call_target="tpu_custom_call" | custom-call | flops 2415919104 | bytes 10485760 | tf_op jit(solution)/shard_map/pallas_call | solution.py:197
  (11 shorter events, 0.0 us)
Async XLA Ops:
  0.6 6.2 %copy-start.4 = (s32[24,16]{0,1:T(8,128)S(1)}, s32[24,16]{0,1:T(8,128)}, u32[]{:S(2)}) copy-start(s32[24,16]{0,1:T(8,128)} %param.13) | copy-start | bytes 4612
  3.2 38.6 %collective-permute-start = (bf16[768,1024]{1,0:T(8,128)(2,1)}, bf16[768,1024]{1,0:T(8,128)(2,1)S(1)}, u32[]{:S(2)}, u32[]{:S(2)}) collective-permute-start(bf16[768,1024]{1,0:T(8,128)(2,1)} %shard_map.119), channel_id=1, source_target_pairs={{0,2},{1,3},{2,0},{3,1},{4,6},{5,7},{6,4},{7,5},{8,10},{9,11},{10,... | collective-permute-start | bytes 4718600 | tf_op jit(solution)/shard_map/ppermute | solution.py:283
  7.6 44.9 %copy-start.5 = (s32[8]{0:T(128)S(1)}, s32[8]{0:T(128)}, u32[]{:S(2)}) copy-start(s32[8]{0:T(128)} %constant.45.clone) | copy-start | bytes 100
  7.6 46.9 %copy-start = (bf16[256,1024]{1,0:T(8,128)(2,1)S(1)}, bf16[256,1024]{1,0:T(8,128)(2,1)}, u32[]{:S(2)}) copy-start(bf16[256,1024]{1,0:T(8,128)(2,1)} %refs_4_.1) | copy-start | bytes 1572868
  7.6 46.9 %copy-start.1 = (bf16[256,1024]{1,0:T(8,128)(2,1)S(1)}, bf16[256,1024]{1,0:T(8,128)(2,1)}, u32[]{:S(2)}) copy-start(bf16[256,1024]{1,0:T(8,128)(2,1)} %refs_5_.1) | copy-start | bytes 1572868
  7.6 46.9 %copy-start.2 = (bf16[256,1024]{1,0:T(8,128)(2,1)S(1)}, bf16[256,1024]{1,0:T(8,128)(2,1)}, u32[]{:S(2)}) copy-start(bf16[256,1024]{1,0:T(8,128)(2,1)} %refs_6_.1) | copy-start | bytes 1572868
  7.6 46.9 %copy-start.3 = (s32[2]{0:T(128)S(1)}, s32[2]{0:T(128)}, u32[]{:S(2)}) copy-start(s32[2]{0:T(128)} %pad_add_fusion.place_ref) | copy-start | bytes 28
  24.1 5.2 %collective-permute-start.1 = (bf16[1,24,896]{2,1,0:T(8,128)(2,1)}, bf16[1,24,896]{2,1,0:T(8,128)(2,1)S(1)}, u32[]{:S(2)}, u32[]{:S(2)}) collective-permute-start(bf16[1,24,896]{2,1,0:T(8,128)(2,1)} %bitcast.3), channel_id=1, source_target_pairs={{0,16},{4,20},{8,24},{12,28},{16,0},{20,4},{24,8},{28,12},{1,17},{... | collective-permute-start | bytes 129032 | tf_op jit(solution)/shard_map/ppermute | solution.py:283
  30.1 4.6 %collective-permute-start.2 = (bf16[2,24,896]{2,1,0:T(8,128)(2,1)S(1)}, bf16[2,24,896]{2,1,0:T(8,128)(2,1)S(1)}, u32[]{:S(2)}, u32[]{:S(2)}) collective-permute-start(bf16[2,24,896]{2,1,0:T(8,128)(2,1)S(1)} %pad_maximum_fusion.2), channel_id=1, source_target_pairs={{0,8},{4,12},{8,0},{12,4},{16,24},{20,28},{24,16},{28,20},{1,9},{5... | collective-permute-start | bytes 258056 | tf_op jit(solution)/shard_map/ppermute | solution.py:283
  35.5 5.5 %collective-permute-start.3 = (bf16[4,24,896]{2,1,0:T(8,128)(2,1)S(1)}, bf16[4,24,896]{2,1,0:T(8,128)(2,1)S(1)}, u32[]{:S(2)}, u32[]{:S(2)}) collective-permute-start(bf16[4,24,896]{2,1,0:T(8,128)(2,1)S(1)} %pad_maximum_fusion.1), channel_id=1, source_target_pairs={{0,4},{4,0},{8,12},{12,8},{16,20},{20,16},{24,28},{28,24},{1,5},{5... | collective-permute-start | bytes 516104 | tf_op jit(solution)/shard_map/ppermute | solution.py:283
  37.1 15.6 %collective-permute-start.7 = (bf16[768,1024]{1,0:T(8,128)(2,1)}, bf16[768,1024]{1,0:T(8,128)(2,1)}, u32[]{:S(2)}, u32[]{:S(2)}) collective-permute-start(bf16[768,1024]{1,0:T(8,128)(2,1)} %shard_map.119), channel_id=1, source_target_pairs={{0,1},{1,0},{2,3},{3,2},{4,5},{5,4},{6,7},{7,6},{8,9},{9,8},{10,11... | collective-permute-start | bytes 4718600 | tf_op jit(solution)/shard_map/ppermute | solution.py:283
  41.8 12.7 %collective-permute-start.8 = (bf16[768,1024]{1,0:T(8,128)(2,1)S(1)}, bf16[768,1024]{1,0:T(8,128)(2,1)}, u32[]{:S(2)}, u32[]{:S(2)}) collective-permute-start(bf16[768,1024]{1,0:T(8,128)(2,1)S(1)} %collective-permute-done.refs_8_), channel_id=1, source_target_pairs={{0,1},{1,0},{2,3},{3,2},{4,5},{5,4},{6,7},{7,6},{8,9},{9,8},{10,11... | collective-permute-start | bytes 4718600 | tf_op jit(solution)/shard_map/ppermute | solution.py:283
  41.9 10.6 %collective-permute-start.5 = (bf16[8,24,896]{2,1,0:T(8,128)(2,1)S(1)}, bf16[8,24,896]{2,1,0:T(8,128)(2,1)}, u32[]{:S(2)}, u32[]{:S(2)}) collective-permute-start(bf16[8,24,896]{2,1,0:T(8,128)(2,1)S(1)} %pad_maximum_fusion.refs_0_), channel_id=1, source_target_pairs={{0,2},{1,3},{2,0},{3,1},{4,6},{5,7},{6,4},{7,5},{8,10},{9,11},{10,... | collective-permute-start | bytes 1032200 | tf_op jit(solution)/shard_map/ppermute | solution.py:283
  42.6 10.1 %collective-permute-start.4 = (bf16[8,24,896]{2,1,0:T(8,128)(2,1)S(1)}, bf16[8,24,896]{2,1,0:T(8,128)(2,1)}, u32[]{:S(2)}, u32[]{:S(2)}) collective-permute-start(bf16[8,24,896]{2,1,0:T(8,128)(2,1)S(1)} %pad_maximum_fusion.refs_0_), channel_id=1, source_target_pairs={{0,1},{1,0},{2,3},{3,2},{4,5},{5,4},{6,7},{7,6},{8,9},{9,8},{10,11... | collective-permute-start | bytes 1032200 | tf_op jit(solution)/shard_map/ppermute | solution.py:283
  52.5 2.0 %collective-permute-start.6 = (bf16[8,24,896]{2,1,0:T(8,128)(2,1)}, bf16[8,24,896]{2,1,0:T(8,128)(2,1)}, u32[]{:S(2)}, u32[]{:S(2)}) collective-permute-start(bf16[8,24,896]{2,1,0:T(8,128)(2,1)} %collective-permute-done.5.refs_2_), channel_id=1, source_target_pairs={{0,1},{1,0},{2,3},{3,2},{4,5},{5,4},{6,7},{7,6},{8,9},{9,8},{10,11... | collective-permute-start | bytes 1032200 | tf_op jit(solution)/shard_map/ppermute | solution.py:283

commit v6 on v5

v6 whole, which is shorter than its diff:
```python
import functools

import jax
import jax.numpy as jnp
from jax import lax
from jax.experimental import pallas as pl
from jax.experimental.pallas import tpu as pltpu
from jax.sharding import PartitionSpec as P

HD = 64
BF = jnp.bfloat16
F32 = jnp.float32
NODES_STEP = 3
WIDE_LIMIT = 256
IDS_COLS = 128
MIB = 1 << 20


def dot_t(a, b):
    return lax.dot_general(a, b, (((1,), (1,)), ((), ())), preferred_element_type=F32)


def t_dot(a, b):
    return lax.dot_general(a, b, (((0,), (0,)), ((), ())), preferred_element_type=F32)


def dot(a, b):
    return jnp.dot(a, b, preferred_element_type=F32)


def attention_kernel(heads, x_ref, w_ref, cot_ref, ids_ref, out_ref, wp, acc_p, acc_m):
    step = pl.program_id(0)
    nodes, seq, width = x_ref.shape
    cols = heads * HD

    @pl.when(step == 0)
    def _():
        for part in range(3):
            for h in range(0, heads, 2):
                a = h * 3 * HD + part * HD
                b = a + 3 * HD
                wp[:, part * cols + h * HD : part * cols + (h + 2) * HD] = jnp.concatenate(
                    [w_ref[:, a : a + HD], w_ref[:, b : b + HD]], axis=1
                )

    own = pl.ds(pl.multiple_of(lax.axis_index("mp") * cols, 128), cols)
    qkv = dot(x_ref[...].reshape(nodes * seq, width), wp[...]).astype(BF)
    lane = lax.broadcasted_iota(jnp.int32, (seq, cols), 1) // HD
    row = lax.broadcasted_iota(jnp.int32, (heads * seq, cols), 0) // seq
    column = lax.broadcasted_iota(jnp.int32, (heads * seq, cols), 1) // HD
    ones = (row == column).astype(F32).astype(BF)
    zero = jnp.zeros((seq, cols), BF)
    for n in range(nodes):
        at = slice(n * seq, (n + 1) * seq)
        q, k, v = (qkv[at, i * cols : (i + 1) * cols] for i in range(3))
        spread = jnp.concatenate([jnp.where(lane == h, q, zero) for h in range(heads)], axis=0)
        s = dot_t(k, spread)
        e = jnp.exp((s - jnp.max(s, axis=0, keepdims=True)) * (HD**-0.5))
        p = (e * (1.0 / jnp.sum(e, axis=0, keepdims=True))).astype(BF)
        weight = dot(p, ones)
        context = jnp.sum(weight * v.astype(F32), axis=0, keepdims=True)
        acc_p[pl.ds(step * nodes + n, 1), :] = context * (1.0 / seq)
        mean = jnp.sum(x_ref[n, :, own].astype(F32), axis=0, keepdims=True)
        acc_m[pl.ds(step * nodes + n, 1), :] = mean * (1.0 / seq)

    @pl.when(step == pl.num_programs(0) - 1)
    def _():
        out_ref[:, :cols] = acc_p[...].astype(BF)
        out_ref[:, cols : 2 * cols] = cot_ref[...]
        out_ref[:, 2 * cols : 3 * cols] = acc_m[...].astype(BF)
        shifted = ids_ref[...] + 1
        rows, fan = shifted.shape
        blank = jnp.zeros((rows, IDS_COLS - 2 * fan), F32)
        pair = [(shifted >> 4).astype(F32), (shifted & 15).astype(F32)]
        out_ref[:, 3 * cols :] = jnp.concatenate(pair + [blank], axis=1).astype(BF)


def attention(texts, w_qkv, cotangent, neighbours):
    node_dev, seq, width = texts.shape
    cols = w_qkv.shape[1] // 3
    heads = cols // HD
    tokens = node_dev * seq
    return pl.pallas_call(
        functools.partial(attention_kernel, heads),
        out_shape=jax.ShapeDtypeStruct((node_dev, 3 * cols + IDS_COLS), BF),
        grid=(node_dev // NODES_STEP,),
        in_specs=[
            pl.BlockSpec((NODES_STEP, seq, width), lambda i: (i, 0, 0)),
            pl.BlockSpec((width, 3 * cols), lambda i: (0, 0)),
            pl.BlockSpec((node_dev, cols), lambda i: (0, 0)),
            pl.BlockSpec(neighbours.shape, lambda i: (0, 0)),
        ],
        out_specs=pl.BlockSpec((node_dev, 3 * cols + IDS_COLS), lambda i: (0, 0)),
        scratch_shapes=[
            pltpu.VMEM((width, 3 * cols), BF),
            pltpu.VMEM((node_dev, cols), F32),
            pltpu.VMEM((node_dev, cols), F32),
        ],
        compiler_params=pltpu.CompilerParams(vmem_limit_bytes=60 * MIB),
        cost_estimate=pl.CostEstimate(
            flops=2 * tokens * width * 3 * cols + 8 * tokens * seq * cols,
            bytes_accessed=2 * tokens * width + 6 * width * cols,
            transcendentals=tokens * seq * heads,
        ),
    )(texts, w_qkv, cotangent, neighbours)


def gelu_parts(z):
    root = 0.7978845608028654
    cube = 0.044715
    t = jnp.tanh(root * (z + cube * (z * z * z)))
    half = 0.5 * (1.0 + t)
    slope = half + 0.5 * z * (1.0 - t * t) * (root * (1.0 + 3.0 * cube * (z * z)))
    return z * half, slope


def graph_kernel(order, fan, *refs):
    parts = 4
    got, blocks, refs = refs[:parts], refs[parts : parts + 12], refs[parts + 12 :]
    (mixed_ref, grad_ref, g_self, g_neigh, g_out), scratch = refs[:5], refs[5:]
    w, pooled, embed, agg, dz, node_grad, mean, cot, sem = scratch
    mp, dp = lax.axis_index("mp"), lax.axis_index("dp")
    side = dp % 2
    groups, node_dev, _ = got[0].shape
    nodes = groups * node_dev
    cols = g_self.shape[0]
    width = parts * cols

    def place(r):
        return pl.ds(pl.multiple_of((mp ^ r) * cols, 128), cols)

    own = place(0)
    copies = []
    for r in range(parts):
        kinds = (0, 1, 2) if r < 2 else (0, 1 + side, 2 - side)
        for i, k in enumerate(kinds):
            copies.append(pltpu.make_async_copy(blocks[3 * r + i], w.at[k, mp ^ r], sem.at[i, r]))
    copies = copies[::3], copies[1::3] + copies[2::3]
    for c in copies[0] + copies[1]:
        c.start()

    def part(r, i, size=cols):
        return got[r][:, :, i : i + size].astype(F32).reshape(nodes, size)

    for r in range(parts):
        pooled[:, place(r)] = part(r, 0).astype(BF)
        cot[:, place(r)] = part(r, cols)
        mean[:, place(r)] = part(r, 2 * cols)

    packed = part(0, 3 * cols, IDS_COLS)
    ids = packed[:, :fan] * 16.0 + packed[:, fan : 2 * fan] - 1.0
    cnt = jnp.maximum(jnp.sum((ids >= 0.0).astype(F32), axis=1, keepdims=True), 1.0)
    place_of = lax.broadcasted_iota(jnp.int32, (1, nodes), 1)
    names = place_of
    for i, o in enumerate(order):
        shift = ((dp ^ o) - i) * node_dev
        inside = (place_of >= i * node_dev) & (place_of < (i + 1) * node_dev)
        names = jnp.where(inside, place_of + shift, names)
    names = names.astype(F32)
    counts = jnp.zeros((nodes, nodes), F32)
    for s in range(fan):
        counts += (ids[:, s : s + 1] == names).astype(F32)
    counts_t = counts.T.astype(BF)
    counts = counts.astype(BF)

    def whole(k):
        return w[k].reshape(width, width)

    for c in copies[0]:
        c.wait()
    embed[...] = (mean[...] + dot(pooled[...], whole(0))).astype(BF)
    agg[...] = (dot(counts, embed[...]) / cnt).astype(BF)
    for c in copies[1]:
        c.wait()
    z = dot(embed[...], whole(1)) + dot(agg[...], whole(2))
    mixed, slope = gelu_parts(z)
    mean[:node_dev, :] = mixed[:node_dev, :]
    mixed_ref[...] = mean[:node_dev, own].astype(BF)
    dz[...] = (cot[...] * slope).astype(BF)
    msg = (dot_t(dz[...], whole(2)) / cnt).astype(BF)
    total = dot_t(dz[...], whole(1)) + dot(counts_t, msg)
    node_grad[...] = total.astype(BF)
    cot[:node_dev, :] = total[:node_dev, :]
    grad_ref[...] = cot[:node_dev, own].astype(BF)
    factor = 1.0 / jnp.sqrt(jnp.float32(nodes))
    g_self[...] = t_dot(embed[:, own], dz[...]) * factor
    g_neigh[...] = t_dot(agg[:, own], dz[...]) * factor
    g_out[...] = t_dot(pooled[:, own], node_grad[...]) * factor


def graph(order, fan, got, weights):
    parts = len(got)
    groups, node_dev, _ = got[0].shape
    cols, width = weights[0][0].shape
    nodes = groups * node_dev
    vmem = pl.BlockSpec(memory_space=pltpu.VMEM)
    slab = jax.ShapeDtypeStruct((node_dev, cols), BF)
    big = jax.ShapeDtypeStruct((cols, width), F32)
    return pl.pallas_call(
        functools.partial(graph_kernel, order, fan),
        out_shape=(slab, slab, big, big, big),
        in_specs=[vmem] * parts + [pl.BlockSpec(memory_space=pl.ANY)] * (3 * parts),
        out_specs=(vmem,) * 5,
        scratch_shapes=[
            pltpu.VMEM((3, parts, cols, width), BF),
            pltpu.VMEM((nodes, width), BF),
            pltpu.VMEM((nodes, width), BF),
            pltpu.VMEM((nodes, width), BF),
            pltpu.VMEM((nodes, width), BF),
            pltpu.VMEM((nodes, width), BF),
            pltpu.VMEM((nodes, width), F32),
            pltpu.VMEM((nodes, width), F32),
            pltpu.SemaphoreType.DMA((3, parts)),
        ],
        compiler_params=pltpu.CompilerParams(vmem_limit_bytes=36 * MIB),
        cost_estimate=pl.CostEstimate(
            flops=2 * nodes * width * width * 6, bytes_accessed=10 * MIB, transcendentals=nodes * width
        ),
    )(*got, *sum(weights, ()))


def graph_wide(order, fan, got, weights):
    mp, dp = lax.axis_index("mp"), lax.axis_index("dp")
    parts = len(got)
    groups, node_dev, _ = got[0].shape
    cols, width = weights[0][0].shape
    nodes = groups * node_dev
    owners = jnp.array(order, jnp.int32) ^ dp
    names = (owners[:, None] * node_dev + jnp.arange(node_dev)[None, :]).reshape(1, 1, nodes)
    order = jnp.arange(parts) ^ mp
    even = dp % 2 == 0
    kinds = [
        [group[0], jnp.where(even, group[1], group[2]), jnp.where(even, group[2], group[1])]
        for group in weights[2:]
    ]
    blocks = [*weights[:2], *kinds]
    w_out, w_self, w_neigh = (
        jnp.stack([group[k] for group in blocks])[order].reshape(width, width) for k in range(3)
    )

    def part(i):
        block = jnp.stack([g[:, :, i * cols : (i + 1) * cols] for g in got])[order]
        return block.transpose(1, 2, 0, 3).reshape(nodes, width)

    pooled = part(0)
    packed = got[0][:, :, 3 * cols :].reshape(nodes, IDS_COLS).astype(jnp.int32)
    ids = packed[:, :fan] * 16 + packed[:, fan : 2 * fan] - 1
    cnt = jnp.maximum(jnp.sum(ids >= 0, axis=1).astype(F32), 1.0)[:, None]
    counts = jnp.sum(ids[:, :, None] == names, axis=1).astype(BF)
    embed = (part(2).astype(F32) + dot(pooled, w_out)).astype(BF)
    agg = (dot(counts, embed) / cnt).astype(BF)
    mixed, slope = gelu_parts(dot(embed, w_self) + dot(agg, w_neigh))
    dz = (part(1).astype(F32) * slope).astype(BF)
    msg = (dot_t(dz, w_neigh) / cnt).astype(BF)
    node_grad = (dot_t(dz, w_self) + t_dot(counts, msg)).astype(BF)
    factor = 1.0 / jnp.sqrt(jnp.float32(nodes))

    def own(a):
        return lax.dynamic_slice_in_dim(a, mp * cols, cols, 1)

    grads = [t_dot(own(a), b) * factor for a, b in ((embed, dz), (agg, dz), (pooled, node_grad))]
    return (own(mixed[:node_dev]).astype(BF), own(node_grad[:node_dev]), *grads)


def join_kernel(*refs):
    out, at = refs[-1], 0
    for ref in refs[:-1]:
        out[at : at + ref.shape[0]] = ref[...]
        at += ref.shape[0]


def join(*blocks):
    count = sum(b.shape[0] for b in blocks)
    if count > 8:
        return jnp.concatenate(blocks)
    vmem = pl.BlockSpec(memory_space=pltpu.VMEM)
    return pl.pallas_call(
        join_kernel,
        out_shape=jax.ShapeDtypeStruct((count, *blocks[0].shape[1:]), BF),
        in_specs=[vmem] * len(blocks),
        out_specs=vmem,
        compiler_params=pltpu.CompilerParams(vmem_limit_bytes=8 * MIB),
    )(*blocks)


def hop(x, axis, bit):
    return lax.ppermute(x, axis, [(i, i ^ bit) for i in range(lax.axis_size(axis))])


def gather_dp(block):
    size = lax.axis_size("dp")
    if size == 8:
        block = join(block, *[hop(block, "dp", i) for i in (2, 4, 6)])
        order, bit = [0, 2, 4, 6], 1
    else:
        order, bit = [0], size // 2
    while bit:
        block = join(block, hop(block, "dp", bit))
        order = order + [i ^ bit for i in order]
        bit //= 2
    return block, order


def per_device(texts, w_qkv, w_out, w_self, w_neigh, neighbours, cotangent):
    node_dev, fan = neighbours.shape
    nodes = node_dev * lax.axis_size("dp")
    even = lax.axis_index("dp") % 2 == 0
    x_half = hop(jnp.where(even, w_self, w_neigh), "mp", 2)
    x_out = hop(w_out, "mp", 2)
    own = (w_out, w_self, w_neigh)

    sent = attention(texts, w_qkv, cotangent, neighbours)[None]
    sent, order = gather_dp(sent)
    y_half = hop(x_half, "dp", 1)
    here = tuple(hop(a, "mp", 1) for a in own)
    across = (x_out, x_half, y_half)
    there = tuple(hop(a, "mp", 1) for a in across)

    got_across = hop(sent, "mp", 2)
    got = (sent, hop(sent, "mp", 1), got_across, hop(got_across, "mp", 1))
    body = graph if nodes <= WIDE_LIMIT else graph_wide
    return body(order, fan, got, (own, here, across, there))


def solution(mesh):
    return jax.shard_map(
        per_device,
        mesh=mesh,
        in_specs=(
            P("dp", None, None),
            P(None, "mp"),
            P("mp", None),
            P("mp", None),
            P("mp", None),
            P("dp", None),
            P("dp", "mp"),
        ),
        out_specs=(P("dp", "mp"), P("dp", "mp"), P("mp", None), P("mp", None), P("mp", None)),
        check_vma=False,
    )
```

time: 63 us -> 68.3 us (1.084)
  waiting for transfers between devices: 21 us -> 29.6 us
  Pallas kernels: 27.2 us -> 22.9 us
  other arithmetic: 3.78 us -> 1.11 us
  local copies, waits for them, and re-layouts: 0.18 us -> 2.16 us
  starting transfers between devices: 9.74 us -> 11.6 us
    ppermute x9 -> x16, waiting for transfers between devices: 21 us -> 29.6 us  [hop(): lax.ppermute(x, axis, [(i, i ^ bit) for i in range(lax.axis_size(axis))])]
    pallas_call x2 -> x3, Pallas kernels: 10.7 us -> 6.97 us  [the longest x1 6.93 us: graph(): pl.pallas_call(functools.partial(graph_kernel, order, fan), out_shape=(sl...]
    concatenate x4 -> x0, other arithmetic: 3.1 us -> none  [the longest x3 2.43 us: per_device(): sent = jnp.concatenate([sent, hop(sent, 'dp', bit)])]
    unnamed x13 -> x9, local copies, waits for them, and re-layouts: 0.1 us -> 2.16 us
    ppermute x9 -> x16, starting transfers between devices: 9.74 us -> 11.6 us  [hop(): lax.ppermute(x, axis, [(i, i ^ bit) for i in range(lax.axis_size(axis))])]
    select_n x0 -> x1, other arithmetic: none -> 1.11 us  [per_device(): x_half = hop(jnp.where(even, w_self, w_neigh), 'mp', 2)]
  transfers between devices with their start and end apart: 9 -> 16, of which waited for: 5 -> 6; matrix products, arithmetic and copies ran while one was open for 6% -> 2% of each run, Pallas kernels for 26% -> 23%
where the time goes in v6:
time: 68.3 us; the launch traced here: 68 us
  waiting for transfers between devices  29.6 us (43%)
  Pallas kernels  22.9 us (34%)
  starting transfers between devices  11.6 us (17%)
  local copies, waits for them, and re-layouts  2.16 us (3%)
  other arithmetic  1.11 us (2%)
  between operations  0.69 us (1%)
    ppermute x16, waiting for transfers between devices, hop(): lax.ppermute(x, axis, [(i, i ^ bit) for i in range(lax.axis_size(axis))])  29.6 us
    pallas_call x1, Pallas kernels, attention(): pl.pallas_call(functools.partial(attention_kernel, heads), out_shape=jax....  15.9 us
    ppermute x16, starting transfers between devices, hop(): lax.ppermute(x, axis, [(i, i ^ bit) for i in range(lax.axis_size(axis))])  11.6 us
    pallas_call x1, Pallas kernels, graph(): pl.pallas_call(functools.partial(graph_kernel, order, fan), out_shape=(sl...  6.93 us
    unnamed x9, local copies, waits for them, and re-layouts  2.16 us
  transfers between devices with their start and end apart: 16, of which 6 were waited for; matrix products, arithmetic and copies ran while one was open for 2% of the time, Pallas kernels for 23%

profile of v6, /device:TPU:0, one launch (start us, length us, event | category | flops | bytes accessed | tf_op | source)
XLA Modules:
  0.0 68.0 jit_solution(15661785014064295315)
XLA Ops:
  0.6 1.1 %broadcast_select_fusion = bf16[256,1024]{1,0:T(8,128)(2,1)S(1)} fusion(bf16[256,1024]{1,0:T(8,128)(2,1)} %refs_5_.1, bf16[256,1024]{1,0:T(8,128)(2,1)} %refs_6_.1, pred[]{:T(512)S(6)} %eq.5), kind=kLoop, calls=%fused_computation | loop fusion | flops 262144 | bytes 1572865 | tf_op jit(solution)/shard_map/jit(_where)/select_n | solution.py:308
  1.8 3.0 %collective-permute-start.11 = (bf16[256,1024]{1,0:T(8,128)(2,1)S(1)}, bf16[256,1024]{1,0:T(8,128)(2,1)S(1)}, u32[]{:S(2)}, u32[]{:S(2)}) collective-permute-start(bf16[256,1024]{1,0:T(8,128)(2,1)S(1)} %broadcast_select_fusion), channel_id=1, source_target_pairs={{0,2},{1,3},{2,0},{3,1},{4,6},{5,7},{6,4},{7,5},{8,10},{9,11},{10,... | collective-permute-start | bytes 1572872 | tf_op jit(solution)/shard_map/ppermute | solution.py:287
  4.8 0.0 collective-permute-start.7
  4.8 1.4 %copy.12.ids_ref = s32[24,16]{1,0:T(8,128)} copy(s32[24,16]{0,1:T(8,128)} %param.12) | data formatting | bytes 3072 | tf_op args[5]
  6.1 15.9 %shard_map.110 = bf16[24,896]{1,0:T(8,128)(2,1)} custom-call(bf16[24,128,1024]{2,1,0:T(8,128)(2,1)} %x_ref.1, bf16[1024,768]{1,0:T(8,128)(2,1)} %w_ref.1, bf16[24,256]{1,0:T(8,128)(2,1)} %cot_ref.1, s32[24,16]{1,0:T(8,128)} %copy.12.ids_ref), custom_call_target="tpu_custom_call" | custom-call | flops 5637144576 | bytes 7864320 | tf_op jit(solution)/shard_map/pallas_call | solution.py:83
  22.0 3.6 %collective-permute-start.2 = (bf16[1,24,896]{2,1,0:T(8,128)(2,1)}, bf16[1,24,896]{2,1,0:T(8,128)(2,1)S(1)}, u32[]{:S(2)}, u32[]{:S(2)}) collective-permute-start(bf16[1,24,896]{2,1,0:T(8,128)(2,1)} %bitcast.1), channel_id=1, source_target_pairs={{0,24},{4,28},{8,16},{12,20},{16,8},{20,12},{24,0},{28,4},{1,25},{... | collective-permute-start | bytes 129032 | tf_op jit(solution)/shard_map/ppermute | solution.py:287
  25.6 0.8 %collective-permute-start = (bf16[1,24,896]{2,1,0:T(8,128)(2,1)}, bf16[1,24,896]{2,1,0:T(8,128)(2,1)S(1)}, u32[]{:S(2)}, u32[]{:S(2)}) collective-permute-start(bf16[1,24,896]{2,1,0:T(8,128)(2,1)} %bitcast.3), channel_id=1, source_target_pairs={{0,8},{4,12},{8,0},{12,4},{16,24},{20,28},{24,16},{28,20},{1,9},{5... | collective-permute-start | bytes 129032 | tf_op jit(solution)/shard_map/ppermute | solution.py:287
  26.4 1.8 %collective-permute-done.2.refs_3_ = bf16[1,24,896]{2,1,0:T(8,128)(2,1)S(1)} collective-permute-done((bf16[1,24,896]{2,1,0:T(8,128)(2,1)}, bf16[1,24,896]{2,1,0:T(8,128)(2,1)S(1)}, u32[]{:S(2)}, u32[]{:S(2)}) %collective-permute-start.2) | collective-permute-done | bytes 43040 | tf_op jit(solution)/shard_map/ppermute | solution.py:287
  28.2 0.5 collective-permute-start.10
  28.7 2.0 %collective-permute-done.1.refs_2_ = bf16[1,24,896]{2,1,0:T(8,128)(2,1)S(1)} collective-permute-done((bf16[1,24,896]{2,1,0:T(8,128)(2,1)}, bf16[1,24,896]{2,1,0:T(8,128)(2,1)S(1)}, u32[]{:S(2)}, u32[]{:S(2)}) %collective-permute-start.1) | collective-permute-done | bytes 43040 | tf_op jit(solution)/shard_map/ppermute | solution.py:287
  30.8 0.0 collective-permute-start.8
  30.8 0.0 collective-permute-done.11.refs_11_
  30.8 1.6 %collective-permute-start.12 = (bf16[256,1024]{1,0:T(8,128)(2,1)S(1)}, bf16[256,1024]{1,0:T(8,128)(2,1)S(1)}, u32[]{:S(2)}, u32[]{:S(2)}) collective-permute-start(bf16[256,1024]{1,0:T(8,128)(2,1)S(1)} %collective-permute-done.11.refs_11_), channel_id=1, source_target_pairs={{0,4},{4,0},{8,12},{12,8},{16,20},{20,16},{24,28},{28,24},{1,5},{5... | collective-permute-start | bytes 1572872 | tf_op jit(solution)/shard_map/ppermute | solution.py:287
  32.4 0.0 collective-permute-done.refs_1_
  32.4 0.8 %copy-done.2 = bf16[24,896]{1,0:T(8,128)(2,1)S(1)} copy-done((bf16[24,896]{1,0:T(8,128)(2,1)S(1)}, bf16[24,896]{1,0:T(8,128)(2,1)}, u32[]{:S(2)}) %copy-start.2) | copy-done | bytes 43032
  33.2 0.6 collective-permute-start.3
  33.8 15.1 %collective-permute-done.3.refs_1_ = bf16[4,24,896]{2,1,0:T(8,128)(2,1)S(1)} collective-permute-done((bf16[4,24,896]{2,1,0:T(8,128)(2,1)S(1)}, bf16[4,24,896]{2,1,0:T(8,128)(2,1)S(1)}, u32[]{:S(2)}, u32[]{:S(2)}) %collective-permute-start.3) | collective-permute-done | bytes 172064 | tf_op jit(solution)/shard_map/ppermute | solution.py:287
  48.8 0.0 collective-permute-start.9
  48.9 0.6 collective-permute-start.5
  49.5 0.0 collective-permute-done.10.refs_10_
  49.5 0.2 collective-permute-start.14
  49.7 0.0 collective-permute-done.8.refs_8_
  49.7 0.3 collective-permute-start.13
  50.0 0.0 collective-permute-done.12.refs_12_
  50.0 0.2 collective-permute-start.15
  50.2 0.5 collective-permute-done.9.refs_9_
  50.7 0.1 collective-permute-start.4
  50.9 8.5 %collective-permute-done.5.refs_2_ = bf16[8,24,896]{2,1,0:T(8,128)(2,1)S(1)} collective-permute-done((bf16[8,24,896]{2,1,0:T(8,128)(2,1)S(1)}, bf16[8,24,896]{2,1,0:T(8,128)(2,1)S(1)}, u32[]{:S(2)}, u32[]{:S(2)}) %collective-permute-start.5) | collective-permute-done | bytes 344096 | tf_op jit(solution)/shard_map/ppermute | solution.py:287
  59.4 0.0 collective-permute-start.6
  59.4 0.0 collective-permute-done.4.refs_1_
  59.4 1.6 %collective-permute-done.6.refs_3_ = bf16[8,24,896]{2,1,0:T(8,128)(2,1)S(1)} collective-permute-done((bf16[8,24,896]{2,1,0:T(8,128)(2,1)S(1)}, bf16[8,24,896]{2,1,0:T(8,128)(2,1)S(1)}, u32[]{:S(2)}, u32[]{:S(2)}) %collective-permute-start.6) | collective-permute-done | bytes 344096 | tf_op jit(solution)/shard_map/ppermute | solution.py:287
  61.1 6.9 %shard_map.113 = (bf16[24,256]{1,0:T(8,128)(2,1)}, bf16[24,256]{1,0:T(8,128)(2,1)}, f32[256,1024]{1,0:T(8,128)}, f32[256,1024]{1,0:T(8,128)}, f32[256,1024]{1,0:T(8,128)}) custom-call(bf16[8,24,896]{2,1,0:T(8,128)(2,1)S(1)} %shard_map.112.refs_0_, bf16[8,24,896]{2,1,0:T(8,128)(2,1)S(1)} %collective-permute-done.4.refs_1_, ...), custom_call_target="tpu_custom_call" | custom-call | flops 2415919104 | bytes 10485760 | tf_op jit(solution)/shard_map/pallas_call | solution.py:199
  (14 shorter events, 0.1 us)
Async XLA Ops:
  1.8 29.0 %collective-permute-start.11 = (bf16[256,1024]{1,0:T(8,128)(2,1)S(1)}, bf16[256,1024]{1,0:T(8,128)(2,1)S(1)}, u32[]{:S(2)}, u32[]{:S(2)}) collective-permute-start(bf16[256,1024]{1,0:T(8,128)(2,1)S(1)} %broadcast_select_fusion), channel_id=1, source_target_pairs={{0,2},{1,3},{2,0},{3,1},{4,6},{5,7},{6,4},{7,5},{8,10},{9,11},{10,... | collective-permute-start | bytes 1572872 | tf_op jit(solution)/shard_map/ppermute | solution.py:287
  4.8 44.1 %collective-permute-start.7 = (bf16[256,1024]{1,0:T(8,128)(2,1)}, bf16[256,1024]{1,0:T(8,128)(2,1)S(1)}, u32[]{:S(2)}, u32[]{:S(2)}) collective-permute-start(bf16[256,1024]{1,0:T(8,128)(2,1)} %refs_4_.1), channel_id=1, source_target_pairs={{0,1},{1,0},{2,3},{3,2},{4,5},{5,4},{6,7},{7,6},{8,9},{9,8},{10,11... | collective-permute-start | bytes 1572872 | tf_op jit(solution)/shard_map/ppermute | solution.py:287
  6.1 22.1 %copy-start.3 = (bf16[256,1024]{1,0:T(8,128)(2,1)S(1)}, bf16[256,1024]{1,0:T(8,128)(2,1)}, u32[]{:S(2)}) copy-start(bf16[256,1024]{1,0:T(8,128)(2,1)} %refs_4_.1) | copy-start | bytes 1572868
  6.1 24.7 %copy-start = (bf16[256,1024]{1,0:T(8,128)(2,1)S(1)}, bf16[256,1024]{1,0:T(8,128)(2,1)}, u32[]{:S(2)}) copy-start(bf16[256,1024]{1,0:T(8,128)(2,1)} %refs_5_.1) | copy-start | bytes 1572868
  6.1 42.7 %copy-start.1 = (bf16[256,1024]{1,0:T(8,128)(2,1)S(1)}, bf16[256,1024]{1,0:T(8,128)(2,1)}, u32[]{:S(2)}) copy-start(bf16[256,1024]{1,0:T(8,128)(2,1)} %refs_6_.1) | copy-start | bytes 1572868
  22.0 6.2 %collective-permute-start.2 = (bf16[1,24,896]{2,1,0:T(8,128)(2,1)}, bf16[1,24,896]{2,1,0:T(8,128)(2,1)S(1)}, u32[]{:S(2)}, u32[]{:S(2)}) collective-permute-start(bf16[1,24,896]{2,1,0:T(8,128)(2,1)} %bitcast.1), channel_id=1, source_target_pairs={{0,24},{4,28},{8,16},{12,20},{16,8},{20,12},{24,0},{28,4},{1,25},{... | collective-permute-start | bytes 129032 | tf_op jit(solution)/shard_map/ppermute | solution.py:287
  25.6 5.2 %collective-permute-start.1 = (bf16[1,24,896]{2,1,0:T(8,128)(2,1)}, bf16[1,24,896]{2,1,0:T(8,128)(2,1)S(1)}, u32[]{:S(2)}, u32[]{:S(2)}) collective-permute-start(bf16[1,24,896]{2,1,0:T(8,128)(2,1)} %bitcast.2), channel_id=1, source_target_pairs={{0,16},{4,20},{8,24},{12,28},{16,0},{20,4},{24,8},{28,12},{1,17},{... | collective-permute-start | bytes 129032 | tf_op jit(solution)/shard_map/ppermute | solution.py:287
  25.6 6.8 %collective-permute-start = (bf16[1,24,896]{2,1,0:T(8,128)(2,1)}, bf16[1,24,896]{2,1,0:T(8,128)(2,1)S(1)}, u32[]{:S(2)}, u32[]{:S(2)}) collective-permute-start(bf16[1,24,896]{2,1,0:T(8,128)(2,1)} %bitcast.3), channel_id=1, source_target_pairs={{0,8},{4,12},{8,0},{12,4},{16,24},{20,28},{24,16},{28,20},{1,9},{5... | collective-permute-start | bytes 129032 | tf_op jit(solution)/shard_map/ppermute | solution.py:287
  28.2 21.3 %collective-permute-start.10 = (bf16[256,1024]{1,0:T(8,128)(2,1)S(1)}, bf16[256,1024]{1,0:T(8,128)(2,1)S(1)}, u32[]{:S(2)}, u32[]{:S(2)}) collective-permute-start(bf16[256,1024]{1,0:T(8,128)(2,1)S(1)} %copy-done.3), channel_id=1, source_target_pairs={{0,2},{1,3},{2,0},{3,1},{4,6},{5,7},{6,4},{7,5},{8,10},{9,11},{10,... | collective-permute-start | bytes 1572872 | tf_op jit(solution)/shard_map/ppermute | solution.py:287
  30.8 18.9 %collective-permute-start.8 = (bf16[256,1024]{1,0:T(8,128)(2,1)S(1)}, bf16[256,1024]{1,0:T(8,128)(2,1)S(1)}, u32[]{:S(2)}, u32[]{:S(2)}) collective-permute-start(bf16[256,1024]{1,0:T(8,128)(2,1)S(1)} %copy-done), channel_id=1, source_target_pairs={{0,1},{1,0},{2,3},{3,2},{4,5},{5,4},{6,7},{7,6},{8,9},{9,8},{10,11... | collective-permute-start | bytes 1572872 | tf_op jit(solution)/shard_map/ppermute | solution.py:287
  30.8 19.2 %collective-permute-start.12 = (bf16[256,1024]{1,0:T(8,128)(2,1)S(1)}, bf16[256,1024]{1,0:T(8,128)(2,1)S(1)}, u32[]{:S(2)}, u32[]{:S(2)}) collective-permute-start(bf16[256,1024]{1,0:T(8,128)(2,1)S(1)} %collective-permute-done.11.refs_11_), channel_id=1, source_target_pairs={{0,4},{4,0},{8,12},{12,8},{16,20},{20,16},{24,28},{28,24},{1,5},{5... | collective-permute-start | bytes 1572872 | tf_op jit(solution)/shard_map/ppermute | solution.py:287
  32.4 0.8 %copy-start.2 = (bf16[24,896]{1,0:T(8,128)(2,1)S(1)}, bf16[24,896]{1,0:T(8,128)(2,1)}, u32[]{:S(2)}) copy-start(bf16[24,896]{1,0:T(8,128)(2,1)} %shard_map.110) | copy-start | bytes 129028
  33.2 15.6 %collective-permute-start.3 = (bf16[4,24,896]{2,1,0:T(8,128)(2,1)S(1)}, bf16[4,24,896]{2,1,0:T(8,128)(2,1)S(1)}, u32[]{:S(2)}, u32[]{:S(2)}) collective-permute-start(bf16[4,24,896]{2,1,0:T(8,128)(2,1)S(1)} %shard_map.111.refs_0_), channel_id=1, source_target_pairs={{0,4},{4,0},{8,12},{12,8},{16,20},{20,16},{24,28},{28,24},{1,5},{5... | collective-permute-start | bytes 516104 | tf_op jit(solution)/shard_map/ppermute | solution.py:287
  48.8 1.9 %collective-permute-start.9 = (bf16[256,1024]{1,0:T(8,128)(2,1)S(1)}, bf16[256,1024]{1,0:T(8,128)(2,1)S(1)}, u32[]{:S(2)}, u32[]{:S(2)}) collective-permute-start(bf16[256,1024]{1,0:T(8,128)(2,1)S(1)} %copy-done.1), channel_id=1, source_target_pairs={{0,1},{1,0},{2,3},{3,2},{4,5},{5,4},{6,7},{7,6},{8,9},{9,8},{10,11... | collective-permute-start | bytes 1572872 | tf_op jit(solution)/shard_map/ppermute | solution.py:287
  48.9 10.5 %collective-permute-start.5 = (bf16[8,24,896]{2,1,0:T(8,128)(2,1)S(1)}, bf16[8,24,896]{2,1,0:T(8,128)(2,1)S(1)}, u32[]{:S(2)}, u32[]{:S(2)}) collective-permute-start(bf16[8,24,896]{2,1,0:T(8,128)(2,1)S(1)} %shard_map.112.refs_0_), channel_id=1, source_target_pairs={{0,2},{1,3},{2,0},{3,1},{4,6},{5,7},{6,4},{7,5},{8,10},{9,11},{10,... | collective-permute-start | bytes 1032200 | tf_op jit(solution)/shard_map/ppermute | solution.py:287
  49.5 11.6 %collective-permute-start.14 = (bf16[256,1024]{1,0:T(8,128)(2,1)S(1)}, bf16[256,1024]{1,0:T(8,128)(2,1)S(1)}, u32[]{:S(2)}, u32[]{:S(2)}) collective-permute-start(bf16[256,1024]{1,0:T(8,128)(2,1)S(1)} %collective-permute-done.11.refs_11_), channel_id=1, source_target_pairs={{0,1},{1,0},{2,3},{3,2},{4,5},{5,4},{6,7},{7,6},{8,9},{9,8},{10,11... | collective-permute-start | bytes 1572872 | tf_op jit(solution)/shard_map/ppermute | solution.py:287
  49.7 11.4 %collective-permute-start.13 = (bf16[256,1024]{1,0:T(8,128)(2,1)S(1)}, bf16[256,1024]{1,0:T(8,128)(2,1)S(1)}, u32[]{:S(2)}, u32[]{:S(2)}) collective-permute-start(bf16[256,1024]{1,0:T(8,128)(2,1)S(1)} %collective-permute-done.10.refs_10_), channel_id=1, source_target_pairs={{0,1},{1,0},{2,3},{3,2},{4,5},{5,4},{6,7},{7,6},{8,9},{9,8},{10,11... | collective-permute-start | bytes 1572872 | tf_op jit(solution)/shard_map/ppermute | solution.py:287
  50.0 11.1 %collective-permute-start.15 = (bf16[256,1024]{1,0:T(8,128)(2,1)S(1)}, bf16[256,1024]{1,0:T(8,128)(2,1)S(1)}, u32[]{:S(2)}, u32[]{:S(2)}) collective-permute-start(bf16[256,1024]{1,0:T(8,128)(2,1)S(1)} %collective-permute-done.12.refs_12_), channel_id=1, source_target_pairs={{0,1},{1,0},{2,3},{3,2},{4,5},{5,4},{6,7},{7,6},{8,9},{9,8},{10,11... | collective-permute-start | bytes 1572872 | tf_op jit(solution)/shard_map/ppermute | solution.py:287
  50.7 8.7 %collective-permute-start.4 = (bf16[8,24,896]{2,1,0:T(8,128)(2,1)S(1)}, bf16[8,24,896]{2,1,0:T(8,128)(2,1)S(1)}, u32[]{:S(2)}, u32[]{:S(2)}) collective-permute-start(bf16[8,24,896]{2,1,0:T(8,128)(2,1)S(1)} %shard_map.112.refs_0_), channel_id=1, source_target_pairs={{0,1},{1,0},{2,3},{3,2},{4,5},{5,4},{6,7},{7,6},{8,9},{9,8},{10,11... | collective-permute-start | bytes 1032200 | tf_op jit(solution)/shard_map/ppermute | solution.py:287
  59.4 1.7 %collective-permute-start.6 = (bf16[8,24,896]{2,1,0:T(8,128)(2,1)S(1)}, bf16[8,24,896]{2,1,0:T(8,128)(2,1)S(1)}, u32[]{:S(2)}, u32[]{:S(2)}) collective-permute-start(bf16[8,24,896]{2,1,0:T(8,128)(2,1)S(1)} %collective-permute-done.5.refs_2_), channel_id=1, source_target_pairs={{0,1},{1,0},{2,3},{3,2},{4,5},{5,4},{6,7},{7,6},{8,9},{9,8},{10,11... | collective-permute-start | bytes 1032200 | tf_op jit(solution)/shard_map/ppermute | solution.py:287

commit v7 on v6

--- a/solution.py
+++ b/solution.py
@@ -13,6 +13,9 @@
 NODES_STEP = 3
 WIDE_LIMIT = 256
 IDS_COLS = 128
+IDS_AT = 32
+LOG2E = 1.4426950408889634
+ATTENTION_VMEM = 58
 MIB = 1 << 20
 
 
@@ -28,10 +31,27 @@
     return jnp.dot(a, b, preferred_element_type=F32)
 
 
-def attention_kernel(heads, x_ref, w_ref, cot_ref, ids_ref, out_ref, wp, acc_p, acc_m):
+def attend(qkv, heads, seq, ones_ref, row, acc_p):
+    cols = heads * HD
+    lane = lax.broadcasted_iota(jnp.int32, (seq, cols), 1) // HD
+    zero = jnp.zeros((seq, cols), BF)
+    for n in range(NODES_STEP):
+        at = slice(n * seq, (n + 1) * seq)
+        q, k, v = (qkv[at, i * cols : (i + 1) * cols] for i in range(3))
+        spread = jnp.concatenate([jnp.where(lane == h, q, zero) for h in range(heads)], axis=0)
+        s = dot_t(k, spread)
+        e = jnp.exp2((s - jnp.max(s, axis=0, keepdims=True)) * (HD**-0.5 * LOG2E))
+        p = (e * (1.0 / jnp.sum(e, axis=0, keepdims=True))).astype(BF)
+        context = jnp.sum(dot(p, ones_ref[...]) * v.astype(F32), axis=0, keepdims=True)
+        acc_p[pl.ds(row + n, 1), :] = context * (1.0 / seq)
+
+
+def attention_kernel(heads, x_ref, w_ref, cot_ref, ids_ref, out_ref, wp, ones, last, acc_p, acc_m):
     step = pl.program_id(0)
     nodes, seq, width = x_ref.shape
+    node_dev = cot_ref.shape[0]
     cols = heads * HD
+    half = NODES_STEP * seq
 
     @pl.when(step == 0)
     def _():
@@ -42,67 +62,76 @@
                 wp[:, part * cols + h * HD : part * cols + (h + 2) * HD] = jnp.concatenate(
                     [w_ref[:, a : a + HD], w_ref[:, b : b + HD]], axis=1
                 )
+        row = lax.broadcasted_iota(jnp.int32, (heads * seq, cols), 0) // seq
+        column = lax.broadcasted_iota(jnp.int32, (heads * seq, cols), 1) // HD
+        ones[...] = (row == column).astype(F32).astype(BF)
+        last[...] = jnp.zeros_like(last)
 
     own = pl.ds(pl.multiple_of(lax.axis_index("mp") * cols, 128), cols)
-    qkv = dot(x_ref[...].reshape(nodes * seq, width), wp[...]).astype(BF)
-    lane = lax.broadcasted_iota(jnp.int32, (seq, cols), 1) // HD
-    row = lax.broadcasted_iota(jnp.int32, (heads * seq, cols), 0) // seq
-    column = lax.broadcasted_iota(jnp.int32, (heads * seq, cols), 1) // HD
-    ones = (row == column).astype(F32).astype(BF)
-    zero = jnp.zeros((seq, cols), BF)
+    begin = step * nodes
+
+    def product(first):
+        return dot(x_ref[first : first + NODES_STEP].reshape(half, width), wp[...]).astype(BF)
+
+    def attend_at(qkv, row):
+        attend(qkv, heads, seq, ones, row, acc_p)
+
+    before = jnp.where(step == 0, node_dev, begin - NODES_STEP)
+    qkv = product(0)
+    attend_at(last, before)
+    last[...] = product(NODES_STEP)
+    attend_at(qkv, begin)
     for n in range(nodes):
-        at = slice(n * seq, (n + 1) * seq)
-        q, k, v = (qkv[at, i * cols : (i + 1) * cols] for i in range(3))
-        spread = jnp.concatenate([jnp.where(lane == h, q, zero) for h in range(heads)], axis=0)
-        s = dot_t(k, spread)
-        e = jnp.exp((s - jnp.max(s, axis=0, keepdims=True)) * (HD**-0.5))
-        p = (e * (1.0 / jnp.sum(e, axis=0, keepdims=True))).astype(BF)
-        weight = dot(p, ones)
-        context = jnp.sum(weight * v.astype(F32), axis=0, keepdims=True)
-        acc_p[pl.ds(step * nodes + n, 1), :] = context * (1.0 / seq)
         mean = jnp.sum(x_ref[n, :, own].astype(F32), axis=0, keepdims=True)
-        acc_m[pl.ds(step * nodes + n, 1), :] = mean * (1.0 / seq)
+        acc_m[pl.ds(begin + n, 1), :] = mean * (1.0 / seq)
 
     @pl.when(step == pl.num_programs(0) - 1)
     def _():
-        out_ref[:, :cols] = acc_p[...].astype(BF)
+        attend_at(last, node_dev - NODES_STEP)
+        out_ref[:, :cols] = acc_p[:node_dev, :].astype(BF)
         out_ref[:, cols : 2 * cols] = cot_ref[...]
         out_ref[:, 2 * cols : 3 * cols] = acc_m[...].astype(BF)
         shifted = ids_ref[...] + 1
-        rows, fan = shifted.shape
-        blank = jnp.zeros((rows, IDS_COLS - 2 * fan), F32)
-        pair = [(shifted >> 4).astype(F32), (shifted & 15).astype(F32)]
-        out_ref[:, 3 * cols :] = jnp.concatenate(pair + [blank], axis=1).astype(BF)
-
-
-def attention(texts, w_qkv, cotangent, neighbours):
+        fan = shifted.shape[0]
+        blank = jnp.zeros((fan, IDS_COLS - 2 * IDS_AT), F32)
+        gap = jnp.zeros((fan, IDS_AT - node_dev), F32)
+        high, low = (shifted >> 4).astype(F32), (shifted & 15).astype(F32)
+        packed = jnp.concatenate([high, gap, low, gap, blank], axis=1)
+        rest = jnp.zeros((node_dev - fan, IDS_COLS), F32)
+        out_ref[:, 3 * cols :] = jnp.concatenate([packed, rest], axis=0).astype(BF)
+
+
+def attention(texts, w_qkv, cotangent, ids):
     node_dev, seq, width = texts.shape
     cols = w_qkv.shape[1] // 3
     heads = cols // HD
     tokens = node_dev * seq
+    nodes = 2 * NODES_STEP
     return pl.pallas_call(
         functools.partial(attention_kernel, heads),
         out_shape=jax.ShapeDtypeStruct((node_dev, 3 * cols + IDS_COLS), BF),
-        grid=(node_dev // NODES_STEP,),
+        grid=(node_dev // nodes,),
         in_specs=[
-            pl.BlockSpec((NODES_STEP, seq, width), lambda i: (i, 0, 0)),
+            pl.BlockSpec((nodes, seq, width), lambda i: (i, 0, 0)),
             pl.BlockSpec((width, 3 * cols), lambda i: (0, 0)),
             pl.BlockSpec((node_dev, cols), lambda i: (0, 0)),
-            pl.BlockSpec(neighbours.shape, lambda i: (0, 0)),
+            pl.BlockSpec(ids.shape, lambda i: (0, 0)),
         ],
         out_specs=pl.BlockSpec((node_dev, 3 * cols + IDS_COLS), lambda i: (0, 0)),
         scratch_shapes=[
             pltpu.VMEM((width, 3 * cols), BF),
-            pltpu.VMEM((node_dev, cols), F32),
+            pltpu.VMEM((heads * seq, cols), BF),
+            pltpu.VMEM((NODES_STEP * seq, 3 * cols), BF),
+            pltpu.VMEM((node_dev + 8, cols), F32),
             pltpu.VMEM((node_dev, cols), F32),
         ],
-        compiler_params=pltpu.CompilerParams(vmem_limit_bytes=60 * MIB),
+        compiler_params=pltpu.CompilerParams(vmem_limit_bytes=ATTENTION_VMEM * MIB),
         cost_estimate=pl.CostEstimate(
             flops=2 * tokens * width * 3 * cols + 8 * tokens * seq * cols,
             bytes_accessed=2 * tokens * width + 6 * width * cols,
             transcendentals=tokens * seq * heads,
         ),
-    )(texts, w_qkv, cotangent, neighbours)
+    )(texts, w_qkv, cotangent, ids)
 
 
 def gelu_parts(z):
@@ -120,7 +149,7 @@
     (mixed_ref, grad_ref, g_self, g_neigh, g_out), scratch = refs[:5], refs[5:]
     w, pooled, embed, agg, dz, node_grad, mean, cot, sem = scratch
     mp, dp = lax.axis_index("mp"), lax.axis_index("dp")
-    side = dp % 2
+    side = (dp // 2) % 2
     groups, node_dev, _ = got[0].shape
     nodes = groups * node_dev
     cols = g_self.shape[0]
@@ -147,21 +176,27 @@
         cot[:, place(r)] = part(r, cols)
         mean[:, place(r)] = part(r, 2 * cols)
 
-    packed = part(0, 3 * cols, IDS_COLS)
-    ids = packed[:, :fan] * 16.0 + packed[:, fan : 2 * fan] - 1.0
-    cnt = jnp.maximum(jnp.sum((ids >= 0.0).astype(F32), axis=1, keepdims=True), 1.0)
-    place_of = lax.broadcasted_iota(jnp.int32, (1, nodes), 1)
+    packed = got[0][:, :, 3 * cols :].astype(F32)
+    ids = jnp.concatenate(
+        [
+            packed[i, :fan, :node_dev] * 16.0 + packed[i, :fan, IDS_AT : IDS_AT + node_dev] - 1.0
+            for i in range(groups)
+        ],
+        axis=1,
+    )
+    place_of = lax.broadcasted_iota(jnp.int32, (nodes, 1), 0)
     names = place_of
     for i, o in enumerate(order):
         shift = ((dp ^ o) - i) * node_dev
         inside = (place_of >= i * node_dev) & (place_of < (i + 1) * node_dev)
         names = jnp.where(inside, place_of + shift, names)
     names = names.astype(F32)
-    counts = jnp.zeros((nodes, nodes), F32)
+    counts_t = jnp.zeros((nodes, nodes), F32)
     for s in range(fan):
-        counts += (ids[:, s : s + 1] == names).astype(F32)
-    counts_t = counts.T.astype(BF)
-    counts = counts.astype(BF)
+        counts_t += (ids[s : s + 1, :] == names).astype(F32)
+    counts = counts_t.T
+    cnt = jnp.maximum(jnp.sum(counts, axis=1, keepdims=True), 1.0)
+    counts, counts_t = counts.astype(BF), counts_t.astype(BF)
 
     def whole(k):
         return w[k].reshape(width, width)
@@ -228,7 +263,7 @@
     owners = jnp.array(order, jnp.int32) ^ dp
     names = (owners[:, None] * node_dev + jnp.arange(node_dev)[None, :]).reshape(1, 1, nodes)
     order = jnp.arange(parts) ^ mp
-    even = dp % 2 == 0
+    even = (dp // 2) % 2 == 0
     kinds = [
         [group[0], jnp.where(even, group[1], group[2]), jnp.where(even, group[2], group[1])]
         for group in weights[2:]
@@ -243,8 +278,9 @@
         return block.transpose(1, 2, 0, 3).reshape(nodes, width)
 
     pooled = part(0)
-    packed = got[0][:, :, 3 * cols :].reshape(nodes, IDS_COLS).astype(jnp.int32)
-    ids = packed[:, :fan] * 16 + packed[:, fan : 2 * fan] - 1
+    packed = got[0][:, :fan, 3 * cols :].astype(jnp.int32)
+    ids = packed[:, :, :node_dev] * 16 + packed[:, :, IDS_AT : IDS_AT + node_dev] - 1
+    ids = ids.transpose(0, 2, 1).reshape(nodes, fan)
     cnt = jnp.maximum(jnp.sum(ids >= 0, axis=1).astype(F32), 1.0)[:, None]
     counts = jnp.sum(ids[:, :, None] == names, axis=1).astype(BF)
     embed = (part(2).astype(F32) + dot(pooled, w_out)).astype(BF)
@@ -283,37 +319,65 @@
     )(*blocks)
 
 
+def pick_kernel(first, second, out, sem):
+    side = (lax.axis_index("dp") // 2) % 2
+
+    @pl.when(side == 0)
+    def _():
+        copy = pltpu.make_async_copy(first, out, sem)
+        copy.start()
+        copy.wait()
+
+    @pl.when(side == 1)
+    def _():
+        copy = pltpu.make_async_copy(second, out, sem)
+        copy.start()
+        copy.wait()
+
+
+def pick(first, second):
+    anywhere = pl.BlockSpec(memory_space=pl.ANY)
+    return pl.pallas_call(
+        pick_kernel,
+        out_shape=jax.ShapeDtypeStruct(first.shape, first.dtype),
+        in_specs=[anywhere, anywhere],
+        out_specs=pl.BlockSpec(memory_space=pltpu.VMEM),
+        scratch_shapes=[pltpu.SemaphoreType.DMA],
+        compiler_params=pltpu.CompilerParams(vmem_limit_bytes=60 * MIB),
+    )(first, second)
+
+
 def hop(x, axis, bit):
     return lax.ppermute(x, axis, [(i, i ^ bit) for i in range(lax.axis_size(axis))])
 
 
-def gather_dp(block):
+def gather_dp(block, later):
     size = lax.axis_size("dp")
     if size == 8:
         block = join(block, *[hop(block, "dp", i) for i in (2, 4, 6)])
         order, bit = [0, 2, 4, 6], 1
+        block, later = lax.optimization_barrier((block, later))
     else:
         order, bit = [0], size // 2
     while bit:
         block = join(block, hop(block, "dp", bit))
         order = order + [i ^ bit for i in order]
         bit //= 2
-    return block, order
+    return block, order, later
 
 
 def per_device(texts, w_qkv, w_out, w_self, w_neigh, neighbours, cotangent):
     node_dev, fan = neighbours.shape
     nodes = node_dev * lax.axis_size("dp")
-    even = lax.axis_index("dp") % 2 == 0
-    x_half = hop(jnp.where(even, w_self, w_neigh), "mp", 2)
+    x_half = hop(pick(w_self, w_neigh), "mp", 2)
     x_out = hop(w_out, "mp", 2)
     own = (w_out, w_self, w_neigh)
 
-    sent = attention(texts, w_qkv, cotangent, neighbours)[None]
-    sent, order = gather_dp(sent)
-    y_half = hop(x_half, "dp", 1)
-    here = tuple(hop(a, "mp", 1) for a in own)
-    across = (x_out, x_half, y_half)
+    sent = attention(texts, w_qkv, cotangent, neighbours.T)[None]
+    sent, order, late = gather_dp(sent, own)
+    z_half = hop(x_half, "dp", 2)
+    here = tuple(hop(a, "mp", 1) for a in late)
+    across = (x_out, x_half, z_half)
     there = tuple(hop(a, "mp", 1) for a in across)
 
     got_across = hop(sent, "mp", 2)

time: 68.3 us -> 59.7 us (0.87)
  waiting for transfers between devices: 29.6 us -> 20.8 us
  Pallas kernels: 22.9 us -> 24.6 us
  local copies, waits for them, and re-layouts: 2.16 us -> 0.8 us
  other arithmetic: 1.11 us -> 0 us
  starting transfers between devices: 11.6 us -> 12.6 us
    ppermute x16, waiting for transfers between devices: 29.6 us -> 20.8 us  [hop(): lax.ppermute(x, axis, [(i, i ^ bit) for i in range(lax.axis_size(axis))])]
    pallas_call x0 -> x1, Pallas kernels: none -> 1.86 us  [pick(): pl.pallas_call(pick_kernel, out_shape=jax.ShapeDtypeStruct(first.shape, f...]
    unnamed x9 -> x8, local copies, waits for them, and re-layouts: 2.16 us -> 0.8 us
    select_n x1 -> x0, other arithmetic: 1.11 us -> none  [per_device(): x_half = hop(jnp.where(even, w_self, w_neigh), 'mp', 2)]
    ppermute x16, starting transfers between devices: 11.6 us -> 12.6 us  [hop(): lax.ppermute(x, axis, [(i, i ^ bit) for i in range(lax.axis_size(axis))])]
  transfers between devices with their start and end apart: 16 -> 16, of which waited for: 6 -> 6; matrix products, arithmetic and copies ran while one was open for 2% -> 0% of each run, Pallas kernels for 23% -> 27%
where the time goes in v7:
time: 59.7 us; the launch traced here: 59.5 us
  Pallas kernels  24.6 us (41%)
  waiting for transfers between devices  20.8 us (35%)
  starting transfers between devices  12.6 us (21%)
  local copies, waits for them, and re-layouts  0.8 us (1%)
  between operations  0.7 us (1%)
    ppermute x16, waiting for transfers between devices, hop(): lax.ppermute(x, axis, [(i, i ^ bit) for i in range(lax.axis_size(axis))])  20.8 us
    pallas_call x1, Pallas kernels, attention(): pl.pallas_call(functools.partial(attention_kernel, heads), out_shape=jax....  15.9 us
    ppermute x16, starting transfers between devices, hop(): lax.ppermute(x, axis, [(i, i ^ bit) for i in range(lax.axis_size(axis))])  12.6 us
    pallas_call x1, Pallas kernels, graph(): pl.pallas_call(functools.partial(graph_kernel, order, fan), out_shape=(sl...  6.8 us
    pallas_call x1, Pallas kernels, pick(): pl.pallas_call(pick_kernel, out_shape=jax.ShapeDtypeStruct(first.shape, f...  1.86 us
  transfers between devices with their start and end apart: 16, of which 6 were waited for; matrix products, arithmetic and copies ran while one was open for 0% of the time, Pallas kernels for 27%

profile of v7, /device:TPU:0, one launch (start us, length us, event | category | flops | bytes accessed | tf_op | source)
XLA Modules:
  0.0 59.5 jit_solution(10078544230411556307)
XLA Ops:
  0.6 1.9 %shard_map.113 = bf16[256,1024]{1,0:T(8,128)(2,1)} custom-call(bf16[256,1024]{1,0:T(8,128)(2,1)} %refs_5_.1, bf16[256,1024]{1,0:T(8,128)(2,1)} %refs_6_.1), custom_call_target="tpu_custom_call" | custom-call | tf_op jit(solution)/shard_map/pallas_call | solution.py:340
  2.5 3.0 %collective-permute-start.11 = (bf16[256,1024]{1,0:T(8,128)(2,1)}, bf16[256,1024]{1,0:T(8,128)(2,1)S(1)}, u32[]{:S(2)}, u32[]{:S(2)}) collective-permute-start(bf16[256,1024]{1,0:T(8,128)(2,1)} %shard_map.113), channel_id=1, source_target_pairs={{0,2},{1,3},{2,0},{3,1},{4,6},{5,7},{6,4},{7,5},{8,10},{9,11},{10,... | collective-permute-start | bytes 1572872 | tf_op jit(solution)/shard_map/ppermute | solution.py:351
  5.5 0.1 collective-permute-start.10
  5.6 15.9 %shard_map.110 = bf16[24,896]{1,0:T(8,128)(2,1)} custom-call(bf16[24,128,1024]{2,1,0:T(8,128)(2,1)} %x_ref.1, bf16[1024,768]{1,0:T(8,128)(2,1)} %w_ref.1, bf16[24,256]{1,0:T(8,128)(2,1)} %cot_ref.1, s32[16,24]{1,0:T(8,128)} %bitcast.6), custom_call_target="tpu_custom_call" | custom-call | flops 5637144576 | bytes 7864320 | tf_op jit(solution)/shard_map/pallas_call | solution.py:110
  21.5 4.1 %collective-permute-start.2 = (bf16[1,24,896]{2,1,0:T(8,128)(2,1)}, bf16[1,24,896]{2,1,0:T(8,128)(2,1)S(1)}, u32[]{:S(2)}, u32[]{:S(2)}) collective-permute-start(bf16[1,24,896]{2,1,0:T(8,128)(2,1)} %bitcast.2), channel_id=1, source_target_pairs={{0,24},{4,28},{8,16},{12,20},{16,8},{20,12},{24,0},{28,4},{1,25},{... | collective-permute-start | bytes 129032 | tf_op jit(solution)/shard_map/ppermute | solution.py:351
  25.6 0.0 collective-permute-start.1
  25.6 0.6 collective-permute-start
  26.1 2.1 %collective-permute-done.2.refs_3_ = bf16[1,24,896]{2,1,0:T(8,128)(2,1)S(1)} collective-permute-done((bf16[1,24,896]{2,1,0:T(8,128)(2,1)}, bf16[1,24,896]{2,1,0:T(8,128)(2,1)S(1)}, u32[]{:S(2)}, u32[]{:S(2)}) %collective-permute-start.2) | collective-permute-done | bytes 43040 | tf_op jit(solution)/shard_map/ppermute | solution.py:351
  28.3 2.4 %collective-permute-done.1.refs_2_ = bf16[1,24,896]{2,1,0:T(8,128)(2,1)S(1)} collective-permute-done((bf16[1,24,896]{2,1,0:T(8,128)(2,1)}, bf16[1,24,896]{2,1,0:T(8,128)(2,1)S(1)}, u32[]{:S(2)}, u32[]{:S(2)}) %collective-permute-start.1) | collective-permute-done | bytes 43040 | tf_op jit(solution)/shard_map/ppermute | solution.py:351
  30.7 0.0 collective-permute-done.refs_1_
  30.7 0.8 %copy-done.2 = bf16[24,896]{1,0:T(8,128)(2,1)S(1)} copy-done((bf16[24,896]{1,0:T(8,128)(2,1)S(1)}, bf16[24,896]{1,0:T(8,128)(2,1)}, u32[]{:S(2)}) %copy-start.2) | copy-done | bytes 43032
  31.5 0.1 collective-permute-start.7
  31.6 0.0 collective-permute-done.11.refs_11_
  31.6 0.1 collective-permute-start.12
  31.7 1.6 %collective-permute-start.3 = (bf16[4,24,896]{2,1,0:T(8,128)(2,1)S(1)}, bf16[4,24,896]{2,1,0:T(8,128)(2,1)S(1)}, u32[]{:S(2)}, u32[]{:S(2)}) collective-permute-start(bf16[4,24,896]{2,1,0:T(8,128)(2,1)S(1)} %shard_map.111.refs_0_), channel_id=1, source_target_pairs={{0,4},{4,0},{8,12},{12,8},{16,20},{20,16},{24,28},{28,24},{1,5},{5... | collective-permute-start | bytes 516104 | tf_op jit(solution)/shard_map/ppermute | solution.py:351
  33.3 5.1 %collective-permute-done.3.refs_1_ = bf16[4,24,896]{2,1,0:T(8,128)(2,1)S(1)} collective-permute-done((bf16[4,24,896]{2,1,0:T(8,128)(2,1)S(1)}, bf16[4,24,896]{2,1,0:T(8,128)(2,1)S(1)}, u32[]{:S(2)}, u32[]{:S(2)}) %collective-permute-start.3) | collective-permute-done | bytes 172064 | tf_op jit(solution)/shard_map/ppermute | solution.py:351
  38.4 1.5 %collective-permute-start.5 = (bf16[8,24,896]{2,1,0:T(8,128)(2,1)S(1)}, bf16[8,24,896]{2,1,0:T(8,128)(2,1)S(1)}, u32[]{:S(2)}, u32[]{:S(2)}) collective-permute-start(bf16[8,24,896]{2,1,0:T(8,128)(2,1)S(1)} %shard_map.112.refs_0_), channel_id=1, source_target_pairs={{0,2},{1,3},{2,0},{3,1},{4,6},{5,7},{6,4},{7,5},{8,10},{9,11},{10,... | collective-permute-start | bytes 1032200 | tf_op jit(solution)/shard_map/ppermute | solution.py:351
  40.0 0.0 collective-permute-start.4
  40.0 0.5 collective-permute-start.8
  40.5 7.5 %collective-permute-done.5.refs_2_ = bf16[8,24,896]{2,1,0:T(8,128)(2,1)S(1)} collective-permute-done((bf16[8,24,896]{2,1,0:T(8,128)(2,1)S(1)}, bf16[8,24,896]{2,1,0:T(8,128)(2,1)S(1)}, u32[]{:S(2)}, u32[]{:S(2)}) %collective-permute-start.5) | collective-permute-done | bytes 344096 | tf_op jit(solution)/shard_map/ppermute | solution.py:351
  48.0 0.0 collective-permute-start.9
  48.0 0.0 collective-permute-done.4.refs_1_
  48.0 0.5 collective-permute-start.14
  48.5 0.0 collective-permute-done.7.refs_7_
  48.5 0.1 collective-permute-start.13
  48.6 0.4 collective-permute-start.15
  49.0 0.0 collective-permute-done.8.refs_8_
  49.0 0.1 collective-permute-start.6
  49.1 0.8 %collective-permute-done.9.refs_9_ = bf16[256,1024]{1,0:T(8,128)(2,1)S(1)} collective-permute-done((bf16[256,1024]{1,0:T(8,128)(2,1)S(1)}, bf16[256,1024]{1,0:T(8,128)(2,1)S(1)}, u32[]{:S(2)}, u32[]{:S(2)}) %collective-permute-start.9) | collective-permute-done | bytes 524320 | tf_op jit(solution)/shard_map/ppermute | solution.py:351
  49.9 2.7 %collective-permute-done.6.refs_3_ = bf16[8,24,896]{2,1,0:T(8,128)(2,1)S(1)} collective-permute-done((bf16[8,24,896]{2,1,0:T(8,128)(2,1)S(1)}, bf16[8,24,896]{2,1,0:T(8,128)(2,1)S(1)}, u32[]{:S(2)}, u32[]{:S(2)}) %collective-permute-start.6) | collective-permute-done | bytes 344096 | tf_op jit(solution)/shard_map/ppermute | solution.py:351
  52.7 0.0 collective-permute-done.14.refs_14_
  52.7 6.8 %shard_map.114 = (bf16[24,256]{1,0:T(8,128)(2,1)}, bf16[24,256]{1,0:T(8,128)(2,1)}, f32[256,1024]{1,0:T(8,128)}, f32[256,1024]{1,0:T(8,128)}, f32[256,1024]{1,0:T(8,128)}) custom-call(bf16[8,24,896]{2,1,0:T(8,128)(2,1)S(1)} %shard_map.112.refs_0_, bf16[8,24,896]{2,1,0:T(8,128)(2,1)S(1)} %collective-permute-done.4.refs_1_, ...), custom_call_target="tpu_custom_call" | custom-call | flops 2415919104 | bytes 10485760 | tf_op jit(solution)/shard_map/pallas_call | solution.py:234
  (13 shorter events, 0.1 us)
Async XLA Ops:
  2.5 29.1 %collective-permute-start.11 = (bf16[256,1024]{1,0:T(8,128)(2,1)}, bf16[256,1024]{1,0:T(8,128)(2,1)S(1)}, u32[]{:S(2)}, u32[]{:S(2)}) collective-permute-start(bf16[256,1024]{1,0:T(8,128)(2,1)} %shard_map.113), channel_id=1, source_target_pairs={{0,2},{1,3},{2,0},{3,1},{4,6},{5,7},{6,4},{7,5},{8,10},{9,11},{10,... | collective-permute-start | bytes 1572872 | tf_op jit(solution)/shard_map/ppermute | solution.py:351
  5.5 34.5 %collective-permute-start.10 = (bf16[256,1024]{1,0:T(8,128)(2,1)}, bf16[256,1024]{1,0:T(8,128)(2,1)S(1)}, u32[]{:S(2)}, u32[]{:S(2)}) collective-permute-start(bf16[256,1024]{1,0:T(8,128)(2,1)} %refs_4_.1), channel_id=1, source_target_pairs={{0,2},{1,3},{2,0},{3,1},{4,6},{5,7},{6,4},{7,5},{8,10},{9,11},{10,... | collective-permute-start | bytes 1572872 | tf_op jit(solution)/shard_map/ppermute | solution.py:351
  5.6 25.9 %copy-start.3 = (bf16[256,1024]{1,0:T(8,128)(2,1)S(1)}, bf16[256,1024]{1,0:T(8,128)(2,1)}, u32[]{:S(2)}) copy-start(bf16[256,1024]{1,0:T(8,128)(2,1)} %refs_4_.1) | copy-start | bytes 1572868
  5.6 34.4 %copy-start = (bf16[256,1024]{1,0:T(8,128)(2,1)S(1)}, bf16[256,1024]{1,0:T(8,128)(2,1)}, u32[]{:S(2)}) copy-start(bf16[256,1024]{1,0:T(8,128)(2,1)} %refs_5_.1) | copy-start | bytes 1572868
  5.6 42.4 %copy-start.1 = (bf16[256,1024]{1,0:T(8,128)(2,1)S(1)}, bf16[256,1024]{1,0:T(8,128)(2,1)}, u32[]{:S(2)}) copy-start(bf16[256,1024]{1,0:T(8,128)(2,1)} %refs_6_.1) | copy-start | bytes 1572868
  21.5 6.7 %collective-permute-start.2 = (bf16[1,24,896]{2,1,0:T(8,128)(2,1)}, bf16[1,24,896]{2,1,0:T(8,128)(2,1)S(1)}, u32[]{:S(2)}, u32[]{:S(2)}) collective-permute-start(bf16[1,24,896]{2,1,0:T(8,128)(2,1)} %bitcast.2), channel_id=1, source_target_pairs={{0,24},{4,28},{8,16},{12,20},{16,8},{20,12},{24,0},{28,4},{1,25},{... | collective-permute-start | bytes 129032 | tf_op jit(solution)/shard_map/ppermute | solution.py:351
  25.6 5.1 %collective-permute-start.1 = (bf16[1,24,896]{2,1,0:T(8,128)(2,1)}, bf16[1,24,896]{2,1,0:T(8,128)(2,1)S(1)}, u32[]{:S(2)}, u32[]{:S(2)}) collective-permute-start(bf16[1,24,896]{2,1,0:T(8,128)(2,1)} %bitcast.3), channel_id=1, source_target_pairs={{0,16},{4,20},{8,24},{12,28},{16,0},{20,4},{24,8},{28,12},{1,17},{... | collective-permute-start | bytes 129032 | tf_op jit(solution)/shard_map/ppermute | solution.py:351
  25.6 5.1 %collective-permute-start = (bf16[1,24,896]{2,1,0:T(8,128)(2,1)}, bf16[1,24,896]{2,1,0:T(8,128)(2,1)S(1)}, u32[]{:S(2)}, u32[]{:S(2)}) collective-permute-start(bf16[1,24,896]{2,1,0:T(8,128)(2,1)} %bitcast.4), channel_id=1, source_target_pairs={{0,8},{4,12},{8,0},{12,4},{16,24},{20,28},{24,16},{28,20},{1,9},{5... | collective-permute-start | bytes 129032 | tf_op jit(solution)/shard_map/ppermute | solution.py:351
  30.7 0.8 %copy-start.2 = (bf16[24,896]{1,0:T(8,128)(2,1)S(1)}, bf16[24,896]{1,0:T(8,128)(2,1)}, u32[]{:S(2)}) copy-start(bf16[24,896]{1,0:T(8,128)(2,1)} %shard_map.110) | copy-start | bytes 129028
  31.5 17.0 %collective-permute-start.7 = (bf16[256,1024]{1,0:T(8,128)(2,1)S(1)}, bf16[256,1024]{1,0:T(8,128)(2,1)S(1)}, u32[]{:S(2)}, u32[]{:S(2)}) collective-permute-start(bf16[256,1024]{1,0:T(8,128)(2,1)S(1)} %copy-done.3), channel_id=1, source_target_pairs={{0,1},{1,0},{2,3},{3,2},{4,5},{5,4},{6,7},{7,6},{8,9},{9,8},{10,11... | collective-permute-start | bytes 1572872 | tf_op jit(solution)/shard_map/ppermute | solution.py:351
  31.6 17.0 %collective-permute-start.12 = (bf16[256,1024]{1,0:T(8,128)(2,1)S(1)}, bf16[256,1024]{1,0:T(8,128)(2,1)S(1)}, u32[]{:S(2)}, u32[]{:S(2)}) collective-permute-start(bf16[256,1024]{1,0:T(8,128)(2,1)S(1)} %collective-permute-done.11.refs_11_), channel_id=1, source_target_pairs={{0,8},{4,12},{8,0},{12,4},{16,24},{20,28},{24,16},{28,20},{1,9},{5... | collective-permute-start | bytes 1572872 | tf_op jit(solution)/shard_map/ppermute | solution.py:351
  31.7 6.7 %collective-permute-start.3 = (bf16[4,24,896]{2,1,0:T(8,128)(2,1)S(1)}, bf16[4,24,896]{2,1,0:T(8,128)(2,1)S(1)}, u32[]{:S(2)}, u32[]{:S(2)}) collective-permute-start(bf16[4,24,896]{2,1,0:T(8,128)(2,1)S(1)} %shard_map.111.refs_0_), channel_id=1, source_target_pairs={{0,4},{4,0},{8,12},{12,8},{16,20},{20,16},{24,28},{28,24},{1,5},{5... | collective-permute-start | bytes 516104 | tf_op jit(solution)/shard_map/ppermute | solution.py:351
  38.4 9.6 %collective-permute-start.5 = (bf16[8,24,896]{2,1,0:T(8,128)(2,1)S(1)}, bf16[8,24,896]{2,1,0:T(8,128)(2,1)S(1)}, u32[]{:S(2)}, u32[]{:S(2)}) collective-permute-start(bf16[8,24,896]{2,1,0:T(8,128)(2,1)S(1)} %shard_map.112.refs_0_), channel_id=1, source_target_pairs={{0,2},{1,3},{2,0},{3,1},{4,6},{5,7},{6,4},{7,5},{8,10},{9,11},{10,... | collective-permute-start | bytes 1032200 | tf_op jit(solution)/shard_map/ppermute | solution.py:351
  40.0 8.0 %collective-permute-start.4 = (bf16[8,24,896]{2,1,0:T(8,128)(2,1)S(1)}, bf16[8,24,896]{2,1,0:T(8,128)(2,1)S(1)}, u32[]{:S(2)}, u32[]{:S(2)}) collective-permute-start(bf16[8,24,896]{2,1,0:T(8,128)(2,1)S(1)} %shard_map.112.refs_0_), channel_id=1, source_target_pairs={{0,1},{1,0},{2,3},{3,2},{4,5},{5,4},{6,7},{7,6},{8,9},{9,8},{10,11... | collective-permute-start | bytes 1032200 | tf_op jit(solution)/shard_map/ppermute | solution.py:351
  40.0 9.1 %collective-permute-start.8 = (bf16[256,1024]{1,0:T(8,128)(2,1)S(1)}, bf16[256,1024]{1,0:T(8,128)(2,1)S(1)}, u32[]{:S(2)}, u32[]{:S(2)}) collective-permute-start(bf16[256,1024]{1,0:T(8,128)(2,1)S(1)} %copy-done), channel_id=1, source_target_pairs={{0,1},{1,0},{2,3},{3,2},{4,5},{5,4},{6,7},{7,6},{8,9},{9,8},{10,11... | collective-permute-start | bytes 1572872 | tf_op jit(solution)/shard_map/ppermute | solution.py:351
  48.0 1.9 %collective-permute-start.9 = (bf16[256,1024]{1,0:T(8,128)(2,1)S(1)}, bf16[256,1024]{1,0:T(8,128)(2,1)S(1)}, u32[]{:S(2)}, u32[]{:S(2)}) collective-permute-start(bf16[256,1024]{1,0:T(8,128)(2,1)S(1)} %copy-done.1), channel_id=1, source_target_pairs={{0,1},{1,0},{2,3},{3,2},{4,5},{5,4},{6,7},{7,6},{8,9},{9,8},{10,11... | collective-permute-start | bytes 1572872 | tf_op jit(solution)/shard_map/ppermute | solution.py:351
  48.0 4.6 %collective-permute-start.14 = (bf16[256,1024]{1,0:T(8,128)(2,1)S(1)}, bf16[256,1024]{1,0:T(8,128)(2,1)S(1)}, u32[]{:S(2)}, u32[]{:S(2)}) collective-permute-start(bf16[256,1024]{1,0:T(8,128)(2,1)S(1)} %collective-permute-done.11.refs_11_), channel_id=1, source_target_pairs={{0,1},{1,0},{2,3},{3,2},{4,5},{5,4},{6,7},{7,6},{8,9},{9,8},{10,11... | collective-permute-start | bytes 1572872 | tf_op jit(solution)/shard_map/ppermute | solution.py:351
  48.5 4.1 %collective-permute-start.13 = (bf16[256,1024]{1,0:T(8,128)(2,1)S(1)}, bf16[256,1024]{1,0:T(8,128)(2,1)S(1)}, u32[]{:S(2)}, u32[]{:S(2)}) collective-permute-start(bf16[256,1024]{1,0:T(8,128)(2,1)S(1)} %collective-permute-done.10.refs_10_), channel_id=1, source_target_pairs={{0,1},{1,0},{2,3},{3,2},{4,5},{5,4},{6,7},{7,6},{8,9},{9,8},{10,11... | collective-permute-start | bytes 1572872 | tf_op jit(solution)/shard_map/ppermute | solution.py:351
  48.6 4.1 %collective-permute-start.15 = (bf16[256,1024]{1,0:T(8,128)(2,1)S(1)}, bf16[256,1024]{1,0:T(8,128)(2,1)S(1)}, u32[]{:S(2)}, u32[]{:S(2)}) collective-permute-start(bf16[256,1024]{1,0:T(8,128)(2,1)S(1)} %collective-permute-done.12.refs_12_), channel_id=1, source_target_pairs={{0,1},{1,0},{2,3},{3,2},{4,5},{5,4},{6,7},{7,6},{8,9},{9,8},{10,11... | collective-permute-start | bytes 1572872 | tf_op jit(solution)/shard_map/ppermute | solution.py:351
  49.0 3.6 %collective-permute-start.6 = (bf16[8,24,896]{2,1,0:T(8,128)(2,1)S(1)}, bf16[8,24,896]{2,1,0:T(8,128)(2,1)S(1)}, u32[]{:S(2)}, u32[]{:S(2)}) collective-permute-start(bf16[8,24,896]{2,1,0:T(8,128)(2,1)S(1)} %collective-permute-done.5.refs_2_), channel_id=1, source_target_pairs={{0,1},{1,0},{2,3},{3,2},{4,5},{5,4},{6,7},{7,6},{8,9},{9,8},{10,11... | collective-permute-start | bytes 1032200 | tf_op jit(solution)/shard_map/ppermute | solution.py:351

commit v8 on v7

--- a/solution.py
+++ b/solution.py
@@ -10,7 +10,7 @@
 HD = 64
 BF = jnp.bfloat16
 F32 = jnp.float32
-NODES_STEP = 3
+NODES_STEP = 6
 WIDE_LIMIT = 256
 IDS_COLS = 128
 IDS_AT = 32
@@ -31,27 +31,26 @@
     return jnp.dot(a, b, preferred_element_type=F32)
 
 
-def attend(qkv, heads, seq, ones_ref, row, acc_p):
-    cols = heads * HD
+def attend(q, k, v, heads):
+    seq, cols = q.shape
     lane = lax.broadcasted_iota(jnp.int32, (seq, cols), 1) // HD
     zero = jnp.zeros((seq, cols), BF)
-    for n in range(NODES_STEP):
-        at = slice(n * seq, (n + 1) * seq)
-        q, k, v = (qkv[at, i * cols : (i + 1) * cols] for i in range(3))
-        spread = jnp.concatenate([jnp.where(lane == h, q, zero) for h in range(heads)], axis=0)
-        s = dot_t(k, spread)
-        e = jnp.exp2((s - jnp.max(s, axis=0, keepdims=True)) * (HD**-0.5 * LOG2E))
-        p = (e * (1.0 / jnp.sum(e, axis=0, keepdims=True))).astype(BF)
-        context = jnp.sum(dot(p, ones_ref[...]) * v.astype(F32), axis=0, keepdims=True)
-        acc_p[pl.ds(row + n, 1), :] = context * (1.0 / seq)
-
-
-def attention_kernel(heads, x_ref, w_ref, cot_ref, ids_ref, out_ref, wp, ones, last, acc_p, acc_m):
+    spread = jnp.concatenate([jnp.where(lane == h, k, zero) for h in range(heads)], axis=0)
+    s = dot_t(spread, q).reshape(heads, seq, seq)
+    e = jnp.exp2((s - jnp.max(s, axis=1, keepdims=True)) * (HD**-0.5 * LOG2E))
+    p = (e * (1.0 / jnp.sum(e, axis=1, keepdims=True))).astype(BF)
+    weight = jnp.sum(p.astype(F32), axis=2, keepdims=True)
+    left = lax.broadcasted_iota(jnp.int32, (seq, 2 * HD), 1) < HD
+    pairs = [jnp.where(left, weight[h], weight[h + 1]) for h in range(0, heads, 2)]
+    context = jnp.concatenate(pairs, axis=1) * v.astype(F32)
+    return jnp.sum(context, axis=0, keepdims=True) * (1.0 / seq)
+
+
+def attention_kernel(heads, x_ref, w_ref, cot_ref, ids_ref, out_ref, wp, acc_p, acc_m):
     step = pl.program_id(0)
     nodes, seq, width = x_ref.shape
     node_dev = cot_ref.shape[0]
     cols = heads * HD
-    half = NODES_STEP * seq
 
     @pl.when(step == 0)
     def _():
@@ -62,33 +61,19 @@
                 wp[:, part * cols + h * HD : part * cols + (h + 2) * HD] = jnp.concatenate(
                     [w_ref[:, a : a + HD], w_ref[:, b : b + HD]], axis=1
                 )
-        row = lax.broadcasted_iota(jnp.int32, (heads * seq, cols), 0) // seq
-        column = lax.broadcasted_iota(jnp.int32, (heads * seq, cols), 1) // HD
-        ones[...] = (row == column).astype(F32).astype(BF)
-        last[...] = jnp.zeros_like(last)
 
     own = pl.ds(pl.multiple_of(lax.axis_index("mp") * cols, 128), cols)
-    begin = step * nodes
-
-    def product(first):
-        return dot(x_ref[first : first + NODES_STEP].reshape(half, width), wp[...]).astype(BF)
-
-    def attend_at(qkv, row):
-        attend(qkv, heads, seq, ones, row, acc_p)
-
-    before = jnp.where(step == 0, node_dev, begin - NODES_STEP)
-    qkv = product(0)
-    attend_at(last, before)
-    last[...] = product(NODES_STEP)
-    attend_at(qkv, begin)
+    qkv = dot(x_ref[...].reshape(nodes * seq, width), wp[...]).astype(BF)
     for n in range(nodes):
+        at = slice(n * seq, (n + 1) * seq)
+        row = pl.ds(step * nodes + n, 1)
+        acc_p[row, :] = attend(*(qkv[at, i * cols : (i + 1) * cols] for i in range(3)), heads)
         mean = jnp.sum(x_ref[n, :, own].astype(F32), axis=0, keepdims=True)
-        acc_m[pl.ds(begin + n, 1), :] = mean * (1.0 / seq)
+        acc_m[row, :] = mean * (1.0 / seq)
 
     @pl.when(step == pl.num_programs(0) - 1)
     def _():
-        attend_at(last, node_dev - NODES_STEP)
-        out_ref[:, :cols] = acc_p[:node_dev, :].astype(BF)
+        out_ref[:, :cols] = acc_p[...].astype(BF)
         out_ref[:, cols : 2 * cols] = cot_ref[...]
         out_ref[:, 2 * cols : 3 * cols] = acc_m[...].astype(BF)
         shifted = ids_ref[...] + 1
@@ -106,7 +91,7 @@
     cols = w_qkv.shape[1] // 3
     heads = cols // HD
     tokens = node_dev * seq
-    nodes = 2 * NODES_STEP
+    nodes = NODES_STEP
     return pl.pallas_call(
         functools.partial(attention_kernel, heads),
         out_shape=jax.ShapeDtypeStruct((node_dev, 3 * cols + IDS_COLS), BF),
@@ -120,9 +105,7 @@
         out_specs=pl.BlockSpec((node_dev, 3 * cols + IDS_COLS), lambda i: (0, 0)),
         scratch_shapes=[
             pltpu.VMEM((width, 3 * cols), BF),
-            pltpu.VMEM((heads * seq, cols), BF),
-            pltpu.VMEM((NODES_STEP * seq, 3 * cols), BF),
-            pltpu.VMEM((node_dev + 8, cols), F32),
+            pltpu.VMEM((node_dev, cols), F32),
             pltpu.VMEM((node_dev, cols), F32),
         ],
         compiler_params=pltpu.CompilerParams(vmem_limit_bytes=ATTENTION_VMEM * MIB),
@@ -299,10 +282,14 @@
 
 
 def join_kernel(*refs):
-    out, at = refs[-1], 0
-    for ref in refs[:-1]:
+    first, *rest, out, sem = refs
+    copy = pltpu.make_async_copy(first, out.at[0 : first.shape[0]], sem)
+    copy.start()
+    at = first.shape[0]
+    for ref in rest:
         out[at : at + ref.shape[0]] = ref[...]
         at += ref.shape[0]
+    copy.wait()
 
 
 def join(*blocks):
@@ -313,38 +300,11 @@
     return pl.pallas_call(
         join_kernel,
         out_shape=jax.ShapeDtypeStruct((count, *blocks[0].shape[1:]), BF),
-        in_specs=[vmem] * len(blocks),
+        in_specs=[pl.BlockSpec(memory_space=pl.ANY)] + [vmem] * (len(blocks) - 1),
         out_specs=vmem,
+        scratch_shapes=[pltpu.SemaphoreType.DMA],
         compiler_params=pltpu.CompilerParams(vmem_limit_bytes=8 * MIB),
     )(*blocks)
-
-
-def pick_kernel(first, second, out, sem):
-    side = (lax.axis_index("dp") // 2) % 2
-
-    @pl.when(side == 0)
-    def _():
-        copy = pltpu.make_async_copy(first, out, sem)
-        copy.start()
-        copy.wait()
-
-    @pl.when(side == 1)
-    def _():
-        copy = pltpu.make_async_copy(second, out, sem)
-        copy.start()
-        copy.wait()
-
-
-def pick(first, second):
-    anywhere = pl.BlockSpec(memory_space=pl.ANY)
-    return pl.pallas_call(
-        pick_kernel,
-        out_shape=jax.ShapeDtypeStruct(first.shape, first.dtype),
-        in_specs=[anywhere, anywhere],
-        out_specs=pl.BlockSpec(memory_space=pltpu.VMEM),
-        scratch_shapes=[pltpu.SemaphoreType.DMA],
-        compiler_params=pltpu.CompilerParams(vmem_limit_bytes=60 * MIB),
-    )(first, second)
 
 
 def hop(x, axis, bit):
@@ -354,9 +314,10 @@
 def gather_dp(block, later):
     size = lax.axis_size("dp")
     if size == 8:
-        block = join(block, *[hop(block, "dp", i) for i in (2, 4, 6)])
+        far = [hop(block, "dp", i) for i in (2, 4, 6)]
+        far[0], later = lax.optimization_barrier((far[0], later))
+        block = join(block, *far)
         order, bit = [0, 2, 4, 6], 1
-        block, later = lax.optimization_barrier((block, later))
     else:
         order, bit = [0], size // 2
     while bit:
@@ -369,14 +330,16 @@
 def per_device(texts, w_qkv, w_out, w_self, w_neigh, neighbours, cotangent):
     node_dev, fan = neighbours.shape
     nodes = node_dev * lax.axis_size("dp")
-    x_half = hop(pick(w_self, w_neigh), "mp", 2)
+    own = (w_out, w_self, w_neigh)
+    even = (lax.axis_index("dp") // 2) % 2 == 0
+    x_half = hop(jnp.where(even, w_self, w_neigh), "mp", 2)
     x_out = hop(w_out, "mp", 2)
-    own = (w_out, w_self, w_neigh)
+    here = tuple(hop(a, "mp", 1) for a in own)
 
     sent = attention(texts, w_qkv, cotangent, neighbours.T)[None]
-    sent, order, late = gather_dp(sent, own)
+    sent, here = lax.optimization_barrier((sent, here))
+    sent, order, x_half = gather_dp(sent, x_half)
     z_half = hop(x_half, "dp", 2)
-    here = tuple(hop(a, "mp", 1) for a in late)
     across = (x_out, x_half, z_half)
     there = tuple(hop(a, "mp", 1) for a in across)
 

time: 59.7 us -> 60.3 us (1.010)
  Pallas kernels: 24.6 us -> 18.6 us
  waiting for transfers between devices: 20.8 us -> 25.8 us
  other arithmetic: 0 us -> 1.1 us
    ppermute x16, waiting for transfers between devices: 20.8 us -> 25.8 us  [hop(): lax.ppermute(x, axis, [(i, i ^ bit) for i in range(lax.axis_size(axis))])]
    pallas_call x1, Pallas kernels: 15.9 us -> 11.5 us  [attention(): pl.pallas_call(functools.partial(attention_kernel, heads), out_shape=jax....]
    pallas_call x1 -> x0, Pallas kernels: 1.86 us -> none  [pick(): pl.pallas_call(pick_kernel, out_shape=jax.ShapeDtypeStruct(first.shape, f...]
    select_n x0 -> x1, other arithmetic: none -> 1.1 us  [per_device(): x_half = hop(jnp.where(even, w_self, w_neigh), 'mp', 2)]
  transfers between devices with their start and end apart: 16 -> 16, of which waited for: 6 -> 5; matrix products, arithmetic and copies ran while one was open for 0% -> 2% of each run, Pallas kernels for 27% -> 20%
where the time goes in v8:
time: 60.3 us; the launch traced here: 60.1 us
  waiting for transfers between devices  25.8 us (43%)
  Pallas kernels  18.6 us (31%)
  starting transfers between devices  13.1 us (22%)
  other arithmetic  1.1 us (2%)
  local copies, waits for them, and re-layouts  0.8 us (1%)
  between operations  0.7 us (1%)
    ppermute x16, waiting for transfers between devices, hop(): lax.ppermute(x, axis, [(i, i ^ bit) for i in range(lax.axis_size(axis))])  25.8 us
    ppermute x16, starting transfers between devices, hop(): lax.ppermute(x, axis, [(i, i ^ bit) for i in range(lax.axis_size(axis))])  13.1 us
    pallas_call x1, Pallas kernels, attention(): pl.pallas_call(functools.partial(attention_kernel, heads), out_shape=jax....  11.5 us
    pallas_call x1, Pallas kernels, graph(): pl.pallas_call(functools.partial(graph_kernel, order, fan), out_shape=(sl...  6.8 us
  transfers between devices with their start and end apart: 16, of which 5 were waited for; matrix products, arithmetic and copies ran while one was open for 2% of the time, Pallas kernels for 20%

profile of v8, /device:TPU:0, one launch (start us, length us, event | category | flops | bytes accessed | tf_op | source)
XLA Modules:
  0.0 60.1 jit_solution(12392773542355652686)
XLA Ops:
  0.6 0.5 collective-permute-start.1
  1.1 0.1 collective-permute-start.2
  1.2 1.1 %broadcast_select_fusion = bf16[256,1024]{1,0:T(8,128)(2,1)S(1)} fusion(bf16[256,1024]{1,0:T(8,128)(2,1)} %refs_5_.1, bf16[256,1024]{1,0:T(8,128)(2,1)} %refs_6_.1, pred[]{:T(512)S(6)} %eq.5), kind=kLoop, calls=%fused_computation | loop fusion | flops 262144 | bytes 1572865 | tf_op jit(solution)/shard_map/jit(_where)/select_n | solution.py:335
  2.3 3.0 %collective-permute-start.4 = (bf16[256,1024]{1,0:T(8,128)(2,1)S(1)}, bf16[256,1024]{1,0:T(8,128)(2,1)S(1)}, u32[]{:S(2)}, u32[]{:S(2)}) collective-permute-start(bf16[256,1024]{1,0:T(8,128)(2,1)S(1)} %broadcast_select_fusion), channel_id=1, source_target_pairs={{0,2},{1,3},{2,0},{3,1},{4,6},{5,7},{6,4},{7,5},{8,10},{9,11},{10,... | collective-permute-start | bytes 1572872 | tf_op jit(solution)/shard_map/ppermute | solution.py:311
  5.3 0.0 collective-permute-start
  5.3 11.5 %shard_map.110 = bf16[24,896]{1,0:T(8,128)(2,1)} custom-call(bf16[24,128,1024]{2,1,0:T(8,128)(2,1)} %x_ref.1, bf16[1024,768]{1,0:T(8,128)(2,1)} %w_ref.1, bf16[24,256]{1,0:T(8,128)(2,1)} %cot_ref.1, s32[16,24]{1,0:T(8,128)} %bitcast.6), custom_call_target="tpu_custom_call" | custom-call | flops 5637144576 | bytes 7864320 | tf_op jit(solution)/shard_map/pallas_call | solution.py:95
  16.9 0.0 collective-permute-done.refs_7_
  16.9 0.0 collective-permute-done.1.refs_8_
  16.9 1.6 %collective-permute-start.3 = (bf16[1,24,896]{2,1,0:T(8,128)(2,1)}, bf16[1,24,896]{2,1,0:T(8,128)(2,1)S(1)}, u32[]{:S(2)}, u32[]{:S(2)}) collective-permute-start(bf16[1,24,896]{2,1,0:T(8,128)(2,1)} %bitcast.2), channel_id=1, source_target_pairs={{0,8},{4,12},{8,0},{12,4},{16,24},{20,28},{24,16},{28,20},{1,9},{5... | collective-permute-start | bytes 129032 | tf_op jit(solution)/shard_map/ppermute | solution.py:311
  18.5 0.5 collective-permute-start.11
  19.1 0.0 collective-permute-done.4.refs_11_
  19.1 2.1 %collective-permute-done.3.refs_1_ = bf16[1,24,896]{2,1,0:T(8,128)(2,1)S(1)} collective-permute-done((bf16[1,24,896]{2,1,0:T(8,128)(2,1)}, bf16[1,24,896]{2,1,0:T(8,128)(2,1)S(1)}, u32[]{:S(2)}, u32[]{:S(2)}) %collective-permute-start.3) | collective-permute-done | bytes 43040 | tf_op jit(solution)/shard_map/ppermute | solution.py:311
  21.2 1.6 %collective-permute-start.12 = (bf16[256,1024]{1,0:T(8,128)(2,1)S(1)}, bf16[256,1024]{1,0:T(8,128)(2,1)S(1)}, u32[]{:S(2)}, u32[]{:S(2)}) collective-permute-start(bf16[256,1024]{1,0:T(8,128)(2,1)S(1)} %collective-permute-done.4.refs_11_), channel_id=1, source_target_pairs={{0,8},{4,12},{8,0},{12,4},{16,24},{20,28},{24,16},{28,20},{1,9},{5... | collective-permute-start | bytes 1572872 | tf_op jit(solution)/shard_map/ppermute | solution.py:311
  22.8 2.5 %collective-permute-start.6 = (bf16[1,24,896]{2,1,0:T(8,128)(2,1)}, bf16[1,24,896]{2,1,0:T(8,128)(2,1)S(1)}, u32[]{:S(2)}, u32[]{:S(2)}) collective-permute-start(bf16[1,24,896]{2,1,0:T(8,128)(2,1)} %bitcast.3), channel_id=1, source_target_pairs={{0,24},{4,28},{8,16},{12,20},{16,8},{20,12},{24,0},{28,4},{1,25},{... | collective-permute-start | bytes 129032 | tf_op jit(solution)/shard_map/ppermute | solution.py:311
  25.2 0.1 collective-permute-start.5
  25.3 12.4 %collective-permute-done.6.refs_3_ = bf16[1,24,896]{2,1,0:T(8,128)(2,1)S(1)} collective-permute-done((bf16[1,24,896]{2,1,0:T(8,128)(2,1)}, bf16[1,24,896]{2,1,0:T(8,128)(2,1)S(1)}, u32[]{:S(2)}, u32[]{:S(2)}) %collective-permute-start.6) | collective-permute-done | bytes 43040 | tf_op jit(solution)/shard_map/ppermute | solution.py:311
  37.8 0.8 %copy-done.2 = bf16[24,896]{1,0:T(8,128)(2,1)S(1)} copy-done((bf16[24,896]{1,0:T(8,128)(2,1)S(1)}, bf16[24,896]{1,0:T(8,128)(2,1)}, u32[]{:S(2)}) %copy-start.2) | copy-done | bytes 43032
  38.6 1.6 %collective-permute-start.7 = (bf16[4,24,896]{2,1,0:T(8,128)(2,1)S(1)}, bf16[4,24,896]{2,1,0:T(8,128)(2,1)S(1)}, u32[]{:S(2)}, u32[]{:S(2)}) collective-permute-start(bf16[4,24,896]{2,1,0:T(8,128)(2,1)S(1)} %shard_map.111.refs_0_), channel_id=1, source_target_pairs={{0,4},{4,0},{8,12},{12,8},{16,20},{20,16},{24,28},{28,24},{1,5},{5... | collective-permute-start | bytes 516104 | tf_op jit(solution)/shard_map/ppermute | solution.py:311
  40.2 3.9 %collective-permute-done.7.refs_1_ = bf16[4,24,896]{2,1,0:T(8,128)(2,1)S(1)} collective-permute-done((bf16[4,24,896]{2,1,0:T(8,128)(2,1)S(1)}, bf16[4,24,896]{2,1,0:T(8,128)(2,1)S(1)}, u32[]{:S(2)}, u32[]{:S(2)}) %collective-permute-start.7) | collective-permute-done | bytes 172064 | tf_op jit(solution)/shard_map/ppermute | solution.py:311
  44.1 0.2 shard_map.112.refs_0_
  44.3 0.6 collective-permute-start.9
  44.9 0.0 collective-permute-done.11.refs_10_
  44.9 0.0 collective-permute-start.13
  44.9 0.5 collective-permute-start.14
  45.4 0.0 collective-permute-done.12.refs_12_
  45.4 0.0 collective-permute-start.15
  45.4 0.5 collective-permute-start.8
  45.9 5.7 %collective-permute-done.9.refs_2_ = bf16[8,24,896]{2,1,0:T(8,128)(2,1)S(1)} collective-permute-done((bf16[8,24,896]{2,1,0:T(8,128)(2,1)S(1)}, bf16[8,24,896]{2,1,0:T(8,128)(2,1)S(1)}, u32[]{:S(2)}, u32[]{:S(2)}) %collective-permute-start.9) | collective-permute-done | bytes 344096 | tf_op jit(solution)/shard_map/ppermute | solution.py:311
  51.6 0.0 collective-permute-start.10
  51.6 0.0 collective-permute-done.13.refs_13_
  51.6 1.6 %collective-permute-done.10.refs_3_ = bf16[8,24,896]{2,1,0:T(8,128)(2,1)S(1)} collective-permute-done((bf16[8,24,896]{2,1,0:T(8,128)(2,1)S(1)}, bf16[8,24,896]{2,1,0:T(8,128)(2,1)S(1)}, u32[]{:S(2)}, u32[]{:S(2)}) %collective-permute-start.10) | collective-permute-done | bytes 344096 | tf_op jit(solution)/shard_map/ppermute | solution.py:311
  53.3 6.8 %shard_map.113 = (bf16[24,256]{1,0:T(8,128)(2,1)}, bf16[24,256]{1,0:T(8,128)(2,1)}, f32[256,1024]{1,0:T(8,128)}, f32[256,1024]{1,0:T(8,128)}, f32[256,1024]{1,0:T(8,128)}) custom-call(bf16[8,24,896]{2,1,0:T(8,128)(2,1)S(1)} %shard_map.112.refs_0_, bf16[8,24,896]{2,1,0:T(8,128)(2,1)S(1)} %collective-permute-done.8.refs_1_, ...), custom_call_target="tpu_custom_call" | custom-call | flops 2415919104 | bytes 10485760 | tf_op jit(solution)/shard_map/pallas_call | solution.py:217
  (13 shorter events, 0.1 us)
Async XLA Ops:
  0.6 16.2 %collective-permute-start.1 = (bf16[256,1024]{1,0:T(8,128)(2,1)}, bf16[256,1024]{1,0:T(8,128)(2,1)S(1)}, u32[]{:S(2)}, u32[]{:S(2)}) collective-permute-start(bf16[256,1024]{1,0:T(8,128)(2,1)} %refs_5_.1), channel_id=1, source_target_pairs={{0,1},{1,0},{2,3},{3,2},{4,5},{5,4},{6,7},{7,6},{8,9},{9,8},{10,11... | collective-permute-start | bytes 1572872 | tf_op jit(solution)/shard_map/ppermute | solution.py:311
  1.1 15.7 %collective-permute-start.2 = (bf16[256,1024]{1,0:T(8,128)(2,1)}, bf16[256,1024]{1,0:T(8,128)(2,1)S(1)}, u32[]{:S(2)}, u32[]{:S(2)}) collective-permute-start(bf16[256,1024]{1,0:T(8,128)(2,1)} %refs_6_.1), channel_id=1, source_target_pairs={{0,1},{1,0},{2,3},{3,2},{4,5},{5,4},{6,7},{7,6},{8,9},{9,8},{10,11... | collective-permute-start | bytes 1572872 | tf_op jit(solution)/shard_map/ppermute | solution.py:311
  2.3 16.7 %collective-permute-start.4 = (bf16[256,1024]{1,0:T(8,128)(2,1)S(1)}, bf16[256,1024]{1,0:T(8,128)(2,1)S(1)}, u32[]{:S(2)}, u32[]{:S(2)}) collective-permute-start(bf16[256,1024]{1,0:T(8,128)(2,1)S(1)} %broadcast_select_fusion), channel_id=1, source_target_pairs={{0,2},{1,3},{2,0},{3,1},{4,6},{5,7},{6,4},{7,5},{8,10},{9,11},{10,... | collective-permute-start | bytes 1572872 | tf_op jit(solution)/shard_map/ppermute | solution.py:311
  5.3 11.6 %collective-permute-start = (bf16[256,1024]{1,0:T(8,128)(2,1)}, bf16[256,1024]{1,0:T(8,128)(2,1)S(1)}, u32[]{:S(2)}, u32[]{:S(2)}) collective-permute-start(bf16[256,1024]{1,0:T(8,128)(2,1)} %refs_4_.1), channel_id=1, source_target_pairs={{0,1},{1,0},{2,3},{3,2},{4,5},{5,4},{6,7},{7,6},{8,9},{9,8},{10,11... | collective-permute-start | bytes 1572872 | tf_op jit(solution)/shard_map/ppermute | solution.py:311
  5.3 13.2 %copy-start.3 = (bf16[256,1024]{1,0:T(8,128)(2,1)S(1)}, bf16[256,1024]{1,0:T(8,128)(2,1)}, u32[]{:S(2)}) copy-start(bf16[256,1024]{1,0:T(8,128)(2,1)} %refs_4_.1) | copy-start | bytes 1572868
  5.3 48.0 %copy-start = (bf16[256,1024]{1,0:T(8,128)(2,1)S(1)}, bf16[256,1024]{1,0:T(8,128)(2,1)}, u32[]{:S(2)}) copy-start(bf16[256,1024]{1,0:T(8,128)(2,1)} %refs_5_.1) | copy-start | bytes 1572868
  5.3 48.0 %copy-start.1 = (bf16[256,1024]{1,0:T(8,128)(2,1)S(1)}, bf16[256,1024]{1,0:T(8,128)(2,1)}, u32[]{:S(2)}) copy-start(bf16[256,1024]{1,0:T(8,128)(2,1)} %refs_6_.1) | copy-start | bytes 1572868
  16.9 4.3 %collective-permute-start.3 = (bf16[1,24,896]{2,1,0:T(8,128)(2,1)}, bf16[1,24,896]{2,1,0:T(8,128)(2,1)S(1)}, u32[]{:S(2)}, u32[]{:S(2)}) collective-permute-start(bf16[1,24,896]{2,1,0:T(8,128)(2,1)} %bitcast.2), channel_id=1, source_target_pairs={{0,8},{4,12},{8,0},{12,4},{16,24},{20,28},{24,16},{28,20},{1,9},{5... | collective-permute-start | bytes 129032 | tf_op jit(solution)/shard_map/ppermute | solution.py:311
  18.5 26.4 %collective-permute-start.11 = (bf16[256,1024]{1,0:T(8,128)(2,1)S(1)}, bf16[256,1024]{1,0:T(8,128)(2,1)S(1)}, u32[]{:S(2)}, u32[]{:S(2)}) collective-permute-start(bf16[256,1024]{1,0:T(8,128)(2,1)S(1)} %copy-done.3), channel_id=1, source_target_pairs={{0,2},{1,3},{2,0},{3,1},{4,6},{5,7},{6,4},{7,5},{8,10},{9,11},{10,... | collective-permute-start | bytes 1572872 | tf_op jit(solution)/shard_map/ppermute | solution.py:311
  21.2 24.2 %collective-permute-start.12 = (bf16[256,1024]{1,0:T(8,128)(2,1)S(1)}, bf16[256,1024]{1,0:T(8,128)(2,1)S(1)}, u32[]{:S(2)}, u32[]{:S(2)}) collective-permute-start(bf16[256,1024]{1,0:T(8,128)(2,1)S(1)} %collective-permute-done.4.refs_11_), channel_id=1, source_target_pairs={{0,8},{4,12},{8,0},{12,4},{16,24},{20,28},{24,16},{28,20},{1,9},{5... | collective-permute-start | bytes 1572872 | tf_op jit(solution)/shard_map/ppermute | solution.py:311
  22.8 15.0 %collective-permute-start.6 = (bf16[1,24,896]{2,1,0:T(8,128)(2,1)}, bf16[1,24,896]{2,1,0:T(8,128)(2,1)S(1)}, u32[]{:S(2)}, u32[]{:S(2)}) collective-permute-start(bf16[1,24,896]{2,1,0:T(8,128)(2,1)} %bitcast.3), channel_id=1, source_target_pairs={{0,24},{4,28},{8,16},{12,20},{16,8},{20,12},{24,0},{28,4},{1,25},{... | collective-permute-start | bytes 129032 | tf_op jit(solution)/shard_map/ppermute | solution.py:311
  25.2 12.5 %collective-permute-start.5 = (bf16[1,24,896]{2,1,0:T(8,128)(2,1)}, bf16[1,24,896]{2,1,0:T(8,128)(2,1)S(1)}, u32[]{:S(2)}, u32[]{:S(2)}) collective-permute-start(bf16[1,24,896]{2,1,0:T(8,128)(2,1)} %bitcast.4), channel_id=1, source_target_pairs={{0,16},{4,20},{8,24},{12,28},{16,0},{20,4},{24,8},{28,12},{1,17},{... | collective-permute-start | bytes 129032 | tf_op jit(solution)/shard_map/ppermute | solution.py:311
  37.8 0.8 %copy-start.2 = (bf16[24,896]{1,0:T(8,128)(2,1)S(1)}, bf16[24,896]{1,0:T(8,128)(2,1)}, u32[]{:S(2)}) copy-start(bf16[24,896]{1,0:T(8,128)(2,1)} %shard_map.110) | copy-start | bytes 129028
  38.6 5.5 %collective-permute-start.7 = (bf16[4,24,896]{2,1,0:T(8,128)(2,1)S(1)}, bf16[4,24,896]{2,1,0:T(8,128)(2,1)S(1)}, u32[]{:S(2)}, u32[]{:S(2)}) collective-permute-start(bf16[4,24,896]{2,1,0:T(8,128)(2,1)S(1)} %shard_map.111.refs_0_), channel_id=1, source_target_pairs={{0,4},{4,0},{8,12},{12,8},{16,20},{20,16},{24,28},{28,24},{1,5},{5... | collective-permute-start | bytes 516104 | tf_op jit(solution)/shard_map/ppermute | solution.py:311
  44.3 7.3 %collective-permute-start.9 = (bf16[8,24,896]{2,1,0:T(8,128)(2,1)S(1)}, bf16[8,24,896]{2,1,0:T(8,128)(2,1)S(1)}, u32[]{:S(2)}, u32[]{:S(2)}) collective-permute-start(bf16[8,24,896]{2,1,0:T(8,128)(2,1)S(1)} %shard_map.112.refs_0_), channel_id=1, source_target_pairs={{0,2},{1,3},{2,0},{3,1},{4,6},{5,7},{6,4},{7,5},{8,10},{9,11},{10,... | collective-permute-start | bytes 1032200 | tf_op jit(solution)/shard_map/ppermute | solution.py:311
  44.9 6.7 %collective-permute-start.13 = (bf16[256,1024]{1,0:T(8,128)(2,1)S(1)}, bf16[256,1024]{1,0:T(8,128)(2,1)S(1)}, u32[]{:S(2)}, u32[]{:S(2)}) collective-permute-start(bf16[256,1024]{1,0:T(8,128)(2,1)S(1)} %collective-permute-done.11.refs_10_), channel_id=1, source_target_pairs={{0,1},{1,0},{2,3},{3,2},{4,5},{5,4},{6,7},{7,6},{8,9},{9,8},{10,11... | collective-permute-start | bytes 1572872 | tf_op jit(solution)/shard_map/ppermute | solution.py:311
  44.9 6.7 %collective-permute-start.14 = (bf16[256,1024]{1,0:T(8,128)(2,1)S(1)}, bf16[256,1024]{1,0:T(8,128)(2,1)S(1)}, u32[]{:S(2)}, u32[]{:S(2)}) collective-permute-start(bf16[256,1024]{1,0:T(8,128)(2,1)S(1)} %collective-permute-done.4.refs_11_), channel_id=1, source_target_pairs={{0,1},{1,0},{2,3},{3,2},{4,5},{5,4},{6,7},{7,6},{8,9},{9,8},{10,11... | collective-permute-start | bytes 1572872 | tf_op jit(solution)/shard_map/ppermute | solution.py:311
  45.4 7.9 %collective-permute-start.15 = (bf16[256,1024]{1,0:T(8,128)(2,1)S(1)}, bf16[256,1024]{1,0:T(8,128)(2,1)S(1)}, u32[]{:S(2)}, u32[]{:S(2)}) collective-permute-start(bf16[256,1024]{1,0:T(8,128)(2,1)S(1)} %collective-permute-done.12.refs_12_), channel_id=1, source_target_pairs={{0,1},{1,0},{2,3},{3,2},{4,5},{5,4},{6,7},{7,6},{8,9},{9,8},{10,11... | collective-permute-start | bytes 1572872 | tf_op jit(solution)/shard_map/ppermute | solution.py:311
  45.4 6.2 %collective-permute-start.8 = (bf16[8,24,896]{2,1,0:T(8,128)(2,1)S(1)}, bf16[8,24,896]{2,1,0:T(8,128)(2,1)S(1)}, u32[]{:S(2)}, u32[]{:S(2)}) collective-permute-start(bf16[8,24,896]{2,1,0:T(8,128)(2,1)S(1)} %shard_map.112.refs_0_), channel_id=1, source_target_pairs={{0,1},{1,0},{2,3},{3,2},{4,5},{5,4},{6,7},{7,6},{8,9},{9,8},{10,11... | collective-permute-start | bytes 1032200 | tf_op jit(solution)/shard_map/ppermute | solution.py:311
  51.6 1.7 %collective-permute-start.10 = (bf16[8,24,896]{2,1,0:T(8,128)(2,1)S(1)}, bf16[8,24,896]{2,1,0:T(8,128)(2,1)S(1)}, u32[]{:S(2)}, u32[]{:S(2)}) collective-permute-start(bf16[8,24,896]{2,1,0:T(8,128)(2,1)S(1)} %collective-permute-done.9.refs_2_), channel_id=1, source_target_pairs={{0,1},{1,0},{2,3},{3,2},{4,5},{5,4},{6,7},{7,6},{8,9},{9,8},{10,11... | collective-permute-start | bytes 1032200 | tf_op jit(solution)/shard_map/ppermute | solution.py:311

commit v9 on v8

--- a/solution.py
+++ b/solution.py
@@ -282,14 +282,10 @@
 
 
 def join_kernel(*refs):
-    first, *rest, out, sem = refs
-    copy = pltpu.make_async_copy(first, out.at[0 : first.shape[0]], sem)
-    copy.start()
-    at = first.shape[0]
-    for ref in rest:
+    out, at = refs[-1], 0
+    for ref in refs[:-1]:
         out[at : at + ref.shape[0]] = ref[...]
         at += ref.shape[0]
-    copy.wait()
 
 
 def join(*blocks):
@@ -300,9 +296,8 @@
     return pl.pallas_call(
         join_kernel,
         out_shape=jax.ShapeDtypeStruct((count, *blocks[0].shape[1:]), BF),
-        in_specs=[pl.BlockSpec(memory_space=pl.ANY)] + [vmem] * (len(blocks) - 1),
+        in_specs=[vmem] * len(blocks),
         out_specs=vmem,
-        scratch_shapes=[pltpu.SemaphoreType.DMA],
         compiler_params=pltpu.CompilerParams(vmem_limit_bytes=8 * MIB),
     )(*blocks)
 
@@ -315,8 +310,9 @@
     size = lax.axis_size("dp")
     if size == 8:
         far = [hop(block, "dp", i) for i in (2, 4, 6)]
-        far[0], later = lax.optimization_barrier((far[0], later))
-        block = join(block, *far)
+        mine = join(block)
+        mine, far, later = lax.optimization_barrier((mine, far, later))
+        block = join(mine, *far)
         order, bit = [0, 2, 4, 6], 1
     else:
         order, bit = [0], size // 2
@@ -332,12 +328,12 @@
     nodes = node_dev * lax.axis_size("dp")
     own = (w_out, w_self, w_neigh)
     even = (lax.axis_index("dp") // 2) % 2 == 0
+    x_out = hop(w_out, "mp", 2)
     x_half = hop(jnp.where(even, w_self, w_neigh), "mp", 2)
-    x_out = hop(w_out, "mp", 2)
     here = tuple(hop(a, "mp", 1) for a in own)
 
     sent = attention(texts, w_qkv, cotangent, neighbours.T)[None]
-    sent, here = lax.optimization_barrier((sent, here))
+    sent, here, x_out = lax.optimization_barrier((sent, here, x_out))
     sent, order, x_half = gather_dp(sent, x_half)
     z_half = hop(x_half, "dp", 2)
     across = (x_out, x_half, z_half)

time: 60.3 us -> 52.6 us (0.87)
  waiting for transfers between devices: 25.8 us -> 16.8 us
  starting transfers between devices: 13.1 us -> 14.6 us
    ppermute x16, waiting for transfers between devices: 25.8 us -> 16.8 us  [hop(): lax.ppermute(x, axis, [(i, i ^ bit) for i in range(lax.axis_size(axis))])]
    ppermute x16, starting transfers between devices: 13.1 us -> 14.6 us  [hop(): lax.ppermute(x, axis, [(i, i ^ bit) for i in range(lax.axis_size(axis))])]
  transfers between devices with their start and end apart: 16 -> 16, of which waited for: 5 -> 5; matrix products, arithmetic and copies ran while one was open for 2% -> 2% of each run, Pallas kernels for 20% -> 22%
where the time goes in v9:
time: 52.6 us; the launch traced here: 52.3 us
  Pallas kernels  18.4 us (35%)
  waiting for transfers between devices  16.8 us (32%)
  starting transfers between devices  14.6 us (28%)
  other arithmetic  1.1 us (2%)
  local copies, waits for them, and re-layouts  0.83 us (2%)
  between operations  0.7 us (1%)
    ppermute x16, waiting for transfers between devices, hop(): lax.ppermute(x, axis, [(i, i ^ bit) for i in range(lax.axis_size(axis))])  16.8 us
    ppermute x16, starting transfers between devices, hop(): lax.ppermute(x, axis, [(i, i ^ bit) for i in range(lax.axis_size(axis))])  14.6 us
    pallas_call x1, Pallas kernels, attention(): pl.pallas_call(functools.partial(attention_kernel, heads), out_shape=jax....  11.5 us
    pallas_call x1, Pallas kernels, graph(): pl.pallas_call(functools.partial(graph_kernel, order, fan), out_shape=(sl...  6.8 us
    select_n x1, other arithmetic, per_device(): x_half = hop(jnp.where(even, w_self, w_neigh), 'mp', 2)  1.1 us
  transfers between devices with their start and end apart: 16, of which 5 were waited for; matrix products, arithmetic and copies ran while one was open for 2% of the time, Pallas kernels for 22%

profile of v9, /device:TPU:0, one launch (start us, length us, event | category | flops | bytes accessed | tf_op | source)
XLA Modules:
  0.0 52.3 jit_solution(2959424356110136034)
XLA Ops:
  0.6 0.5 collective-permute-start
  1.1 2.6 %collective-permute-start.3 = (bf16[256,1024]{1,0:T(8,128)(2,1)}, bf16[256,1024]{1,0:T(8,128)(2,1)S(1)}, u32[]{:S(2)}, u32[]{:S(2)}) collective-permute-start(bf16[256,1024]{1,0:T(8,128)(2,1)} %refs_4_.1), channel_id=1, source_target_pairs={{0,2},{1,3},{2,0},{3,1},{4,6},{5,7},{6,4},{7,5},{8,10},{9,11},{10,... | collective-permute-start | bytes 1572872 | tf_op jit(solution)/shard_map/ppermute | solution.py:306
  3.7 0.2 collective-permute-start.1
  3.9 0.3 collective-permute-start.2
  4.2 1.1 %broadcast_select_fusion = bf16[256,1024]{1,0:T(8,128)(2,1)S(1)} fusion(bf16[256,1024]{1,0:T(8,128)(2,1)} %refs_5_.1, bf16[256,1024]{1,0:T(8,128)(2,1)} %refs_6_.1, pred[]{:T(512)S(6)} %eq.5), kind=kLoop, calls=%fused_computation | loop fusion | flops 262144 | bytes 1572865 | tf_op jit(solution)/shard_map/jit(_where)/select_n | solution.py:332
  5.3 0.1 collective-permute-start.7
  5.5 11.5 %shard_map.110 = bf16[24,896]{1,0:T(8,128)(2,1)} custom-call(bf16[24,128,1024]{2,1,0:T(8,128)(2,1)} %x_ref.1, bf16[1024,768]{1,0:T(8,128)(2,1)} %w_ref.1, bf16[24,256]{1,0:T(8,128)(2,1)} %cot_ref.1, s32[16,24]{1,0:T(8,128)} %bitcast.6), custom_call_target="tpu_custom_call" | custom-call | flops 5637144576 | bytes 7864320 | tf_op jit(solution)/shard_map/pallas_call | solution.py:95
  17.0 0.0 collective-permute-done.refs_7_
  17.0 0.0 collective-permute-done.3.refs_10_
  17.0 0.0 collective-permute-done.1.refs_8_
  17.0 0.0 collective-permute-done.2.refs_9_
  17.0 4.1 %collective-permute-start.6 = (bf16[1,24,896]{2,1,0:T(8,128)(2,1)}, bf16[1,24,896]{2,1,0:T(8,128)(2,1)S(1)}, u32[]{:S(2)}, u32[]{:S(2)}) collective-permute-start(bf16[1,24,896]{2,1,0:T(8,128)(2,1)} %bitcast.2), channel_id=1, source_target_pairs={{0,24},{4,28},{8,16},{12,20},{16,8},{20,12},{24,0},{28,4},{1,25},{... | collective-permute-start | bytes 129032 | tf_op jit(solution)/shard_map/ppermute | solution.py:306
  21.2 0.0 collective-permute-start.5
  21.2 0.6 %collective-permute-start.4 = (bf16[1,24,896]{2,1,0:T(8,128)(2,1)}, bf16[1,24,896]{2,1,0:T(8,128)(2,1)S(1)}, u32[]{:S(2)}, u32[]{:S(2)}) collective-permute-start(bf16[1,24,896]{2,1,0:T(8,128)(2,1)} %bitcast.4), channel_id=1, source_target_pairs={{0,8},{4,12},{8,0},{12,4},{16,24},{20,28},{24,16},{28,20},{1,9},{5... | collective-permute-start | bytes 129032 | tf_op jit(solution)/shard_map/ppermute | solution.py:306
  21.8 0.8 %copy-done.2 = bf16[24,896]{1,0:T(8,128)(2,1)S(1)} copy-done((bf16[24,896]{1,0:T(8,128)(2,1)S(1)}, bf16[24,896]{1,0:T(8,128)(2,1)}, u32[]{:S(2)}) %copy-start.2) | copy-done | bytes 43032
  22.6 5.0 %collective-permute-done.7.refs_11_ = bf16[256,1024]{1,0:T(8,128)(2,1)S(1)} collective-permute-done((bf16[256,1024]{1,0:T(8,128)(2,1)S(1)}, bf16[256,1024]{1,0:T(8,128)(2,1)S(1)}, u32[]{:S(2)}, u32[]{:S(2)}) %collective-permute-start.7) | collective-permute-done | bytes 524320 | tf_op jit(solution)/shard_map/ppermute | solution.py:306
  27.7 0.0 collective-permute-done.6.refs_3_
  27.7 0.0 collective-permute-done.5.refs_2_
  27.7 0.0 collective-permute-done.4.refs_1_
  27.7 1.9 %collective-permute-start.12 = (bf16[256,1024]{1,0:T(8,128)(2,1)S(1)}, bf16[256,1024]{1,0:T(8,128)(2,1)S(1)}, u32[]{:S(2)}, u32[]{:S(2)}) collective-permute-start(bf16[256,1024]{1,0:T(8,128)(2,1)S(1)} %collective-permute-done.7.refs_11_), channel_id=1, source_target_pairs={{0,8},{4,12},{8,0},{12,4},{16,24},{20,28},{24,16},{28,20},{1,9},{5... | collective-permute-start | bytes 1572872 | tf_op jit(solution)/shard_map/ppermute | solution.py:306
  29.6 1.6 %collective-permute-start.8 = (bf16[4,24,896]{2,1,0:T(8,128)(2,1)S(1)}, bf16[4,24,896]{2,1,0:T(8,128)(2,1)S(1)}, u32[]{:S(2)}, u32[]{:S(2)}) collective-permute-start(bf16[4,24,896]{2,1,0:T(8,128)(2,1)S(1)} %shard_map.112.refs_0_), channel_id=1, source_target_pairs={{0,4},{4,0},{8,12},{12,8},{16,20},{20,16},{24,28},{28,24},{1,5},{5... | collective-permute-start | bytes 516104 | tf_op jit(solution)/shard_map/ppermute | solution.py:306
  31.2 4.1 %collective-permute-done.8.refs_1_ = bf16[4,24,896]{2,1,0:T(8,128)(2,1)S(1)} collective-permute-done((bf16[4,24,896]{2,1,0:T(8,128)(2,1)S(1)}, bf16[4,24,896]{2,1,0:T(8,128)(2,1)S(1)}, u32[]{:S(2)}, u32[]{:S(2)}) %collective-permute-start.8) | collective-permute-done | bytes 172064 | tf_op jit(solution)/shard_map/ppermute | solution.py:306
  35.4 1.6 %collective-permute-start.10 = (bf16[8,24,896]{2,1,0:T(8,128)(2,1)S(1)}, bf16[8,24,896]{2,1,0:T(8,128)(2,1)S(1)}, u32[]{:S(2)}, u32[]{:S(2)}) collective-permute-start(bf16[8,24,896]{2,1,0:T(8,128)(2,1)S(1)} %shard_map.113.refs_0_), channel_id=1, source_target_pairs={{0,2},{1,3},{2,0},{3,1},{4,6},{5,7},{6,4},{7,5},{8,10},{9,11},{10,... | collective-permute-start | bytes 1032200 | tf_op jit(solution)/shard_map/ppermute | solution.py:306
  36.9 0.0 collective-permute-start.13
  36.9 0.5 collective-permute-start.14
  37.4 4.0 %collective-permute-done.12.refs_12_ = bf16[256,1024]{1,0:T(8,128)(2,1)S(1)} collective-permute-done((bf16[256,1024]{1,0:T(8,128)(2,1)S(1)}, bf16[256,1024]{1,0:T(8,128)(2,1)S(1)}, u32[]{:S(2)}, u32[]{:S(2)}) %collective-permute-start.12) | collective-permute-done | bytes 524320 | tf_op jit(solution)/shard_map/ppermute | solution.py:306
  41.4 0.0 collective-permute-start.15
  41.4 0.5 collective-permute-start.9
  41.9 1.9 %collective-permute-done.10.refs_2_ = bf16[8,24,896]{2,1,0:T(8,128)(2,1)S(1)} collective-permute-done((bf16[8,24,896]{2,1,0:T(8,128)(2,1)S(1)}, bf16[8,24,896]{2,1,0:T(8,128)(2,1)S(1)}, u32[]{:S(2)}, u32[]{:S(2)}) %collective-permute-start.10) | collective-permute-done | bytes 344096 | tf_op jit(solution)/shard_map/ppermute | solution.py:306
  43.9 0.0 collective-permute-start.11
  43.9 1.6 %collective-permute-done.11.refs_3_ = bf16[8,24,896]{2,1,0:T(8,128)(2,1)S(1)} collective-permute-done((bf16[8,24,896]{2,1,0:T(8,128)(2,1)S(1)}, bf16[8,24,896]{2,1,0:T(8,128)(2,1)S(1)}, u32[]{:S(2)}, u32[]{:S(2)}) %collective-permute-start.11) | collective-permute-done | bytes 344096 | tf_op jit(solution)/shard_map/ppermute | solution.py:306
  45.5 6.8 %shard_map.114 = (bf16[24,256]{1,0:T(8,128)(2,1)}, bf16[24,256]{1,0:T(8,128)(2,1)}, f32[256,1024]{1,0:T(8,128)}, f32[256,1024]{1,0:T(8,128)}, f32[256,1024]{1,0:T(8,128)}) custom-call(bf16[8,24,896]{2,1,0:T(8,128)(2,1)S(1)} %shard_map.113.refs_0_, bf16[8,24,896]{2,1,0:T(8,128)(2,1)S(1)} %collective-permute-done.9.refs_1_, ...), custom_call_target="tpu_custom_call" | custom-call | flops 2415919104 | bytes 10485760 | tf_op jit(solution)/shard_map/pallas_call | solution.py:217
  (14 shorter events, 0.1 us)
Async XLA Ops:
  0.6 16.4 %collective-permute-start = (bf16[256,1024]{1,0:T(8,128)(2,1)}, bf16[256,1024]{1,0:T(8,128)(2,1)S(1)}, u32[]{:S(2)}, u32[]{:S(2)}) collective-permute-start(bf16[256,1024]{1,0:T(8,128)(2,1)} %refs_4_.1), channel_id=1, source_target_pairs={{0,1},{1,0},{2,3},{3,2},{4,5},{5,4},{6,7},{7,6},{8,9},{9,8},{10,11... | collective-permute-start | bytes 1572872 | tf_op jit(solution)/shard_map/ppermute | solution.py:306
  1.1 15.9 %collective-permute-start.3 = (bf16[256,1024]{1,0:T(8,128)(2,1)}, bf16[256,1024]{1,0:T(8,128)(2,1)S(1)}, u32[]{:S(2)}, u32[]{:S(2)}) collective-permute-start(bf16[256,1024]{1,0:T(8,128)(2,1)} %refs_4_.1), channel_id=1, source_target_pairs={{0,2},{1,3},{2,0},{3,1},{4,6},{5,7},{6,4},{7,5},{8,10},{9,11},{10,... | collective-permute-start | bytes 1572872 | tf_op jit(solution)/shard_map/ppermute | solution.py:306
  3.7 13.3 %collective-permute-start.1 = (bf16[256,1024]{1,0:T(8,128)(2,1)}, bf16[256,1024]{1,0:T(8,128)(2,1)S(1)}, u32[]{:S(2)}, u32[]{:S(2)}) collective-permute-start(bf16[256,1024]{1,0:T(8,128)(2,1)} %refs_5_.1), channel_id=1, source_target_pairs={{0,1},{1,0},{2,3},{3,2},{4,5},{5,4},{6,7},{7,6},{8,9},{9,8},{10,11... | collective-permute-start | bytes 1572872 | tf_op jit(solution)/shard_map/ppermute | solution.py:306
  3.9 13.2 %collective-permute-start.2 = (bf16[256,1024]{1,0:T(8,128)(2,1)}, bf16[256,1024]{1,0:T(8,128)(2,1)S(1)}, u32[]{:S(2)}, u32[]{:S(2)}) collective-permute-start(bf16[256,1024]{1,0:T(8,128)(2,1)} %refs_6_.1), channel_id=1, source_target_pairs={{0,1},{1,0},{2,3},{3,2},{4,5},{5,4},{6,7},{7,6},{8,9},{9,8},{10,11... | collective-permute-start | bytes 1572872 | tf_op jit(solution)/shard_map/ppermute | solution.py:306
  5.3 22.3 %collective-permute-start.7 = (bf16[256,1024]{1,0:T(8,128)(2,1)S(1)}, bf16[256,1024]{1,0:T(8,128)(2,1)S(1)}, u32[]{:S(2)}, u32[]{:S(2)}) collective-permute-start(bf16[256,1024]{1,0:T(8,128)(2,1)S(1)} %broadcast_select_fusion), channel_id=1, source_target_pairs={{0,2},{1,3},{2,0},{3,1},{4,6},{5,7},{6,4},{7,5},{8,10},{9,11},{10,... | collective-permute-start | bytes 1572872 | tf_op jit(solution)/shard_map/ppermute | solution.py:306
  5.5 40.0 %copy-start = (bf16[256,1024]{1,0:T(8,128)(2,1)S(1)}, bf16[256,1024]{1,0:T(8,128)(2,1)}, u32[]{:S(2)}) copy-start(bf16[256,1024]{1,0:T(8,128)(2,1)} %refs_5_.1) | copy-start | bytes 1572868
  5.5 40.0 %copy-start.1 = (bf16[256,1024]{1,0:T(8,128)(2,1)S(1)}, bf16[256,1024]{1,0:T(8,128)(2,1)}, u32[]{:S(2)}) copy-start(bf16[256,1024]{1,0:T(8,128)(2,1)} %refs_6_.1) | copy-start | bytes 1572868
  5.5 40.0 %copy-start.3 = (bf16[256,1024]{1,0:T(8,128)(2,1)S(1)}, bf16[256,1024]{1,0:T(8,128)(2,1)}, u32[]{:S(2)}) copy-start(bf16[256,1024]{1,0:T(8,128)(2,1)} %refs_4_.1) | copy-start | bytes 1572868
  17.0 10.6 %collective-permute-start.6 = (bf16[1,24,896]{2,1,0:T(8,128)(2,1)}, bf16[1,24,896]{2,1,0:T(8,128)(2,1)S(1)}, u32[]{:S(2)}, u32[]{:S(2)}) collective-permute-start(bf16[1,24,896]{2,1,0:T(8,128)(2,1)} %bitcast.2), channel_id=1, source_target_pairs={{0,24},{4,28},{8,16},{12,20},{16,8},{20,12},{24,0},{28,4},{1,25},{... | collective-permute-start | bytes 129032 | tf_op jit(solution)/shard_map/ppermute | solution.py:306
  21.2 6.5 %collective-permute-start.5 = (bf16[1,24,896]{2,1,0:T(8,128)(2,1)}, bf16[1,24,896]{2,1,0:T(8,128)(2,1)S(1)}, u32[]{:S(2)}, u32[]{:S(2)}) collective-permute-start(bf16[1,24,896]{2,1,0:T(8,128)(2,1)} %bitcast.3), channel_id=1, source_target_pairs={{0,16},{4,20},{8,24},{12,28},{16,0},{20,4},{24,8},{28,12},{1,17},{... | collective-permute-start | bytes 129032 | tf_op jit(solution)/shard_map/ppermute | solution.py:306
  21.2 6.5 %collective-permute-start.4 = (bf16[1,24,896]{2,1,0:T(8,128)(2,1)}, bf16[1,24,896]{2,1,0:T(8,128)(2,1)S(1)}, u32[]{:S(2)}, u32[]{:S(2)}) collective-permute-start(bf16[1,24,896]{2,1,0:T(8,128)(2,1)} %bitcast.4), channel_id=1, source_target_pairs={{0,8},{4,12},{8,0},{12,4},{16,24},{20,28},{24,16},{28,20},{1,9},{5... | collective-permute-start | bytes 129032 | tf_op jit(solution)/shard_map/ppermute | solution.py:306
  21.8 0.8 %copy-start.2 = (bf16[24,896]{1,0:T(8,128)(2,1)S(1)}, bf16[24,896]{1,0:T(8,128)(2,1)}, u32[]{:S(2)}) copy-start(bf16[24,896]{1,0:T(8,128)(2,1)} %shard_map.110) | copy-start | bytes 129028
  27.7 13.7 %collective-permute-start.12 = (bf16[256,1024]{1,0:T(8,128)(2,1)S(1)}, bf16[256,1024]{1,0:T(8,128)(2,1)S(1)}, u32[]{:S(2)}, u32[]{:S(2)}) collective-permute-start(bf16[256,1024]{1,0:T(8,128)(2,1)S(1)} %collective-permute-done.7.refs_11_), channel_id=1, source_target_pairs={{0,8},{4,12},{8,0},{12,4},{16,24},{20,28},{24,16},{28,20},{1,9},{5... | collective-permute-start | bytes 1572872 | tf_op jit(solution)/shard_map/ppermute | solution.py:306
  29.6 5.7 %collective-permute-start.8 = (bf16[4,24,896]{2,1,0:T(8,128)(2,1)S(1)}, bf16[4,24,896]{2,1,0:T(8,128)(2,1)S(1)}, u32[]{:S(2)}, u32[]{:S(2)}) collective-permute-start(bf16[4,24,896]{2,1,0:T(8,128)(2,1)S(1)} %shard_map.112.refs_0_), channel_id=1, source_target_pairs={{0,4},{4,0},{8,12},{12,8},{16,20},{20,16},{24,28},{28,24},{1,5},{5... | collective-permute-start | bytes 516104 | tf_op jit(solution)/shard_map/ppermute | solution.py:306
  35.4 8.5 %collective-permute-start.10 = (bf16[8,24,896]{2,1,0:T(8,128)(2,1)S(1)}, bf16[8,24,896]{2,1,0:T(8,128)(2,1)S(1)}, u32[]{:S(2)}, u32[]{:S(2)}) collective-permute-start(bf16[8,24,896]{2,1,0:T(8,128)(2,1)S(1)} %shard_map.113.refs_0_), channel_id=1, source_target_pairs={{0,2},{1,3},{2,0},{3,1},{4,6},{5,7},{6,4},{7,5},{8,10},{9,11},{10,... | collective-permute-start | bytes 1032200 | tf_op jit(solution)/shard_map/ppermute | solution.py:306
  36.9 6.9 %collective-permute-start.13 = (bf16[256,1024]{1,0:T(8,128)(2,1)S(1)}, bf16[256,1024]{1,0:T(8,128)(2,1)S(1)}, u32[]{:S(2)}, u32[]{:S(2)}) collective-permute-start(bf16[256,1024]{1,0:T(8,128)(2,1)S(1)} %collective-permute-done.3.refs_10_), channel_id=1, source_target_pairs={{0,1},{1,0},{2,3},{3,2},{4,5},{5,4},{6,7},{7,6},{8,9},{9,8},{10,11... | collective-permute-start | bytes 1572872 | tf_op jit(solution)/shard_map/ppermute | solution.py:306
  36.9 6.9 %collective-permute-start.14 = (bf16[256,1024]{1,0:T(8,128)(2,1)S(1)}, bf16[256,1024]{1,0:T(8,128)(2,1)S(1)}, u32[]{:S(2)}, u32[]{:S(2)}) collective-permute-start(bf16[256,1024]{1,0:T(8,128)(2,1)S(1)} %collective-permute-done.7.refs_11_), channel_id=1, source_target_pairs={{0,1},{1,0},{2,3},{3,2},{4,5},{5,4},{6,7},{7,6},{8,9},{9,8},{10,11... | collective-permute-start | bytes 1572872 | tf_op jit(solution)/shard_map/ppermute | solution.py:306
  41.4 4.1 %collective-permute-start.15 = (bf16[256,1024]{1,0:T(8,128)(2,1)S(1)}, bf16[256,1024]{1,0:T(8,128)(2,1)S(1)}, u32[]{:S(2)}, u32[]{:S(2)}) collective-permute-start(bf16[256,1024]{1,0:T(8,128)(2,1)S(1)} %collective-permute-done.12.refs_12_), channel_id=1, source_target_pairs={{0,1},{1,0},{2,3},{3,2},{4,5},{5,4},{6,7},{7,6},{8,9},{9,8},{10,11... | collective-permute-start | bytes 1572872 | tf_op jit(solution)/shard_map/ppermute | solution.py:306
  41.4 2.4 %collective-permute-start.9 = (bf16[8,24,896]{2,1,0:T(8,128)(2,1)S(1)}, bf16[8,24,896]{2,1,0:T(8,128)(2,1)S(1)}, u32[]{:S(2)}, u32[]{:S(2)}) collective-permute-start(bf16[8,24,896]{2,1,0:T(8,128)(2,1)S(1)} %shard_map.113.refs_0_), channel_id=1, source_target_pairs={{0,1},{1,0},{2,3},{3,2},{4,5},{5,4},{6,7},{7,6},{8,9},{9,8},{10,11... | collective-permute-start | bytes 1032200 | tf_op jit(solution)/shard_map/ppermute | solution.py:306
  43.9 1.7 %collective-permute-start.11 = (bf16[8,24,896]{2,1,0:T(8,128)(2,1)S(1)}, bf16[8,24,896]{2,1,0:T(8,128)(2,1)S(1)}, u32[]{:S(2)}, u32[]{:S(2)}) collective-permute-start(bf16[8,24,896]{2,1,0:T(8,128)(2,1)S(1)} %collective-permute-done.10.refs_2_), channel_id=1, source_target_pairs={{0,1},{1,0},{2,3},{3,2},{4,5},{5,4},{6,7},{7,6},{8,9},{9,8},{10,11... | collective-permute-start | bytes 1032200 | tf_op jit(solution)/shard_map/ppermute | solution.py:306

commit v10 on v9

--- a/solution.py
+++ b/solution.py
@@ -14,6 +14,7 @@
 WIDE_LIMIT = 256
 IDS_COLS = 128
 IDS_AT = 32
+TOP = 16
 LOG2E = 1.4426950408889634
 ATTENTION_VMEM = 58
 MIB = 1 << 20
@@ -73,17 +74,32 @@
 
     @pl.when(step == pl.num_programs(0) - 1)
     def _():
-        out_ref[:, :cols] = acc_p[...].astype(BF)
-        out_ref[:, cols : 2 * cols] = cot_ref[...]
-        out_ref[:, 2 * cols : 3 * cols] = acc_m[...].astype(BF)
+        rows = jnp.concatenate([acc_p[...], cot_ref[...].astype(F32), acc_m[...]], axis=1)
         shifted = ids_ref[...] + 1
         fan = shifted.shape[0]
-        blank = jnp.zeros((fan, IDS_COLS - 2 * IDS_AT), F32)
         gap = jnp.zeros((fan, IDS_AT - node_dev), F32)
         high, low = (shifted >> 4).astype(F32), (shifted & 15).astype(F32)
-        packed = jnp.concatenate([high, gap, low, gap, blank], axis=1)
-        rest = jnp.zeros((node_dev - fan, IDS_COLS), F32)
-        out_ref[:, 3 * cols :] = jnp.concatenate([packed, rest], axis=0).astype(BF)
+        blank = jnp.zeros((fan, IDS_COLS - 2 * IDS_AT), F32)
+        ids = jnp.concatenate([high, gap, low, gap, blank], axis=1)
+        wide = 3 * cols
+        rest = jnp.concatenate([rows[TOP:, : wide // 2], rows[TOP:, wide // 2 :]], axis=0)
+        out_ref[:, :wide] = rows[:TOP].astype(BF)
+        out_ref[:, wide : wide + wide // 2] = rest.astype(BF)
+        out_ref[:, wide + wide // 2 :] = ids.astype(BF)
+
+
+def unpack(got, cols, part):
+    got = got.astype(F32)
+    wide, at = 3 * cols, part * cols
+    pieces, left = [], at
+    while left < at + cols:
+        side, inside = divmod(left, wide // 2)
+        right = min(at + cols, (side + 1) * (wide // 2))
+        low = wide + inside
+        pieces.append(got[:, side * (TOP // 2) : (side + 1) * (TOP // 2), low : low + right - left])
+        left = right
+    rest = jnp.concatenate(pieces, axis=2) if len(pieces) > 1 else pieces[0]
+    return jnp.concatenate([got[:, :, at : at + cols], rest], axis=1)
 
 
 def attention(texts, w_qkv, cotangent, ids):
@@ -92,9 +108,10 @@
     heads = cols // HD
     tokens = node_dev * seq
     nodes = NODES_STEP
+    packed = (TOP, 3 * cols + 3 * cols // 2 + IDS_COLS)
     return pl.pallas_call(
         functools.partial(attention_kernel, heads),
-        out_shape=jax.ShapeDtypeStruct((node_dev, 3 * cols + IDS_COLS), BF),
+        out_shape=jax.ShapeDtypeStruct(packed, BF),
         grid=(node_dev // nodes,),
         in_specs=[
             pl.BlockSpec((nodes, seq, width), lambda i: (i, 0, 0)),
@@ -102,7 +119,7 @@
             pl.BlockSpec((node_dev, cols), lambda i: (0, 0)),
             pl.BlockSpec(ids.shape, lambda i: (0, 0)),
         ],
-        out_specs=pl.BlockSpec((node_dev, 3 * cols + IDS_COLS), lambda i: (0, 0)),
+        out_specs=pl.BlockSpec(packed, lambda i: (0, 0)),
         scratch_shapes=[
             pltpu.VMEM((width, 3 * cols), BF),
             pltpu.VMEM((node_dev, cols), F32),
@@ -126,40 +143,29 @@
     return z * half, slope
 
 
-def graph_kernel(order, fan, *refs):
+def graph_kernel(order, fan, node_dev, *refs):
     parts = 4
-    got, blocks, refs = refs[:parts], refs[parts : parts + 12], refs[parts + 12 :]
-    (mixed_ref, grad_ref, g_self, g_neigh, g_out), scratch = refs[:5], refs[5:]
-    w, pooled, embed, agg, dz, node_grad, mean, cot, sem = scratch
+    got, blocks, refs = refs[:parts], refs[parts : 4 * parts], refs[4 * parts :]
+    mixed_ref, grad_ref, g_self, g_neigh, g_out, both, dz, mean, cot = refs
     mp, dp = lax.axis_index("mp"), lax.axis_index("dp")
     side = (dp // 2) % 2
-    groups, node_dev, _ = got[0].shape
+    groups = got[0].shape[0]
     nodes = groups * node_dev
-    cols = g_self.shape[0]
-    width = parts * cols
+    cols, width = g_self.shape
 
     def place(r):
         return pl.ds(pl.multiple_of((mp ^ r) * cols, 128), cols)
 
+    def part(r, i):
+        return unpack(got[r][...], cols, i).reshape(nodes, cols)
+
     own = place(0)
-    copies = []
+    pooled = [part(r, 0).astype(BF) for r in range(parts)]
     for r in range(parts):
-        kinds = (0, 1, 2) if r < 2 else (0, 1 + side, 2 - side)
-        for i, k in enumerate(kinds):
-            copies.append(pltpu.make_async_copy(blocks[3 * r + i], w.at[k, mp ^ r], sem.at[i, r]))
-    copies = copies[::3], copies[1::3] + copies[2::3]
-    for c in copies[0] + copies[1]:
-        c.start()
-
-    def part(r, i, size=cols):
-        return got[r][:, :, i : i + size].astype(F32).reshape(nodes, size)
-
-    for r in range(parts):
-        pooled[:, place(r)] = part(r, 0).astype(BF)
-        cot[:, place(r)] = part(r, cols)
-        mean[:, place(r)] = part(r, 2 * cols)
-
-    packed = got[0][:, :, 3 * cols :].astype(F32)
+        cot[:, place(r)] = part(r, 1)
+        mean[:, place(r)] = part(r, 2)
+
+    packed = got[0][:, :, got[0].shape[2] - IDS_COLS :].astype(F32)
     ids = jnp.concatenate(
         [
             packed[i, :fan, :node_dev] * 16.0 + packed[i, :fan, IDS_AT : IDS_AT + node_dev] - 1.0
@@ -178,57 +184,53 @@
     for s in range(fan):
         counts_t += (ids[s : s + 1, :] == names).astype(F32)
     counts = counts_t.T
-    cnt = jnp.maximum(jnp.sum(counts, axis=1, keepdims=True), 1.0)
+    share = 1.0 / jnp.maximum(jnp.sum(counts, axis=1, keepdims=True), 1.0)
     counts, counts_t = counts.astype(BF), counts_t.astype(BF)
 
-    def whole(k):
-        return w[k].reshape(width, width)
-
-    for c in copies[0]:
-        c.wait()
-    embed[...] = (mean[...] + dot(pooled[...], whole(0))).astype(BF)
-    agg[...] = (dot(counts, embed[...]) / cnt).astype(BF)
-    for c in copies[1]:
-        c.wait()
-    z = dot(embed[...], whole(1)) + dot(agg[...], whole(2))
+    sums = sum(dot(pooled[r], blocks[3 * r][...]) for r in range(parts))
+    both[0] = (mean[...] + sums).astype(BF)
+    both[1] = (dot(counts, both[0]) * share).astype(BF)
+    z = 0.0
+    for r in range(parts):
+        first = 0 if r < 2 else side
+        z += dot(both[first, :, place(r)], blocks[3 * r + 1][...])
+        z += dot(both[1 - first, :, place(r)], blocks[3 * r + 2][...])
     mixed, slope = gelu_parts(z)
     mean[:node_dev, :] = mixed[:node_dev, :]
     mixed_ref[...] = mean[:node_dev, own].astype(BF)
     dz[...] = (cot[...] * slope).astype(BF)
-    msg = (dot_t(dz[...], whole(2)) / cnt).astype(BF)
-    total = dot_t(dz[...], whole(1)) + dot(counts_t, msg)
-    node_grad[...] = total.astype(BF)
-    cot[:node_dev, :] = total[:node_dev, :]
-    grad_ref[...] = cot[:node_dev, own].astype(BF)
     factor = 1.0 / jnp.sqrt(jnp.float32(nodes))
-    g_self[...] = t_dot(embed[:, own], dz[...]) * factor
-    g_neigh[...] = t_dot(agg[:, own], dz[...]) * factor
-    g_out[...] = t_dot(pooled[:, own], node_grad[...]) * factor
-
-
-def graph(order, fan, got, weights):
+    for r in range(parts):
+        to_self = dot_t(dz[...], blocks[3 * r + 1][...])
+        to_agg = dot_t(dz[...], blocks[3 * r + 2][...])
+        if r >= 2:
+            even = side == 0
+            to_self, to_agg = jnp.where(even, to_self, to_agg), jnp.where(even, to_agg, to_self)
+        total = to_self + dot(counts_t, (to_agg * share).astype(BF))
+        if r == 0:
+            grad_ref[...] = total[:node_dev, :].astype(BF)
+        g_out[:, place(r)] = t_dot(pooled[0], total.astype(BF)) * factor
+    g_self[...] = t_dot(both[0, :, own], dz[...]) * factor
+    g_neigh[...] = t_dot(both[1, :, own], dz[...]) * factor
+
+
+def graph(order, fan, node_dev, got, weights):
     parts = len(got)
-    groups, node_dev, _ = got[0].shape
     cols, width = weights[0][0].shape
-    nodes = groups * node_dev
+    nodes = got[0].shape[0] * node_dev
     vmem = pl.BlockSpec(memory_space=pltpu.VMEM)
     slab = jax.ShapeDtypeStruct((node_dev, cols), BF)
     big = jax.ShapeDtypeStruct((cols, width), F32)
     return pl.pallas_call(
-        functools.partial(graph_kernel, order, fan),
+        functools.partial(graph_kernel, order, fan, node_dev),
         out_shape=(slab, slab, big, big, big),
-        in_specs=[vmem] * parts + [pl.BlockSpec(memory_space=pl.ANY)] * (3 * parts),
+        in_specs=[vmem] * (4 * parts),
         out_specs=(vmem,) * 5,
         scratch_shapes=[
-            pltpu.VMEM((3, parts, cols, width), BF),
-            pltpu.VMEM((nodes, width), BF),
-            pltpu.VMEM((nodes, width), BF),
-            pltpu.VMEM((nodes, width), BF),
-            pltpu.VMEM((nodes, width), BF),
+            pltpu.VMEM((2, nodes, width), BF),
             pltpu.VMEM((nodes, width), BF),
             pltpu.VMEM((nodes, width), F32),
             pltpu.VMEM((nodes, width), F32),
-            pltpu.SemaphoreType.DMA((3, parts)),
         ],
         compiler_params=pltpu.CompilerParams(vmem_limit_bytes=36 * MIB),
         cost_estimate=pl.CostEstimate(
@@ -237,12 +239,11 @@
     )(*got, *sum(weights, ()))
 
 
-def graph_wide(order, fan, got, weights):
+def graph_wide(order, fan, node_dev, got, weights):
     mp, dp = lax.axis_index("mp"), lax.axis_index("dp")
     parts = len(got)
-    groups, node_dev, _ = got[0].shape
     cols, width = weights[0][0].shape
-    nodes = groups * node_dev
+    nodes = got[0].shape[0] * node_dev
     owners = jnp.array(order, jnp.int32) ^ dp
     names = (owners[:, None] * node_dev + jnp.arange(node_dev)[None, :]).reshape(1, 1, nodes)
     order = jnp.arange(parts) ^ mp
@@ -257,19 +258,19 @@
     )
 
     def part(i):
-        block = jnp.stack([g[:, :, i * cols : (i + 1) * cols] for g in got])[order]
+        block = jnp.stack([unpack(g, cols, i) for g in got])[order]
         return block.transpose(1, 2, 0, 3).reshape(nodes, width)
 
-    pooled = part(0)
-    packed = got[0][:, :fan, 3 * cols :].astype(jnp.int32)
+    pooled = part(0).astype(BF)
+    packed = got[0][:, :fan, got[0].shape[2] - IDS_COLS :].astype(jnp.int32)
     ids = packed[:, :, :node_dev] * 16 + packed[:, :, IDS_AT : IDS_AT + node_dev] - 1
     ids = ids.transpose(0, 2, 1).reshape(nodes, fan)
     cnt = jnp.maximum(jnp.sum(ids >= 0, axis=1).astype(F32), 1.0)[:, None]
     counts = jnp.sum(ids[:, :, None] == names, axis=1).astype(BF)
-    embed = (part(2).astype(F32) + dot(pooled, w_out)).astype(BF)
+    embed = (part(2) + dot(pooled, w_out)).astype(BF)
     agg = (dot(counts, embed) / cnt).astype(BF)
     mixed, slope = gelu_parts(dot(embed, w_self) + dot(agg, w_neigh))
-    dz = (part(1).astype(F32) * slope).astype(BF)
+    dz = (part(1) * slope).astype(BF)
     msg = (dot_t(dz, w_neigh) / cnt).astype(BF)
     node_grad = (dot_t(dz, w_self) + t_dot(counts, msg)).astype(BF)
     factor = 1.0 / jnp.sqrt(jnp.float32(nodes))
@@ -328,13 +329,14 @@
     nodes = node_dev * lax.axis_size("dp")
     own = (w_out, w_self, w_neigh)
     even = (lax.axis_index("dp") // 2) % 2 == 0
-    x_out = hop(w_out, "mp", 2)
     x_half = hop(jnp.where(even, w_self, w_neigh), "mp", 2)
     here = tuple(hop(a, "mp", 1) for a in own)
 
     sent = attention(texts, w_qkv, cotangent, neighbours.T)[None]
-    sent, here, x_out = lax.optimization_barrier((sent, here, x_out))
+    sent, here, x_half, w_out = lax.optimization_barrier((sent, here, x_half, w_out))
+    x_out = hop(w_out, "mp", 2)
     sent, order, x_half = gather_dp(sent, x_half)
+    sent, x_out = lax.optimization_barrier((sent, x_out))
     z_half = hop(x_half, "dp", 2)
     across = (x_out, x_half, z_half)
     there = tuple(hop(a, "mp", 1) for a in across)
@@ -342,7 +344,7 @@
     got_across = hop(sent, "mp", 2)
     got = (sent, hop(sent, "mp", 1), got_across, hop(got_across, "mp", 1))
     body = graph if nodes <= WIDE_LIMIT else graph_wide
-    return body(order, fan, got, (own, here, across, there))
+    return body(order, fan, node_dev, got, (own, here, across, there))
 
 
 def solution(mesh):

time: 52.6 us -> 49.8 us (0.947)
  waiting for transfers between devices: 16.8 us -> 15.2 us
  starting transfers between devices: 14.6 us -> 13 us
    ppermute x16, starting transfers between devices: 14.6 us -> 13 us  [hop(): lax.ppermute(x, axis, [(i, i ^ bit) for i in range(lax.axis_size(axis))])]
    ppermute x16, waiting for transfers between devices: 16.8 us -> 15.2 us  [hop(): lax.ppermute(x, axis, [(i, i ^ bit) for i in range(lax.axis_size(axis))])]
  transfers between devices with their start and end apart: 16 -> 16, of which waited for: 5 -> 8; matrix products, arithmetic and copies ran while one was open for 2% -> 2% of each run, Pallas kernels for 22% -> 23%
where the time goes in v10:
time: 49.8 us; the launch traced here: 49.6 us
  Pallas kernels  18.8 us (38%)
  waiting for transfers between devices  15.2 us (31%)
  starting transfers between devices  13 us (26%)
  other arithmetic  1.1 us (2%)
  local copies, waits for them, and re-layouts  0.82 us (2%)
  between operations  0.69 us (1%)
    ppermute x16, waiting for transfers between devices, hop(): lax.ppermute(x, axis, [(i, i ^ bit) for i in range(lax.axis_size(axis))])  15.2 us
    ppermute x16, starting transfers between devices, hop(): lax.ppermute(x, axis, [(i, i ^ bit) for i in range(lax.axis_size(axis))])  13 us
    pallas_call x1, Pallas kernels, attention(): pl.pallas_call(functools.partial(attention_kernel, heads), out_shape=jax....  11.5 us
    pallas_call x1, Pallas kernels, graph(): pl.pallas_call(functools.partial(graph_kernel, order, fan, node_dev), out...  7.21 us
    select_n x1, other arithmetic, per_device(): x_half = hop(jnp.where(even, w_self, w_neigh), 'mp', 2)  1.1 us
  transfers between devices with their start and end apart: 16, of which 8 were waited for; matrix products, arithmetic and copies ran while one was open for 2% of the time, Pallas kernels for 23%

profile of v10, /device:TPU:0, one launch (start us, length us, event | category | flops | bytes accessed | tf_op | source)
XLA Modules:
  0.0 49.6 jit_solution(8339447015998219054)
XLA Ops:
  0.6 0.5 %collective-permute-start.1 = (bf16[256,1024]{1,0:T(8,128)(2,1)}, bf16[256,1024]{1,0:T(8,128)(2,1)S(1)}, u32[]{:S(2)}, u32[]{:S(2)}) collective-permute-start(bf16[256,1024]{1,0:T(8,128)(2,1)} %refs_5_.1), channel_id=1, source_target_pairs={{0,1},{1,0},{2,3},{3,2},{4,5},{5,4},{6,7},{7,6},{8,9},{9,8},{10,11... | collective-permute-start | bytes 1572872 | tf_op jit(solution)/shard_map/ppermute | solution.py:307
  1.1 0.1 collective-permute-start.2
  1.2 1.1 %broadcast_select_fusion = bf16[256,1024]{1,0:T(8,128)(2,1)S(1)} fusion(bf16[256,1024]{1,0:T(8,128)(2,1)} %refs_5_.1, bf16[256,1024]{1,0:T(8,128)(2,1)} %refs_6_.1, pred[]{:T(512)S(6)} %eq.5), kind=kLoop, calls=%fused_computation | loop fusion | flops 262144 | bytes 1572865 | tf_op jit(solution)/shard_map/jit(_where)/select_n | solution.py:332
  2.3 3.0 %collective-permute-start.3 = (bf16[256,1024]{1,0:T(8,128)(2,1)S(1)}, bf16[256,1024]{1,0:T(8,128)(2,1)S(1)}, u32[]{:S(2)}, u32[]{:S(2)}) collective-permute-start(bf16[256,1024]{1,0:T(8,128)(2,1)S(1)} %broadcast_select_fusion), channel_id=1, source_target_pairs={{0,2},{1,3},{2,0},{3,1},{4,6},{5,7},{6,4},{7,5},{8,10},{9,11},{10,... | collective-permute-start | bytes 1572872 | tf_op jit(solution)/shard_map/ppermute | solution.py:307
  5.3 0.0 collective-permute-start
  5.3 11.5 %shard_map.110 = bf16[16,1280]{1,0:T(8,128)(2,1)} custom-call(bf16[24,128,1024]{2,1,0:T(8,128)(2,1)} %x_ref.1, bf16[1024,768]{1,0:T(8,128)(2,1)} %w_ref.1, bf16[24,256]{1,0:T(8,128)(2,1)} %cot_ref.1, s32[16,24]{1,0:T(8,128)} %bitcast.6), custom_call_target="tpu_custom_call" | custom-call | flops 5637144576 | bytes 7864320 | tf_op jit(solution)/shard_map/pallas_call | solution.py:112
  16.9 0.6 %collective-permute-done.3.refs_11_ = bf16[256,1024]{1,0:T(8,128)(2,1)S(1)} collective-permute-done((bf16[256,1024]{1,0:T(8,128)(2,1)S(1)}, bf16[256,1024]{1,0:T(8,128)(2,1)S(1)}, u32[]{:S(2)}, u32[]{:S(2)}) %collective-permute-start.3) | collective-permute-done | bytes 524320 | tf_op jit(solution)/shard_map/ppermute | solution.py:307
  17.5 0.0 collective-permute-done.refs_7_
  17.5 0.0 collective-permute-done.2.refs_9_
  17.5 1.8 %collective-permute-start.8 = (bf16[256,1024]{1,0:T(8,128)(2,1)S(1)}, bf16[256,1024]{1,0:T(8,128)(2,1)S(1)}, u32[]{:S(2)}, u32[]{:S(2)}) collective-permute-start(bf16[256,1024]{1,0:T(8,128)(2,1)S(1)} %copy-done.3), channel_id=1, source_target_pairs={{0,2},{1,3},{2,0},{3,1},{4,6},{5,7},{6,4},{7,5},{8,10},{9,11},{10,... | collective-permute-start | bytes 1572872 | tf_op jit(solution)/shard_map/ppermute | solution.py:307
  19.3 3.6 %collective-permute-start.6 = (bf16[1,16,1280]{2,1,0:T(8,128)(2,1)}, bf16[1,16,1280]{2,1,0:T(8,128)(2,1)S(1)}, u32[]{:S(2)}, u32[]{:S(2)}) collective-permute-start(bf16[1,16,1280]{2,1,0:T(8,128)(2,1)} %bitcast.2), channel_id=1, source_target_pairs={{0,24},{4,28},{8,16},{12,20},{16,8},{20,12},{24,0},{28,4},{1,25},{... | collective-permute-start | bytes 122888 | tf_op jit(solution)/shard_map/ppermute | solution.py:307
  22.9 0.0 collective-permute-start.5
  22.9 0.8 %collective-permute-start.4 = (bf16[1,16,1280]{2,1,0:T(8,128)(2,1)}, bf16[1,16,1280]{2,1,0:T(8,128)(2,1)S(1)}, u32[]{:S(2)}, u32[]{:S(2)}) collective-permute-start(bf16[1,16,1280]{2,1,0:T(8,128)(2,1)} %bitcast.4), channel_id=1, source_target_pairs={{0,8},{4,12},{8,0},{12,4},{16,24},{20,28},{24,16},{28,20},{1,9},{5... | collective-permute-start | bytes 122888 | tf_op jit(solution)/shard_map/ppermute | solution.py:307
  23.7 0.8 %copy-done.2 = bf16[16,1280]{1,0:T(8,128)(2,1)S(1)} copy-done((bf16[16,1280]{1,0:T(8,128)(2,1)S(1)}, bf16[16,1280]{1,0:T(8,128)(2,1)}, u32[]{:S(2)}) %copy-start.2) | copy-done | bytes 40984
  24.5 0.8 %collective-permute-done.6.refs_3_ = bf16[1,16,1280]{2,1,0:T(8,128)(2,1)S(1)} collective-permute-done((bf16[1,16,1280]{2,1,0:T(8,128)(2,1)}, bf16[1,16,1280]{2,1,0:T(8,128)(2,1)S(1)}, u32[]{:S(2)}, u32[]{:S(2)}) %collective-permute-start.6) | collective-permute-done | bytes 40992 | tf_op jit(solution)/shard_map/ppermute | solution.py:307
  25.4 2.7 %collective-permute-done.5.refs_2_ = bf16[1,16,1280]{2,1,0:T(8,128)(2,1)S(1)} collective-permute-done((bf16[1,16,1280]{2,1,0:T(8,128)(2,1)}, bf16[1,16,1280]{2,1,0:T(8,128)(2,1)S(1)}, u32[]{:S(2)}, u32[]{:S(2)}) %collective-permute-start.5) | collective-permute-done | bytes 40992 | tf_op jit(solution)/shard_map/ppermute | solution.py:307
  28.0 1.6 %collective-permute-start.7 = (bf16[4,16,1280]{2,1,0:T(8,128)(2,1)S(1)}, bf16[4,16,1280]{2,1,0:T(8,128)(2,1)S(1)}, u32[]{:S(2)}, u32[]{:S(2)}) collective-permute-start(bf16[4,16,1280]{2,1,0:T(8,128)(2,1)S(1)} %shard_map.112.refs_0_), channel_id=1, source_target_pairs={{0,4},{4,0},{8,12},{12,8},{16,20},{20,16},{24,28},{28,24},{1,5},{5... | collective-permute-start | bytes 491528 | tf_op jit(solution)/shard_map/ppermute | solution.py:307
  29.6 3.8 %collective-permute-done.7.refs_1_ = bf16[4,16,1280]{2,1,0:T(8,128)(2,1)S(1)} collective-permute-done((bf16[4,16,1280]{2,1,0:T(8,128)(2,1)S(1)}, bf16[4,16,1280]{2,1,0:T(8,128)(2,1)S(1)}, u32[]{:S(2)}, u32[]{:S(2)}) %collective-permute-start.7) | collective-permute-done | bytes 163872 | tf_op jit(solution)/shard_map/ppermute | solution.py:307
  33.5 0.6 %collective-permute-start.10 = (bf16[8,16,1280]{2,1,0:T(8,128)(2,1)S(1)}, bf16[8,16,1280]{2,1,0:T(8,128)(2,1)S(1)}, u32[]{:S(2)}, u32[]{:S(2)}) collective-permute-start(bf16[8,16,1280]{2,1,0:T(8,128)(2,1)S(1)} %shard_map.113.refs_0_), channel_id=1, source_target_pairs={{0,2},{1,3},{2,0},{3,1},{4,6},{5,7},{6,4},{7,5},{8,10},{9,11},{10,... | collective-permute-start | bytes 983048 | tf_op jit(solution)/shard_map/ppermute | solution.py:307
  34.1 0.0 collective-permute-start.14
  34.1 0.5 %collective-permute-start.13 = (bf16[256,1024]{1,0:T(8,128)(2,1)S(1)}, bf16[256,1024]{1,0:T(8,128)(2,1)S(1)}, u32[]{:S(2)}, u32[]{:S(2)}) collective-permute-start(bf16[256,1024]{1,0:T(8,128)(2,1)S(1)} %collective-permute-done.8.refs_10_), channel_id=1, source_target_pairs={{0,1},{1,0},{2,3},{3,2},{4,5},{5,4},{6,7},{7,6},{8,9},{9,8},{10,11... | collective-permute-start | bytes 1572872 | tf_op jit(solution)/shard_map/ppermute | solution.py:307
  34.6 4.9 %collective-permute-done.12.refs_12_ = bf16[256,1024]{1,0:T(8,128)(2,1)S(1)} collective-permute-done((bf16[256,1024]{1,0:T(8,128)(2,1)S(1)}, bf16[256,1024]{1,0:T(8,128)(2,1)S(1)}, u32[]{:S(2)}, u32[]{:S(2)}) %collective-permute-start.12) | collective-permute-done | bytes 524320 | tf_op jit(solution)/shard_map/ppermute | solution.py:307
  39.5 0.0 collective-permute-start.15
  39.5 0.5 %collective-permute-start.9 = (bf16[8,16,1280]{2,1,0:T(8,128)(2,1)S(1)}, bf16[8,16,1280]{2,1,0:T(8,128)(2,1)S(1)}, u32[]{:S(2)}, u32[]{:S(2)}) collective-permute-start(bf16[8,16,1280]{2,1,0:T(8,128)(2,1)S(1)} %shard_map.113.refs_0_), channel_id=1, source_target_pairs={{0,1},{1,0},{2,3},{3,2},{4,5},{5,4},{6,7},{7,6},{8,9},{9,8},{10,11... | collective-permute-start | bytes 983048 | tf_op jit(solution)/shard_map/ppermute | solution.py:307
  40.0 0.6 %collective-permute-done.10.refs_2_ = bf16[8,16,1280]{2,1,0:T(8,128)(2,1)S(1)} collective-permute-done((bf16[8,16,1280]{2,1,0:T(8,128)(2,1)S(1)}, bf16[8,16,1280]{2,1,0:T(8,128)(2,1)S(1)}, u32[]{:S(2)}, u32[]{:S(2)}) %collective-permute-start.10) | collective-permute-done | bytes 327712 | tf_op jit(solution)/shard_map/ppermute | solution.py:307
  40.6 0.0 collective-permute-start.11
  40.6 0.0 collective-permute-done.14.refs_14_
  40.6 1.3 %collective-permute-done.9.refs_1_ = bf16[8,16,1280]{2,1,0:T(8,128)(2,1)S(1)} collective-permute-done((bf16[8,16,1280]{2,1,0:T(8,128)(2,1)S(1)}, bf16[8,16,1280]{2,1,0:T(8,128)(2,1)S(1)}, u32[]{:S(2)}, u32[]{:S(2)}) %collective-permute-start.9) | collective-permute-done | bytes 327712 | tf_op jit(solution)/shard_map/ppermute | solution.py:307
  41.9 0.0 collective-permute-done.13.refs_13_
  41.9 0.0 collective-permute-done.15.refs_15_
  41.9 0.5 collective-permute-done.11.refs_3_
  42.4 7.2 %shard_map.114 = (bf16[24,256]{1,0:T(8,128)(2,1)}, bf16[24,256]{1,0:T(8,128)(2,1)}, f32[256,1024]{1,0:T(8,128)}, f32[256,1024]{1,0:T(8,128)}, f32[256,1024]{1,0:T(8,128)}) custom-call(bf16[8,16,1280]{2,1,0:T(8,128)(2,1)S(1)} %shard_map.113.refs_0_, bf16[8,16,1280]{2,1,0:T(8,128)(2,1)S(1)} %collective-permute-done.9.refs_1_, ...), custom_call_target="tpu_custom_call" | custom-call | flops 2415919104 | bytes 10485760 | tf_op jit(solution)/shard_map/pallas_call | solution.py:224
  (14 shorter events, 0.1 us)
Async XLA Ops:
  0.6 16.9 %collective-permute-start.1 = (bf16[256,1024]{1,0:T(8,128)(2,1)}, bf16[256,1024]{1,0:T(8,128)(2,1)S(1)}, u32[]{:S(2)}, u32[]{:S(2)}) collective-permute-start(bf16[256,1024]{1,0:T(8,128)(2,1)} %refs_5_.1), channel_id=1, source_target_pairs={{0,1},{1,0},{2,3},{3,2},{4,5},{5,4},{6,7},{7,6},{8,9},{9,8},{10,11... | collective-permute-start | bytes 1572872 | tf_op jit(solution)/shard_map/ppermute | solution.py:307
  1.1 16.3 %collective-permute-start.2 = (bf16[256,1024]{1,0:T(8,128)(2,1)}, bf16[256,1024]{1,0:T(8,128)(2,1)S(1)}, u32[]{:S(2)}, u32[]{:S(2)}) collective-permute-start(bf16[256,1024]{1,0:T(8,128)(2,1)} %refs_6_.1), channel_id=1, source_target_pairs={{0,1},{1,0},{2,3},{3,2},{4,5},{5,4},{6,7},{7,6},{8,9},{9,8},{10,11... | collective-permute-start | bytes 1572872 | tf_op jit(solution)/shard_map/ppermute | solution.py:307
  2.3 15.2 %collective-permute-start.3 = (bf16[256,1024]{1,0:T(8,128)(2,1)S(1)}, bf16[256,1024]{1,0:T(8,128)(2,1)S(1)}, u32[]{:S(2)}, u32[]{:S(2)}) collective-permute-start(bf16[256,1024]{1,0:T(8,128)(2,1)S(1)} %broadcast_select_fusion), channel_id=1, source_target_pairs={{0,2},{1,3},{2,0},{3,1},{4,6},{5,7},{6,4},{7,5},{8,10},{9,11},{10,... | collective-permute-start | bytes 1572872 | tf_op jit(solution)/shard_map/ppermute | solution.py:307
  5.3 12.2 %collective-permute-start = (bf16[256,1024]{1,0:T(8,128)(2,1)}, bf16[256,1024]{1,0:T(8,128)(2,1)S(1)}, u32[]{:S(2)}, u32[]{:S(2)}) collective-permute-start(bf16[256,1024]{1,0:T(8,128)(2,1)} %refs_4_.1), channel_id=1, source_target_pairs={{0,1},{1,0},{2,3},{3,2},{4,5},{5,4},{6,7},{7,6},{8,9},{9,8},{10,11... | collective-permute-start | bytes 1572872 | tf_op jit(solution)/shard_map/ppermute | solution.py:307
  5.3 12.2 %copy-start.3 = (bf16[256,1024]{1,0:T(8,128)(2,1)S(1)}, bf16[256,1024]{1,0:T(8,128)(2,1)}, u32[]{:S(2)}) copy-start(bf16[256,1024]{1,0:T(8,128)(2,1)} %refs_4_.1) | copy-start | bytes 1572868
  5.3 37.0 %copy-start = (bf16[256,1024]{1,0:T(8,128)(2,1)S(1)}, bf16[256,1024]{1,0:T(8,128)(2,1)}, u32[]{:S(2)}) copy-start(bf16[256,1024]{1,0:T(8,128)(2,1)} %refs_5_.1) | copy-start | bytes 1572868
  5.3 37.0 %copy-start.1 = (bf16[256,1024]{1,0:T(8,128)(2,1)S(1)}, bf16[256,1024]{1,0:T(8,128)(2,1)}, u32[]{:S(2)}) copy-start(bf16[256,1024]{1,0:T(8,128)(2,1)} %refs_6_.1) | copy-start | bytes 1572868
  17.5 16.0 %collective-permute-start.8 = (bf16[256,1024]{1,0:T(8,128)(2,1)S(1)}, bf16[256,1024]{1,0:T(8,128)(2,1)S(1)}, u32[]{:S(2)}, u32[]{:S(2)}) collective-permute-start(bf16[256,1024]{1,0:T(8,128)(2,1)S(1)} %copy-done.3), channel_id=1, source_target_pairs={{0,2},{1,3},{2,0},{3,1},{4,6},{5,7},{6,4},{7,5},{8,10},{9,11},{10,... | collective-permute-start | bytes 1572872 | tf_op jit(solution)/shard_map/ppermute | solution.py:307
  19.3 6.1 %collective-permute-start.6 = (bf16[1,16,1280]{2,1,0:T(8,128)(2,1)}, bf16[1,16,1280]{2,1,0:T(8,128)(2,1)S(1)}, u32[]{:S(2)}, u32[]{:S(2)}) collective-permute-start(bf16[1,16,1280]{2,1,0:T(8,128)(2,1)} %bitcast.2), channel_id=1, source_target_pairs={{0,24},{4,28},{8,16},{12,20},{16,8},{20,12},{24,0},{28,4},{1,25},{... | collective-permute-start | bytes 122888 | tf_op jit(solution)/shard_map/ppermute | solution.py:307
  22.9 5.1 %collective-permute-start.5 = (bf16[1,16,1280]{2,1,0:T(8,128)(2,1)}, bf16[1,16,1280]{2,1,0:T(8,128)(2,1)S(1)}, u32[]{:S(2)}, u32[]{:S(2)}) collective-permute-start(bf16[1,16,1280]{2,1,0:T(8,128)(2,1)} %bitcast.3), channel_id=1, source_target_pairs={{0,16},{4,20},{8,24},{12,28},{16,0},{20,4},{24,8},{28,12},{1,17},{... | collective-permute-start | bytes 122888 | tf_op jit(solution)/shard_map/ppermute | solution.py:307
  22.9 5.1 %collective-permute-start.4 = (bf16[1,16,1280]{2,1,0:T(8,128)(2,1)}, bf16[1,16,1280]{2,1,0:T(8,128)(2,1)S(1)}, u32[]{:S(2)}, u32[]{:S(2)}) collective-permute-start(bf16[1,16,1280]{2,1,0:T(8,128)(2,1)} %bitcast.4), channel_id=1, source_target_pairs={{0,8},{4,12},{8,0},{12,4},{16,24},{20,28},{24,16},{28,20},{1,9},{5... | collective-permute-start | bytes 122888 | tf_op jit(solution)/shard_map/ppermute | solution.py:307
  23.7 0.8 %copy-start.2 = (bf16[16,1280]{1,0:T(8,128)(2,1)S(1)}, bf16[16,1280]{1,0:T(8,128)(2,1)}, u32[]{:S(2)}) copy-start(bf16[16,1280]{1,0:T(8,128)(2,1)} %shard_map.110) | copy-start | bytes 122884
  28.0 11.5 %collective-permute-start.12 = (bf16[256,1024]{1,0:T(8,128)(2,1)S(1)}, bf16[256,1024]{1,0:T(8,128)(2,1)S(1)}, u32[]{:S(2)}, u32[]{:S(2)}) collective-permute-start(bf16[256,1024]{1,0:T(8,128)(2,1)S(1)} %collective-permute-done.3.refs_11_), channel_id=1, source_target_pairs={{0,8},{4,12},{8,0},{12,4},{16,24},{20,28},{24,16},{28,20},{1,9},{5... | collective-permute-start | bytes 1572872 | tf_op jit(solution)/shard_map/ppermute | solution.py:307
  28.0 5.4 %collective-permute-start.7 = (bf16[4,16,1280]{2,1,0:T(8,128)(2,1)S(1)}, bf16[4,16,1280]{2,1,0:T(8,128)(2,1)S(1)}, u32[]{:S(2)}, u32[]{:S(2)}) collective-permute-start(bf16[4,16,1280]{2,1,0:T(8,128)(2,1)S(1)} %shard_map.112.refs_0_), channel_id=1, source_target_pairs={{0,4},{4,0},{8,12},{12,8},{16,20},{20,16},{24,28},{28,24},{1,5},{5... | collective-permute-start | bytes 491528 | tf_op jit(solution)/shard_map/ppermute | solution.py:307
  33.5 7.1 %collective-permute-start.10 = (bf16[8,16,1280]{2,1,0:T(8,128)(2,1)S(1)}, bf16[8,16,1280]{2,1,0:T(8,128)(2,1)S(1)}, u32[]{:S(2)}, u32[]{:S(2)}) collective-permute-start(bf16[8,16,1280]{2,1,0:T(8,128)(2,1)S(1)} %shard_map.113.refs_0_), channel_id=1, source_target_pairs={{0,2},{1,3},{2,0},{3,1},{4,6},{5,7},{6,4},{7,5},{8,10},{9,11},{10,... | collective-permute-start | bytes 983048 | tf_op jit(solution)/shard_map/ppermute | solution.py:307
  34.1 6.5 %collective-permute-start.14 = (bf16[256,1024]{1,0:T(8,128)(2,1)S(1)}, bf16[256,1024]{1,0:T(8,128)(2,1)S(1)}, u32[]{:S(2)}, u32[]{:S(2)}) collective-permute-start(bf16[256,1024]{1,0:T(8,128)(2,1)S(1)} %collective-permute-done.3.refs_11_), channel_id=1, source_target_pairs={{0,1},{1,0},{2,3},{3,2},{4,5},{5,4},{6,7},{7,6},{8,9},{9,8},{10,11... | collective-permute-start | bytes 1572872 | tf_op jit(solution)/shard_map/ppermute | solution.py:307
  34.1 7.8 %collective-permute-start.13 = (bf16[256,1024]{1,0:T(8,128)(2,1)S(1)}, bf16[256,1024]{1,0:T(8,128)(2,1)S(1)}, u32[]{:S(2)}, u32[]{:S(2)}) collective-permute-start(bf16[256,1024]{1,0:T(8,128)(2,1)S(1)} %collective-permute-done.8.refs_10_), channel_id=1, source_target_pairs={{0,1},{1,0},{2,3},{3,2},{4,5},{5,4},{6,7},{7,6},{8,9},{9,8},{10,11... | collective-permute-start | bytes 1572872 | tf_op jit(solution)/shard_map/ppermute | solution.py:307
  39.5 2.4 %collective-permute-start.15 = (bf16[256,1024]{1,0:T(8,128)(2,1)S(1)}, bf16[256,1024]{1,0:T(8,128)(2,1)S(1)}, u32[]{:S(2)}, u32[]{:S(2)}) collective-permute-start(bf16[256,1024]{1,0:T(8,128)(2,1)S(1)} %collective-permute-done.12.refs_12_), channel_id=1, source_target_pairs={{0,1},{1,0},{2,3},{3,2},{4,5},{5,4},{6,7},{7,6},{8,9},{9,8},{10,11... | collective-permute-start | bytes 1572872 | tf_op jit(solution)/shard_map/ppermute | solution.py:307
  39.5 2.4 %collective-permute-start.9 = (bf16[8,16,1280]{2,1,0:T(8,128)(2,1)S(1)}, bf16[8,16,1280]{2,1,0:T(8,128)(2,1)S(1)}, u32[]{:S(2)}, u32[]{:S(2)}) collective-permute-start(bf16[8,16,1280]{2,1,0:T(8,128)(2,1)S(1)} %shard_map.113.refs_0_), channel_id=1, source_target_pairs={{0,1},{1,0},{2,3},{3,2},{4,5},{5,4},{6,7},{7,6},{8,9},{9,8},{10,11... | collective-permute-start | bytes 983048 | tf_op jit(solution)/shard_map/ppermute | solution.py:307
  40.6 1.7 %collective-permute-start.11 = (bf16[8,16,1280]{2,1,0:T(8,128)(2,1)S(1)}, bf16[8,16,1280]{2,1,0:T(8,128)(2,1)S(1)}, u32[]{:S(2)}, u32[]{:S(2)}) collective-permute-start(bf16[8,16,1280]{2,1,0:T(8,128)(2,1)S(1)} %collective-permute-done.10.refs_2_), channel_id=1, source_target_pairs={{0,1},{1,0},{2,3},{3,2},{4,5},{5,4},{6,7},{7,6},{8,9},{9,8},{10,11... | collective-permute-start | bytes 983048 | tf_op jit(solution)/shard_map/ppermute | solution.py:307

commit v11 on v10

--- a/solution.py
+++ b/solution.py
@@ -143,27 +143,21 @@
     return z * half, slope
 
 
-def graph_kernel(order, fan, node_dev, *refs):
+def block_place(r, cols):
+    return pl.ds(pl.multiple_of((lax.axis_index("mp") ^ r) * cols, 128), cols)
+
+
+def embed_kernel(order, fan, node_dev, *refs):
     parts = 4
-    got, blocks, refs = refs[:parts], refs[parts : 4 * parts], refs[4 * parts :]
-    mixed_ref, grad_ref, g_self, g_neigh, g_out, both, dz, mean, cot = refs
-    mp, dp = lax.axis_index("mp"), lax.axis_index("dp")
-    side = (dp // 2) % 2
+    got, blocks, refs = refs[:parts], refs[parts : 2 * parts], refs[2 * parts :]
+    both, cot, pooled_ref, counts_ref, share_ref, mean = refs
+    dp = lax.axis_index("dp")
     groups = got[0].shape[0]
     nodes = groups * node_dev
-    cols, width = g_self.shape
-
-    def place(r):
-        return pl.ds(pl.multiple_of((mp ^ r) * cols, 128), cols)
+    cols = blocks[0].shape[0]
 
     def part(r, i):
         return unpack(got[r][...], cols, i).reshape(nodes, cols)
-
-    own = place(0)
-    pooled = [part(r, 0).astype(BF) for r in range(parts)]
-    for r in range(parts):
-        cot[:, place(r)] = part(r, 1)
-        mean[:, place(r)] = part(r, 2)
 
     packed = got[0][:, :, got[0].shape[2] - IDS_COLS :].astype(F32)
     ids = jnp.concatenate(
@@ -185,33 +179,61 @@
         counts_t += (ids[s : s + 1, :] == names).astype(F32)
     counts = counts_t.T
     share = 1.0 / jnp.maximum(jnp.sum(counts, axis=1, keepdims=True), 1.0)
-    counts, counts_t = counts.astype(BF), counts_t.astype(BF)
-
-    sums = sum(dot(pooled[r], blocks[3 * r][...]) for r in range(parts))
+    counts_ref[...] = counts_t.astype(BF)
+    share_ref[...] = jnp.broadcast_to(share, share_ref.shape)
+
+    pooled = [part(r, 0).astype(BF) for r in range(parts)]
+    pooled_ref[...] = pooled[0]
+    for r in range(parts):
+        cot[:, block_place(r, cols)] = part(r, 1).astype(BF)
+        mean[:, block_place(r, cols)] = part(r, 2)
+    sums = sum(dot(pooled[r], blocks[r][...]) for r in range(parts))
     both[0] = (mean[...] + sums).astype(BF)
-    both[1] = (dot(counts, both[0]) * share).astype(BF)
+    both[1] = (dot(counts.astype(BF), both[0]) * share).astype(BF)
+
+
+def graph_kernel(node_dev, both, cot, pooled, counts, share_ref, *refs):
+    parts = 4
+    blocks, refs = refs[: 2 * parts], refs[2 * parts :]
+    mixed_ref, grad_ref, g_self, g_neigh, g_out, dz, wide, grads, sem = refs
+    side = (lax.axis_index("dp") // 2) % 2
+    cols, width = g_self.shape
+    nodes = counts.shape[0]
+    factor = 1.0 / jnp.sqrt(jnp.float32(nodes))
+    own = block_place(0, cols)
+
     z = 0.0
     for r in range(parts):
         first = 0 if r < 2 else side
-        z += dot(both[first, :, place(r)], blocks[3 * r + 1][...])
-        z += dot(both[1 - first, :, place(r)], blocks[3 * r + 2][...])
+        z += dot(both[first, :, block_place(r, cols)], blocks[2 * r][...])
+        z += dot(both[1 - first, :, block_place(r, cols)], blocks[2 * r + 1][...])
     mixed, slope = gelu_parts(z)
-    mean[:node_dev, :] = mixed[:node_dev, :]
-    mixed_ref[...] = mean[:node_dev, own].astype(BF)
-    dz[...] = (cot[...] * slope).astype(BF)
-    factor = 1.0 / jnp.sqrt(jnp.float32(nodes))
+    dz[...] = (cot[...].astype(F32) * slope).astype(BF)
+    wide[...] = mixed[:node_dev, :]
+    mixed_ref[...] = wide[:, own].astype(BF)
+
+    copies = []
+    for i, out in enumerate((g_self, g_neigh)):
+        grads[i] = t_dot(both[i, :, own], dz[...]) * factor
+        copies.append(pltpu.make_async_copy(grads.at[i], out, sem.at[i]))
+        copies[-1].start()
+    share = share_ref[:, :1]
     for r in range(parts):
-        to_self = dot_t(dz[...], blocks[3 * r + 1][...])
-        to_agg = dot_t(dz[...], blocks[3 * r + 2][...])
+        to_self, to_agg = dot_t(dz[...], blocks[2 * r][...]), dot_t(dz[...], blocks[2 * r + 1][...])
         if r >= 2:
             even = side == 0
             to_self, to_agg = jnp.where(even, to_self, to_agg), jnp.where(even, to_agg, to_self)
-        total = to_self + dot(counts_t, (to_agg * share).astype(BF))
+        total = to_self + dot(counts[...], (to_agg * share).astype(BF))
         if r == 0:
             grad_ref[...] = total[:node_dev, :].astype(BF)
-        g_out[:, place(r)] = t_dot(pooled[0], total.astype(BF)) * factor
-    g_self[...] = t_dot(both[0, :, own], dz[...]) * factor
-    g_neigh[...] = t_dot(both[1, :, own], dz[...]) * factor
+        at = slice(r * cols, (r + 1) * cols)
+        grads[2, :, at] = t_dot(pooled[...], total.astype(BF)) * factor
+        copies.append(
+            pltpu.make_async_copy(grads.at[2, :, at], g_out.at[:, block_place(r, cols)], sem.at[2 + r])
+        )
+        copies[-1].start()
+    for copy in copies:
+        copy.wait()
 
 
 def graph(order, fan, node_dev, got, weights):
@@ -219,24 +241,42 @@
     cols, width = weights[0][0].shape
     nodes = got[0].shape[0] * node_dev
     vmem = pl.BlockSpec(memory_space=pltpu.VMEM)
+    known = pl.pallas_call(
+        functools.partial(embed_kernel, order, fan, node_dev),
+        out_shape=(
+            jax.ShapeDtypeStruct((2, nodes, width), BF),
+            jax.ShapeDtypeStruct((nodes, width), BF),
+            jax.ShapeDtypeStruct((nodes, cols), BF),
+            jax.ShapeDtypeStruct((nodes, nodes), BF),
+            jax.ShapeDtypeStruct((nodes, 128), F32),
+        ),
+        in_specs=[vmem] * (2 * parts),
+        out_specs=(vmem,) * 5,
+        scratch_shapes=[pltpu.VMEM((nodes, width), F32)],
+        compiler_params=pltpu.CompilerParams(vmem_limit_bytes=24 * MIB),
+        cost_estimate=pl.CostEstimate(
+            flops=2 * nodes * width * width * 2, bytes_accessed=4 * MIB, transcendentals=0
+        ),
+    )(*got, *[group[0] for group in weights])
     slab = jax.ShapeDtypeStruct((node_dev, cols), BF)
     big = jax.ShapeDtypeStruct((cols, width), F32)
+    anywhere = pl.BlockSpec(memory_space=pl.ANY)
     return pl.pallas_call(
-        functools.partial(graph_kernel, order, fan, node_dev),
+        functools.partial(graph_kernel, node_dev),
         out_shape=(slab, slab, big, big, big),
-        in_specs=[vmem] * (4 * parts),
-        out_specs=(vmem,) * 5,
+        in_specs=[vmem] * (5 + 2 * parts),
+        out_specs=(vmem, vmem, anywhere, anywhere, anywhere),
         scratch_shapes=[
-            pltpu.VMEM((2, nodes, width), BF),
             pltpu.VMEM((nodes, width), BF),
-            pltpu.VMEM((nodes, width), F32),
-            pltpu.VMEM((nodes, width), F32),
+            pltpu.VMEM((node_dev, width), F32),
+            pltpu.VMEM((3, cols, width), F32),
+            pltpu.SemaphoreType.DMA((2 + parts,)),
         ],
         compiler_params=pltpu.CompilerParams(vmem_limit_bytes=36 * MIB),
         cost_estimate=pl.CostEstimate(
-            flops=2 * nodes * width * width * 6, bytes_accessed=10 * MIB, transcendentals=nodes * width
+            flops=2 * nodes * width * width * 5, bytes_accessed=8 * MIB, transcendentals=nodes * width
         ),
-    )(*got, *sum(weights, ()))
+    )(*known, *sum((group[1:] for group in weights), ()))
 
 
 def graph_wide(order, fan, node_dev, got, weights):
@@ -310,11 +350,11 @@
 def gather_dp(block, later):
     size = lax.axis_size("dp")
     if size == 8:
-        far = [hop(block, "dp", i) for i in (2, 4, 6)]
+        far = [hop(block, "dp", i) for i in range(1, size)]
         mine = join(block)
         mine, far, later = lax.optimization_barrier((mine, far, later))
         block = join(mine, *far)
-        order, bit = [0, 2, 4, 6], 1
+        order, bit = list(range(size)), 0
     else:
         order, bit = [0], size // 2
     while bit:
@@ -329,12 +369,13 @@
     nodes = node_dev * lax.axis_size("dp")
     own = (w_out, w_self, w_neigh)
     even = (lax.axis_index("dp") // 2) % 2 == 0
-    x_half = hop(jnp.where(even, w_self, w_neigh), "mp", 2)
+    picked, w_out = lax.optimization_barrier((jnp.where(even, w_self, w_neigh), w_out))
+    x_half = hop(picked, "mp", 2)
+    x_out = hop(w_out, "mp", 2)
     here = tuple(hop(a, "mp", 1) for a in own)
 
     sent = attention(texts, w_qkv, cotangent, neighbours.T)[None]
-    sent, here, x_half, w_out = lax.optimization_barrier((sent, here, x_half, w_out))
-    x_out = hop(w_out, "mp", 2)
+    sent, here, x_half = lax.optimization_barrier((sent, here, x_half))
     sent, order, x_half = gather_dp(sent, x_half)
     sent, x_out = lax.optimization_barrier((sent, x_out))
     z_half = hop(x_half, "dp", 2)

time: 49.8 us -> 55.8 us (1.12)
  starting transfers between devices: 13 us -> 17.7 us
  waiting for transfers between devices: 15.2 us -> 16.4 us
    ppermute x16 -> x19, starting transfers between devices: 13 us -> 17.7 us  [hop(): lax.ppermute(x, axis, [(i, i ^ bit) for i in range(lax.axis_size(axis))])]
    ppermute x16 -> x19, waiting for transfers between devices: 15.2 us -> 16.4 us  [hop(): lax.ppermute(x, axis, [(i, i ^ bit) for i in range(lax.axis_size(axis))])]
    pallas_call x1 -> x2, Pallas kernels: 7.21 us -> 7.29 us  [the longest x1 6.22 us: graph(): pl.pallas_call(functools.partial(graph_kernel, node_dev), out_shape=(slab...]
  transfers between devices with their start and end apart: 16 -> 19, of which waited for: 8 -> 9; matrix products, arithmetic and copies ran while one was open for 2% -> 2% of each run, Pallas kernels for 23% -> 23%
where the time goes in v11:
time: 55.8 us; the launch traced here: 55.5 us
  Pallas kernels  18.8 us (34%)
  starting transfers between devices  17.7 us (32%)
  waiting for transfers between devices  16.4 us (29%)
  other arithmetic  1.1 us (2%)
  local copies, waits for them, and re-layouts  0.82 us (1%)
  between operations  0.71 us (1%)
    ppermute x19, starting transfers between devices, hop(): lax.ppermute(x, axis, [(i, i ^ bit) for i in range(lax.axis_size(axis))])  17.7 us
    ppermute x19, waiting for transfers between devices, hop(): lax.ppermute(x, axis, [(i, i ^ bit) for i in range(lax.axis_size(axis))])  16.4 us
    pallas_call x1, Pallas kernels, attention(): pl.pallas_call(functools.partial(attention_kernel, heads), out_shape=jax....  11.5 us
    pallas_call x1, Pallas kernels, graph(): pl.pallas_call(functools.partial(graph_kernel, node_dev), out_shape=(slab...  6.22 us
  transfers between devices with their start and end apart: 19, of which 9 were waited for; matrix products, arithmetic and copies ran while one was open for 2% of the time, Pallas kernels for 23%

profile of v11, /device:TPU:0, one launch (start us, length us, event | category | flops | bytes accessed | tf_op | source)
XLA Modules:
  0.0 55.5 jit_solution(15164029506793946022)
XLA Ops:
  0.6 0.5 collective-permute-start
  1.1 0.1 collective-permute-start.1
  1.2 0.4 collective-permute-start.2
  1.7 1.1 %broadcast_select_fusion = bf16[256,1024]{1,0:T(8,128)(2,1)S(1)} fusion(bf16[256,1024]{1,0:T(8,128)(2,1)} %refs_0_.1, bf16[256,1024]{1,0:T(8,128)(2,1)} %refs_1_.1, pred[]{:T(512)S(6)} %eq.5), kind=kLoop, calls=%fused_computation | loop fusion | flops 262144 | bytes 1572865 | tf_op jit(solution)/shard_map/jit(_where)/select_n | solution.py:372
  2.8 2.6 %collective-permute-start.3 = (bf16[256,1024]{1,0:T(8,128)(2,1)S(1)}, bf16[256,1024]{1,0:T(8,128)(2,1)S(1)}, u32[]{:S(2)}, u32[]{:S(2)}) collective-permute-start(bf16[256,1024]{1,0:T(8,128)(2,1)S(1)} %broadcast_select_fusion), channel_id=1, source_target_pairs={{0,2},{1,3},{2,0},{3,1},{4,6},{5,7},{6,4},{7,5},{8,10},{9,11},{10,... | collective-permute-start | bytes 1572872 | tf_op jit(solution)/shard_map/ppermute | solution.py:347
  5.4 0.1 collective-permute-start.11
  5.5 11.5 %shard_map.110 = bf16[16,1280]{1,0:T(8,128)(2,1)} custom-call(bf16[24,128,1024]{2,1,0:T(8,128)(2,1)} %x_ref.1, bf16[1024,768]{1,0:T(8,128)(2,1)} %w_ref.1, bf16[24,256]{1,0:T(8,128)(2,1)} %cot_ref.1, s32[16,24]{1,0:T(8,128)} %bitcast.10), custom_call_target="tpu_custom_call" | custom-call | flops 5637144576 | bytes 7864320 | tf_op jit(solution)/shard_map/pallas_call | solution.py:112
  17.0 1.2 %collective-permute-done.3.refs_4_ = bf16[256,1024]{1,0:T(8,128)(2,1)S(1)} collective-permute-done((bf16[256,1024]{1,0:T(8,128)(2,1)S(1)}, bf16[256,1024]{1,0:T(8,128)(2,1)S(1)}, u32[]{:S(2)}, u32[]{:S(2)}) %collective-permute-start.3) | collective-permute-done | bytes 524320 | tf_op jit(solution)/shard_map/ppermute | solution.py:347
  18.2 0.0 collective-permute-done.2.refs_3_
  18.2 5.1 %collective-permute-start.10 = (bf16[1,16,1280]{2,1,0:T(8,128)(2,1)}, bf16[1,16,1280]{2,1,0:T(8,128)(2,1)S(1)}, u32[]{:S(2)}, u32[]{:S(2)}) collective-permute-start(bf16[1,16,1280]{2,1,0:T(8,128)(2,1)} %bitcast.2), channel_id=1, source_target_pairs={{0,28},{4,24},{8,20},{12,16},{16,12},{20,8},{24,4},{28,0},{1,29},{... | collective-permute-start | bytes 122888 | tf_op jit(solution)/shard_map/ppermute | solution.py:347
  23.3 0.2 collective-permute-start.9
  23.5 0.7 %collective-permute-start.8 = (bf16[1,16,1280]{2,1,0:T(8,128)(2,1)}, bf16[1,16,1280]{2,1,0:T(8,128)(2,1)S(1)}, u32[]{:S(2)}, u32[]{:S(2)}) collective-permute-start(bf16[1,16,1280]{2,1,0:T(8,128)(2,1)} %bitcast.4), channel_id=1, source_target_pairs={{0,20},{4,16},{8,28},{12,24},{16,4},{20,0},{24,12},{28,8},{1,21},{... | collective-permute-start | bytes 122888 | tf_op jit(solution)/shard_map/ppermute | solution.py:347
  24.2 2.0 %collective-permute-start.7 = (bf16[1,16,1280]{2,1,0:T(8,128)(2,1)}, bf16[1,16,1280]{2,1,0:T(8,128)(2,1)S(1)}, u32[]{:S(2)}, u32[]{:S(2)}) collective-permute-start(bf16[1,16,1280]{2,1,0:T(8,128)(2,1)} %bitcast.5), channel_id=1, source_target_pairs={{0,16},{4,20},{8,24},{12,28},{16,0},{20,4},{24,8},{28,12},{1,17},{... | collective-permute-start | bytes 122888 | tf_op jit(solution)/shard_map/ppermute | solution.py:347
  26.3 2.3 %collective-permute-start.6 = (bf16[1,16,1280]{2,1,0:T(8,128)(2,1)}, bf16[1,16,1280]{2,1,0:T(8,128)(2,1)S(1)}, u32[]{:S(2)}, u32[]{:S(2)}) collective-permute-start(bf16[1,16,1280]{2,1,0:T(8,128)(2,1)} %bitcast.6), channel_id=1, source_target_pairs={{0,12},{4,8},{8,4},{12,0},{16,28},{20,24},{24,20},{28,16},{1,13},{... | collective-permute-start | bytes 122888 | tf_op jit(solution)/shard_map/ppermute | solution.py:347
  28.6 0.9 %collective-permute-done.9.refs_6_ = bf16[1,16,1280]{2,1,0:T(8,128)(2,1)S(1)} collective-permute-done((bf16[1,16,1280]{2,1,0:T(8,128)(2,1)}, bf16[1,16,1280]{2,1,0:T(8,128)(2,1)S(1)}, u32[]{:S(2)}, u32[]{:S(2)}) %collective-permute-start.9) | collective-permute-done | bytes 40992 | tf_op jit(solution)/shard_map/ppermute | solution.py:347
  29.5 1.0 %collective-permute-done.8.refs_5_ = bf16[1,16,1280]{2,1,0:T(8,128)(2,1)S(1)} collective-permute-done((bf16[1,16,1280]{2,1,0:T(8,128)(2,1)}, bf16[1,16,1280]{2,1,0:T(8,128)(2,1)S(1)}, u32[]{:S(2)}, u32[]{:S(2)}) %collective-permute-start.8) | collective-permute-done | bytes 40992 | tf_op jit(solution)/shard_map/ppermute | solution.py:347
  30.5 0.8 %copy-done.3 = bf16[16,1280]{1,0:T(8,128)(2,1)S(1)} copy-done((bf16[16,1280]{1,0:T(8,128)(2,1)S(1)}, bf16[16,1280]{1,0:T(8,128)(2,1)}, u32[]{:S(2)}) %copy-start.3) | copy-done | bytes 40984
  31.4 0.0 collective-permute-done.7.refs_4_
  31.4 0.2 collective-permute-done.6.refs_3_
  31.5 2.2 %collective-permute-done.5.refs_2_ = bf16[1,16,1280]{2,1,0:T(8,128)(2,1)S(1)} collective-permute-done((bf16[1,16,1280]{2,1,0:T(8,128)(2,1)}, bf16[1,16,1280]{2,1,0:T(8,128)(2,1)S(1)}, u32[]{:S(2)}, u32[]{:S(2)}) %collective-permute-start.5) | collective-permute-done | bytes 40992 | tf_op jit(solution)/shard_map/ppermute | solution.py:347
  33.7 1.0 %collective-permute-done.4.refs_1_ = bf16[1,16,1280]{2,1,0:T(8,128)(2,1)S(1)} collective-permute-done((bf16[1,16,1280]{2,1,0:T(8,128)(2,1)}, bf16[1,16,1280]{2,1,0:T(8,128)(2,1)S(1)}, u32[]{:S(2)}, u32[]{:S(2)}) %collective-permute-start.4) | collective-permute-done | bytes 40992 | tf_op jit(solution)/shard_map/ppermute | solution.py:347
  34.7 1.0 %collective-permute-start.16 = (bf16[256,1024]{1,0:T(8,128)(2,1)S(1)}, bf16[256,1024]{1,0:T(8,128)(2,1)S(1)}, u32[]{:S(2)}, u32[]{:S(2)}) collective-permute-start(bf16[256,1024]{1,0:T(8,128)(2,1)S(1)} %collective-permute-done.3.refs_4_), channel_id=1, source_target_pairs={{0,8},{4,12},{8,0},{12,4},{16,24},{20,28},{24,16},{28,20},{1,9},{5... | collective-permute-start | bytes 1572872 | tf_op jit(solution)/shard_map/ppermute | solution.py:347
  35.8 1.6 %collective-permute-start.13 = (bf16[8,16,1280]{2,1,0:T(8,128)(2,1)S(1)}, bf16[8,16,1280]{2,1,0:T(8,128)(2,1)S(1)}, u32[]{:S(2)}, u32[]{:S(2)}) collective-permute-start(bf16[8,16,1280]{2,1,0:T(8,128)(2,1)S(1)} %shard_map.112.refs_0_), channel_id=1, source_target_pairs={{0,2},{1,3},{2,0},{3,1},{4,6},{5,7},{6,4},{7,5},{8,10},{9,11},{10,... | collective-permute-start | bytes 983048 | tf_op jit(solution)/shard_map/ppermute | solution.py:347
  37.3 0.0 collective-permute-start.15
  37.3 0.5 collective-permute-start.17
  37.8 7.5 %collective-permute-done.16.refs_5_ = bf16[256,1024]{1,0:T(8,128)(2,1)S(1)} collective-permute-done((bf16[256,1024]{1,0:T(8,128)(2,1)S(1)}, bf16[256,1024]{1,0:T(8,128)(2,1)S(1)}, u32[]{:S(2)}, u32[]{:S(2)}) %collective-permute-start.16) | collective-permute-done | bytes 524320 | tf_op jit(solution)/shard_map/ppermute | solution.py:347
  45.4 0.5 collective-permute-start.12
  45.9 0.0 collective-permute-start.14
  45.9 1.9 %collective-permute-done.12.refs_1_ = bf16[8,16,1280]{2,1,0:T(8,128)(2,1)S(1)} collective-permute-done((bf16[8,16,1280]{2,1,0:T(8,128)(2,1)S(1)}, bf16[8,16,1280]{2,1,0:T(8,128)(2,1)S(1)}, u32[]{:S(2)}, u32[]{:S(2)}) %collective-permute-start.12) | collective-permute-done | bytes 327712 | tf_op jit(solution)/shard_map/ppermute | solution.py:347
  47.7 0.5 collective-permute-done.14.refs_3_
  48.2 1.1 %shard_map.113 = (bf16[2,192,1024]{2,1,0:T(8,128)(2,1)S(1)}, bf16[192,1024]{1,0:T(8,128)(2,1)S(1)}, bf16[192,256]{1,0:T(8,128)(2,1)S(1)}, bf16[192,192]{1,0:T(8,128)(2,1)S(1)}, f32[192,128]{1,0:T(8,128)S(1)}) custom-call(bf16[8,16,1280]{2,1,0:T(8,128)(2,1)S(1)} %shard_map.112.refs_0_, bf16[8,16,1280]{2,1,0:T(8,128)(2,1)S(1)} %collective-permute-done.12.refs_1_, ...), custom_call_target="tpu_custom_call" | custom-call | flops 805306368 | bytes 4194304 | tf_op jit(solution)/shard_map/pallas_call | solution.py:244
  49.3 6.2 %shard_map.114 = (bf16[24,256]{1,0:T(8,128)(2,1)}, bf16[24,256]{1,0:T(8,128)(2,1)}, f32[256,1024]{1,0:T(8,128)}, f32[256,1024]{1,0:T(8,128)}, f32[256,1024]{1,0:T(8,128)}) custom-call(bf16[2,192,1024]{2,1,0:T(8,128)(2,1)S(1)} %get-tuple-element.43.both, bf16[192,1024]{1,0:T(8,128)(2,1)S(1)} %get-tuple-element.44.cot, ...), custom_call_target="tpu_custom_call" | custom-call | flops 2013265920 | bytes 8388608 | tf_op jit(solution)/shard_map/pallas_call | solution.py:264
  (20 shorter events, 0.1 us)
Async XLA Ops:
  0.6 17.5 %collective-permute-start = (bf16[256,1024]{1,0:T(8,128)(2,1)}, bf16[256,1024]{1,0:T(8,128)(2,1)S(1)}, u32[]{:S(2)}, u32[]{:S(2)}) collective-permute-start(bf16[256,1024]{1,0:T(8,128)(2,1)} %refs_4_.1), channel_id=1, source_target_pairs={{0,1},{1,0},{2,3},{3,2},{4,5},{5,4},{6,7},{7,6},{8,9},{9,8},{10,11... | collective-permute-start | bytes 1572872 | tf_op jit(solution)/shard_map/ppermute | solution.py:347
  1.1 17.0 %collective-permute-start.1 = (bf16[256,1024]{1,0:T(8,128)(2,1)}, bf16[256,1024]{1,0:T(8,128)(2,1)S(1)}, u32[]{:S(2)}, u32[]{:S(2)}) collective-permute-start(bf16[256,1024]{1,0:T(8,128)(2,1)} %refs_0_.1), channel_id=1, source_target_pairs={{0,1},{1,0},{2,3},{3,2},{4,5},{5,4},{6,7},{7,6},{8,9},{9,8},{10,11... | collective-permute-start | bytes 1572872 | tf_op jit(solution)/shard_map/ppermute | solution.py:347
  1.2 17.0 %collective-permute-start.2 = (bf16[256,1024]{1,0:T(8,128)(2,1)}, bf16[256,1024]{1,0:T(8,128)(2,1)S(1)}, u32[]{:S(2)}, u32[]{:S(2)}) collective-permute-start(bf16[256,1024]{1,0:T(8,128)(2,1)} %refs_1_.1), channel_id=1, source_target_pairs={{0,1},{1,0},{2,3},{3,2},{4,5},{5,4},{6,7},{7,6},{8,9},{9,8},{10,11... | collective-permute-start | bytes 1572872 | tf_op jit(solution)/shard_map/ppermute | solution.py:347
  2.8 15.4 %collective-permute-start.3 = (bf16[256,1024]{1,0:T(8,128)(2,1)S(1)}, bf16[256,1024]{1,0:T(8,128)(2,1)S(1)}, u32[]{:S(2)}, u32[]{:S(2)}) collective-permute-start(bf16[256,1024]{1,0:T(8,128)(2,1)S(1)} %broadcast_select_fusion), channel_id=1, source_target_pairs={{0,2},{1,3},{2,0},{3,1},{4,6},{5,7},{6,4},{7,5},{8,10},{9,11},{10,... | collective-permute-start | bytes 1572872 | tf_op jit(solution)/shard_map/ppermute | solution.py:347
  5.4 30.4 %collective-permute-start.11 = (bf16[256,1024]{1,0:T(8,128)(2,1)}, bf16[256,1024]{1,0:T(8,128)(2,1)S(1)}, u32[]{:S(2)}, u32[]{:S(2)}) collective-permute-start(bf16[256,1024]{1,0:T(8,128)(2,1)} %refs_4_.1), channel_id=1, source_target_pairs={{0,2},{1,3},{2,0},{3,1},{4,6},{5,7},{6,4},{7,5},{8,10},{9,11},{10,... | collective-permute-start | bytes 1572872 | tf_op jit(solution)/shard_map/ppermute | solution.py:347
  5.5 42.7 %copy-start.2 = (bf16[256,1024]{1,0:T(8,128)(2,1)S(1)}, bf16[256,1024]{1,0:T(8,128)(2,1)}, u32[]{:S(2)}) copy-start(bf16[256,1024]{1,0:T(8,128)(2,1)} %refs_4_.1) | copy-start | bytes 1572868
  5.5 43.8 %copy-start = (bf16[256,1024]{1,0:T(8,128)(2,1)S(1)}, bf16[256,1024]{1,0:T(8,128)(2,1)}, u32[]{:S(2)}) copy-start(bf16[256,1024]{1,0:T(8,128)(2,1)} %refs_0_.1) | copy-start | bytes 1572868
  5.5 43.8 %copy-start.1 = (bf16[256,1024]{1,0:T(8,128)(2,1)S(1)}, bf16[256,1024]{1,0:T(8,128)(2,1)}, u32[]{:S(2)}) copy-start(bf16[256,1024]{1,0:T(8,128)(2,1)} %refs_1_.1) | copy-start | bytes 1572868
  18.2 8.1 %collective-permute-start.10 = (bf16[1,16,1280]{2,1,0:T(8,128)(2,1)}, bf16[1,16,1280]{2,1,0:T(8,128)(2,1)S(1)}, u32[]{:S(2)}, u32[]{:S(2)}) collective-permute-start(bf16[1,16,1280]{2,1,0:T(8,128)(2,1)} %bitcast.2), channel_id=1, source_target_pairs={{0,28},{4,24},{8,20},{12,16},{16,12},{20,8},{24,4},{28,0},{1,29},{... | collective-permute-start | bytes 122888 | tf_op jit(solution)/shard_map/ppermute | solution.py:347
  23.3 6.2 %collective-permute-start.9 = (bf16[1,16,1280]{2,1,0:T(8,128)(2,1)}, bf16[1,16,1280]{2,1,0:T(8,128)(2,1)S(1)}, u32[]{:S(2)}, u32[]{:S(2)}) collective-permute-start(bf16[1,16,1280]{2,1,0:T(8,128)(2,1)} %bitcast.3), channel_id=1, source_target_pairs={{0,24},{4,28},{8,16},{12,20},{16,8},{20,12},{24,0},{28,4},{1,25},{... | collective-permute-start | bytes 122888 | tf_op jit(solution)/shard_map/ppermute | solution.py:347
  23.5 7.0 %collective-permute-start.8 = (bf16[1,16,1280]{2,1,0:T(8,128)(2,1)}, bf16[1,16,1280]{2,1,0:T(8,128)(2,1)S(1)}, u32[]{:S(2)}, u32[]{:S(2)}) collective-permute-start(bf16[1,16,1280]{2,1,0:T(8,128)(2,1)} %bitcast.4), channel_id=1, source_target_pairs={{0,20},{4,16},{8,28},{12,24},{16,4},{20,0},{24,12},{28,8},{1,21},{... | collective-permute-start | bytes 122888 | tf_op jit(solution)/shard_map/ppermute | solution.py:347
  24.2 7.1 %collective-permute-start.7 = (bf16[1,16,1280]{2,1,0:T(8,128)(2,1)}, bf16[1,16,1280]{2,1,0:T(8,128)(2,1)S(1)}, u32[]{:S(2)}, u32[]{:S(2)}) collective-permute-start(bf16[1,16,1280]{2,1,0:T(8,128)(2,1)} %bitcast.5), channel_id=1, source_target_pairs={{0,16},{4,20},{8,24},{12,28},{16,0},{20,4},{24,8},{28,12},{1,17},{... | collective-permute-start | bytes 122888 | tf_op jit(solution)/shard_map/ppermute | solution.py:347
  26.3 5.2 %collective-permute-start.6 = (bf16[1,16,1280]{2,1,0:T(8,128)(2,1)}, bf16[1,16,1280]{2,1,0:T(8,128)(2,1)S(1)}, u32[]{:S(2)}, u32[]{:S(2)}) collective-permute-start(bf16[1,16,1280]{2,1,0:T(8,128)(2,1)} %bitcast.6), channel_id=1, source_target_pairs={{0,12},{4,8},{8,4},{12,0},{16,28},{20,24},{24,20},{28,16},{1,13},{... | collective-permute-start | bytes 122888 | tf_op jit(solution)/shard_map/ppermute | solution.py:347
  29.5 4.2 %collective-permute-start.5 = (bf16[1,16,1280]{2,1,0:T(8,128)(2,1)}, bf16[1,16,1280]{2,1,0:T(8,128)(2,1)S(1)}, u32[]{:S(2)}, u32[]{:S(2)}) collective-permute-start(bf16[1,16,1280]{2,1,0:T(8,128)(2,1)} %bitcast.7), channel_id=1, source_target_pairs={{0,8},{4,12},{8,0},{12,4},{16,24},{20,28},{24,16},{28,20},{1,9},{5... | collective-permute-start | bytes 122888 | tf_op jit(solution)/shard_map/ppermute | solution.py:347
  30.5 4.2 %collective-permute-start.4 = (bf16[1,16,1280]{2,1,0:T(8,128)(2,1)}, bf16[1,16,1280]{2,1,0:T(8,128)(2,1)S(1)}, u32[]{:S(2)}, u32[]{:S(2)}) collective-permute-start(bf16[1,16,1280]{2,1,0:T(8,128)(2,1)} %bitcast.8), channel_id=1, source_target_pairs={{0,4},{4,0},{8,12},{12,8},{16,20},{20,16},{24,28},{28,24},{1,5},{5... | collective-permute-start | bytes 122888 | tf_op jit(solution)/shard_map/ppermute | solution.py:347
  30.5 0.8 %copy-start.3 = (bf16[16,1280]{1,0:T(8,128)(2,1)S(1)}, bf16[16,1280]{1,0:T(8,128)(2,1)}, u32[]{:S(2)}) copy-start(bf16[16,1280]{1,0:T(8,128)(2,1)} %shard_map.110) | copy-start | bytes 122884
  34.7 10.6 %collective-permute-start.16 = (bf16[256,1024]{1,0:T(8,128)(2,1)S(1)}, bf16[256,1024]{1,0:T(8,128)(2,1)S(1)}, u32[]{:S(2)}, u32[]{:S(2)}) collective-permute-start(bf16[256,1024]{1,0:T(8,128)(2,1)S(1)} %collective-permute-done.3.refs_4_), channel_id=1, source_target_pairs={{0,8},{4,12},{8,0},{12,4},{16,24},{20,28},{24,16},{28,20},{1,9},{5... | collective-permute-start | bytes 1572872 | tf_op jit(solution)/shard_map/ppermute | solution.py:347
  35.8 10.1 %collective-permute-start.13 = (bf16[8,16,1280]{2,1,0:T(8,128)(2,1)S(1)}, bf16[8,16,1280]{2,1,0:T(8,128)(2,1)S(1)}, u32[]{:S(2)}, u32[]{:S(2)}) collective-permute-start(bf16[8,16,1280]{2,1,0:T(8,128)(2,1)S(1)} %shard_map.112.refs_0_), channel_id=1, source_target_pairs={{0,2},{1,3},{2,0},{3,1},{4,6},{5,7},{6,4},{7,5},{8,10},{9,11},{10,... | collective-permute-start | bytes 983048 | tf_op jit(solution)/shard_map/ppermute | solution.py:347
  37.3 10.4 %collective-permute-start.15 = (bf16[256,1024]{1,0:T(8,128)(2,1)S(1)}, bf16[256,1024]{1,0:T(8,128)(2,1)S(1)}, u32[]{:S(2)}, u32[]{:S(2)}) collective-permute-start(bf16[256,1024]{1,0:T(8,128)(2,1)S(1)} %collective-permute-done.11.refs_6_), channel_id=1, source_target_pairs={{0,1},{1,0},{2,3},{3,2},{4,5},{5,4},{6,7},{7,6},{8,9},{9,8},{10,11... | collective-permute-start | bytes 1572872 | tf_op jit(solution)/shard_map/ppermute | solution.py:347
  37.3 11.9 %collective-permute-start.17 = (bf16[256,1024]{1,0:T(8,128)(2,1)S(1)}, bf16[256,1024]{1,0:T(8,128)(2,1)S(1)}, u32[]{:S(2)}, u32[]{:S(2)}) collective-permute-start(bf16[256,1024]{1,0:T(8,128)(2,1)S(1)} %collective-permute-done.3.refs_4_), channel_id=1, source_target_pairs={{0,1},{1,0},{2,3},{3,2},{4,5},{5,4},{6,7},{7,6},{8,9},{9,8},{10,11... | collective-permute-start | bytes 1572872 | tf_op jit(solution)/shard_map/ppermute | solution.py:347
  45.4 3.9 %collective-permute-start.18 = (bf16[256,1024]{1,0:T(8,128)(2,1)S(1)}, bf16[256,1024]{1,0:T(8,128)(2,1)S(1)}, u32[]{:S(2)}, u32[]{:S(2)}) collective-permute-start(bf16[256,1024]{1,0:T(8,128)(2,1)S(1)} %collective-permute-done.16.refs_5_), channel_id=1, source_target_pairs={{0,1},{1,0},{2,3},{3,2},{4,5},{5,4},{6,7},{7,6},{8,9},{9,8},{10,11... | collective-permute-start | bytes 1572872 | tf_op jit(solution)/shard_map/ppermute | solution.py:347
  45.4 2.4 %collective-permute-start.12 = (bf16[8,16,1280]{2,1,0:T(8,128)(2,1)S(1)}, bf16[8,16,1280]{2,1,0:T(8,128)(2,1)S(1)}, u32[]{:S(2)}, u32[]{:S(2)}) collective-permute-start(bf16[8,16,1280]{2,1,0:T(8,128)(2,1)S(1)} %shard_map.112.refs_0_), channel_id=1, source_target_pairs={{0,1},{1,0},{2,3},{3,2},{4,5},{5,4},{6,7},{7,6},{8,9},{9,8},{10,11... | collective-permute-start | bytes 983048 | tf_op jit(solution)/shard_map/ppermute | solution.py:347
  45.9 2.3 %collective-permute-start.14 = (bf16[8,16,1280]{2,1,0:T(8,128)(2,1)S(1)}, bf16[8,16,1280]{2,1,0:T(8,128)(2,1)S(1)}, u32[]{:S(2)}, u32[]{:S(2)}) collective-permute-start(bf16[8,16,1280]{2,1,0:T(8,128)(2,1)S(1)} %collective-permute-done.13.refs_2_), channel_id=1, source_target_pairs={{0,1},{1,0},{2,3},{3,2},{4,5},{5,4},{6,7},{7,6},{8,9},{9,8},{10,11... | collective-permute-start | bytes 983048 | tf_op jit(solution)/shard_map/ppermute | solution.py:347

commit v12 on v11

--- a/solution.py
+++ b/solution.py
@@ -350,11 +350,11 @@
 def gather_dp(block, later):
     size = lax.axis_size("dp")
     if size == 8:
-        far = [hop(block, "dp", i) for i in range(1, size)]
+        far = [hop(block, "dp", i) for i in (2, 4, 6)]
         mine = join(block)
         mine, far, later = lax.optimization_barrier((mine, far, later))
         block = join(mine, *far)
-        order, bit = list(range(size)), 0
+        order, bit = [0, 2, 4, 6], 1
     else:
         order, bit = [0], size // 2
     while bit:

time: 55.8 us -> 49.5 us (0.89)
  starting transfers between devices: 17.7 us -> 12.7 us
  waiting for transfers between devices: 16.4 us -> 15.1 us
    ppermute x19 -> x16, starting transfers between devices: 17.7 us -> 12.7 us  [hop(): lax.ppermute(x, axis, [(i, i ^ bit) for i in range(lax.axis_size(axis))])]
    ppermute x19 -> x16, waiting for transfers between devices: 16.4 us -> 15.1 us  [hop(): lax.ppermute(x, axis, [(i, i ^ bit) for i in range(lax.axis_size(axis))])]
  transfers between devices with their start and end apart: 19 -> 16, of which waited for: 9 -> 8; matrix products, arithmetic and copies ran while one was open for 2% -> 2% of each run, Pallas kernels for 23% -> 26%
where the time goes in v12:
time: 49.5 us; the launch traced here: 49.2 us
  Pallas kernels  18.9 us (38%)
  waiting for transfers between devices  15.1 us (31%)
  starting transfers between devices  12.7 us (26%)
  other arithmetic  1.1 us (2%)
  local copies, waits for them, and re-layouts  0.82 us (2%)
  between operations  0.71 us (1%)
    ppermute x16, waiting for transfers between devices, hop(): lax.ppermute(x, axis, [(i, i ^ bit) for i in range(lax.axis_size(axis))])  15.1 us
    ppermute x16, starting transfers between devices, hop(): lax.ppermute(x, axis, [(i, i ^ bit) for i in range(lax.axis_size(axis))])  12.7 us
    pallas_call x1, Pallas kernels, attention(): pl.pallas_call(functools.partial(attention_kernel, heads), out_shape=jax....  11.5 us
    pallas_call x1, Pallas kernels, graph(): pl.pallas_call(functools.partial(graph_kernel, node_dev), out_shape=(slab...  6.22 us
    select_n x1, other arithmetic, per_device(): jnp.where(even, w_self, w_neigh)  1.1 us
    pallas_call x1, Pallas kernels, graph(): pl.pallas_call(functools.partial(embed_kernel, order, fan, node_dev), out...  1.07 us
  transfers between devices with their start and end apart: 16, of which 8 were waited for; matrix products, arithmetic and copies ran while one was open for 2% of the time, Pallas kernels for 26%

profile of v12, /device:TPU:0, one launch (start us, length us, event | category | flops | bytes accessed | tf_op | source)
XLA Modules:
  0.0 49.2 jit_solution(704732535459762130)
XLA Ops:
  0.6 0.5 %collective-permute-start = (bf16[256,1024]{1,0:T(8,128)(2,1)}, bf16[256,1024]{1,0:T(8,128)(2,1)S(1)}, u32[]{:S(2)}, u32[]{:S(2)}) collective-permute-start(bf16[256,1024]{1,0:T(8,128)(2,1)} %refs_4_.1), channel_id=1, source_target_pairs={{0,1},{1,0},{2,3},{3,2},{4,5},{5,4},{6,7},{7,6},{8,9},{9,8},{10,11... | collective-permute-start | bytes 1572872 | tf_op jit(solution)/shard_map/ppermute | solution.py:347
  1.1 0.1 collective-permute-start.1
  1.2 0.4 collective-permute-start.2
  1.7 1.1 %broadcast_select_fusion = bf16[256,1024]{1,0:T(8,128)(2,1)S(1)} fusion(bf16[256,1024]{1,0:T(8,128)(2,1)} %refs_0_.1, bf16[256,1024]{1,0:T(8,128)(2,1)} %refs_1_.1, pred[]{:T(512)S(6)} %eq.5), kind=kLoop, calls=%fused_computation | loop fusion | flops 262144 | bytes 1572865 | tf_op jit(solution)/shard_map/jit(_where)/select_n | solution.py:372
  2.8 2.6 %collective-permute-start.3 = (bf16[256,1024]{1,0:T(8,128)(2,1)S(1)}, bf16[256,1024]{1,0:T(8,128)(2,1)S(1)}, u32[]{:S(2)}, u32[]{:S(2)}) collective-permute-start(bf16[256,1024]{1,0:T(8,128)(2,1)S(1)} %broadcast_select_fusion), channel_id=1, source_target_pairs={{0,2},{1,3},{2,0},{3,1},{4,6},{5,7},{6,4},{7,5},{8,10},{9,11},{10,... | collective-permute-start | bytes 1572872 | tf_op jit(solution)/shard_map/ppermute | solution.py:347
  5.4 0.1 collective-permute-start.8
  5.5 11.5 %shard_map.110 = bf16[16,1280]{1,0:T(8,128)(2,1)} custom-call(bf16[24,128,1024]{2,1,0:T(8,128)(2,1)} %x_ref.1, bf16[1024,768]{1,0:T(8,128)(2,1)} %w_ref.1, bf16[24,256]{1,0:T(8,128)(2,1)} %cot_ref.1, s32[16,24]{1,0:T(8,128)} %bitcast.6), custom_call_target="tpu_custom_call" | custom-call | flops 5637144576 | bytes 7864320 | tf_op jit(solution)/shard_map/pallas_call | solution.py:112
  17.0 1.2 %collective-permute-done.3.refs_4_ = bf16[256,1024]{1,0:T(8,128)(2,1)S(1)} collective-permute-done((bf16[256,1024]{1,0:T(8,128)(2,1)S(1)}, bf16[256,1024]{1,0:T(8,128)(2,1)S(1)}, u32[]{:S(2)}, u32[]{:S(2)}) %collective-permute-start.3) | collective-permute-done | bytes 524320 | tf_op jit(solution)/shard_map/ppermute | solution.py:347
  18.2 0.0 collective-permute-done.2.refs_3_
  18.2 4.1 %collective-permute-start.6 = (bf16[1,16,1280]{2,1,0:T(8,128)(2,1)}, bf16[1,16,1280]{2,1,0:T(8,128)(2,1)S(1)}, u32[]{:S(2)}, u32[]{:S(2)}) collective-permute-start(bf16[1,16,1280]{2,1,0:T(8,128)(2,1)} %bitcast.2), channel_id=1, source_target_pairs={{0,24},{4,28},{8,16},{12,20},{16,8},{20,12},{24,0},{28,4},{1,25},{... | collective-permute-start | bytes 122888 | tf_op jit(solution)/shard_map/ppermute | solution.py:347
  22.3 0.6 %collective-permute-start.4 = (bf16[1,16,1280]{2,1,0:T(8,128)(2,1)}, bf16[1,16,1280]{2,1,0:T(8,128)(2,1)S(1)}, u32[]{:S(2)}, u32[]{:S(2)}) collective-permute-start(bf16[1,16,1280]{2,1,0:T(8,128)(2,1)} %bitcast.4), channel_id=1, source_target_pairs={{0,8},{4,12},{8,0},{12,4},{16,24},{20,28},{24,16},{28,20},{1,9},{5... | collective-permute-start | bytes 122888 | tf_op jit(solution)/shard_map/ppermute | solution.py:347
  22.9 0.8 %copy-done.3 = bf16[16,1280]{1,0:T(8,128)(2,1)S(1)} copy-done((bf16[16,1280]{1,0:T(8,128)(2,1)S(1)}, bf16[16,1280]{1,0:T(8,128)(2,1)}, u32[]{:S(2)}) %copy-start.3) | copy-done | bytes 40984
  23.8 1.2 %collective-permute-done.6.refs_3_ = bf16[1,16,1280]{2,1,0:T(8,128)(2,1)S(1)} collective-permute-done((bf16[1,16,1280]{2,1,0:T(8,128)(2,1)}, bf16[1,16,1280]{2,1,0:T(8,128)(2,1)S(1)}, u32[]{:S(2)}, u32[]{:S(2)}) %collective-permute-start.6) | collective-permute-done | bytes 40992 | tf_op jit(solution)/shard_map/ppermute | solution.py:347
  24.9 2.5 %collective-permute-done.5.refs_2_ = bf16[1,16,1280]{2,1,0:T(8,128)(2,1)S(1)} collective-permute-done((bf16[1,16,1280]{2,1,0:T(8,128)(2,1)}, bf16[1,16,1280]{2,1,0:T(8,128)(2,1)S(1)}, u32[]{:S(2)}, u32[]{:S(2)}) %collective-permute-start.5) | collective-permute-done | bytes 40992 | tf_op jit(solution)/shard_map/ppermute | solution.py:347
  27.4 0.0 collective-permute-done.4.refs_1_
  27.4 0.0 collective-permute-start.13
  27.4 1.6 %collective-permute-start.7 = (bf16[4,16,1280]{2,1,0:T(8,128)(2,1)S(1)}, bf16[4,16,1280]{2,1,0:T(8,128)(2,1)S(1)}, u32[]{:S(2)}, u32[]{:S(2)}) collective-permute-start(bf16[4,16,1280]{2,1,0:T(8,128)(2,1)S(1)} %shard_map.112.refs_0_), channel_id=1, source_target_pairs={{0,4},{4,0},{8,12},{12,8},{16,20},{20,16},{24,28},{28,24},{1,5},{5... | collective-permute-start | bytes 491528 | tf_op jit(solution)/shard_map/ppermute | solution.py:347
  29.0 3.8 %collective-permute-done.7.refs_1_ = bf16[4,16,1280]{2,1,0:T(8,128)(2,1)S(1)} collective-permute-done((bf16[4,16,1280]{2,1,0:T(8,128)(2,1)S(1)}, bf16[4,16,1280]{2,1,0:T(8,128)(2,1)S(1)}, u32[]{:S(2)}, u32[]{:S(2)}) %collective-permute-start.7) | collective-permute-done | bytes 163872 | tf_op jit(solution)/shard_map/ppermute | solution.py:347
  32.9 0.0 collective-permute-done.8.refs_6_
  32.9 1.6 %collective-permute-start.10 = (bf16[8,16,1280]{2,1,0:T(8,128)(2,1)S(1)}, bf16[8,16,1280]{2,1,0:T(8,128)(2,1)S(1)}, u32[]{:S(2)}, u32[]{:S(2)}) collective-permute-start(bf16[8,16,1280]{2,1,0:T(8,128)(2,1)S(1)} %shard_map.113.refs_0_), channel_id=1, source_target_pairs={{0,2},{1,3},{2,0},{3,1},{4,6},{5,7},{6,4},{7,5},{8,10},{9,11},{10,... | collective-permute-start | bytes 983048 | tf_op jit(solution)/shard_map/ppermute | solution.py:347
  34.4 0.5 %collective-permute-start.14 = (bf16[256,1024]{1,0:T(8,128)(2,1)S(1)}, bf16[256,1024]{1,0:T(8,128)(2,1)S(1)}, u32[]{:S(2)}, u32[]{:S(2)}) collective-permute-start(bf16[256,1024]{1,0:T(8,128)(2,1)S(1)} %collective-permute-done.3.refs_4_), channel_id=1, source_target_pairs={{0,1},{1,0},{2,3},{3,2},{4,5},{5,4},{6,7},{7,6},{8,9},{9,8},{10,11... | collective-permute-start | bytes 1572872 | tf_op jit(solution)/shard_map/ppermute | solution.py:347
  34.9 4.1 %collective-permute-done.13.refs_5_ = bf16[256,1024]{1,0:T(8,128)(2,1)S(1)} collective-permute-done((bf16[256,1024]{1,0:T(8,128)(2,1)S(1)}, bf16[256,1024]{1,0:T(8,128)(2,1)S(1)}, u32[]{:S(2)}, u32[]{:S(2)}) %collective-permute-start.13) | collective-permute-done | bytes 524320 | tf_op jit(solution)/shard_map/ppermute | solution.py:347
  39.0 0.0 collective-permute-start.15
  39.0 0.5 %collective-permute-start.9 = (bf16[8,16,1280]{2,1,0:T(8,128)(2,1)S(1)}, bf16[8,16,1280]{2,1,0:T(8,128)(2,1)S(1)}, u32[]{:S(2)}, u32[]{:S(2)}) collective-permute-start(bf16[8,16,1280]{2,1,0:T(8,128)(2,1)S(1)} %shard_map.113.refs_0_), channel_id=1, source_target_pairs={{0,1},{1,0},{2,3},{3,2},{4,5},{5,4},{6,7},{7,6},{8,9},{9,8},{10,11... | collective-permute-start | bytes 983048 | tf_op jit(solution)/shard_map/ppermute | solution.py:347
  39.5 0.5 collective-permute-done.10.refs_2_
  40.0 0.0 collective-permute-start.11
  40.0 1.4 %collective-permute-done.9.refs_1_ = bf16[8,16,1280]{2,1,0:T(8,128)(2,1)S(1)} collective-permute-done((bf16[8,16,1280]{2,1,0:T(8,128)(2,1)S(1)}, bf16[8,16,1280]{2,1,0:T(8,128)(2,1)S(1)}, u32[]{:S(2)}, u32[]{:S(2)}) %collective-permute-start.9) | collective-permute-done | bytes 327712 | tf_op jit(solution)/shard_map/ppermute | solution.py:347
  41.4 0.0 collective-permute-done.12.refs_7_
  41.4 0.5 collective-permute-done.11.refs_3_
  41.9 1.1 %shard_map.114 = (bf16[2,192,1024]{2,1,0:T(8,128)(2,1)S(1)}, bf16[192,1024]{1,0:T(8,128)(2,1)S(1)}, bf16[192,256]{1,0:T(8,128)(2,1)S(1)}, bf16[192,192]{1,0:T(8,128)(2,1)S(1)}, f32[192,128]{1,0:T(8,128)S(1)}) custom-call(bf16[8,16,1280]{2,1,0:T(8,128)(2,1)S(1)} %shard_map.113.refs_0_, bf16[8,16,1280]{2,1,0:T(8,128)(2,1)S(1)} %collective-permute-done.9.refs_1_, ...), custom_call_target="tpu_custom_call" | custom-call | flops 805306368 | bytes 4194304 | tf_op jit(solution)/shard_map/pallas_call | solution.py:244
  43.0 0.0 collective-permute-done.14.refs_6_
  43.0 6.2 %shard_map.115 = (bf16[24,256]{1,0:T(8,128)(2,1)}, bf16[24,256]{1,0:T(8,128)(2,1)}, f32[256,1024]{1,0:T(8,128)}, f32[256,1024]{1,0:T(8,128)}, f32[256,1024]{1,0:T(8,128)}) custom-call(bf16[2,192,1024]{2,1,0:T(8,128)(2,1)S(1)} %get-tuple-element.35.both, bf16[192,1024]{1,0:T(8,128)(2,1)S(1)} %get-tuple-element.36.cot, ...), custom_call_target="tpu_custom_call" | custom-call | flops 2013265920 | bytes 8388608 | tf_op jit(solution)/shard_map/pallas_call | solution.py:264
  (15 shorter events, 0.1 us)
Async XLA Ops:
  0.6 17.5 %collective-permute-start = (bf16[256,1024]{1,0:T(8,128)(2,1)}, bf16[256,1024]{1,0:T(8,128)(2,1)S(1)}, u32[]{:S(2)}, u32[]{:S(2)}) collective-permute-start(bf16[256,1024]{1,0:T(8,128)(2,1)} %refs_4_.1), channel_id=1, source_target_pairs={{0,1},{1,0},{2,3},{3,2},{4,5},{5,4},{6,7},{7,6},{8,9},{9,8},{10,11... | collective-permute-start | bytes 1572872 | tf_op jit(solution)/shard_map/ppermute | solution.py:347
  1.1 17.0 %collective-permute-start.1 = (bf16[256,1024]{1,0:T(8,128)(2,1)}, bf16[256,1024]{1,0:T(8,128)(2,1)S(1)}, u32[]{:S(2)}, u32[]{:S(2)}) collective-permute-start(bf16[256,1024]{1,0:T(8,128)(2,1)} %refs_0_.1), channel_id=1, source_target_pairs={{0,1},{1,0},{2,3},{3,2},{4,5},{5,4},{6,7},{7,6},{8,9},{9,8},{10,11... | collective-permute-start | bytes 1572872 | tf_op jit(solution)/shard_map/ppermute | solution.py:347
  1.2 17.0 %collective-permute-start.2 = (bf16[256,1024]{1,0:T(8,128)(2,1)}, bf16[256,1024]{1,0:T(8,128)(2,1)S(1)}, u32[]{:S(2)}, u32[]{:S(2)}) collective-permute-start(bf16[256,1024]{1,0:T(8,128)(2,1)} %refs_1_.1), channel_id=1, source_target_pairs={{0,1},{1,0},{2,3},{3,2},{4,5},{5,4},{6,7},{7,6},{8,9},{9,8},{10,11... | collective-permute-start | bytes 1572872 | tf_op jit(solution)/shard_map/ppermute | solution.py:347
  2.8 15.4 %collective-permute-start.3 = (bf16[256,1024]{1,0:T(8,128)(2,1)S(1)}, bf16[256,1024]{1,0:T(8,128)(2,1)S(1)}, u32[]{:S(2)}, u32[]{:S(2)}) collective-permute-start(bf16[256,1024]{1,0:T(8,128)(2,1)S(1)} %broadcast_select_fusion), channel_id=1, source_target_pairs={{0,2},{1,3},{2,0},{3,1},{4,6},{5,7},{6,4},{7,5},{8,10},{9,11},{10,... | collective-permute-start | bytes 1572872 | tf_op jit(solution)/shard_map/ppermute | solution.py:347
  5.4 27.5 %collective-permute-start.8 = (bf16[256,1024]{1,0:T(8,128)(2,1)}, bf16[256,1024]{1,0:T(8,128)(2,1)S(1)}, u32[]{:S(2)}, u32[]{:S(2)}) collective-permute-start(bf16[256,1024]{1,0:T(8,128)(2,1)} %refs_4_.1), channel_id=1, source_target_pairs={{0,2},{1,3},{2,0},{3,1},{4,6},{5,7},{6,4},{7,5},{8,10},{9,11},{10,... | collective-permute-start | bytes 1572872 | tf_op jit(solution)/shard_map/ppermute | solution.py:347
  5.5 36.4 %copy-start.2 = (bf16[256,1024]{1,0:T(8,128)(2,1)S(1)}, bf16[256,1024]{1,0:T(8,128)(2,1)}, u32[]{:S(2)}) copy-start(bf16[256,1024]{1,0:T(8,128)(2,1)} %refs_4_.1) | copy-start | bytes 1572868
  5.5 37.5 %copy-start = (bf16[256,1024]{1,0:T(8,128)(2,1)S(1)}, bf16[256,1024]{1,0:T(8,128)(2,1)}, u32[]{:S(2)}) copy-start(bf16[256,1024]{1,0:T(8,128)(2,1)} %refs_0_.1) | copy-start | bytes 1572868
  5.5 37.5 %copy-start.1 = (bf16[256,1024]{1,0:T(8,128)(2,1)S(1)}, bf16[256,1024]{1,0:T(8,128)(2,1)}, u32[]{:S(2)}) copy-start(bf16[256,1024]{1,0:T(8,128)(2,1)} %refs_1_.1) | copy-start | bytes 1572868
  18.2 6.7 %collective-permute-start.6 = (bf16[1,16,1280]{2,1,0:T(8,128)(2,1)}, bf16[1,16,1280]{2,1,0:T(8,128)(2,1)S(1)}, u32[]{:S(2)}, u32[]{:S(2)}) collective-permute-start(bf16[1,16,1280]{2,1,0:T(8,128)(2,1)} %bitcast.2), channel_id=1, source_target_pairs={{0,24},{4,28},{8,16},{12,20},{16,8},{20,12},{24,0},{28,4},{1,25},{... | collective-permute-start | bytes 122888 | tf_op jit(solution)/shard_map/ppermute | solution.py:347
  22.3 5.1 %collective-permute-start.5 = (bf16[1,16,1280]{2,1,0:T(8,128)(2,1)}, bf16[1,16,1280]{2,1,0:T(8,128)(2,1)S(1)}, u32[]{:S(2)}, u32[]{:S(2)}) collective-permute-start(bf16[1,16,1280]{2,1,0:T(8,128)(2,1)} %bitcast.3), channel_id=1, source_target_pairs={{0,16},{4,20},{8,24},{12,28},{16,0},{20,4},{24,8},{28,12},{1,17},{... | collective-permute-start | bytes 122888 | tf_op jit(solution)/shard_map/ppermute | solution.py:347
  22.3 5.1 %collective-permute-start.4 = (bf16[1,16,1280]{2,1,0:T(8,128)(2,1)}, bf16[1,16,1280]{2,1,0:T(8,128)(2,1)S(1)}, u32[]{:S(2)}, u32[]{:S(2)}) collective-permute-start(bf16[1,16,1280]{2,1,0:T(8,128)(2,1)} %bitcast.4), channel_id=1, source_target_pairs={{0,8},{4,12},{8,0},{12,4},{16,24},{20,28},{24,16},{28,20},{1,9},{5... | collective-permute-start | bytes 122888 | tf_op jit(solution)/shard_map/ppermute | solution.py:347
  22.9 0.8 %copy-start.3 = (bf16[16,1280]{1,0:T(8,128)(2,1)S(1)}, bf16[16,1280]{1,0:T(8,128)(2,1)}, u32[]{:S(2)}) copy-start(bf16[16,1280]{1,0:T(8,128)(2,1)} %shard_map.110) | copy-start | bytes 122884
  27.4 11.6 %collective-permute-start.13 = (bf16[256,1024]{1,0:T(8,128)(2,1)S(1)}, bf16[256,1024]{1,0:T(8,128)(2,1)S(1)}, u32[]{:S(2)}, u32[]{:S(2)}) collective-permute-start(bf16[256,1024]{1,0:T(8,128)(2,1)S(1)} %collective-permute-done.3.refs_4_), channel_id=1, source_target_pairs={{0,8},{4,12},{8,0},{12,4},{16,24},{20,28},{24,16},{28,20},{1,9},{5... | collective-permute-start | bytes 1572872 | tf_op jit(solution)/shard_map/ppermute | solution.py:347
  27.4 5.4 %collective-permute-start.7 = (bf16[4,16,1280]{2,1,0:T(8,128)(2,1)S(1)}, bf16[4,16,1280]{2,1,0:T(8,128)(2,1)S(1)}, u32[]{:S(2)}, u32[]{:S(2)}) collective-permute-start(bf16[4,16,1280]{2,1,0:T(8,128)(2,1)S(1)} %shard_map.112.refs_0_), channel_id=1, source_target_pairs={{0,4},{4,0},{8,12},{12,8},{16,20},{20,16},{24,28},{28,24},{1,5},{5... | collective-permute-start | bytes 491528 | tf_op jit(solution)/shard_map/ppermute | solution.py:347
  32.9 7.1 %collective-permute-start.10 = (bf16[8,16,1280]{2,1,0:T(8,128)(2,1)S(1)}, bf16[8,16,1280]{2,1,0:T(8,128)(2,1)S(1)}, u32[]{:S(2)}, u32[]{:S(2)}) collective-permute-start(bf16[8,16,1280]{2,1,0:T(8,128)(2,1)S(1)} %shard_map.113.refs_0_), channel_id=1, source_target_pairs={{0,2},{1,3},{2,0},{3,1},{4,6},{5,7},{6,4},{7,5},{8,10},{9,11},{10,... | collective-permute-start | bytes 983048 | tf_op jit(solution)/shard_map/ppermute | solution.py:347
  34.4 7.0 %collective-permute-start.12 = (bf16[256,1024]{1,0:T(8,128)(2,1)S(1)}, bf16[256,1024]{1,0:T(8,128)(2,1)S(1)}, u32[]{:S(2)}, u32[]{:S(2)}) collective-permute-start(bf16[256,1024]{1,0:T(8,128)(2,1)S(1)} %collective-permute-done.8.refs_6_), channel_id=1, source_target_pairs={{0,1},{1,0},{2,3},{3,2},{4,5},{5,4},{6,7},{7,6},{8,9},{9,8},{10,11... | collective-permute-start | bytes 1572872 | tf_op jit(solution)/shard_map/ppermute | solution.py:347
  34.4 8.5 %collective-permute-start.14 = (bf16[256,1024]{1,0:T(8,128)(2,1)S(1)}, bf16[256,1024]{1,0:T(8,128)(2,1)S(1)}, u32[]{:S(2)}, u32[]{:S(2)}) collective-permute-start(bf16[256,1024]{1,0:T(8,128)(2,1)S(1)} %collective-permute-done.3.refs_4_), channel_id=1, source_target_pairs={{0,1},{1,0},{2,3},{3,2},{4,5},{5,4},{6,7},{7,6},{8,9},{9,8},{10,11... | collective-permute-start | bytes 1572872 | tf_op jit(solution)/shard_map/ppermute | solution.py:347
  39.0 3.9 %collective-permute-start.15 = (bf16[256,1024]{1,0:T(8,128)(2,1)S(1)}, bf16[256,1024]{1,0:T(8,128)(2,1)S(1)}, u32[]{:S(2)}, u32[]{:S(2)}) collective-permute-start(bf16[256,1024]{1,0:T(8,128)(2,1)S(1)} %collective-permute-done.13.refs_5_), channel_id=1, source_target_pairs={{0,1},{1,0},{2,3},{3,2},{4,5},{5,4},{6,7},{7,6},{8,9},{9,8},{10,11... | collective-permute-start | bytes 1572872 | tf_op jit(solution)/shard_map/ppermute | solution.py:347
  39.0 2.4 %collective-permute-start.9 = (bf16[8,16,1280]{2,1,0:T(8,128)(2,1)S(1)}, bf16[8,16,1280]{2,1,0:T(8,128)(2,1)S(1)}, u32[]{:S(2)}, u32[]{:S(2)}) collective-permute-start(bf16[8,16,1280]{2,1,0:T(8,128)(2,1)S(1)} %shard_map.113.refs_0_), channel_id=1, source_target_pairs={{0,1},{1,0},{2,3},{3,2},{4,5},{5,4},{6,7},{7,6},{8,9},{9,8},{10,11... | collective-permute-start | bytes 983048 | tf_op jit(solution)/shard_map/ppermute | solution.py:347
  40.0 1.9 %collective-permute-start.11 = (bf16[8,16,1280]{2,1,0:T(8,128)(2,1)S(1)}, bf16[8,16,1280]{2,1,0:T(8,128)(2,1)S(1)}, u32[]{:S(2)}, u32[]{:S(2)}) collective-permute-start(bf16[8,16,1280]{2,1,0:T(8,128)(2,1)S(1)} %collective-permute-done.10.refs_2_), channel_id=1, source_target_pairs={{0,1},{1,0},{2,3},{3,2},{4,5},{5,4},{6,7},{7,6},{8,9},{9,8},{10,11... | collective-permute-start | bytes 983048 | tf_op jit(solution)/shard_map/ppermute | solution.py:347

commit v13 on v12

--- a/solution.py
+++ b/solution.py
@@ -10,8 +10,7 @@
 HD = 64
 BF = jnp.bfloat16
 F32 = jnp.float32
-NODES_STEP = 6
-WIDE_LIMIT = 256
+NODES_STEP = 8
 IDS_COLS = 128
 IDS_AT = 32
 TOP = 16
@@ -32,19 +31,23 @@
     return jnp.dot(a, b, preferred_element_type=F32)
 
 
-def attend(q, k, v, heads):
+def attend(q, k, v):
     seq, cols = q.shape
-    lane = lax.broadcasted_iota(jnp.int32, (seq, cols), 1) // HD
-    zero = jnp.zeros((seq, cols), BF)
-    spread = jnp.concatenate([jnp.where(lane == h, k, zero) for h in range(heads)], axis=0)
-    s = dot_t(spread, q).reshape(heads, seq, seq)
-    e = jnp.exp2((s - jnp.max(s, axis=1, keepdims=True)) * (HD**-0.5 * LOG2E))
-    p = (e * (1.0 / jnp.sum(e, axis=1, keepdims=True))).astype(BF)
-    weight = jnp.sum(p.astype(F32), axis=2, keepdims=True)
-    left = lax.broadcasted_iota(jnp.int32, (seq, 2 * HD), 1) < HD
-    pairs = [jnp.where(left, weight[h], weight[h + 1]) for h in range(0, heads, 2)]
-    context = jnp.concatenate(pairs, axis=1) * v.astype(F32)
-    return jnp.sum(context, axis=0, keepdims=True) * (1.0 / seq)
+    pair = 2 * HD
+    left = lax.broadcasted_iota(jnp.int32, (seq, pair), 1) < HD
+    zero = jnp.zeros((seq, pair), BF)
+    out = []
+    for at in range(0, cols, pair):
+        both = q[:, at : at + pair]
+        spread = jnp.concatenate([jnp.where(left, both, zero), jnp.where(left, zero, both)], axis=0)
+        s = dot_t(k[:, at : at + pair], spread)
+        e = jnp.exp2((s - jnp.max(s, axis=0, keepdims=True)) * (HD**-0.5 * LOG2E))
+        p = (e * (1.0 / jnp.sum(e, axis=0, keepdims=True))).astype(BF).astype(F32)
+        first = jnp.sum(p[:, :seq], axis=1, keepdims=True)
+        second = jnp.sum(p[:, seq:], axis=1, keepdims=True)
+        context = jnp.where(left, first, second) * v[:, at : at + pair].astype(F32)
+        out.append(jnp.sum(context, axis=0, keepdims=True) * (1.0 / seq))
+    return jnp.concatenate(out, axis=1)
 
 
 def attention_kernel(heads, x_ref, w_ref, cot_ref, ids_ref, out_ref, wp, acc_p, acc_m):
@@ -68,7 +71,7 @@
     for n in range(nodes):
         at = slice(n * seq, (n + 1) * seq)
         row = pl.ds(step * nodes + n, 1)
-        acc_p[row, :] = attend(*(qkv[at, i * cols : (i + 1) * cols] for i in range(3)), heads)
+        acc_p[row, :] = attend(*(qkv[at, i * cols : (i + 1) * cols] for i in range(3)))
         mean = jnp.sum(x_ref[n, :, own].astype(F32), axis=0, keepdims=True)
         acc_m[row, :] = mean * (1.0 / seq)
 
@@ -148,16 +151,27 @@
 
 
 def embed_kernel(order, fan, node_dev, *refs):
-    parts = 4
-    got, blocks, refs = refs[:parts], refs[parts : 2 * parts], refs[2 * parts :]
+    parts, near, far, diagonal = 4, refs[0:2], refs[2:4], refs[4:6]
+    blocks, refs = refs[6 : 6 + parts], refs[6 + parts :]
     both, cot, pooled_ref, counts_ref, share_ref, mean = refs
     dp = lax.axis_index("dp")
-    groups = got[0].shape[0]
+    some = near[0].shape[0]
+    groups = 2 * some
     nodes = groups * node_dev
     cols = blocks[0].shape[0]
 
+    def payload(r):
+        core = r % 2
+        if r < 2:
+            pieces = [near[core][...], far[core][:some]]
+        else:
+            pieces = [far[core][some:], diagonal[core][...]]
+        return jnp.concatenate(pieces, axis=0)
+
+    got = [payload(r) for r in range(parts)]
+
     def part(r, i):
-        return unpack(got[r][...], cols, i).reshape(nodes, cols)
+        return unpack(got[r], cols, i).reshape(nodes, cols)
 
     packed = got[0][:, :, got[0].shape[2] - IDS_COLS :].astype(F32)
     ids = jnp.concatenate(
@@ -237,9 +251,9 @@
 
 
 def graph(order, fan, node_dev, got, weights):
-    parts = len(got)
+    parts = len(weights)
     cols, width = weights[0][0].shape
-    nodes = got[0].shape[0] * node_dev
+    nodes = len(order) * node_dev
     vmem = pl.BlockSpec(memory_space=pltpu.VMEM)
     known = pl.pallas_call(
         functools.partial(embed_kernel, order, fan, node_dev),
@@ -250,7 +264,7 @@
             jax.ShapeDtypeStruct((nodes, nodes), BF),
             jax.ShapeDtypeStruct((nodes, 128), F32),
         ),
-        in_specs=[vmem] * (2 * parts),
+        in_specs=[vmem] * (len(got) + parts),
         out_specs=(vmem,) * 5,
         scratch_shapes=[pltpu.VMEM((nodes, width), F32)],
         compiler_params=pltpu.CompilerParams(vmem_limit_bytes=24 * MIB),
@@ -347,45 +361,80 @@
     return lax.ppermute(x, axis, [(i, i ^ bit) for i in range(lax.axis_size(axis))])
 
 
-def gather_dp(block, later):
-    size = lax.axis_size("dp")
-    if size == 8:
-        far = [hop(block, "dp", i) for i in (2, 4, 6)]
-        mine = join(block)
-        mine, far, later = lax.optimization_barrier((mine, far, later))
-        block = join(mine, *far)
-        order, bit = [0, 2, 4, 6], 1
-    else:
-        order, bit = [0], size // 2
+def cross_kernel(y, x, y_part, x_part, both):
+    half = y.shape[0] // 2
+    y_part[...] = y[:half]
+    x_part[...] = x[half:]
+    both[: 2 * half] = y[...]
+    both[2 * half :] = x[...]
+
+
+def cross(y, x):
+    count, rows, cols = y.shape
+    vmem = pl.BlockSpec(memory_space=pltpu.VMEM)
+    half = jax.ShapeDtypeStruct((count // 2, rows, cols), BF)
+    return pl.pallas_call(
+        cross_kernel,
+        out_shape=(half, half, jax.ShapeDtypeStruct((2 * count, rows, cols), BF)),
+        in_specs=[vmem] * 2,
+        out_specs=(vmem,) * 3,
+        compiler_params=pltpu.CompilerParams(vmem_limit_bytes=8 * MIB),
+    )(y, x)
+
+
+def core(x):
+    return hop(x, "mp", 1)
+
+
+def gather(block, x_half, x_out):
+    z = [hop(block, "dp", i) for i in (2, 4, 6)]
+    mine = join(block)
+    mine, z, x_half = lax.optimization_barrier((mine, z, x_half))
+    block = join(mine, *z)
+    order = [0, 2, 4, 6, 1, 3, 5, 7]
+    z_half = hop(x_half, "dp", 2)
+    y, x, same = hop(block, "dp", 1), hop(block, "mp", 2), core(block)
+    y_part, x_part, far = cross(y, x)
+    y_part, x_out = lax.optimization_barrier((y_part, x_out))
+    y_part, x_part = hop(y_part, "mp", 2), hop(x_part, "dp", 1)
+    far = join(far)
+    far, x_half, x_out = lax.optimization_barrier((far, x_half, x_out))
+    core_far = core(far)
+    y_part, x_part, core_far, same = lax.optimization_barrier((y_part, x_part, core_far, same))
+    diagonal = join(y_part, x_part)
+    z_half, core_diagonal = lax.optimization_barrier((z_half, core(diagonal)))
+    got = (block, same, far, core_far, diagonal, core_diagonal)
+    return got, order, (x_out, x_half, z_half), (core(x_out), core(x_half), core(z_half))
+
+
+def gather_wide(block):
+    order, bit = [0], lax.axis_size("dp") // 2
     while bit:
         block = join(block, hop(block, "dp", bit))
         order = order + [i ^ bit for i in order]
         bit //= 2
-    return block, order, later
+    across = hop(block, "mp", 2)
+    return (block, hop(block, "mp", 1), across, hop(across, "mp", 1)), order
 
 
 def per_device(texts, w_qkv, w_out, w_self, w_neigh, neighbours, cotangent):
     node_dev, fan = neighbours.shape
-    nodes = node_dev * lax.axis_size("dp")
     own = (w_out, w_self, w_neigh)
     even = (lax.axis_index("dp") // 2) % 2 == 0
     picked, w_out = lax.optimization_barrier((jnp.where(even, w_self, w_neigh), w_out))
     x_half = hop(picked, "mp", 2)
     x_out = hop(w_out, "mp", 2)
-    here = tuple(hop(a, "mp", 1) for a in own)
+    here = tuple(core(a) for a in own)
 
     sent = attention(texts, w_qkv, cotangent, neighbours.T)[None]
     sent, here, x_half = lax.optimization_barrier((sent, here, x_half))
-    sent, order, x_half = gather_dp(sent, x_half)
-    sent, x_out = lax.optimization_barrier((sent, x_out))
-    z_half = hop(x_half, "dp", 2)
-    across = (x_out, x_half, z_half)
-    there = tuple(hop(a, "mp", 1) for a in across)
-
-    got_across = hop(sent, "mp", 2)
-    got = (sent, hop(sent, "mp", 1), got_across, hop(got_across, "mp", 1))
-    body = graph if nodes <= WIDE_LIMIT else graph_wide
-    return body(order, fan, node_dev, got, (own, here, across, there))
+    if lax.axis_size("dp") == 8:
+        got, order, across, there = gather(sent, x_half, x_out)
+        return graph(order, fan, node_dev, got, (own, here, across, there))
+    got, order = gather_wide(sent)
+    across = (x_out, x_half, hop(x_half, "dp", 2))
+    there = tuple(core(a) for a in across)
+    return graph_wide(order, fan, node_dev, got, (own, here, across, there))
 
 
 def solution(mesh):

time: 49.5 us -> 50.1 us (1.012)
  starting transfers between devices: 12.7 us -> 14.8 us
  waiting for transfers between devices: 15.1 us -> 14 us
    ppermute x16 -> x19, starting transfers between devices: 12.7 us -> 14.8 us  [hop(): lax.ppermute(x, axis, [(i, i ^ bit) for i in range(lax.axis_size(axis))])]
    ppermute x16 -> x19, waiting for transfers between devices: 15.1 us -> 14 us  [hop(): lax.ppermute(x, axis, [(i, i ^ bit) for i in range(lax.axis_size(axis))])]
  transfers between devices with their start and end apart: 16 -> 19, of which waited for: 8 -> 10; matrix products, arithmetic and copies ran while one was open for 2% -> 2% of each run, Pallas kernels for 26% -> 24%
where the time goes in v13:
time: 50.1 us; the launch traced here: 49.9 us
  Pallas kernels  18.4 us (37%)
  starting transfers between devices  14.8 us (30%)
  waiting for transfers between devices  14 us (28%)
  other arithmetic  1.1 us (2%)
  local copies, waits for them, and re-layouts  0.82 us (2%)
  between operations  0.72 us (1%)
    ppermute x19, starting transfers between devices, hop(): lax.ppermute(x, axis, [(i, i ^ bit) for i in range(lax.axis_size(axis))])  14.8 us
    ppermute x19, waiting for transfers between devices, hop(): lax.ppermute(x, axis, [(i, i ^ bit) for i in range(lax.axis_size(axis))])  14 us
    pallas_call x1, Pallas kernels, attention(): pl.pallas_call(functools.partial(attention_kernel, heads), out_shape=jax....  11.1 us
    pallas_call x1, Pallas kernels, graph(): pl.pallas_call(functools.partial(graph_kernel, node_dev), out_shape=(slab...  6.21 us
    select_n x1, other arithmetic, per_device(): jnp.where(even, w_self, w_neigh)  1.1 us
    pallas_call x1, Pallas kernels, graph(): pl.pallas_call(functools.partial(embed_kernel, order, fan, node_dev), out...  1.03 us
  transfers between devices with their start and end apart: 19, of which 10 were waited for; matrix products, arithmetic and copies ran while one was open for 2% of the time, Pallas kernels for 24%

profile of v13, /device:TPU:0, one launch (start us, length us, event | category | flops | bytes accessed | tf_op | source)
XLA Modules:
  0.0 49.9 jit_solution(3697563523170533495)
XLA Ops:
  0.6 0.5 %collective-permute-start = (bf16[256,1024]{1,0:T(8,128)(2,1)}, bf16[256,1024]{1,0:T(8,128)(2,1)S(1)}, u32[]{:S(2)}, u32[]{:S(2)}) collective-permute-start(bf16[256,1024]{1,0:T(8,128)(2,1)} %refs_6_.1), channel_id=1, source_target_pairs={{0,1},{1,0},{2,3},{3,2},{4,5},{5,4},{6,7},{7,6},{8,9},{9,8},{10,11... | collective-permute-start | bytes 1572872 | tf_op jit(solution)/shard_map/ppermute | solution.py:361
  1.1 0.1 collective-permute-start.1
  1.2 0.4 collective-permute-start.2
  1.7 1.1 %broadcast_select_fusion = bf16[256,1024]{1,0:T(8,128)(2,1)S(1)} fusion(bf16[256,1024]{1,0:T(8,128)(2,1)} %refs_0_.1, bf16[256,1024]{1,0:T(8,128)(2,1)} %refs_1_.1, pred[]{:T(512)S(6)} %eq.5), kind=kLoop, calls=%fused_computation | loop fusion | flops 262144 | bytes 1572865 | tf_op jit(solution)/shard_map/jit(_where)/select_n | solution.py:424
  2.8 2.6 %collective-permute-start.3 = (bf16[256,1024]{1,0:T(8,128)(2,1)S(1)}, bf16[256,1024]{1,0:T(8,128)(2,1)S(1)}, u32[]{:S(2)}, u32[]{:S(2)}) collective-permute-start(bf16[256,1024]{1,0:T(8,128)(2,1)S(1)} %broadcast_select_fusion), channel_id=1, source_target_pairs={{0,2},{1,3},{2,0},{3,1},{4,6},{5,7},{6,4},{7,5},{8,10},{9,11},{10,... | collective-permute-start | bytes 1572872 | tf_op jit(solution)/shard_map/ppermute | solution.py:361
  5.4 0.1 collective-permute-start.9
  5.5 11.1 %shard_map.110 = bf16[16,1280]{1,0:T(8,128)(2,1)} custom-call(bf16[24,128,1024]{2,1,0:T(8,128)(2,1)} %x_ref.1, bf16[1024,768]{1,0:T(8,128)(2,1)} %w_ref.1, bf16[24,256]{1,0:T(8,128)(2,1)} %cot_ref.1, s32[16,24]{1,0:T(8,128)} %bitcast.6), custom_call_target="tpu_custom_call" | custom-call | flops 5637144576 | bytes 7864320 | tf_op jit(solution)/shard_map/pallas_call | solution.py:115
  16.6 1.6 %collective-permute-done.3.refs_4_ = bf16[256,1024]{1,0:T(8,128)(2,1)S(1)} collective-permute-done((bf16[256,1024]{1,0:T(8,128)(2,1)S(1)}, bf16[256,1024]{1,0:T(8,128)(2,1)S(1)}, u32[]{:S(2)}, u32[]{:S(2)}) %collective-permute-start.3) | collective-permute-done | bytes 524320 | tf_op jit(solution)/shard_map/ppermute | solution.py:361
  18.2 0.0 collective-permute-done.refs_7_
  18.2 4.1 %collective-permute-start.6 = (bf16[1,16,1280]{2,1,0:T(8,128)(2,1)}, bf16[1,16,1280]{2,1,0:T(8,128)(2,1)S(1)}, u32[]{:S(2)}, u32[]{:S(2)}) collective-permute-start(bf16[1,16,1280]{2,1,0:T(8,128)(2,1)} %bitcast.2), channel_id=1, source_target_pairs={{0,24},{4,28},{8,16},{12,20},{16,8},{20,12},{24,0},{28,4},{1,25},{... | collective-permute-start | bytes 122888 | tf_op jit(solution)/shard_map/ppermute | solution.py:361
  22.3 0.6 %collective-permute-start.4 = (bf16[1,16,1280]{2,1,0:T(8,128)(2,1)}, bf16[1,16,1280]{2,1,0:T(8,128)(2,1)S(1)}, u32[]{:S(2)}, u32[]{:S(2)}) collective-permute-start(bf16[1,16,1280]{2,1,0:T(8,128)(2,1)} %bitcast.4), channel_id=1, source_target_pairs={{0,8},{4,12},{8,0},{12,4},{16,24},{20,28},{24,16},{28,20},{1,9},{5... | collective-permute-start | bytes 122888 | tf_op jit(solution)/shard_map/ppermute | solution.py:361
  22.9 0.8 %copy-done.3 = bf16[16,1280]{1,0:T(8,128)(2,1)S(1)} copy-done((bf16[16,1280]{1,0:T(8,128)(2,1)S(1)}, bf16[16,1280]{1,0:T(8,128)(2,1)}, u32[]{:S(2)}) %copy-start.3) | copy-done | bytes 40984
  23.8 1.2 %collective-permute-done.6.refs_3_ = bf16[1,16,1280]{2,1,0:T(8,128)(2,1)S(1)} collective-permute-done((bf16[1,16,1280]{2,1,0:T(8,128)(2,1)}, bf16[1,16,1280]{2,1,0:T(8,128)(2,1)S(1)}, u32[]{:S(2)}, u32[]{:S(2)}) %collective-permute-start.6) | collective-permute-done | bytes 40992 | tf_op jit(solution)/shard_map/ppermute | solution.py:361
  24.9 2.5 %collective-permute-done.5.refs_2_ = bf16[1,16,1280]{2,1,0:T(8,128)(2,1)S(1)} collective-permute-done((bf16[1,16,1280]{2,1,0:T(8,128)(2,1)}, bf16[1,16,1280]{2,1,0:T(8,128)(2,1)S(1)}, u32[]{:S(2)}, u32[]{:S(2)}) %collective-permute-start.5) | collective-permute-done | bytes 40992 | tf_op jit(solution)/shard_map/ppermute | solution.py:361
  27.4 1.6 %collective-permute-start.8 = (bf16[4,16,1280]{2,1,0:T(8,128)(2,1)S(1)}, bf16[4,16,1280]{2,1,0:T(8,128)(2,1)S(1)}, u32[]{:S(2)}, u32[]{:S(2)}) collective-permute-start(bf16[4,16,1280]{2,1,0:T(8,128)(2,1)S(1)} %shard_map.112.refs_0_), channel_id=1, source_target_pairs={{0,2},{1,3},{2,0},{3,1},{4,6},{5,7},{6,4},{7,5},{8,10},{9,11},{10,... | collective-permute-start | bytes 491528 | tf_op jit(solution)/shard_map/ppermute | solution.py:361
  29.0 1.5 %collective-permute-start.7 = (bf16[4,16,1280]{2,1,0:T(8,128)(2,1)S(1)}, bf16[4,16,1280]{2,1,0:T(8,128)(2,1)S(1)}, u32[]{:S(2)}, u32[]{:S(2)}) collective-permute-start(bf16[4,16,1280]{2,1,0:T(8,128)(2,1)S(1)} %shard_map.112.refs_0_), channel_id=1, source_target_pairs={{0,4},{4,0},{8,12},{12,8},{16,20},{20,16},{24,28},{28,24},{1,5},{5... | collective-permute-start | bytes 491528 | tf_op jit(solution)/shard_map/ppermute | solution.py:361
  30.5 2.3 %collective-permute-done.8.x = bf16[4,16,1280]{2,1,0:T(8,128)(2,1)S(1)} collective-permute-done((bf16[4,16,1280]{2,1,0:T(8,128)(2,1)S(1)}, bf16[4,16,1280]{2,1,0:T(8,128)(2,1)S(1)}, u32[]{:S(2)}, u32[]{:S(2)}) %collective-permute-start.8) | collective-permute-done | bytes 163872 | tf_op jit(solution)/shard_map/ppermute | solution.py:361
  32.8 1.5 %collective-permute-done.7.y = bf16[4,16,1280]{2,1,0:T(8,128)(2,1)S(1)} collective-permute-done((bf16[4,16,1280]{2,1,0:T(8,128)(2,1)S(1)}, bf16[4,16,1280]{2,1,0:T(8,128)(2,1)S(1)}, u32[]{:S(2)}, u32[]{:S(2)}) %collective-permute-start.7) | collective-permute-done | bytes 163872 | tf_op jit(solution)/shard_map/ppermute | solution.py:361
  34.4 0.1 collective-permute-start.12
  34.5 0.5 collective-permute-start.13
  35.0 0.5 %collective-permute-start.10 = (bf16[2,16,1280]{2,1,0:T(8,128)(2,1)S(1)}, bf16[2,16,1280]{2,1,0:T(8,128)(2,1)S(1)}, u32[]{:S(2)}, u32[]{:S(2)}) collective-permute-start(bf16[2,16,1280]{2,1,0:T(8,128)(2,1)S(1)} %get-tuple-element.45), channel_id=1, source_target_pairs={{0,2},{1,3},{2,0},{3,1},{4,6},{5,7},{6,4},{7,5},{8,10},{9,11},{10,... | collective-permute-start | bytes 245768 | tf_op jit(solution)/shard_map/ppermute | solution.py:361
  35.5 1.5 %collective-permute-start.11 = (bf16[2,16,1280]{2,1,0:T(8,128)(2,1)S(1)}, bf16[2,16,1280]{2,1,0:T(8,128)(2,1)S(1)}, u32[]{:S(2)}, u32[]{:S(2)}) collective-permute-start(bf16[2,16,1280]{2,1,0:T(8,128)(2,1)S(1)} %get-tuple-element.46), channel_id=1, source_target_pairs={{0,4},{4,0},{8,12},{12,8},{16,20},{20,16},{24,28},{28,24},{1,5},{5... | collective-permute-start | bytes 245768 | tf_op jit(solution)/shard_map/ppermute | solution.py:361
  37.0 2.4 %collective-permute-done.10.refs_0_ = bf16[2,16,1280]{2,1,0:T(8,128)(2,1)S(1)} collective-permute-done((bf16[2,16,1280]{2,1,0:T(8,128)(2,1)S(1)}, bf16[2,16,1280]{2,1,0:T(8,128)(2,1)S(1)}, u32[]{:S(2)}, u32[]{:S(2)}) %collective-permute-start.10) | collective-permute-done | bytes 81952 | tf_op jit(solution)/shard_map/ppermute | solution.py:361
  39.4 0.5 %collective-permute-done.11.refs_1_ = bf16[2,16,1280]{2,1,0:T(8,128)(2,1)S(1)} collective-permute-done((bf16[2,16,1280]{2,1,0:T(8,128)(2,1)S(1)}, bf16[2,16,1280]{2,1,0:T(8,128)(2,1)S(1)}, u32[]{:S(2)}, u32[]{:S(2)}) %collective-permute-start.11) | collective-permute-done | bytes 81952 | tf_op jit(solution)/shard_map/ppermute | solution.py:361
  40.0 0.1 collective-permute-start.15
  40.0 0.5 collective-permute-start.16
  40.5 0.1 collective-permute-start.17
  40.6 0.9 %collective-permute-done.14.refs_5_ = bf16[256,1024]{1,0:T(8,128)(2,1)S(1)} collective-permute-done((bf16[256,1024]{1,0:T(8,128)(2,1)S(1)}, bf16[256,1024]{1,0:T(8,128)(2,1)S(1)}, u32[]{:S(2)}, u32[]{:S(2)}) %collective-permute-start.14) | collective-permute-done | bytes 524320 | tf_op jit(solution)/shard_map/ppermute | solution.py:361
  41.6 0.6 %collective-permute-done.16.refs_9_ = bf16[256,1024]{1,0:T(8,128)(2,1)S(1)} collective-permute-done((bf16[256,1024]{1,0:T(8,128)(2,1)S(1)}, bf16[256,1024]{1,0:T(8,128)(2,1)S(1)}, u32[]{:S(2)}, u32[]{:S(2)}) %collective-permute-start.16) | collective-permute-done | bytes 524320 | tf_op jit(solution)/shard_map/ppermute | solution.py:361
  42.2 1.0 %shard_map.116 = (bf16[2,192,1024]{2,1,0:T(8,128)(2,1)S(1)}, bf16[192,1024]{1,0:T(8,128)(2,1)S(1)}, bf16[192,256]{1,0:T(8,128)(2,1)S(1)}, bf16[192,192]{1,0:T(8,128)(2,1)S(1)}, f32[192,128]{1,0:T(8,128)S(1)}) custom-call(bf16[4,16,1280]{2,1,0:T(8,128)(2,1)S(1)} %shard_map.112.refs_0_, bf16[4,16,1280]{2,1,0:T(8,128)(2,1)S(1)} %collective-permute-done.13.refs_1_, ...), custom_call_target="tpu_custom_call" | custom-call | flops 805306368 | bytes 4194304 | tf_op jit(solution)/shard_map/pallas_call | solution.py:258
  43.2 0.4 collective-permute-done.18.refs_7_
  43.7 6.2 %shard_map.117 = (bf16[24,256]{1,0:T(8,128)(2,1)}, bf16[24,256]{1,0:T(8,128)(2,1)}, f32[256,1024]{1,0:T(8,128)}, f32[256,1024]{1,0:T(8,128)}, f32[256,1024]{1,0:T(8,128)}) custom-call(bf16[2,192,1024]{2,1,0:T(8,128)(2,1)S(1)} %get-tuple-element.58.both, bf16[192,1024]{1,0:T(8,128)(2,1)S(1)} %get-tuple-element.59.cot, ...), custom_call_target="tpu_custom_call" | custom-call | flops 2013265920 | bytes 8388608 | tf_op jit(solution)/shard_map/pallas_call | solution.py:278
  (23 shorter events, 0.1 us)
Async XLA Ops:
  0.6 17.5 %collective-permute-start = (bf16[256,1024]{1,0:T(8,128)(2,1)}, bf16[256,1024]{1,0:T(8,128)(2,1)S(1)}, u32[]{:S(2)}, u32[]{:S(2)}) collective-permute-start(bf16[256,1024]{1,0:T(8,128)(2,1)} %refs_6_.1), channel_id=1, source_target_pairs={{0,1},{1,0},{2,3},{3,2},{4,5},{5,4},{6,7},{7,6},{8,9},{9,8},{10,11... | collective-permute-start | bytes 1572872 | tf_op jit(solution)/shard_map/ppermute | solution.py:361
  1.1 17.0 %collective-permute-start.1 = (bf16[256,1024]{1,0:T(8,128)(2,1)}, bf16[256,1024]{1,0:T(8,128)(2,1)S(1)}, u32[]{:S(2)}, u32[]{:S(2)}) collective-permute-start(bf16[256,1024]{1,0:T(8,128)(2,1)} %refs_0_.1), channel_id=1, source_target_pairs={{0,1},{1,0},{2,3},{3,2},{4,5},{5,4},{6,7},{7,6},{8,9},{9,8},{10,11... | collective-permute-start | bytes 1572872 | tf_op jit(solution)/shard_map/ppermute | solution.py:361
  1.2 17.0 %collective-permute-start.2 = (bf16[256,1024]{1,0:T(8,128)(2,1)}, bf16[256,1024]{1,0:T(8,128)(2,1)S(1)}, u32[]{:S(2)}, u32[]{:S(2)}) collective-permute-start(bf16[256,1024]{1,0:T(8,128)(2,1)} %refs_1_.1), channel_id=1, source_target_pairs={{0,1},{1,0},{2,3},{3,2},{4,5},{5,4},{6,7},{7,6},{8,9},{9,8},{10,11... | collective-permute-start | bytes 1572872 | tf_op jit(solution)/shard_map/ppermute | solution.py:361
  2.8 15.4 %collective-permute-start.3 = (bf16[256,1024]{1,0:T(8,128)(2,1)S(1)}, bf16[256,1024]{1,0:T(8,128)(2,1)S(1)}, u32[]{:S(2)}, u32[]{:S(2)}) collective-permute-start(bf16[256,1024]{1,0:T(8,128)(2,1)S(1)} %broadcast_select_fusion), channel_id=1, source_target_pairs={{0,2},{1,3},{2,0},{3,1},{4,6},{5,7},{6,4},{7,5},{8,10},{9,11},{10,... | collective-permute-start | bytes 1572872 | tf_op jit(solution)/shard_map/ppermute | solution.py:361
  5.4 29.0 %collective-permute-start.9 = (bf16[256,1024]{1,0:T(8,128)(2,1)}, bf16[256,1024]{1,0:T(8,128)(2,1)S(1)}, u32[]{:S(2)}, u32[]{:S(2)}) collective-permute-start(bf16[256,1024]{1,0:T(8,128)(2,1)} %refs_6_.1), channel_id=1, source_target_pairs={{0,2},{1,3},{2,0},{3,1},{4,6},{5,7},{6,4},{7,5},{8,10},{9,11},{10,... | collective-permute-start | bytes 1572872 | tf_op jit(solution)/shard_map/ppermute | solution.py:361
  5.5 36.7 %copy-start.2 = (bf16[256,1024]{1,0:T(8,128)(2,1)S(1)}, bf16[256,1024]{1,0:T(8,128)(2,1)}, u32[]{:S(2)}) copy-start(bf16[256,1024]{1,0:T(8,128)(2,1)} %refs_6_.1) | copy-start | bytes 1572868
  5.5 38.2 %copy-start = (bf16[256,1024]{1,0:T(8,128)(2,1)S(1)}, bf16[256,1024]{1,0:T(8,128)(2,1)}, u32[]{:S(2)}) copy-start(bf16[256,1024]{1,0:T(8,128)(2,1)} %refs_0_.1) | copy-start | bytes 1572868
  5.5 38.2 %copy-start.1 = (bf16[256,1024]{1,0:T(8,128)(2,1)S(1)}, bf16[256,1024]{1,0:T(8,128)(2,1)}, u32[]{:S(2)}) copy-start(bf16[256,1024]{1,0:T(8,128)(2,1)} %refs_1_.1) | copy-start | bytes 1572868
  18.2 6.7 %collective-permute-start.6 = (bf16[1,16,1280]{2,1,0:T(8,128)(2,1)}, bf16[1,16,1280]{2,1,0:T(8,128)(2,1)S(1)}, u32[]{:S(2)}, u32[]{:S(2)}) collective-permute-start(bf16[1,16,1280]{2,1,0:T(8,128)(2,1)} %bitcast.2), channel_id=1, source_target_pairs={{0,24},{4,28},{8,16},{12,20},{16,8},{20,12},{24,0},{28,4},{1,25},{... | collective-permute-start | bytes 122888 | tf_op jit(solution)/shard_map/ppermute | solution.py:361
  22.3 5.1 %collective-permute-start.5 = (bf16[1,16,1280]{2,1,0:T(8,128)(2,1)}, bf16[1,16,1280]{2,1,0:T(8,128)(2,1)S(1)}, u32[]{:S(2)}, u32[]{:S(2)}) collective-permute-start(bf16[1,16,1280]{2,1,0:T(8,128)(2,1)} %bitcast.3), channel_id=1, source_target_pairs={{0,16},{4,20},{8,24},{12,28},{16,0},{20,4},{24,8},{28,12},{1,17},{... | collective-permute-start | bytes 122888 | tf_op jit(solution)/shard_map/ppermute | solution.py:361
  22.3 5.1 %collective-permute-start.4 = (bf16[1,16,1280]{2,1,0:T(8,128)(2,1)}, bf16[1,16,1280]{2,1,0:T(8,128)(2,1)S(1)}, u32[]{:S(2)}, u32[]{:S(2)}) collective-permute-start(bf16[1,16,1280]{2,1,0:T(8,128)(2,1)} %bitcast.4), channel_id=1, source_target_pairs={{0,8},{4,12},{8,0},{12,4},{16,24},{20,28},{24,16},{28,20},{1,9},{5... | collective-permute-start | bytes 122888 | tf_op jit(solution)/shard_map/ppermute | solution.py:361
  22.9 0.8 %copy-start.3 = (bf16[16,1280]{1,0:T(8,128)(2,1)S(1)}, bf16[16,1280]{1,0:T(8,128)(2,1)}, u32[]{:S(2)}) copy-start(bf16[16,1280]{1,0:T(8,128)(2,1)} %shard_map.110) | copy-start | bytes 122884
  27.4 5.4 %collective-permute-start.8 = (bf16[4,16,1280]{2,1,0:T(8,128)(2,1)S(1)}, bf16[4,16,1280]{2,1,0:T(8,128)(2,1)S(1)}, u32[]{:S(2)}, u32[]{:S(2)}) collective-permute-start(bf16[4,16,1280]{2,1,0:T(8,128)(2,1)S(1)} %shard_map.112.refs_0_), channel_id=1, source_target_pairs={{0,2},{1,3},{2,0},{3,1},{4,6},{5,7},{6,4},{7,5},{8,10},{9,11},{10,... | collective-permute-start | bytes 491528 | tf_op jit(solution)/shard_map/ppermute | solution.py:361
  29.0 5.3 %collective-permute-start.7 = (bf16[4,16,1280]{2,1,0:T(8,128)(2,1)S(1)}, bf16[4,16,1280]{2,1,0:T(8,128)(2,1)S(1)}, u32[]{:S(2)}, u32[]{:S(2)}) collective-permute-start(bf16[4,16,1280]{2,1,0:T(8,128)(2,1)S(1)} %shard_map.112.refs_0_), channel_id=1, source_target_pairs={{0,4},{4,0},{8,12},{12,8},{16,20},{20,16},{24,28},{28,24},{1,5},{5... | collective-permute-start | bytes 491528 | tf_op jit(solution)/shard_map/ppermute | solution.py:361
  30.5 11.1 %collective-permute-start.14 = (bf16[256,1024]{1,0:T(8,128)(2,1)S(1)}, bf16[256,1024]{1,0:T(8,128)(2,1)S(1)}, u32[]{:S(2)}, u32[]{:S(2)}) collective-permute-start(bf16[256,1024]{1,0:T(8,128)(2,1)S(1)} %collective-permute-done.3.refs_4_), channel_id=1, source_target_pairs={{0,8},{4,12},{8,0},{12,4},{16,24},{20,28},{24,16},{28,20},{1,9},{5... | collective-permute-start | bytes 1572872 | tf_op jit(solution)/shard_map/ppermute | solution.py:361
  34.4 5.6 %collective-permute-start.12 = (bf16[8,16,1280]{2,1,0:T(8,128)(2,1)S(1)}, bf16[8,16,1280]{2,1,0:T(8,128)(2,1)S(1)}, u32[]{:S(2)}, u32[]{:S(2)}) collective-permute-start(bf16[8,16,1280]{2,1,0:T(8,128)(2,1)S(1)} %shard_map.114.refs_2_), channel_id=1, source_target_pairs={{0,1},{1,0},{2,3},{3,2},{4,5},{5,4},{6,7},{7,6},{8,9},{9,8},{10,11... | collective-permute-start | bytes 983048 | tf_op jit(solution)/shard_map/ppermute | solution.py:361
  34.5 2.6 %collective-permute-start.13 = (bf16[4,16,1280]{2,1,0:T(8,128)(2,1)S(1)}, bf16[4,16,1280]{2,1,0:T(8,128)(2,1)S(1)}, u32[]{:S(2)}, u32[]{:S(2)}) collective-permute-start(bf16[4,16,1280]{2,1,0:T(8,128)(2,1)S(1)} %shard_map.112.refs_0_), channel_id=1, source_target_pairs={{0,1},{1,0},{2,3},{3,2},{4,5},{5,4},{6,7},{7,6},{8,9},{9,8},{10,11... | collective-permute-start | bytes 491528 | tf_op jit(solution)/shard_map/ppermute | solution.py:361
  35.0 4.4 %collective-permute-start.10 = (bf16[2,16,1280]{2,1,0:T(8,128)(2,1)S(1)}, bf16[2,16,1280]{2,1,0:T(8,128)(2,1)S(1)}, u32[]{:S(2)}, u32[]{:S(2)}) collective-permute-start(bf16[2,16,1280]{2,1,0:T(8,128)(2,1)S(1)} %get-tuple-element.45), channel_id=1, source_target_pairs={{0,2},{1,3},{2,0},{3,1},{4,6},{5,7},{6,4},{7,5},{8,10},{9,11},{10,... | collective-permute-start | bytes 245768 | tf_op jit(solution)/shard_map/ppermute | solution.py:361
  35.5 4.4 %collective-permute-start.11 = (bf16[2,16,1280]{2,1,0:T(8,128)(2,1)S(1)}, bf16[2,16,1280]{2,1,0:T(8,128)(2,1)S(1)}, u32[]{:S(2)}, u32[]{:S(2)}) collective-permute-start(bf16[2,16,1280]{2,1,0:T(8,128)(2,1)S(1)} %get-tuple-element.46), channel_id=1, source_target_pairs={{0,4},{4,0},{8,12},{12,8},{16,20},{20,16},{24,28},{28,24},{1,5},{5... | collective-permute-start | bytes 245768 | tf_op jit(solution)/shard_map/ppermute | solution.py:361
  40.0 1.6 %collective-permute-start.15 = (bf16[4,16,1280]{2,1,0:T(8,128)(2,1)S(1)}, bf16[4,16,1280]{2,1,0:T(8,128)(2,1)S(1)}, u32[]{:S(2)}, u32[]{:S(2)}) collective-permute-start(bf16[4,16,1280]{2,1,0:T(8,128)(2,1)S(1)} %shard_map.115.refs_4_), channel_id=1, source_target_pairs={{0,1},{1,0},{2,3},{3,2},{4,5},{5,4},{6,7},{7,6},{8,9},{9,8},{10,11... | collective-permute-start | bytes 491528 | tf_op jit(solution)/shard_map/ppermute | solution.py:361
  40.0 2.1 %collective-permute-start.16 = (bf16[256,1024]{1,0:T(8,128)(2,1)S(1)}, bf16[256,1024]{1,0:T(8,128)(2,1)S(1)}, u32[]{:S(2)}, u32[]{:S(2)}) collective-permute-start(bf16[256,1024]{1,0:T(8,128)(2,1)S(1)} %collective-permute-done.9.refs_8_), channel_id=1, source_target_pairs={{0,1},{1,0},{2,3},{3,2},{4,5},{5,4},{6,7},{7,6},{8,9},{9,8},{10,11... | collective-permute-start | bytes 1572872 | tf_op jit(solution)/shard_map/ppermute | solution.py:361
  40.5 2.7 %collective-permute-start.17 = (bf16[256,1024]{1,0:T(8,128)(2,1)S(1)}, bf16[256,1024]{1,0:T(8,128)(2,1)S(1)}, u32[]{:S(2)}, u32[]{:S(2)}) collective-permute-start(bf16[256,1024]{1,0:T(8,128)(2,1)S(1)} %collective-permute-done.3.refs_4_), channel_id=1, source_target_pairs={{0,1},{1,0},{2,3},{3,2},{4,5},{5,4},{6,7},{7,6},{8,9},{9,8},{10,11... | collective-permute-start | bytes 1572872 | tf_op jit(solution)/shard_map/ppermute | solution.py:361
  41.6 2.1 %collective-permute-start.18 = (bf16[256,1024]{1,0:T(8,128)(2,1)S(1)}, bf16[256,1024]{1,0:T(8,128)(2,1)S(1)}, u32[]{:S(2)}, u32[]{:S(2)}) collective-permute-start(bf16[256,1024]{1,0:T(8,128)(2,1)S(1)} %collective-permute-done.14.refs_5_), channel_id=1, source_target_pairs={{0,1},{1,0},{2,3},{3,2},{4,5},{5,4},{6,7},{7,6},{8,9},{9,8},{10,11... | collective-permute-start | bytes 1572872 | tf_op jit(solution)/shard_map/ppermute | solution.py:361

commit v14 on v12

--- a/solution.py
+++ b/solution.py
@@ -10,13 +10,13 @@
 HD = 64
 BF = jnp.bfloat16
 F32 = jnp.float32
-NODES_STEP = 6
+NODES_STEP = 8
 WIDE_LIMIT = 256
 IDS_COLS = 128
 IDS_AT = 32
 TOP = 16
 LOG2E = 1.4426950408889634
-ATTENTION_VMEM = 58
+ATTENTION_VMEM = 50
 MIB = 1 << 20
 
 
@@ -32,29 +32,40 @@
     return jnp.dot(a, b, preferred_element_type=F32)
 
 
-def attend(q, k, v, heads):
+def attend(q, k, v):
     seq, cols = q.shape
-    lane = lax.broadcasted_iota(jnp.int32, (seq, cols), 1) // HD
-    zero = jnp.zeros((seq, cols), BF)
-    spread = jnp.concatenate([jnp.where(lane == h, k, zero) for h in range(heads)], axis=0)
-    s = dot_t(spread, q).reshape(heads, seq, seq)
-    e = jnp.exp2((s - jnp.max(s, axis=1, keepdims=True)) * (HD**-0.5 * LOG2E))
-    p = (e * (1.0 / jnp.sum(e, axis=1, keepdims=True))).astype(BF)
-    weight = jnp.sum(p.astype(F32), axis=2, keepdims=True)
-    left = lax.broadcasted_iota(jnp.int32, (seq, 2 * HD), 1) < HD
-    pairs = [jnp.where(left, weight[h], weight[h + 1]) for h in range(0, heads, 2)]
-    context = jnp.concatenate(pairs, axis=1) * v.astype(F32)
-    return jnp.sum(context, axis=0, keepdims=True) * (1.0 / seq)
-
-
-def attention_kernel(heads, x_ref, w_ref, cot_ref, ids_ref, out_ref, wp, acc_p, acc_m):
+    pair = 2 * HD
+    left = lax.broadcasted_iota(jnp.int32, (seq, pair), 1) < HD
+    zero = jnp.zeros((seq, pair), BF)
+    out = []
+    for at in range(0, cols, pair):
+        both = q[:, at : at + pair]
+        spread = jnp.concatenate([jnp.where(left, both, zero), jnp.where(left, zero, both)], axis=0)
+        s = dot_t(k[:, at : at + pair], spread)
+        e = jnp.exp2((s - jnp.max(s, axis=0, keepdims=True)) * (HD**-0.5 * LOG2E))
+        p = (e * (1.0 / jnp.sum(e, axis=0, keepdims=True))).astype(BF).astype(F32)
+        first = jnp.sum(p[:, :seq], axis=1, keepdims=True)
+        second = jnp.sum(p[:, seq:], axis=1, keepdims=True)
+        context = jnp.where(left, first, second) * v[:, at : at + pair].astype(F32)
+        out.append(jnp.sum(context, axis=0, keepdims=True) * (1.0 / seq))
+    return jnp.concatenate(out, axis=1)
+
+
+def attention_kernel(
+    heads, texts_ref, w_ref, cot_ref, ids_ref, out_ref, wp, acc_p, acc_m, held, sem
+):
     step = pl.program_id(0)
-    nodes, seq, width = x_ref.shape
+    nodes, seq, width = held.shape[1:]
     node_dev = cot_ref.shape[0]
     cols = heads * HD
 
+    def fetch(i):
+        source = texts_ref.at[pl.ds(i * nodes, nodes)]
+        return pltpu.make_async_copy(source, held.at[i % 2], sem.at[i % 2])
+
     @pl.when(step == 0)
     def _():
+        fetch(0).start()
         for part in range(3):
             for h in range(0, heads, 2):
                 a = h * 3 * HD + part * HD
@@ -63,12 +74,18 @@
                     [w_ref[:, a : a + HD], w_ref[:, b : b + HD]], axis=1
                 )
 
+    @pl.when(step + 1 < pl.num_programs(0))
+    def _():
+        fetch(step + 1).start()
+
+    fetch(step).wait()
+    x_ref = held.at[step % 2]
     own = pl.ds(pl.multiple_of(lax.axis_index("mp") * cols, 128), cols)
     qkv = dot(x_ref[...].reshape(nodes * seq, width), wp[...]).astype(BF)
     for n in range(nodes):
         at = slice(n * seq, (n + 1) * seq)
         row = pl.ds(step * nodes + n, 1)
-        acc_p[row, :] = attend(*(qkv[at, i * cols : (i + 1) * cols] for i in range(3)), heads)
+        acc_p[row, :] = attend(*(qkv[at, i * cols : (i + 1) * cols] for i in range(3)))
         mean = jnp.sum(x_ref[n, :, own].astype(F32), axis=0, keepdims=True)
         acc_m[row, :] = mean * (1.0 / seq)
 
@@ -114,7 +131,7 @@
         out_shape=jax.ShapeDtypeStruct(packed, BF),
         grid=(node_dev // nodes,),
         in_specs=[
-            pl.BlockSpec((nodes, seq, width), lambda i: (i, 0, 0)),
+            pl.BlockSpec(memory_space=pl.ANY),
             pl.BlockSpec((width, 3 * cols), lambda i: (0, 0)),
             pl.BlockSpec((node_dev, cols), lambda i: (0, 0)),
             pl.BlockSpec(ids.shape, lambda i: (0, 0)),
@@ -124,6 +141,8 @@
             pltpu.VMEM((width, 3 * cols), BF),
             pltpu.VMEM((node_dev, cols), F32),
             pltpu.VMEM((node_dev, cols), F32),
+            pltpu.VMEM((2, nodes, seq, width), BF),
+            pltpu.SemaphoreType.DMA((2,)),
         ],
         compiler_params=pltpu.CompilerParams(vmem_limit_bytes=ATTENTION_VMEM * MIB),
         cost_estimate=pl.CostEstimate(

time: 49.5 us -> 49.6 us (level)
  Pallas kernels: 18.9 us -> 16.8 us
  local copies, waits for them, and re-layouts: 0.82 us -> 2.82 us
    pallas_call x1, Pallas kernels: 11.5 us -> 9.46 us  [attention(): pl.pallas_call(functools.partial(attention_kernel, heads), out_shape=jax....]
    unnamed x8 -> x12, local copies, waits for them, and re-layouts: 0.82 us -> 2.82 us
  transfers between devices with their start and end apart: 16 -> 16, of which waited for: 8 -> 8; matrix products, arithmetic and copies ran while one was open for 2% -> 2% of each run, Pallas kernels for 26% -> 21%
where the time goes in v14:
time: 49.6 us; the launch traced here: 49.3 us
  Pallas kernels  16.8 us (34%)
  waiting for transfers between devices  15.2 us (31%)
  starting transfers between devices  12.7 us (26%)
  local copies, waits for them, and re-layouts  2.82 us (6%)
  other arithmetic  1.1 us (2%)
  between operations  0.72 us (1%)
    ppermute x16, waiting for transfers between devices, hop(): lax.ppermute(x, axis, [(i, i ^ bit) for i in range(lax.axis_size(axis))])  15.2 us
    ppermute x16, starting transfers between devices, hop(): lax.ppermute(x, axis, [(i, i ^ bit) for i in range(lax.axis_size(axis))])  12.7 us
    pallas_call x1, Pallas kernels, attention(): pl.pallas_call(functools.partial(attention_kernel, heads), out_shape=jax....  9.46 us
    pallas_call x1, Pallas kernels, graph(): pl.pallas_call(functools.partial(graph_kernel, node_dev), out_shape=(slab...  6.22 us
    unnamed x12, local copies, waits for them, and re-layouts  2.82 us
    select_n x1, other arithmetic, per_device(): jnp.where(even, w_self, w_neigh)  1.1 us
    pallas_call x1, Pallas kernels, graph(): pl.pallas_call(functools.partial(embed_kernel, order, fan, node_dev), out...  1.07 us
  transfers between devices with their start and end apart: 16, of which 8 were waited for; matrix products, arithmetic and copies ran while one was open for 2% of the time, Pallas kernels for 21%

profile of v14, /device:TPU:0, one launch (start us, length us, event | category | flops | bytes accessed | tf_op | source)
XLA Modules:
  0.0 49.3 jit_solution(16013684869496304397)
XLA Ops:
  0.6 0.5 %collective-permute-start = (bf16[256,1024]{1,0:T(8,128)(2,1)}, bf16[256,1024]{1,0:T(8,128)(2,1)S(1)}, u32[]{:S(2)}, u32[]{:S(2)}) collective-permute-start(bf16[256,1024]{1,0:T(8,128)(2,1)} %refs_4_.1), channel_id=1, source_target_pairs={{0,1},{1,0},{2,3},{3,2},{4,5},{5,4},{6,7},{7,6},{8,9},{9,8},{10,11... | collective-permute-start | bytes 1572872 | tf_op jit(solution)/shard_map/ppermute | solution.py:366
  1.1 0.1 collective-permute-start.1
  1.2 0.4 collective-permute-start.2
  1.7 1.1 %broadcast_select_fusion = bf16[256,1024]{1,0:T(8,128)(2,1)S(1)} fusion(bf16[256,1024]{1,0:T(8,128)(2,1)} %refs_0_.1, bf16[256,1024]{1,0:T(8,128)(2,1)} %refs_1_.1, pred[]{:T(512)S(6)} %eq.5), kind=kLoop, calls=%fused_computation | loop fusion | flops 262144 | bytes 1572865 | tf_op jit(solution)/shard_map/jit(_where)/select_n | solution.py:391
  2.8 2.6 %collective-permute-start.3 = (bf16[256,1024]{1,0:T(8,128)(2,1)S(1)}, bf16[256,1024]{1,0:T(8,128)(2,1)S(1)}, u32[]{:S(2)}, u32[]{:S(2)}) collective-permute-start(bf16[256,1024]{1,0:T(8,128)(2,1)S(1)} %broadcast_select_fusion), channel_id=1, source_target_pairs={{0,2},{1,3},{2,0},{3,1},{4,6},{5,7},{6,4},{7,5},{8,10},{9,11},{10,... | collective-permute-start | bytes 1572872 | tf_op jit(solution)/shard_map/ppermute | solution.py:366
  5.4 0.1 collective-permute-start.8
  5.5 1.4 %copy-done.3 = bf16[1024,768]{1,0:T(8,128)(2,1)S(1)} copy-done((bf16[1024,768]{1,0:T(8,128)(2,1)S(1)}, bf16[1024,768]{1,0:T(8,128)(2,1)}, u32[]{:S(2)}) %copy-start.3) | copy-done | bytes 1572888
  6.9 0.7 %copy-done.4 = bf16[24,256]{1,0:T(8,128)(2,1)S(1)} copy-done((bf16[24,256]{1,0:T(8,128)(2,1)S(1)}, bf16[24,256]{1,0:T(8,128)(2,1)}, u32[]{:S(2)}) %copy-start.4) | copy-done | bytes 12312
  7.6 0.7 %copy-done.5 = s32[24,16]{0,1:T(8,128)S(1)} copy-done((s32[24,16]{0,1:T(8,128)S(1)}, s32[24,16]{0,1:T(8,128)}, u32[]{:S(2)}) %copy-start.5) | copy-done | bytes 1560
  8.3 9.5 %shard_map.110 = bf16[16,1280]{1,0:T(8,128)(2,1)S(1)} custom-call(bf16[24,128,1024]{2,1,0:T(8,128)(2,1)} %texts_ref.1, bf16[1024,768]{1,0:T(8,128)(2,1)S(1)} %copy-done.3, bf16[24,256]{1,0:T(8,128)(2,1)S(1)} %copy-done.4, s32[16,24]{1,0:T(8,128)S(1)} %bitcast.6), custom_call_target="tpu_custom_call" | custom-call | flops 5637144576 | bytes 7864320 | tf_op jit(solution)/shard_map/pallas_call | solution.py:129
  17.8 0.4 collective-permute-done.3.refs_4_
  18.2 4.1 %collective-permute-start.6 = (bf16[1,16,1280]{2,1,0:T(8,128)(2,1)S(1)}, bf16[1,16,1280]{2,1,0:T(8,128)(2,1)S(1)}, u32[]{:S(2)}, u32[]{:S(2)}) collective-permute-start(bf16[1,16,1280]{2,1,0:T(8,128)(2,1)S(1)} %bitcast.2), channel_id=1, source_target_pairs={{0,24},{4,28},{8,16},{12,20},{16,8},{20,12},{24,0},{28,4},{1,25},{... | collective-permute-start | bytes 122888 | tf_op jit(solution)/shard_map/ppermute | solution.py:366
  22.3 0.0 collective-permute-start.5
  22.3 0.6 %collective-permute-start.4 = (bf16[1,16,1280]{2,1,0:T(8,128)(2,1)S(1)}, bf16[1,16,1280]{2,1,0:T(8,128)(2,1)S(1)}, u32[]{:S(2)}, u32[]{:S(2)}) collective-permute-start(bf16[1,16,1280]{2,1,0:T(8,128)(2,1)S(1)} %bitcast.4), channel_id=1, source_target_pairs={{0,8},{4,12},{8,0},{12,4},{16,24},{20,28},{24,16},{28,20},{1,9},{5... | collective-permute-start | bytes 122888 | tf_op jit(solution)/shard_map/ppermute | solution.py:366
  23.0 1.6 %collective-permute-done.6.refs_3_ = bf16[1,16,1280]{2,1,0:T(8,128)(2,1)S(1)} collective-permute-done((bf16[1,16,1280]{2,1,0:T(8,128)(2,1)S(1)}, bf16[1,16,1280]{2,1,0:T(8,128)(2,1)S(1)}, u32[]{:S(2)}, u32[]{:S(2)}) %collective-permute-start.6) | collective-permute-done | bytes 40992 | tf_op jit(solution)/shard_map/ppermute | solution.py:366
  24.5 2.7 %collective-permute-done.5.refs_2_ = bf16[1,16,1280]{2,1,0:T(8,128)(2,1)S(1)} collective-permute-done((bf16[1,16,1280]{2,1,0:T(8,128)(2,1)S(1)}, bf16[1,16,1280]{2,1,0:T(8,128)(2,1)S(1)}, u32[]{:S(2)}, u32[]{:S(2)}) %collective-permute-start.5) | collective-permute-done | bytes 40992 | tf_op jit(solution)/shard_map/ppermute | solution.py:366
  27.2 0.0 collective-permute-done.4.refs_1_
  27.2 1.6 %collective-permute-start.7 = (bf16[4,16,1280]{2,1,0:T(8,128)(2,1)S(1)}, bf16[4,16,1280]{2,1,0:T(8,128)(2,1)S(1)}, u32[]{:S(2)}, u32[]{:S(2)}) collective-permute-start(bf16[4,16,1280]{2,1,0:T(8,128)(2,1)S(1)} %shard_map.112.refs_0_), channel_id=1, source_target_pairs={{0,4},{4,0},{8,12},{12,8},{16,20},{20,16},{24,28},{28,24},{1,5},{5... | collective-permute-start | bytes 491528 | tf_op jit(solution)/shard_map/ppermute | solution.py:366
  28.8 3.8 %collective-permute-done.7.refs_1_ = bf16[4,16,1280]{2,1,0:T(8,128)(2,1)S(1)} collective-permute-done((bf16[4,16,1280]{2,1,0:T(8,128)(2,1)S(1)}, bf16[4,16,1280]{2,1,0:T(8,128)(2,1)S(1)}, u32[]{:S(2)}, u32[]{:S(2)}) %collective-permute-start.7) | collective-permute-done | bytes 163872 | tf_op jit(solution)/shard_map/ppermute | solution.py:366
  32.6 0.0 collective-permute-done.8.refs_6_
  32.7 1.6 %collective-permute-start.10 = (bf16[8,16,1280]{2,1,0:T(8,128)(2,1)S(1)}, bf16[8,16,1280]{2,1,0:T(8,128)(2,1)S(1)}, u32[]{:S(2)}, u32[]{:S(2)}) collective-permute-start(bf16[8,16,1280]{2,1,0:T(8,128)(2,1)S(1)} %shard_map.113.refs_0_), channel_id=1, source_target_pairs={{0,2},{1,3},{2,0},{3,1},{4,6},{5,7},{6,4},{7,5},{8,10},{9,11},{10,... | collective-permute-start | bytes 983048 | tf_op jit(solution)/shard_map/ppermute | solution.py:366
  34.2 0.5 %collective-permute-start.14 = (bf16[256,1024]{1,0:T(8,128)(2,1)S(1)}, bf16[256,1024]{1,0:T(8,128)(2,1)S(1)}, u32[]{:S(2)}, u32[]{:S(2)}) collective-permute-start(bf16[256,1024]{1,0:T(8,128)(2,1)S(1)} %collective-permute-done.3.refs_4_), channel_id=1, source_target_pairs={{0,1},{1,0},{2,3},{3,2},{4,5},{5,4},{6,7},{7,6},{8,9},{9,8},{10,11... | collective-permute-start | bytes 1572872 | tf_op jit(solution)/shard_map/ppermute | solution.py:366
  34.7 4.4 %collective-permute-done.13.refs_5_ = bf16[256,1024]{1,0:T(8,128)(2,1)S(1)} collective-permute-done((bf16[256,1024]{1,0:T(8,128)(2,1)S(1)}, bf16[256,1024]{1,0:T(8,128)(2,1)S(1)}, u32[]{:S(2)}, u32[]{:S(2)}) %collective-permute-start.13) | collective-permute-done | bytes 524320 | tf_op jit(solution)/shard_map/ppermute | solution.py:366
  39.1 0.0 collective-permute-start.15
  39.1 0.5 %collective-permute-start.9 = (bf16[8,16,1280]{2,1,0:T(8,128)(2,1)S(1)}, bf16[8,16,1280]{2,1,0:T(8,128)(2,1)S(1)}, u32[]{:S(2)}, u32[]{:S(2)}) collective-permute-start(bf16[8,16,1280]{2,1,0:T(8,128)(2,1)S(1)} %shard_map.113.refs_0_), channel_id=1, source_target_pairs={{0,1},{1,0},{2,3},{3,2},{4,5},{5,4},{6,7},{7,6},{8,9},{9,8},{10,11... | collective-permute-start | bytes 983048 | tf_op jit(solution)/shard_map/ppermute | solution.py:366
  39.6 0.1 collective-permute-done.10.refs_2_
  39.8 1.7 %collective-permute-done.9.refs_1_ = bf16[8,16,1280]{2,1,0:T(8,128)(2,1)S(1)} collective-permute-done((bf16[8,16,1280]{2,1,0:T(8,128)(2,1)S(1)}, bf16[8,16,1280]{2,1,0:T(8,128)(2,1)S(1)}, u32[]{:S(2)}, u32[]{:S(2)}) %collective-permute-start.9) | collective-permute-done | bytes 327712 | tf_op jit(solution)/shard_map/ppermute | solution.py:366
  41.5 0.0 collective-permute-done.12.refs_7_
  41.5 0.5 collective-permute-done.11.refs_3_
  42.0 1.1 %shard_map.114 = (bf16[2,192,1024]{2,1,0:T(8,128)(2,1)S(1)}, bf16[192,1024]{1,0:T(8,128)(2,1)S(1)}, bf16[192,256]{1,0:T(8,128)(2,1)S(1)}, bf16[192,192]{1,0:T(8,128)(2,1)S(1)}, f32[192,128]{1,0:T(8,128)S(1)}) custom-call(bf16[8,16,1280]{2,1,0:T(8,128)(2,1)S(1)} %shard_map.113.refs_0_, bf16[8,16,1280]{2,1,0:T(8,128)(2,1)S(1)} %collective-permute-done.9.refs_1_, ...), custom_call_target="tpu_custom_call" | custom-call | flops 805306368 | bytes 4194304 | tf_op jit(solution)/shard_map/pallas_call | solution.py:263
  43.1 0.0 collective-permute-done.15.refs_7_
  43.1 6.2 %shard_map.115 = (bf16[24,256]{1,0:T(8,128)(2,1)}, bf16[24,256]{1,0:T(8,128)(2,1)}, f32[256,1024]{1,0:T(8,128)}, f32[256,1024]{1,0:T(8,128)}, f32[256,1024]{1,0:T(8,128)}) custom-call(bf16[2,192,1024]{2,1,0:T(8,128)(2,1)S(1)} %get-tuple-element.35.both, bf16[192,1024]{1,0:T(8,128)(2,1)S(1)} %get-tuple-element.36.cot, ...), custom_call_target="tpu_custom_call" | custom-call | flops 2013265920 | bytes 8388608 | tf_op jit(solution)/shard_map/pallas_call | solution.py:283
  (19 shorter events, 0.1 us)
Async XLA Ops:
  0.6 17.5 %collective-permute-start = (bf16[256,1024]{1,0:T(8,128)(2,1)}, bf16[256,1024]{1,0:T(8,128)(2,1)S(1)}, u32[]{:S(2)}, u32[]{:S(2)}) collective-permute-start(bf16[256,1024]{1,0:T(8,128)(2,1)} %refs_4_.1), channel_id=1, source_target_pairs={{0,1},{1,0},{2,3},{3,2},{4,5},{5,4},{6,7},{7,6},{8,9},{9,8},{10,11... | collective-permute-start | bytes 1572872 | tf_op jit(solution)/shard_map/ppermute | solution.py:366
  1.1 17.0 %collective-permute-start.1 = (bf16[256,1024]{1,0:T(8,128)(2,1)}, bf16[256,1024]{1,0:T(8,128)(2,1)S(1)}, u32[]{:S(2)}, u32[]{:S(2)}) collective-permute-start(bf16[256,1024]{1,0:T(8,128)(2,1)} %refs_0_.1), channel_id=1, source_target_pairs={{0,1},{1,0},{2,3},{3,2},{4,5},{5,4},{6,7},{7,6},{8,9},{9,8},{10,11... | collective-permute-start | bytes 1572872 | tf_op jit(solution)/shard_map/ppermute | solution.py:366
  1.2 17.0 %collective-permute-start.2 = (bf16[256,1024]{1,0:T(8,128)(2,1)}, bf16[256,1024]{1,0:T(8,128)(2,1)S(1)}, u32[]{:S(2)}, u32[]{:S(2)}) collective-permute-start(bf16[256,1024]{1,0:T(8,128)(2,1)} %refs_1_.1), channel_id=1, source_target_pairs={{0,1},{1,0},{2,3},{3,2},{4,5},{5,4},{6,7},{7,6},{8,9},{9,8},{10,11... | collective-permute-start | bytes 1572872 | tf_op jit(solution)/shard_map/ppermute | solution.py:366
  2.8 15.4 %collective-permute-start.3 = (bf16[256,1024]{1,0:T(8,128)(2,1)S(1)}, bf16[256,1024]{1,0:T(8,128)(2,1)S(1)}, u32[]{:S(2)}, u32[]{:S(2)}) collective-permute-start(bf16[256,1024]{1,0:T(8,128)(2,1)S(1)} %broadcast_select_fusion), channel_id=1, source_target_pairs={{0,2},{1,3},{2,0},{3,1},{4,6},{5,7},{6,4},{7,5},{8,10},{9,11},{10,... | collective-permute-start | bytes 1572872 | tf_op jit(solution)/shard_map/ppermute | solution.py:366
  5.4 27.2 %collective-permute-start.8 = (bf16[256,1024]{1,0:T(8,128)(2,1)}, bf16[256,1024]{1,0:T(8,128)(2,1)S(1)}, u32[]{:S(2)}, u32[]{:S(2)}) collective-permute-start(bf16[256,1024]{1,0:T(8,128)(2,1)} %refs_4_.1), channel_id=1, source_target_pairs={{0,2},{1,3},{2,0},{3,1},{4,6},{5,7},{6,4},{7,5},{8,10},{9,11},{10,... | collective-permute-start | bytes 1572872 | tf_op jit(solution)/shard_map/ppermute | solution.py:366
  5.5 1.4 %copy-start.3 = (bf16[1024,768]{1,0:T(8,128)(2,1)S(1)}, bf16[1024,768]{1,0:T(8,128)(2,1)}, u32[]{:S(2)}) copy-start(bf16[1024,768]{1,0:T(8,128)(2,1)} %w_ref.1) | copy-start | bytes 4718596
  6.9 0.7 %copy-start.4 = (bf16[24,256]{1,0:T(8,128)(2,1)S(1)}, bf16[24,256]{1,0:T(8,128)(2,1)}, u32[]{:S(2)}) copy-start(bf16[24,256]{1,0:T(8,128)(2,1)} %cot_ref.1) | copy-start | bytes 36868
  7.6 0.7 %copy-start.5 = (s32[24,16]{0,1:T(8,128)S(1)}, s32[24,16]{0,1:T(8,128)}, u32[]{:S(2)}) copy-start(s32[24,16]{0,1:T(8,128)} %param.12) | copy-start | bytes 4612
  8.3 33.7 %copy-start.2 = (bf16[256,1024]{1,0:T(8,128)(2,1)S(1)}, bf16[256,1024]{1,0:T(8,128)(2,1)}, u32[]{:S(2)}) copy-start(bf16[256,1024]{1,0:T(8,128)(2,1)} %refs_4_.1) | copy-start | bytes 1572868
  8.3 34.8 %copy-start = (bf16[256,1024]{1,0:T(8,128)(2,1)S(1)}, bf16[256,1024]{1,0:T(8,128)(2,1)}, u32[]{:S(2)}) copy-start(bf16[256,1024]{1,0:T(8,128)(2,1)} %refs_0_.1) | copy-start | bytes 1572868
  8.3 34.8 %copy-start.1 = (bf16[256,1024]{1,0:T(8,128)(2,1)S(1)}, bf16[256,1024]{1,0:T(8,128)(2,1)}, u32[]{:S(2)}) copy-start(bf16[256,1024]{1,0:T(8,128)(2,1)} %refs_1_.1) | copy-start | bytes 1572868
  18.2 6.4 %collective-permute-start.6 = (bf16[1,16,1280]{2,1,0:T(8,128)(2,1)S(1)}, bf16[1,16,1280]{2,1,0:T(8,128)(2,1)S(1)}, u32[]{:S(2)}, u32[]{:S(2)}) collective-permute-start(bf16[1,16,1280]{2,1,0:T(8,128)(2,1)S(1)} %bitcast.2), channel_id=1, source_target_pairs={{0,24},{4,28},{8,16},{12,20},{16,8},{20,12},{24,0},{28,4},{1,25},{... | collective-permute-start | bytes 122888 | tf_op jit(solution)/shard_map/ppermute | solution.py:366
  22.3 4.9 %collective-permute-start.5 = (bf16[1,16,1280]{2,1,0:T(8,128)(2,1)S(1)}, bf16[1,16,1280]{2,1,0:T(8,128)(2,1)S(1)}, u32[]{:S(2)}, u32[]{:S(2)}) collective-permute-start(bf16[1,16,1280]{2,1,0:T(8,128)(2,1)S(1)} %bitcast.3), channel_id=1, source_target_pairs={{0,16},{4,20},{8,24},{12,28},{16,0},{20,4},{24,8},{28,12},{1,17},{... | collective-permute-start | bytes 122888 | tf_op jit(solution)/shard_map/ppermute | solution.py:366
  22.3 4.9 %collective-permute-start.4 = (bf16[1,16,1280]{2,1,0:T(8,128)(2,1)S(1)}, bf16[1,16,1280]{2,1,0:T(8,128)(2,1)S(1)}, u32[]{:S(2)}, u32[]{:S(2)}) collective-permute-start(bf16[1,16,1280]{2,1,0:T(8,128)(2,1)S(1)} %bitcast.4), channel_id=1, source_target_pairs={{0,8},{4,12},{8,0},{12,4},{16,24},{20,28},{24,16},{28,20},{1,9},{5... | collective-permute-start | bytes 122888 | tf_op jit(solution)/shard_map/ppermute | solution.py:366
  27.2 11.9 %collective-permute-start.13 = (bf16[256,1024]{1,0:T(8,128)(2,1)S(1)}, bf16[256,1024]{1,0:T(8,128)(2,1)S(1)}, u32[]{:S(2)}, u32[]{:S(2)}) collective-permute-start(bf16[256,1024]{1,0:T(8,128)(2,1)S(1)} %collective-permute-done.3.refs_4_), channel_id=1, source_target_pairs={{0,8},{4,12},{8,0},{12,4},{16,24},{20,28},{24,16},{28,20},{1,9},{5... | collective-permute-start | bytes 1572872 | tf_op jit(solution)/shard_map/ppermute | solution.py:366
  27.2 5.4 %collective-permute-start.7 = (bf16[4,16,1280]{2,1,0:T(8,128)(2,1)S(1)}, bf16[4,16,1280]{2,1,0:T(8,128)(2,1)S(1)}, u32[]{:S(2)}, u32[]{:S(2)}) collective-permute-start(bf16[4,16,1280]{2,1,0:T(8,128)(2,1)S(1)} %shard_map.112.refs_0_), channel_id=1, source_target_pairs={{0,4},{4,0},{8,12},{12,8},{16,20},{20,16},{24,28},{28,24},{1,5},{5... | collective-permute-start | bytes 491528 | tf_op jit(solution)/shard_map/ppermute | solution.py:366
  32.7 7.1 %collective-permute-start.10 = (bf16[8,16,1280]{2,1,0:T(8,128)(2,1)S(1)}, bf16[8,16,1280]{2,1,0:T(8,128)(2,1)S(1)}, u32[]{:S(2)}, u32[]{:S(2)}) collective-permute-start(bf16[8,16,1280]{2,1,0:T(8,128)(2,1)S(1)} %shard_map.113.refs_0_), channel_id=1, source_target_pairs={{0,2},{1,3},{2,0},{3,1},{4,6},{5,7},{6,4},{7,5},{8,10},{9,11},{10,... | collective-permute-start | bytes 983048 | tf_op jit(solution)/shard_map/ppermute | solution.py:366
  34.2 7.3 %collective-permute-start.12 = (bf16[256,1024]{1,0:T(8,128)(2,1)S(1)}, bf16[256,1024]{1,0:T(8,128)(2,1)S(1)}, u32[]{:S(2)}, u32[]{:S(2)}) collective-permute-start(bf16[256,1024]{1,0:T(8,128)(2,1)S(1)} %collective-permute-done.8.refs_6_), channel_id=1, source_target_pairs={{0,1},{1,0},{2,3},{3,2},{4,5},{5,4},{6,7},{7,6},{8,9},{9,8},{10,11... | collective-permute-start | bytes 1572872 | tf_op jit(solution)/shard_map/ppermute | solution.py:366
  34.2 8.9 %collective-permute-start.14 = (bf16[256,1024]{1,0:T(8,128)(2,1)S(1)}, bf16[256,1024]{1,0:T(8,128)(2,1)S(1)}, u32[]{:S(2)}, u32[]{:S(2)}) collective-permute-start(bf16[256,1024]{1,0:T(8,128)(2,1)S(1)} %collective-permute-done.3.refs_4_), channel_id=1, source_target_pairs={{0,1},{1,0},{2,3},{3,2},{4,5},{5,4},{6,7},{7,6},{8,9},{9,8},{10,11... | collective-permute-start | bytes 1572872 | tf_op jit(solution)/shard_map/ppermute | solution.py:366
  39.1 3.9 %collective-permute-start.15 = (bf16[256,1024]{1,0:T(8,128)(2,1)S(1)}, bf16[256,1024]{1,0:T(8,128)(2,1)S(1)}, u32[]{:S(2)}, u32[]{:S(2)}) collective-permute-start(bf16[256,1024]{1,0:T(8,128)(2,1)S(1)} %collective-permute-done.13.refs_5_), channel_id=1, source_target_pairs={{0,1},{1,0},{2,3},{3,2},{4,5},{5,4},{6,7},{7,6},{8,9},{9,8},{10,11... | collective-permute-start | bytes 1572872 | tf_op jit(solution)/shard_map/ppermute | solution.py:366
  39.1 2.4 %collective-permute-start.9 = (bf16[8,16,1280]{2,1,0:T(8,128)(2,1)S(1)}, bf16[8,16,1280]{2,1,0:T(8,128)(2,1)S(1)}, u32[]{:S(2)}, u32[]{:S(2)}) collective-permute-start(bf16[8,16,1280]{2,1,0:T(8,128)(2,1)S(1)} %shard_map.113.refs_0_), channel_id=1, source_target_pairs={{0,1},{1,0},{2,3},{3,2},{4,5},{5,4},{6,7},{7,6},{8,9},{9,8},{10,11... | collective-permute-start | bytes 983048 | tf_op jit(solution)/shard_map/ppermute | solution.py:366
  39.8 2.2 %collective-permute-start.11 = (bf16[8,16,1280]{2,1,0:T(8,128)(2,1)S(1)}, bf16[8,16,1280]{2,1,0:T(8,128)(2,1)S(1)}, u32[]{:S(2)}, u32[]{:S(2)}) collective-permute-start(bf16[8,16,1280]{2,1,0:T(8,128)(2,1)S(1)} %collective-permute-done.10.refs_2_), channel_id=1, source_target_pairs={{0,1},{1,0},{2,3},{3,2},{4,5},{5,4},{6,7},{7,6},{8,9},{9,8},{10,11... | collective-permute-start | bytes 983048 | tf_op jit(solution)/shard_map/ppermute | solution.py:366

commit v15 on v14

--- a/solution.py
+++ b/solution.py
@@ -16,7 +16,7 @@
 IDS_AT = 32
 TOP = 16
 LOG2E = 1.4426950408889634
-ATTENTION_VMEM = 50
+ATTENTION_VMEM = 58
 MIB = 1 << 20
 
 
@@ -52,7 +52,7 @@
 
 
 def attention_kernel(
-    heads, texts_ref, w_ref, cot_ref, ids_ref, out_ref, wp, acc_p, acc_m, held, sem
+    heads, texts_ref, w_hbm, cot_ref, ids_ref, out_ref, wp, acc_p, acc_m, held, w_ref, sem
 ):
     step = pl.program_id(0)
     nodes, seq, width = held.shape[1:]
@@ -65,7 +65,10 @@
 
     @pl.when(step == 0)
     def _():
+        weights = pltpu.make_async_copy(w_hbm, w_ref, sem.at[2])
+        weights.start()
         fetch(0).start()
+        weights.wait()
         for part in range(3):
             for h in range(0, heads, 2):
                 a = h * 3 * HD + part * HD
@@ -132,7 +135,7 @@
         grid=(node_dev // nodes,),
         in_specs=[
             pl.BlockSpec(memory_space=pl.ANY),
-            pl.BlockSpec((width, 3 * cols), lambda i: (0, 0)),
+            pl.BlockSpec(memory_space=pl.ANY),
             pl.BlockSpec((node_dev, cols), lambda i: (0, 0)),
             pl.BlockSpec(ids.shape, lambda i: (0, 0)),
         ],
@@ -142,7 +145,8 @@
             pltpu.VMEM((node_dev, cols), F32),
             pltpu.VMEM((node_dev, cols), F32),
             pltpu.VMEM((2, nodes, seq, width), BF),
-            pltpu.SemaphoreType.DMA((2,)),
+            pltpu.VMEM((width, 3 * cols), BF),
+            pltpu.SemaphoreType.DMA((3,)),
         ],
         compiler_params=pltpu.CompilerParams(vmem_limit_bytes=ATTENTION_VMEM * MIB),
         cost_estimate=pl.CostEstimate(

time: 49.6 us -> 49.5 us (level)
  local copies, waits for them, and re-layouts: 2.82 us -> 0.82 us
  Pallas kernels: 16.8 us -> 18.6 us
    unnamed x12 -> x8, local copies, waits for them, and re-layouts: 2.82 us -> 0.82 us
    pallas_call x1, Pallas kernels: 9.46 us -> 11.3 us  [attention(): pl.pallas_call(functools.partial(attention_kernel, heads), out_shape=jax....]
  transfers between devices with their start and end apart: 16 -> 16, of which waited for: 8 -> 8; matrix products, arithmetic and copies ran while one was open for 2% -> 2% of each run, Pallas kernels for 21% -> 25%
where the time goes in v15:
time: 49.5 us; the launch traced here: 49.2 us
  Pallas kernels  18.6 us (38%)
  waiting for transfers between devices  15.3 us (31%)
  starting transfers between devices  12.7 us (26%)
  other arithmetic  1.1 us (2%)
  local copies, waits for them, and re-layouts  0.82 us (2%)
  between operations  0.72 us (1%)
    ppermute x16, waiting for transfers between devices, hop(): lax.ppermute(x, axis, [(i, i ^ bit) for i in range(lax.axis_size(axis))])  15.3 us
    ppermute x16, starting transfers between devices, hop(): lax.ppermute(x, axis, [(i, i ^ bit) for i in range(lax.axis_size(axis))])  12.7 us
    pallas_call x1, Pallas kernels, attention(): pl.pallas_call(functools.partial(attention_kernel, heads), out_shape=jax....  11.3 us
    pallas_call x1, Pallas kernels, graph(): pl.pallas_call(functools.partial(graph_kernel, node_dev), out_shape=(slab...  6.22 us
    select_n x1, other arithmetic, per_device(): jnp.where(even, w_self, w_neigh)  1.1 us
    pallas_call x1, Pallas kernels, graph(): pl.pallas_call(functools.partial(embed_kernel, order, fan, node_dev), out...  1.07 us
  transfers between devices with their start and end apart: 16, of which 8 were waited for; matrix products, arithmetic and copies ran while one was open for 2% of the time, Pallas kernels for 25%

profile of v15, /device:TPU:0, one launch (start us, length us, event | category | flops | bytes accessed | tf_op | source)
XLA Modules:
  0.0 49.2 jit_solution(7819917920881903554)
XLA Ops:
  0.6 0.5 %collective-permute-start = (bf16[256,1024]{1,0:T(8,128)(2,1)}, bf16[256,1024]{1,0:T(8,128)(2,1)S(1)}, u32[]{:S(2)}, u32[]{:S(2)}) collective-permute-start(bf16[256,1024]{1,0:T(8,128)(2,1)} %refs_4_.1), channel_id=1, source_target_pairs={{0,1},{1,0},{2,3},{3,2},{4,5},{5,4},{6,7},{7,6},{8,9},{9,8},{10,11... | collective-permute-start | bytes 1572872 | tf_op jit(solution)/shard_map/ppermute | solution.py:370
  1.1 0.1 collective-permute-start.1
  1.2 0.4 collective-permute-start.2
  1.7 1.1 %broadcast_select_fusion = bf16[256,1024]{1,0:T(8,128)(2,1)S(1)} fusion(bf16[256,1024]{1,0:T(8,128)(2,1)} %refs_0_.1, bf16[256,1024]{1,0:T(8,128)(2,1)} %refs_1_.1, pred[]{:T(512)S(6)} %eq.5), kind=kLoop, calls=%fused_computation | loop fusion | flops 262144 | bytes 1572865 | tf_op jit(solution)/shard_map/jit(_where)/select_n | solution.py:395
  2.8 2.6 %collective-permute-start.3 = (bf16[256,1024]{1,0:T(8,128)(2,1)S(1)}, bf16[256,1024]{1,0:T(8,128)(2,1)S(1)}, u32[]{:S(2)}, u32[]{:S(2)}) collective-permute-start(bf16[256,1024]{1,0:T(8,128)(2,1)S(1)} %broadcast_select_fusion), channel_id=1, source_target_pairs={{0,2},{1,3},{2,0},{3,1},{4,6},{5,7},{6,4},{7,5},{8,10},{9,11},{10,... | collective-permute-start | bytes 1572872 | tf_op jit(solution)/shard_map/ppermute | solution.py:370
  5.4 0.1 collective-permute-start.8
  5.5 11.3 %shard_map.110 = bf16[16,1280]{1,0:T(8,128)(2,1)} custom-call(bf16[24,128,1024]{2,1,0:T(8,128)(2,1)} %texts_ref.1, bf16[1024,768]{1,0:T(8,128)(2,1)} %w_hbm.1, bf16[24,256]{1,0:T(8,128)(2,1)} %cot_ref.1, s32[16,24]{1,0:T(8,128)} %bitcast.6), custom_call_target="tpu_custom_call" | custom-call | flops 5637144576 | bytes 7864320 | tf_op jit(solution)/shard_map/pallas_call | solution.py:132
  16.8 1.4 %collective-permute-done.3.refs_4_ = bf16[256,1024]{1,0:T(8,128)(2,1)S(1)} collective-permute-done((bf16[256,1024]{1,0:T(8,128)(2,1)S(1)}, bf16[256,1024]{1,0:T(8,128)(2,1)S(1)}, u32[]{:S(2)}, u32[]{:S(2)}) %collective-permute-start.3) | collective-permute-done | bytes 524320 | tf_op jit(solution)/shard_map/ppermute | solution.py:370
  18.2 0.0 collective-permute-done.2.refs_3_
  18.2 4.1 %collective-permute-start.6 = (bf16[1,16,1280]{2,1,0:T(8,128)(2,1)}, bf16[1,16,1280]{2,1,0:T(8,128)(2,1)S(1)}, u32[]{:S(2)}, u32[]{:S(2)}) collective-permute-start(bf16[1,16,1280]{2,1,0:T(8,128)(2,1)} %bitcast.2), channel_id=1, source_target_pairs={{0,24},{4,28},{8,16},{12,20},{16,8},{20,12},{24,0},{28,4},{1,25},{... | collective-permute-start | bytes 122888 | tf_op jit(solution)/shard_map/ppermute | solution.py:370
  22.3 0.6 %collective-permute-start.4 = (bf16[1,16,1280]{2,1,0:T(8,128)(2,1)}, bf16[1,16,1280]{2,1,0:T(8,128)(2,1)S(1)}, u32[]{:S(2)}, u32[]{:S(2)}) collective-permute-start(bf16[1,16,1280]{2,1,0:T(8,128)(2,1)} %bitcast.4), channel_id=1, source_target_pairs={{0,8},{4,12},{8,0},{12,4},{16,24},{20,28},{24,16},{28,20},{1,9},{5... | collective-permute-start | bytes 122888 | tf_op jit(solution)/shard_map/ppermute | solution.py:370
  22.9 0.8 %copy-done.3 = bf16[16,1280]{1,0:T(8,128)(2,1)S(1)} copy-done((bf16[16,1280]{1,0:T(8,128)(2,1)S(1)}, bf16[16,1280]{1,0:T(8,128)(2,1)}, u32[]{:S(2)}) %copy-start.3) | copy-done | bytes 40984
  23.8 1.2 %collective-permute-done.6.refs_3_ = bf16[1,16,1280]{2,1,0:T(8,128)(2,1)S(1)} collective-permute-done((bf16[1,16,1280]{2,1,0:T(8,128)(2,1)}, bf16[1,16,1280]{2,1,0:T(8,128)(2,1)S(1)}, u32[]{:S(2)}, u32[]{:S(2)}) %collective-permute-start.6) | collective-permute-done | bytes 40992 | tf_op jit(solution)/shard_map/ppermute | solution.py:370
  24.9 2.5 %collective-permute-done.5.refs_2_ = bf16[1,16,1280]{2,1,0:T(8,128)(2,1)S(1)} collective-permute-done((bf16[1,16,1280]{2,1,0:T(8,128)(2,1)}, bf16[1,16,1280]{2,1,0:T(8,128)(2,1)S(1)}, u32[]{:S(2)}, u32[]{:S(2)}) %collective-permute-start.5) | collective-permute-done | bytes 40992 | tf_op jit(solution)/shard_map/ppermute | solution.py:370
  27.4 0.0 collective-permute-done.4.refs_1_
  27.4 0.0 collective-permute-start.13
  27.4 1.6 %collective-permute-start.7 = (bf16[4,16,1280]{2,1,0:T(8,128)(2,1)S(1)}, bf16[4,16,1280]{2,1,0:T(8,128)(2,1)S(1)}, u32[]{:S(2)}, u32[]{:S(2)}) collective-permute-start(bf16[4,16,1280]{2,1,0:T(8,128)(2,1)S(1)} %shard_map.112.refs_0_), channel_id=1, source_target_pairs={{0,4},{4,0},{8,12},{12,8},{16,20},{20,16},{24,28},{28,24},{1,5},{5... | collective-permute-start | bytes 491528 | tf_op jit(solution)/shard_map/ppermute | solution.py:370
  29.0 3.8 %collective-permute-done.7.refs_1_ = bf16[4,16,1280]{2,1,0:T(8,128)(2,1)S(1)} collective-permute-done((bf16[4,16,1280]{2,1,0:T(8,128)(2,1)S(1)}, bf16[4,16,1280]{2,1,0:T(8,128)(2,1)S(1)}, u32[]{:S(2)}, u32[]{:S(2)}) %collective-permute-start.7) | collective-permute-done | bytes 163872 | tf_op jit(solution)/shard_map/ppermute | solution.py:370
  32.9 0.0 collective-permute-done.8.refs_6_
  32.9 1.6 %collective-permute-start.10 = (bf16[8,16,1280]{2,1,0:T(8,128)(2,1)S(1)}, bf16[8,16,1280]{2,1,0:T(8,128)(2,1)S(1)}, u32[]{:S(2)}, u32[]{:S(2)}) collective-permute-start(bf16[8,16,1280]{2,1,0:T(8,128)(2,1)S(1)} %shard_map.113.refs_0_), channel_id=1, source_target_pairs={{0,2},{1,3},{2,0},{3,1},{4,6},{5,7},{6,4},{7,5},{8,10},{9,11},{10,... | collective-permute-start | bytes 983048 | tf_op jit(solution)/shard_map/ppermute | solution.py:370
  34.4 0.5 %collective-permute-start.14 = (bf16[256,1024]{1,0:T(8,128)(2,1)S(1)}, bf16[256,1024]{1,0:T(8,128)(2,1)S(1)}, u32[]{:S(2)}, u32[]{:S(2)}) collective-permute-start(bf16[256,1024]{1,0:T(8,128)(2,1)S(1)} %collective-permute-done.3.refs_4_), channel_id=1, source_target_pairs={{0,1},{1,0},{2,3},{3,2},{4,5},{5,4},{6,7},{7,6},{8,9},{9,8},{10,11... | collective-permute-start | bytes 1572872 | tf_op jit(solution)/shard_map/ppermute | solution.py:370
  34.9 4.1 %collective-permute-done.13.refs_5_ = bf16[256,1024]{1,0:T(8,128)(2,1)S(1)} collective-permute-done((bf16[256,1024]{1,0:T(8,128)(2,1)S(1)}, bf16[256,1024]{1,0:T(8,128)(2,1)S(1)}, u32[]{:S(2)}, u32[]{:S(2)}) %collective-permute-start.13) | collective-permute-done | bytes 524320 | tf_op jit(solution)/shard_map/ppermute | solution.py:370
  39.0 0.0 collective-permute-start.15
  39.0 0.5 %collective-permute-start.9 = (bf16[8,16,1280]{2,1,0:T(8,128)(2,1)S(1)}, bf16[8,16,1280]{2,1,0:T(8,128)(2,1)S(1)}, u32[]{:S(2)}, u32[]{:S(2)}) collective-permute-start(bf16[8,16,1280]{2,1,0:T(8,128)(2,1)S(1)} %shard_map.113.refs_0_), channel_id=1, source_target_pairs={{0,1},{1,0},{2,3},{3,2},{4,5},{5,4},{6,7},{7,6},{8,9},{9,8},{10,11... | collective-permute-start | bytes 983048 | tf_op jit(solution)/shard_map/ppermute | solution.py:370
  39.5 0.5 collective-permute-done.10.refs_2_
  40.0 0.0 collective-permute-start.11
  40.0 1.4 %collective-permute-done.9.refs_1_ = bf16[8,16,1280]{2,1,0:T(8,128)(2,1)S(1)} collective-permute-done((bf16[8,16,1280]{2,1,0:T(8,128)(2,1)S(1)}, bf16[8,16,1280]{2,1,0:T(8,128)(2,1)S(1)}, u32[]{:S(2)}, u32[]{:S(2)}) %collective-permute-start.9) | collective-permute-done | bytes 327712 | tf_op jit(solution)/shard_map/ppermute | solution.py:370
  41.4 0.0 collective-permute-done.12.refs_7_
  41.4 0.5 collective-permute-done.11.refs_3_
  41.9 1.1 %shard_map.114 = (bf16[2,192,1024]{2,1,0:T(8,128)(2,1)S(1)}, bf16[192,1024]{1,0:T(8,128)(2,1)S(1)}, bf16[192,256]{1,0:T(8,128)(2,1)S(1)}, bf16[192,192]{1,0:T(8,128)(2,1)S(1)}, f32[192,128]{1,0:T(8,128)S(1)}) custom-call(bf16[8,16,1280]{2,1,0:T(8,128)(2,1)S(1)} %shard_map.113.refs_0_, bf16[8,16,1280]{2,1,0:T(8,128)(2,1)S(1)} %collective-permute-done.9.refs_1_, ...), custom_call_target="tpu_custom_call" | custom-call | flops 805306368 | bytes 4194304 | tf_op jit(solution)/shard_map/pallas_call | solution.py:267
  43.0 0.0 collective-permute-done.14.refs_6_
  43.0 6.2 %shard_map.115 = (bf16[24,256]{1,0:T(8,128)(2,1)}, bf16[24,256]{1,0:T(8,128)(2,1)}, f32[256,1024]{1,0:T(8,128)}, f32[256,1024]{1,0:T(8,128)}, f32[256,1024]{1,0:T(8,128)}) custom-call(bf16[2,192,1024]{2,1,0:T(8,128)(2,1)S(1)} %get-tuple-element.35.both, bf16[192,1024]{1,0:T(8,128)(2,1)S(1)} %get-tuple-element.36.cot, ...), custom_call_target="tpu_custom_call" | custom-call | flops 2013265920 | bytes 8388608 | tf_op jit(solution)/shard_map/pallas_call | solution.py:287
  (15 shorter events, 0.1 us)
Async XLA Ops:
  0.6 17.5 %collective-permute-start = (bf16[256,1024]{1,0:T(8,128)(2,1)}, bf16[256,1024]{1,0:T(8,128)(2,1)S(1)}, u32[]{:S(2)}, u32[]{:S(2)}) collective-permute-start(bf16[256,1024]{1,0:T(8,128)(2,1)} %refs_4_.1), channel_id=1, source_target_pairs={{0,1},{1,0},{2,3},{3,2},{4,5},{5,4},{6,7},{7,6},{8,9},{9,8},{10,11... | collective-permute-start | bytes 1572872 | tf_op jit(solution)/shard_map/ppermute | solution.py:370
  1.1 17.0 %collective-permute-start.1 = (bf16[256,1024]{1,0:T(8,128)(2,1)}, bf16[256,1024]{1,0:T(8,128)(2,1)S(1)}, u32[]{:S(2)}, u32[]{:S(2)}) collective-permute-start(bf16[256,1024]{1,0:T(8,128)(2,1)} %refs_0_.1), channel_id=1, source_target_pairs={{0,1},{1,0},{2,3},{3,2},{4,5},{5,4},{6,7},{7,6},{8,9},{9,8},{10,11... | collective-permute-start | bytes 1572872 | tf_op jit(solution)/shard_map/ppermute | solution.py:370
  1.2 17.0 %collective-permute-start.2 = (bf16[256,1024]{1,0:T(8,128)(2,1)}, bf16[256,1024]{1,0:T(8,128)(2,1)S(1)}, u32[]{:S(2)}, u32[]{:S(2)}) collective-permute-start(bf16[256,1024]{1,0:T(8,128)(2,1)} %refs_1_.1), channel_id=1, source_target_pairs={{0,1},{1,0},{2,3},{3,2},{4,5},{5,4},{6,7},{7,6},{8,9},{9,8},{10,11... | collective-permute-start | bytes 1572872 | tf_op jit(solution)/shard_map/ppermute | solution.py:370
  2.8 15.4 %collective-permute-start.3 = (bf16[256,1024]{1,0:T(8,128)(2,1)S(1)}, bf16[256,1024]{1,0:T(8,128)(2,1)S(1)}, u32[]{:S(2)}, u32[]{:S(2)}) collective-permute-start(bf16[256,1024]{1,0:T(8,128)(2,1)S(1)} %broadcast_select_fusion), channel_id=1, source_target_pairs={{0,2},{1,3},{2,0},{3,1},{4,6},{5,7},{6,4},{7,5},{8,10},{9,11},{10,... | collective-permute-start | bytes 1572872 | tf_op jit(solution)/shard_map/ppermute | solution.py:370
  5.4 27.5 %collective-permute-start.8 = (bf16[256,1024]{1,0:T(8,128)(2,1)}, bf16[256,1024]{1,0:T(8,128)(2,1)S(1)}, u32[]{:S(2)}, u32[]{:S(2)}) collective-permute-start(bf16[256,1024]{1,0:T(8,128)(2,1)} %refs_4_.1), channel_id=1, source_target_pairs={{0,2},{1,3},{2,0},{3,1},{4,6},{5,7},{6,4},{7,5},{8,10},{9,11},{10,... | collective-permute-start | bytes 1572872 | tf_op jit(solution)/shard_map/ppermute | solution.py:370
  5.5 36.4 %copy-start.2 = (bf16[256,1024]{1,0:T(8,128)(2,1)S(1)}, bf16[256,1024]{1,0:T(8,128)(2,1)}, u32[]{:S(2)}) copy-start(bf16[256,1024]{1,0:T(8,128)(2,1)} %refs_4_.1) | copy-start | bytes 1572868
  5.5 37.5 %copy-start = (bf16[256,1024]{1,0:T(8,128)(2,1)S(1)}, bf16[256,1024]{1,0:T(8,128)(2,1)}, u32[]{:S(2)}) copy-start(bf16[256,1024]{1,0:T(8,128)(2,1)} %refs_0_.1) | copy-start | bytes 1572868
  5.5 37.5 %copy-start.1 = (bf16[256,1024]{1,0:T(8,128)(2,1)S(1)}, bf16[256,1024]{1,0:T(8,128)(2,1)}, u32[]{:S(2)}) copy-start(bf16[256,1024]{1,0:T(8,128)(2,1)} %refs_1_.1) | copy-start | bytes 1572868
  18.2 6.7 %collective-permute-start.6 = (bf16[1,16,1280]{2,1,0:T(8,128)(2,1)}, bf16[1,16,1280]{2,1,0:T(8,128)(2,1)S(1)}, u32[]{:S(2)}, u32[]{:S(2)}) collective-permute-start(bf16[1,16,1280]{2,1,0:T(8,128)(2,1)} %bitcast.2), channel_id=1, source_target_pairs={{0,24},{4,28},{8,16},{12,20},{16,8},{20,12},{24,0},{28,4},{1,25},{... | collective-permute-start | bytes 122888 | tf_op jit(solution)/shard_map/ppermute | solution.py:370
  22.3 5.1 %collective-permute-start.5 = (bf16[1,16,1280]{2,1,0:T(8,128)(2,1)}, bf16[1,16,1280]{2,1,0:T(8,128)(2,1)S(1)}, u32[]{:S(2)}, u32[]{:S(2)}) collective-permute-start(bf16[1,16,1280]{2,1,0:T(8,128)(2,1)} %bitcast.3), channel_id=1, source_target_pairs={{0,16},{4,20},{8,24},{12,28},{16,0},{20,4},{24,8},{28,12},{1,17},{... | collective-permute-start | bytes 122888 | tf_op jit(solution)/shard_map/ppermute | solution.py:370
  22.3 5.1 %collective-permute-start.4 = (bf16[1,16,1280]{2,1,0:T(8,128)(2,1)}, bf16[1,16,1280]{2,1,0:T(8,128)(2,1)S(1)}, u32[]{:S(2)}, u32[]{:S(2)}) collective-permute-start(bf16[1,16,1280]{2,1,0:T(8,128)(2,1)} %bitcast.4), channel_id=1, source_target_pairs={{0,8},{4,12},{8,0},{12,4},{16,24},{20,28},{24,16},{28,20},{1,9},{5... | collective-permute-start | bytes 122888 | tf_op jit(solution)/shard_map/ppermute | solution.py:370
  22.9 0.8 %copy-start.3 = (bf16[16,1280]{1,0:T(8,128)(2,1)S(1)}, bf16[16,1280]{1,0:T(8,128)(2,1)}, u32[]{:S(2)}) copy-start(bf16[16,1280]{1,0:T(8,128)(2,1)} %shard_map.110) | copy-start | bytes 122884
  27.4 11.6 %collective-permute-start.13 = (bf16[256,1024]{1,0:T(8,128)(2,1)S(1)}, bf16[256,1024]{1,0:T(8,128)(2,1)S(1)}, u32[]{:S(2)}, u32[]{:S(2)}) collective-permute-start(bf16[256,1024]{1,0:T(8,128)(2,1)S(1)} %collective-permute-done.3.refs_4_), channel_id=1, source_target_pairs={{0,8},{4,12},{8,0},{12,4},{16,24},{20,28},{24,16},{28,20},{1,9},{5... | collective-permute-start | bytes 1572872 | tf_op jit(solution)/shard_map/ppermute | solution.py:370
  27.4 5.4 %collective-permute-start.7 = (bf16[4,16,1280]{2,1,0:T(8,128)(2,1)S(1)}, bf16[4,16,1280]{2,1,0:T(8,128)(2,1)S(1)}, u32[]{:S(2)}, u32[]{:S(2)}) collective-permute-start(bf16[4,16,1280]{2,1,0:T(8,128)(2,1)S(1)} %shard_map.112.refs_0_), channel_id=1, source_target_pairs={{0,4},{4,0},{8,12},{12,8},{16,20},{20,16},{24,28},{28,24},{1,5},{5... | collective-permute-start | bytes 491528 | tf_op jit(solution)/shard_map/ppermute | solution.py:370
  32.9 7.1 %collective-permute-start.10 = (bf16[8,16,1280]{2,1,0:T(8,128)(2,1)S(1)}, bf16[8,16,1280]{2,1,0:T(8,128)(2,1)S(1)}, u32[]{:S(2)}, u32[]{:S(2)}) collective-permute-start(bf16[8,16,1280]{2,1,0:T(8,128)(2,1)S(1)} %shard_map.113.refs_0_), channel_id=1, source_target_pairs={{0,2},{1,3},{2,0},{3,1},{4,6},{5,7},{6,4},{7,5},{8,10},{9,11},{10,... | collective-permute-start | bytes 983048 | tf_op jit(solution)/shard_map/ppermute | solution.py:370
  34.4 7.0 %collective-permute-start.12 = (bf16[256,1024]{1,0:T(8,128)(2,1)S(1)}, bf16[256,1024]{1,0:T(8,128)(2,1)S(1)}, u32[]{:S(2)}, u32[]{:S(2)}) collective-permute-start(bf16[256,1024]{1,0:T(8,128)(2,1)S(1)} %collective-permute-done.8.refs_6_), channel_id=1, source_target_pairs={{0,1},{1,0},{2,3},{3,2},{4,5},{5,4},{6,7},{7,6},{8,9},{9,8},{10,11... | collective-permute-start | bytes 1572872 | tf_op jit(solution)/shard_map/ppermute | solution.py:370
  34.4 8.5 %collective-permute-start.14 = (bf16[256,1024]{1,0:T(8,128)(2,1)S(1)}, bf16[256,1024]{1,0:T(8,128)(2,1)S(1)}, u32[]{:S(2)}, u32[]{:S(2)}) collective-permute-start(bf16[256,1024]{1,0:T(8,128)(2,1)S(1)} %collective-permute-done.3.refs_4_), channel_id=1, source_target_pairs={{0,1},{1,0},{2,3},{3,2},{4,5},{5,4},{6,7},{7,6},{8,9},{9,8},{10,11... | collective-permute-start | bytes 1572872 | tf_op jit(solution)/shard_map/ppermute | solution.py:370
  39.0 3.9 %collective-permute-start.15 = (bf16[256,1024]{1,0:T(8,128)(2,1)S(1)}, bf16[256,1024]{1,0:T(8,128)(2,1)S(1)}, u32[]{:S(2)}, u32[]{:S(2)}) collective-permute-start(bf16[256,1024]{1,0:T(8,128)(2,1)S(1)} %collective-permute-done.13.refs_5_), channel_id=1, source_target_pairs={{0,1},{1,0},{2,3},{3,2},{4,5},{5,4},{6,7},{7,6},{8,9},{9,8},{10,11... | collective-permute-start | bytes 1572872 | tf_op jit(solution)/shard_map/ppermute | solution.py:370
  39.0 2.4 %collective-permute-start.9 = (bf16[8,16,1280]{2,1,0:T(8,128)(2,1)S(1)}, bf16[8,16,1280]{2,1,0:T(8,128)(2,1)S(1)}, u32[]{:S(2)}, u32[]{:S(2)}) collective-permute-start(bf16[8,16,1280]{2,1,0:T(8,128)(2,1)S(1)} %shard_map.113.refs_0_), channel_id=1, source_target_pairs={{0,1},{1,0},{2,3},{3,2},{4,5},{5,4},{6,7},{7,6},{8,9},{9,8},{10,11... | collective-permute-start | bytes 983048 | tf_op jit(solution)/shard_map/ppermute | solution.py:370
  40.0 1.9 %collective-permute-start.11 = (bf16[8,16,1280]{2,1,0:T(8,128)(2,1)S(1)}, bf16[8,16,1280]{2,1,0:T(8,128)(2,1)S(1)}, u32[]{:S(2)}, u32[]{:S(2)}) collective-permute-start(bf16[8,16,1280]{2,1,0:T(8,128)(2,1)S(1)} %collective-permute-done.10.refs_2_), channel_id=1, source_target_pairs={{0,1},{1,0},{2,3},{3,2},{4,5},{5,4},{6,7},{7,6},{8,9},{9,8},{10,11... | collective-permute-start | bytes 983048 | tf_op jit(solution)/shard_map/ppermute | solution.py:370

commit v16 on v15

--- a/solution.py
+++ b/solution.py
@@ -17,6 +17,7 @@
 TOP = 16
 LOG2E = 1.4426950408889634
 ATTENTION_VMEM = 58
+COPIES = 4
 MIB = 1 << 20
 
 
@@ -59,16 +60,30 @@
     node_dev = cot_ref.shape[0]
     cols = heads * HD
 
+    some, deep = nodes // COPIES, width // COPIES
+
     def fetch(i):
-        source = texts_ref.at[pl.ds(i * nodes, nodes)]
-        return pltpu.make_async_copy(source, held.at[i % 2], sem.at[i % 2])
+        return [
+            pltpu.make_async_copy(
+                texts_ref.at[pl.ds(i * nodes + c * some, some)],
+                held.at[i % 2, pl.ds(c * some, some)],
+                sem.at[i % 2, c],
+            )
+            for c in range(COPIES)
+        ]
 
     @pl.when(step == 0)
     def _():
-        weights = pltpu.make_async_copy(w_hbm, w_ref, sem.at[2])
-        weights.start()
-        fetch(0).start()
-        weights.wait()
+        weights = [
+            pltpu.make_async_copy(
+                w_hbm.at[pl.ds(c * deep, deep)], w_ref.at[pl.ds(c * deep, deep)], sem.at[2, c]
+            )
+            for c in range(COPIES)
+        ]
+        for copy in weights + fetch(0):
+            copy.start()
+        for copy in weights:
+            copy.wait()
         for part in range(3):
             for h in range(0, heads, 2):
                 a = h * 3 * HD + part * HD
@@ -79,9 +94,11 @@
 
     @pl.when(step + 1 < pl.num_programs(0))
     def _():
-        fetch(step + 1).start()
-
-    fetch(step).wait()
+        for copy in fetch(step + 1):
+            copy.start()
+
+    for copy in fetch(step):
+        copy.wait()
     x_ref = held.at[step % 2]
     own = pl.ds(pl.multiple_of(lax.axis_index("mp") * cols, 128), cols)
     qkv = dot(x_ref[...].reshape(nodes * seq, width), wp[...]).astype(BF)
@@ -146,7 +163,7 @@
             pltpu.VMEM((node_dev, cols), F32),
             pltpu.VMEM((2, nodes, seq, width), BF),
             pltpu.VMEM((width, 3 * cols), BF),
-            pltpu.SemaphoreType.DMA((3,)),
+            pltpu.SemaphoreType.DMA((3, COPIES)),
         ],
         compiler_params=pltpu.CompilerParams(vmem_limit_bytes=ATTENTION_VMEM * MIB),
         cost_estimate=pl.CostEstimate(
@@ -398,7 +415,7 @@
     here = tuple(hop(a, "mp", 1) for a in own)
 
     sent = attention(texts, w_qkv, cotangent, neighbours.T)[None]
-    sent, here, x_half = lax.optimization_barrier((sent, here, x_half))
+    sent, here = lax.optimization_barrier((sent, here))
     sent, order, x_half = gather_dp(sent, x_half)
     sent, x_out = lax.optimization_barrier((sent, x_out))
     z_half = hop(x_half, "dp", 2)

time: 49.5 us -> 48.8 us (0.986)
  waiting for transfers between devices: 15.3 us -> 14.4 us
    ppermute x16, waiting for transfers between devices: 15.3 us -> 14.4 us  [hop(): lax.ppermute(x, axis, [(i, i ^ bit) for i in range(lax.axis_size(axis))])]
  transfers between devices with their start and end apart: 16 -> 16, of which waited for: 8 -> 7; matrix products, arithmetic and copies ran while one was open for 2% -> 2% of each run, Pallas kernels for 25% -> 26%
where the time goes in v16:
time: 48.8 us; the launch traced here: 48.6 us
  Pallas kernels  18.6 us (38%)
  waiting for transfers between devices  14.4 us (30%)
  starting transfers between devices  12.9 us (26%)
  other arithmetic  1.1 us (2%)
  local copies, waits for them, and re-layouts  0.82 us (2%)
  between operations  0.74 us (2%)
    ppermute x16, waiting for transfers between devices, hop(): lax.ppermute(x, axis, [(i, i ^ bit) for i in range(lax.axis_size(axis))])  14.4 us
    ppermute x16, starting transfers between devices, hop(): lax.ppermute(x, axis, [(i, i ^ bit) for i in range(lax.axis_size(axis))])  12.9 us
    pallas_call x1, Pallas kernels, attention(): pl.pallas_call(functools.partial(attention_kernel, heads), out_shape=jax....  11.3 us
    pallas_call x1, Pallas kernels, graph(): pl.pallas_call(functools.partial(graph_kernel, node_dev), out_shape=(slab...  6.22 us
    select_n x1, other arithmetic, per_device(): jnp.where(even, w_self, w_neigh)  1.1 us
    pallas_call x1, Pallas kernels, graph(): pl.pallas_call(functools.partial(embed_kernel, order, fan, node_dev), out...  1.07 us
  transfers between devices with their start and end apart: 16, of which 7 were waited for; matrix products, arithmetic and copies ran while one was open for 2% of the time, Pallas kernels for 26%

profile of v16, /device:TPU:0, one launch (start us, length us, event | category | flops | bytes accessed | tf_op | source)
XLA Modules:
  0.0 48.6 jit_solution(12229501992790832559)
XLA Ops:
  0.6 0.5 %collective-permute-start = (bf16[256,1024]{1,0:T(8,128)(2,1)}, bf16[256,1024]{1,0:T(8,128)(2,1)S(1)}, u32[]{:S(2)}, u32[]{:S(2)}) collective-permute-start(bf16[256,1024]{1,0:T(8,128)(2,1)} %refs_4_.1), channel_id=1, source_target_pairs={{0,1},{1,0},{2,3},{3,2},{4,5},{5,4},{6,7},{7,6},{8,9},{9,8},{10,11... | collective-permute-start | bytes 1572872 | tf_op jit(solution)/shard_map/ppermute | solution.py:387
  1.1 0.1 collective-permute-start.1
  1.2 0.4 collective-permute-start.2
  1.7 1.1 %broadcast_select_fusion = bf16[256,1024]{1,0:T(8,128)(2,1)S(1)} fusion(bf16[256,1024]{1,0:T(8,128)(2,1)} %refs_0_.1, bf16[256,1024]{1,0:T(8,128)(2,1)} %refs_1_.1, pred[]{:T(512)S(6)} %eq.5), kind=kLoop, calls=%fused_computation | loop fusion | flops 262144 | bytes 1572865 | tf_op jit(solution)/shard_map/jit(_where)/select_n | solution.py:412
  2.8 2.6 %collective-permute-start.6 = (bf16[256,1024]{1,0:T(8,128)(2,1)S(1)}, bf16[256,1024]{1,0:T(8,128)(2,1)S(1)}, u32[]{:S(2)}, u32[]{:S(2)}) collective-permute-start(bf16[256,1024]{1,0:T(8,128)(2,1)S(1)} %broadcast_select_fusion), channel_id=1, source_target_pairs={{0,2},{1,3},{2,0},{3,1},{4,6},{5,7},{6,4},{7,5},{8,10},{9,11},{10,... | collective-permute-start | bytes 1572872 | tf_op jit(solution)/shard_map/ppermute | solution.py:387
  5.4 0.1 collective-permute-start.8
  5.5 11.3 %shard_map.110 = bf16[16,1280]{1,0:T(8,128)(2,1)} custom-call(bf16[24,128,1024]{2,1,0:T(8,128)(2,1)} %texts_ref.1, bf16[1024,768]{1,0:T(8,128)(2,1)} %w_hbm.1, bf16[24,256]{1,0:T(8,128)(2,1)} %cot_ref.1, s32[16,24]{1,0:T(8,128)} %bitcast.6), custom_call_target="tpu_custom_call" | custom-call | flops 5637144576 | bytes 7864320 | tf_op jit(solution)/shard_map/pallas_call | solution.py:149
  16.8 0.0 collective-permute-done.1.refs_2_
  16.8 0.0 collective-permute-done.2.refs_3_
  16.8 4.1 %collective-permute-start.5 = (bf16[1,16,1280]{2,1,0:T(8,128)(2,1)}, bf16[1,16,1280]{2,1,0:T(8,128)(2,1)S(1)}, u32[]{:S(2)}, u32[]{:S(2)}) collective-permute-start(bf16[1,16,1280]{2,1,0:T(8,128)(2,1)} %bitcast.2), channel_id=1, source_target_pairs={{0,24},{4,28},{8,16},{12,20},{16,8},{20,12},{24,0},{28,4},{1,25},{... | collective-permute-start | bytes 122888 | tf_op jit(solution)/shard_map/ppermute | solution.py:387
  21.0 0.0 collective-permute-start.4
  21.0 0.6 %collective-permute-start.3 = (bf16[1,16,1280]{2,1,0:T(8,128)(2,1)}, bf16[1,16,1280]{2,1,0:T(8,128)(2,1)S(1)}, u32[]{:S(2)}, u32[]{:S(2)}) collective-permute-start(bf16[1,16,1280]{2,1,0:T(8,128)(2,1)} %bitcast.4), channel_id=1, source_target_pairs={{0,8},{4,12},{8,0},{12,4},{16,24},{20,28},{24,16},{28,20},{1,9},{5... | collective-permute-start | bytes 122888 | tf_op jit(solution)/shard_map/ppermute | solution.py:387
  21.6 0.8 %copy-done.3 = bf16[16,1280]{1,0:T(8,128)(2,1)S(1)} copy-done((bf16[16,1280]{1,0:T(8,128)(2,1)S(1)}, bf16[16,1280]{1,0:T(8,128)(2,1)}, u32[]{:S(2)}) %copy-start.3) | copy-done | bytes 40984
  22.4 0.8 %collective-permute-done.5.refs_3_ = bf16[1,16,1280]{2,1,0:T(8,128)(2,1)S(1)} collective-permute-done((bf16[1,16,1280]{2,1,0:T(8,128)(2,1)}, bf16[1,16,1280]{2,1,0:T(8,128)(2,1)S(1)}, u32[]{:S(2)}, u32[]{:S(2)}) %collective-permute-start.5) | collective-permute-done | bytes 40992 | tf_op jit(solution)/shard_map/ppermute | solution.py:387
  23.2 2.9 %collective-permute-done.4.refs_2_ = bf16[1,16,1280]{2,1,0:T(8,128)(2,1)S(1)} collective-permute-done((bf16[1,16,1280]{2,1,0:T(8,128)(2,1)}, bf16[1,16,1280]{2,1,0:T(8,128)(2,1)S(1)}, u32[]{:S(2)}, u32[]{:S(2)}) %collective-permute-start.4) | collective-permute-done | bytes 40992 | tf_op jit(solution)/shard_map/ppermute | solution.py:387
  26.1 0.0 collective-permute-done.3.refs_1_
  26.1 0.2 collective-permute-start.13
  26.3 1.6 %collective-permute-start.7 = (bf16[4,16,1280]{2,1,0:T(8,128)(2,1)S(1)}, bf16[4,16,1280]{2,1,0:T(8,128)(2,1)S(1)}, u32[]{:S(2)}, u32[]{:S(2)}) collective-permute-start(bf16[4,16,1280]{2,1,0:T(8,128)(2,1)S(1)} %shard_map.112.refs_0_), channel_id=1, source_target_pairs={{0,4},{4,0},{8,12},{12,8},{16,20},{20,16},{24,28},{28,24},{1,5},{5... | collective-permute-start | bytes 491528 | tf_op jit(solution)/shard_map/ppermute | solution.py:387
  27.9 3.8 %collective-permute-done.7.refs_1_ = bf16[4,16,1280]{2,1,0:T(8,128)(2,1)S(1)} collective-permute-done((bf16[4,16,1280]{2,1,0:T(8,128)(2,1)S(1)}, bf16[4,16,1280]{2,1,0:T(8,128)(2,1)S(1)}, u32[]{:S(2)}, u32[]{:S(2)}) %collective-permute-start.7) | collective-permute-done | bytes 163872 | tf_op jit(solution)/shard_map/ppermute | solution.py:387
  31.7 1.6 %collective-permute-start.10 = (bf16[8,16,1280]{2,1,0:T(8,128)(2,1)S(1)}, bf16[8,16,1280]{2,1,0:T(8,128)(2,1)S(1)}, u32[]{:S(2)}, u32[]{:S(2)}) collective-permute-start(bf16[8,16,1280]{2,1,0:T(8,128)(2,1)S(1)} %shard_map.113.refs_0_), channel_id=1, source_target_pairs={{0,2},{1,3},{2,0},{3,1},{4,6},{5,7},{6,4},{7,5},{8,10},{9,11},{10,... | collective-permute-start | bytes 983048 | tf_op jit(solution)/shard_map/ppermute | solution.py:387
  33.3 0.0 collective-permute-start.12
  33.3 0.5 %collective-permute-start.14 = (bf16[256,1024]{1,0:T(8,128)(2,1)S(1)}, bf16[256,1024]{1,0:T(8,128)(2,1)S(1)}, u32[]{:S(2)}, u32[]{:S(2)}) collective-permute-start(bf16[256,1024]{1,0:T(8,128)(2,1)S(1)} %collective-permute-done.6.refs_4_), channel_id=1, source_target_pairs={{0,1},{1,0},{2,3},{3,2},{4,5},{5,4},{6,7},{7,6},{8,9},{9,8},{10,11... | collective-permute-start | bytes 1572872 | tf_op jit(solution)/shard_map/ppermute | solution.py:387
  33.8 4.6 %collective-permute-done.13.refs_5_ = bf16[256,1024]{1,0:T(8,128)(2,1)S(1)} collective-permute-done((bf16[256,1024]{1,0:T(8,128)(2,1)S(1)}, bf16[256,1024]{1,0:T(8,128)(2,1)S(1)}, u32[]{:S(2)}, u32[]{:S(2)}) %collective-permute-start.13) | collective-permute-done | bytes 524320 | tf_op jit(solution)/shard_map/ppermute | solution.py:387
  38.4 0.0 collective-permute-start.15
  38.4 0.5 %collective-permute-start.9 = (bf16[8,16,1280]{2,1,0:T(8,128)(2,1)S(1)}, bf16[8,16,1280]{2,1,0:T(8,128)(2,1)S(1)}, u32[]{:S(2)}, u32[]{:S(2)}) collective-permute-start(bf16[8,16,1280]{2,1,0:T(8,128)(2,1)S(1)} %shard_map.113.refs_0_), channel_id=1, source_target_pairs={{0,1},{1,0},{2,3},{3,2},{4,5},{5,4},{6,7},{7,6},{8,9},{9,8},{10,11... | collective-permute-start | bytes 983048 | tf_op jit(solution)/shard_map/ppermute | solution.py:387
  38.9 0.1 collective-permute-done.10.refs_2_
  39.0 0.0 collective-permute-start.11
  39.0 1.7 %collective-permute-done.9.refs_1_ = bf16[8,16,1280]{2,1,0:T(8,128)(2,1)S(1)} collective-permute-done((bf16[8,16,1280]{2,1,0:T(8,128)(2,1)S(1)}, bf16[8,16,1280]{2,1,0:T(8,128)(2,1)S(1)}, u32[]{:S(2)}, u32[]{:S(2)}) %collective-permute-start.9) | collective-permute-done | bytes 327712 | tf_op jit(solution)/shard_map/ppermute | solution.py:387
  40.8 0.0 collective-permute-done.12.refs_7_
  40.8 0.5 collective-permute-done.11.refs_3_
  41.2 1.1 %shard_map.114 = (bf16[2,192,1024]{2,1,0:T(8,128)(2,1)S(1)}, bf16[192,1024]{1,0:T(8,128)(2,1)S(1)}, bf16[192,256]{1,0:T(8,128)(2,1)S(1)}, bf16[192,192]{1,0:T(8,128)(2,1)S(1)}, f32[192,128]{1,0:T(8,128)S(1)}) custom-call(bf16[8,16,1280]{2,1,0:T(8,128)(2,1)S(1)} %shard_map.113.refs_0_, bf16[8,16,1280]{2,1,0:T(8,128)(2,1)S(1)} %collective-permute-done.9.refs_1_, ...), custom_call_target="tpu_custom_call" | custom-call | flops 805306368 | bytes 4194304 | tf_op jit(solution)/shard_map/pallas_call | solution.py:284
  42.3 6.2 %shard_map.115 = (bf16[24,256]{1,0:T(8,128)(2,1)}, bf16[24,256]{1,0:T(8,128)(2,1)}, f32[256,1024]{1,0:T(8,128)}, f32[256,1024]{1,0:T(8,128)}, f32[256,1024]{1,0:T(8,128)}) custom-call(bf16[2,192,1024]{2,1,0:T(8,128)(2,1)S(1)} %get-tuple-element.33.both, bf16[192,1024]{1,0:T(8,128)(2,1)S(1)} %get-tuple-element.34.cot, ...), custom_call_target="tpu_custom_call" | custom-call | flops 2013265920 | bytes 8388608 | tf_op jit(solution)/shard_map/pallas_call | solution.py:304
  (15 shorter events, 0.1 us)
Async XLA Ops:
  0.6 16.2 %collective-permute-start = (bf16[256,1024]{1,0:T(8,128)(2,1)}, bf16[256,1024]{1,0:T(8,128)(2,1)S(1)}, u32[]{:S(2)}, u32[]{:S(2)}) collective-permute-start(bf16[256,1024]{1,0:T(8,128)(2,1)} %refs_4_.1), channel_id=1, source_target_pairs={{0,1},{1,0},{2,3},{3,2},{4,5},{5,4},{6,7},{7,6},{8,9},{9,8},{10,11... | collective-permute-start | bytes 1572872 | tf_op jit(solution)/shard_map/ppermute | solution.py:387
  1.1 15.7 %collective-permute-start.1 = (bf16[256,1024]{1,0:T(8,128)(2,1)}, bf16[256,1024]{1,0:T(8,128)(2,1)S(1)}, u32[]{:S(2)}, u32[]{:S(2)}) collective-permute-start(bf16[256,1024]{1,0:T(8,128)(2,1)} %refs_0_.1), channel_id=1, source_target_pairs={{0,1},{1,0},{2,3},{3,2},{4,5},{5,4},{6,7},{7,6},{8,9},{9,8},{10,11... | collective-permute-start | bytes 1572872 | tf_op jit(solution)/shard_map/ppermute | solution.py:387
  1.2 15.6 %collective-permute-start.2 = (bf16[256,1024]{1,0:T(8,128)(2,1)}, bf16[256,1024]{1,0:T(8,128)(2,1)S(1)}, u32[]{:S(2)}, u32[]{:S(2)}) collective-permute-start(bf16[256,1024]{1,0:T(8,128)(2,1)} %refs_1_.1), channel_id=1, source_target_pairs={{0,1},{1,0},{2,3},{3,2},{4,5},{5,4},{6,7},{7,6},{8,9},{9,8},{10,11... | collective-permute-start | bytes 1572872 | tf_op jit(solution)/shard_map/ppermute | solution.py:387
  2.8 19.6 %collective-permute-start.6 = (bf16[256,1024]{1,0:T(8,128)(2,1)S(1)}, bf16[256,1024]{1,0:T(8,128)(2,1)S(1)}, u32[]{:S(2)}, u32[]{:S(2)}) collective-permute-start(bf16[256,1024]{1,0:T(8,128)(2,1)S(1)} %broadcast_select_fusion), channel_id=1, source_target_pairs={{0,2},{1,3},{2,0},{3,1},{4,6},{5,7},{6,4},{7,5},{8,10},{9,11},{10,... | collective-permute-start | bytes 1572872 | tf_op jit(solution)/shard_map/ppermute | solution.py:387
  5.4 26.3 %collective-permute-start.8 = (bf16[256,1024]{1,0:T(8,128)(2,1)}, bf16[256,1024]{1,0:T(8,128)(2,1)S(1)}, u32[]{:S(2)}, u32[]{:S(2)}) collective-permute-start(bf16[256,1024]{1,0:T(8,128)(2,1)} %refs_4_.1), channel_id=1, source_target_pairs={{0,2},{1,3},{2,0},{3,1},{4,6},{5,7},{6,4},{7,5},{8,10},{9,11},{10,... | collective-permute-start | bytes 1572872 | tf_op jit(solution)/shard_map/ppermute | solution.py:387
  5.5 35.8 %copy-start.2 = (bf16[256,1024]{1,0:T(8,128)(2,1)S(1)}, bf16[256,1024]{1,0:T(8,128)(2,1)}, u32[]{:S(2)}) copy-start(bf16[256,1024]{1,0:T(8,128)(2,1)} %refs_4_.1) | copy-start | bytes 1572868
  5.5 36.9 %copy-start = (bf16[256,1024]{1,0:T(8,128)(2,1)S(1)}, bf16[256,1024]{1,0:T(8,128)(2,1)}, u32[]{:S(2)}) copy-start(bf16[256,1024]{1,0:T(8,128)(2,1)} %refs_0_.1) | copy-start | bytes 1572868
  5.5 36.9 %copy-start.1 = (bf16[256,1024]{1,0:T(8,128)(2,1)S(1)}, bf16[256,1024]{1,0:T(8,128)(2,1)}, u32[]{:S(2)}) copy-start(bf16[256,1024]{1,0:T(8,128)(2,1)} %refs_1_.1) | copy-start | bytes 1572868
  16.8 6.4 %collective-permute-start.5 = (bf16[1,16,1280]{2,1,0:T(8,128)(2,1)}, bf16[1,16,1280]{2,1,0:T(8,128)(2,1)S(1)}, u32[]{:S(2)}, u32[]{:S(2)}) collective-permute-start(bf16[1,16,1280]{2,1,0:T(8,128)(2,1)} %bitcast.2), channel_id=1, source_target_pairs={{0,24},{4,28},{8,16},{12,20},{16,8},{20,12},{24,0},{28,4},{1,25},{... | collective-permute-start | bytes 122888 | tf_op jit(solution)/shard_map/ppermute | solution.py:387
  21.0 5.1 %collective-permute-start.4 = (bf16[1,16,1280]{2,1,0:T(8,128)(2,1)}, bf16[1,16,1280]{2,1,0:T(8,128)(2,1)S(1)}, u32[]{:S(2)}, u32[]{:S(2)}) collective-permute-start(bf16[1,16,1280]{2,1,0:T(8,128)(2,1)} %bitcast.3), channel_id=1, source_target_pairs={{0,16},{4,20},{8,24},{12,28},{16,0},{20,4},{24,8},{28,12},{1,17},{... | collective-permute-start | bytes 122888 | tf_op jit(solution)/shard_map/ppermute | solution.py:387
  21.0 5.1 %collective-permute-start.3 = (bf16[1,16,1280]{2,1,0:T(8,128)(2,1)}, bf16[1,16,1280]{2,1,0:T(8,128)(2,1)S(1)}, u32[]{:S(2)}, u32[]{:S(2)}) collective-permute-start(bf16[1,16,1280]{2,1,0:T(8,128)(2,1)} %bitcast.4), channel_id=1, source_target_pairs={{0,8},{4,12},{8,0},{12,4},{16,24},{20,28},{24,16},{28,20},{1,9},{5... | collective-permute-start | bytes 122888 | tf_op jit(solution)/shard_map/ppermute | solution.py:387
  21.6 0.8 %copy-start.3 = (bf16[16,1280]{1,0:T(8,128)(2,1)S(1)}, bf16[16,1280]{1,0:T(8,128)(2,1)}, u32[]{:S(2)}) copy-start(bf16[16,1280]{1,0:T(8,128)(2,1)} %shard_map.110) | copy-start | bytes 122884
  26.1 12.3 %collective-permute-start.13 = (bf16[256,1024]{1,0:T(8,128)(2,1)S(1)}, bf16[256,1024]{1,0:T(8,128)(2,1)S(1)}, u32[]{:S(2)}, u32[]{:S(2)}) collective-permute-start(bf16[256,1024]{1,0:T(8,128)(2,1)S(1)} %collective-permute-done.6.refs_4_), channel_id=1, source_target_pairs={{0,8},{4,12},{8,0},{12,4},{16,24},{20,28},{24,16},{28,20},{1,9},{5... | collective-permute-start | bytes 1572872 | tf_op jit(solution)/shard_map/ppermute | solution.py:387
  26.3 5.4 %collective-permute-start.7 = (bf16[4,16,1280]{2,1,0:T(8,128)(2,1)S(1)}, bf16[4,16,1280]{2,1,0:T(8,128)(2,1)S(1)}, u32[]{:S(2)}, u32[]{:S(2)}) collective-permute-start(bf16[4,16,1280]{2,1,0:T(8,128)(2,1)S(1)} %shard_map.112.refs_0_), channel_id=1, source_target_pairs={{0,4},{4,0},{8,12},{12,8},{16,20},{20,16},{24,28},{28,24},{1,5},{5... | collective-permute-start | bytes 491528 | tf_op jit(solution)/shard_map/ppermute | solution.py:387
  31.7 7.3 %collective-permute-start.10 = (bf16[8,16,1280]{2,1,0:T(8,128)(2,1)S(1)}, bf16[8,16,1280]{2,1,0:T(8,128)(2,1)S(1)}, u32[]{:S(2)}, u32[]{:S(2)}) collective-permute-start(bf16[8,16,1280]{2,1,0:T(8,128)(2,1)S(1)} %shard_map.113.refs_0_), channel_id=1, source_target_pairs={{0,2},{1,3},{2,0},{3,1},{4,6},{5,7},{6,4},{7,5},{8,10},{9,11},{10,... | collective-permute-start | bytes 983048 | tf_op jit(solution)/shard_map/ppermute | solution.py:387
  33.3 7.5 %collective-permute-start.12 = (bf16[256,1024]{1,0:T(8,128)(2,1)S(1)}, bf16[256,1024]{1,0:T(8,128)(2,1)S(1)}, u32[]{:S(2)}, u32[]{:S(2)}) collective-permute-start(bf16[256,1024]{1,0:T(8,128)(2,1)S(1)} %collective-permute-done.8.refs_6_), channel_id=1, source_target_pairs={{0,1},{1,0},{2,3},{3,2},{4,5},{5,4},{6,7},{7,6},{8,9},{9,8},{10,11... | collective-permute-start | bytes 1572872 | tf_op jit(solution)/shard_map/ppermute | solution.py:387
  33.3 9.0 %collective-permute-start.14 = (bf16[256,1024]{1,0:T(8,128)(2,1)S(1)}, bf16[256,1024]{1,0:T(8,128)(2,1)S(1)}, u32[]{:S(2)}, u32[]{:S(2)}) collective-permute-start(bf16[256,1024]{1,0:T(8,128)(2,1)S(1)} %collective-permute-done.6.refs_4_), channel_id=1, source_target_pairs={{0,1},{1,0},{2,3},{3,2},{4,5},{5,4},{6,7},{7,6},{8,9},{9,8},{10,11... | collective-permute-start | bytes 1572872 | tf_op jit(solution)/shard_map/ppermute | solution.py:387
  38.4 3.9 %collective-permute-start.15 = (bf16[256,1024]{1,0:T(8,128)(2,1)S(1)}, bf16[256,1024]{1,0:T(8,128)(2,1)S(1)}, u32[]{:S(2)}, u32[]{:S(2)}) collective-permute-start(bf16[256,1024]{1,0:T(8,128)(2,1)S(1)} %collective-permute-done.13.refs_5_), channel_id=1, source_target_pairs={{0,1},{1,0},{2,3},{3,2},{4,5},{5,4},{6,7},{7,6},{8,9},{9,8},{10,11... | collective-permute-start | bytes 1572872 | tf_op jit(solution)/shard_map/ppermute | solution.py:387
  38.4 2.4 %collective-permute-start.9 = (bf16[8,16,1280]{2,1,0:T(8,128)(2,1)S(1)}, bf16[8,16,1280]{2,1,0:T(8,128)(2,1)S(1)}, u32[]{:S(2)}, u32[]{:S(2)}) collective-permute-start(bf16[8,16,1280]{2,1,0:T(8,128)(2,1)S(1)} %shard_map.113.refs_0_), channel_id=1, source_target_pairs={{0,1},{1,0},{2,3},{3,2},{4,5},{5,4},{6,7},{7,6},{8,9},{9,8},{10,11... | collective-permute-start | bytes 983048 | tf_op jit(solution)/shard_map/ppermute | solution.py:387
  39.0 2.2 %collective-permute-start.11 = (bf16[8,16,1280]{2,1,0:T(8,128)(2,1)S(1)}, bf16[8,16,1280]{2,1,0:T(8,128)(2,1)S(1)}, u32[]{:S(2)}, u32[]{:S(2)}) collective-permute-start(bf16[8,16,1280]{2,1,0:T(8,128)(2,1)S(1)} %collective-permute-done.10.refs_2_), channel_id=1, source_target_pairs={{0,1},{1,0},{2,3},{3,2},{4,5},{5,4},{6,7},{7,6},{8,9},{9,8},{10,11... | collective-permute-start | bytes 983048 | tf_op jit(solution)/shard_map/ppermute | solution.py:387

commit v17 on v16

--- a/solution.py
+++ b/solution.py
@@ -419,11 +419,13 @@
     sent, order, x_half = gather_dp(sent, x_half)
     sent, x_out = lax.optimization_barrier((sent, x_out))
     z_half = hop(x_half, "dp", 2)
+    core_sent = hop(sent, "mp", 1)
+    z_half, core_sent = lax.optimization_barrier((z_half, core_sent))
     across = (x_out, x_half, z_half)
     there = tuple(hop(a, "mp", 1) for a in across)
 
     got_across = hop(sent, "mp", 2)
-    got = (sent, hop(sent, "mp", 1), got_across, hop(got_across, "mp", 1))
+    got = (sent, core_sent, got_across, hop(got_across, "mp", 1))
     body = graph if nodes <= WIDE_LIMIT else graph_wide
     return body(order, fan, node_dev, got, (own, here, across, there))
 

time: 48.8 us -> 51.2 us (1.049)
  waiting for transfers between devices: 14.4 us -> 17.1 us
    ppermute x16, waiting for transfers between devices: 14.4 us -> 17.1 us  [hop(): lax.ppermute(x, axis, [(i, i ^ bit) for i in range(lax.axis_size(axis))])]
  transfers between devices with their start and end apart: 16 -> 16, of which waited for: 7 -> 6; matrix products, arithmetic and copies ran while one was open for 2% -> 2% of each run, Pallas kernels for 26% -> 24%
where the time goes in v17:
time: 51.2 us; the launch traced here: 50.9 us
  Pallas kernels  18.6 us (36%)
  waiting for transfers between devices  17.1 us (33%)
  starting transfers between devices  12.5 us (24%)
  other arithmetic  1.1 us (2%)
  local copies, waits for them, and re-layouts  0.82 us (2%)
  between operations  0.74 us (1%)
    ppermute x16, waiting for transfers between devices, hop(): lax.ppermute(x, axis, [(i, i ^ bit) for i in range(lax.axis_size(axis))])  17.1 us
    ppermute x16, starting transfers between devices, hop(): lax.ppermute(x, axis, [(i, i ^ bit) for i in range(lax.axis_size(axis))])  12.5 us
    pallas_call x1, Pallas kernels, attention(): pl.pallas_call(functools.partial(attention_kernel, heads), out_shape=jax....  11.3 us
    pallas_call x1, Pallas kernels, graph(): pl.pallas_call(functools.partial(graph_kernel, node_dev), out_shape=(slab...  6.22 us
    select_n x1, other arithmetic, per_device(): jnp.where(even, w_self, w_neigh)  1.1 us
    pallas_call x1, Pallas kernels, graph(): pl.pallas_call(functools.partial(embed_kernel, order, fan, node_dev), out...  1.06 us
  transfers between devices with their start and end apart: 16, of which 6 were waited for; matrix products, arithmetic and copies ran while one was open for 2% of the time, Pallas kernels for 24%

profile of v17, /device:TPU:0, one launch (start us, length us, event | category | flops | bytes accessed | tf_op | source)
XLA Modules:
  0.0 50.9 jit_solution(15331340398671556566)
XLA Ops:
  0.6 0.5 %collective-permute-start = (bf16[256,1024]{1,0:T(8,128)(2,1)}, bf16[256,1024]{1,0:T(8,128)(2,1)S(1)}, u32[]{:S(2)}, u32[]{:S(2)}) collective-permute-start(bf16[256,1024]{1,0:T(8,128)(2,1)} %refs_4_.1), channel_id=1, source_target_pairs={{0,1},{1,0},{2,3},{3,2},{4,5},{5,4},{6,7},{7,6},{8,9},{9,8},{10,11... | collective-permute-start | bytes 1572872 | tf_op jit(solution)/shard_map/ppermute | solution.py:387
  1.1 0.1 collective-permute-start.1
  1.2 0.4 collective-permute-start.2
  1.7 1.1 %broadcast_select_fusion = bf16[256,1024]{1,0:T(8,128)(2,1)S(1)} fusion(bf16[256,1024]{1,0:T(8,128)(2,1)} %refs_0_.1, bf16[256,1024]{1,0:T(8,128)(2,1)} %refs_1_.1, pred[]{:T(512)S(6)} %eq.5), kind=kLoop, calls=%fused_computation | loop fusion | flops 262144 | bytes 1572865 | tf_op jit(solution)/shard_map/jit(_where)/select_n | solution.py:412
  2.8 2.6 %collective-permute-start.6 = (bf16[256,1024]{1,0:T(8,128)(2,1)S(1)}, bf16[256,1024]{1,0:T(8,128)(2,1)S(1)}, u32[]{:S(2)}, u32[]{:S(2)}) collective-permute-start(bf16[256,1024]{1,0:T(8,128)(2,1)S(1)} %broadcast_select_fusion), channel_id=1, source_target_pairs={{0,2},{1,3},{2,0},{3,1},{4,6},{5,7},{6,4},{7,5},{8,10},{9,11},{10,... | collective-permute-start | bytes 1572872 | tf_op jit(solution)/shard_map/ppermute | solution.py:387
  5.4 0.1 collective-permute-start.8
  5.5 11.3 %shard_map.110 = bf16[16,1280]{1,0:T(8,128)(2,1)} custom-call(bf16[24,128,1024]{2,1,0:T(8,128)(2,1)} %texts_ref.1, bf16[1024,768]{1,0:T(8,128)(2,1)} %w_hbm.1, bf16[24,256]{1,0:T(8,128)(2,1)} %cot_ref.1, s32[16,24]{1,0:T(8,128)} %bitcast.6), custom_call_target="tpu_custom_call" | custom-call | flops 5637144576 | bytes 7864320 | tf_op jit(solution)/shard_map/pallas_call | solution.py:149
  16.8 0.0 collective-permute-done.refs_5_
  16.8 0.0 collective-permute-done.2.refs_3_
  16.8 4.1 %collective-permute-start.5 = (bf16[1,16,1280]{2,1,0:T(8,128)(2,1)}, bf16[1,16,1280]{2,1,0:T(8,128)(2,1)S(1)}, u32[]{:S(2)}, u32[]{:S(2)}) collective-permute-start(bf16[1,16,1280]{2,1,0:T(8,128)(2,1)} %bitcast.2), channel_id=1, source_target_pairs={{0,24},{4,28},{8,16},{12,20},{16,8},{20,12},{24,0},{28,4},{1,25},{... | collective-permute-start | bytes 122888 | tf_op jit(solution)/shard_map/ppermute | solution.py:387
  21.0 0.6 %collective-permute-start.3 = (bf16[1,16,1280]{2,1,0:T(8,128)(2,1)}, bf16[1,16,1280]{2,1,0:T(8,128)(2,1)S(1)}, u32[]{:S(2)}, u32[]{:S(2)}) collective-permute-start(bf16[1,16,1280]{2,1,0:T(8,128)(2,1)} %bitcast.4), channel_id=1, source_target_pairs={{0,8},{4,12},{8,0},{12,4},{16,24},{20,28},{24,16},{28,20},{1,9},{5... | collective-permute-start | bytes 122888 | tf_op jit(solution)/shard_map/ppermute | solution.py:387
  21.6 0.8 %copy-done.3 = bf16[16,1280]{1,0:T(8,128)(2,1)S(1)} copy-done((bf16[16,1280]{1,0:T(8,128)(2,1)S(1)}, bf16[16,1280]{1,0:T(8,128)(2,1)}, u32[]{:S(2)}) %copy-start.3) | copy-done | bytes 40984
  22.4 0.0 collective-permute-done.6.refs_4_
  22.4 0.8 %collective-permute-done.5.refs_3_ = bf16[1,16,1280]{2,1,0:T(8,128)(2,1)S(1)} collective-permute-done((bf16[1,16,1280]{2,1,0:T(8,128)(2,1)}, bf16[1,16,1280]{2,1,0:T(8,128)(2,1)S(1)}, u32[]{:S(2)}, u32[]{:S(2)}) %collective-permute-start.5) | collective-permute-done | bytes 40992 | tf_op jit(solution)/shard_map/ppermute | solution.py:387
  23.2 2.9 %collective-permute-done.4.refs_2_ = bf16[1,16,1280]{2,1,0:T(8,128)(2,1)S(1)} collective-permute-done((bf16[1,16,1280]{2,1,0:T(8,128)(2,1)}, bf16[1,16,1280]{2,1,0:T(8,128)(2,1)S(1)}, u32[]{:S(2)}, u32[]{:S(2)}) %collective-permute-start.4) | collective-permute-done | bytes 40992 | tf_op jit(solution)/shard_map/ppermute | solution.py:387
  26.1 0.2 collective-permute-start.9
  26.3 1.6 %collective-permute-start.7 = (bf16[4,16,1280]{2,1,0:T(8,128)(2,1)S(1)}, bf16[4,16,1280]{2,1,0:T(8,128)(2,1)S(1)}, u32[]{:S(2)}, u32[]{:S(2)}) collective-permute-start(bf16[4,16,1280]{2,1,0:T(8,128)(2,1)S(1)} %shard_map.112.refs_0_), channel_id=1, source_target_pairs={{0,4},{4,0},{8,12},{12,8},{16,20},{20,16},{24,28},{28,24},{1,5},{5... | collective-permute-start | bytes 491528 | tf_op jit(solution)/shard_map/ppermute | solution.py:387
  27.9 3.8 %collective-permute-done.7.refs_1_ = bf16[4,16,1280]{2,1,0:T(8,128)(2,1)S(1)} collective-permute-done((bf16[4,16,1280]{2,1,0:T(8,128)(2,1)S(1)}, bf16[4,16,1280]{2,1,0:T(8,128)(2,1)S(1)}, u32[]{:S(2)}, u32[]{:S(2)}) %collective-permute-start.7) | collective-permute-done | bytes 163872 | tf_op jit(solution)/shard_map/ppermute | solution.py:387
  31.7 0.0 collective-permute-done.8.refs_6_
  31.7 0.1 collective-permute-start.10
  31.8 1.6 %collective-permute-start.11 = (bf16[8,16,1280]{2,1,0:T(8,128)(2,1)S(1)}, bf16[8,16,1280]{2,1,0:T(8,128)(2,1)S(1)}, u32[]{:S(2)}, u32[]{:S(2)}) collective-permute-start(bf16[8,16,1280]{2,1,0:T(8,128)(2,1)S(1)} %shard_map.113.refs_0_), channel_id=1, source_target_pairs={{0,2},{1,3},{2,0},{3,1},{4,6},{5,7},{6,4},{7,5},{8,10},{9,11},{10,... | collective-permute-start | bytes 983048 | tf_op jit(solution)/shard_map/ppermute | solution.py:387
  33.4 0.2 collective-permute-start.13
  33.5 0.3 collective-permute-start.14
  33.9 4.5 %collective-permute-done.9.refs_5_ = bf16[256,1024]{1,0:T(8,128)(2,1)S(1)} collective-permute-done((bf16[256,1024]{1,0:T(8,128)(2,1)S(1)}, bf16[256,1024]{1,0:T(8,128)(2,1)S(1)}, u32[]{:S(2)}, u32[]{:S(2)}) %collective-permute-start.9) | collective-permute-done | bytes 524320 | tf_op jit(solution)/shard_map/ppermute | solution.py:387
  38.4 0.0 collective-permute-start.15
  38.4 3.5 %collective-permute-done.11.refs_2_ = bf16[8,16,1280]{2,1,0:T(8,128)(2,1)S(1)} collective-permute-done((bf16[8,16,1280]{2,1,0:T(8,128)(2,1)S(1)}, bf16[8,16,1280]{2,1,0:T(8,128)(2,1)S(1)}, u32[]{:S(2)}, u32[]{:S(2)}) %collective-permute-start.11) | collective-permute-done | bytes 327712 | tf_op jit(solution)/shard_map/ppermute | solution.py:387
  41.9 0.0 collective-permute-done.13.refs_7_
  41.9 1.6 %collective-permute-done.12.refs_3_ = bf16[8,16,1280]{2,1,0:T(8,128)(2,1)S(1)} collective-permute-done((bf16[8,16,1280]{2,1,0:T(8,128)(2,1)S(1)}, bf16[8,16,1280]{2,1,0:T(8,128)(2,1)S(1)}, u32[]{:S(2)}, u32[]{:S(2)}) %collective-permute-start.12) | collective-permute-done | bytes 327712 | tf_op jit(solution)/shard_map/ppermute | solution.py:387
  43.6 1.1 %shard_map.114 = (bf16[2,192,1024]{2,1,0:T(8,128)(2,1)S(1)}, bf16[192,1024]{1,0:T(8,128)(2,1)S(1)}, bf16[192,256]{1,0:T(8,128)(2,1)S(1)}, bf16[192,192]{1,0:T(8,128)(2,1)S(1)}, f32[192,128]{1,0:T(8,128)S(1)}) custom-call(bf16[8,16,1280]{2,1,0:T(8,128)(2,1)S(1)} %shard_map.113.refs_0_, bf16[8,16,1280]{2,1,0:T(8,128)(2,1)S(1)} %collective-permute-done.10.refs_1_, ...), custom_call_target="tpu_custom_call" | custom-call | flops 805306368 | bytes 4194304 | tf_op jit(solution)/shard_map/pallas_call | solution.py:284
  44.6 0.0 collective-permute-done.14.refs_6_
  44.6 0.0 collective-permute-done.15.refs_7_
  44.7 6.2 %shard_map.115 = (bf16[24,256]{1,0:T(8,128)(2,1)}, bf16[24,256]{1,0:T(8,128)(2,1)}, f32[256,1024]{1,0:T(8,128)}, f32[256,1024]{1,0:T(8,128)}, f32[256,1024]{1,0:T(8,128)}) custom-call(bf16[2,192,1024]{2,1,0:T(8,128)(2,1)S(1)} %get-tuple-element.37.both, bf16[192,1024]{1,0:T(8,128)(2,1)S(1)} %get-tuple-element.38.cot, ...), custom_call_target="tpu_custom_call" | custom-call | flops 2013265920 | bytes 8388608 | tf_op jit(solution)/shard_map/pallas_call | solution.py:304
  (15 shorter events, 0.1 us)
Async XLA Ops:
  0.6 16.2 %collective-permute-start = (bf16[256,1024]{1,0:T(8,128)(2,1)}, bf16[256,1024]{1,0:T(8,128)(2,1)S(1)}, u32[]{:S(2)}, u32[]{:S(2)}) collective-permute-start(bf16[256,1024]{1,0:T(8,128)(2,1)} %refs_4_.1), channel_id=1, source_target_pairs={{0,1},{1,0},{2,3},{3,2},{4,5},{5,4},{6,7},{7,6},{8,9},{9,8},{10,11... | collective-permute-start | bytes 1572872 | tf_op jit(solution)/shard_map/ppermute | solution.py:387
  1.1 15.7 %collective-permute-start.1 = (bf16[256,1024]{1,0:T(8,128)(2,1)}, bf16[256,1024]{1,0:T(8,128)(2,1)S(1)}, u32[]{:S(2)}, u32[]{:S(2)}) collective-permute-start(bf16[256,1024]{1,0:T(8,128)(2,1)} %refs_0_.1), channel_id=1, source_target_pairs={{0,1},{1,0},{2,3},{3,2},{4,5},{5,4},{6,7},{7,6},{8,9},{9,8},{10,11... | collective-permute-start | bytes 1572872 | tf_op jit(solution)/shard_map/ppermute | solution.py:387
  1.2 15.6 %collective-permute-start.2 = (bf16[256,1024]{1,0:T(8,128)(2,1)}, bf16[256,1024]{1,0:T(8,128)(2,1)S(1)}, u32[]{:S(2)}, u32[]{:S(2)}) collective-permute-start(bf16[256,1024]{1,0:T(8,128)(2,1)} %refs_1_.1), channel_id=1, source_target_pairs={{0,1},{1,0},{2,3},{3,2},{4,5},{5,4},{6,7},{7,6},{8,9},{9,8},{10,11... | collective-permute-start | bytes 1572872 | tf_op jit(solution)/shard_map/ppermute | solution.py:387
  2.8 19.6 %collective-permute-start.6 = (bf16[256,1024]{1,0:T(8,128)(2,1)S(1)}, bf16[256,1024]{1,0:T(8,128)(2,1)S(1)}, u32[]{:S(2)}, u32[]{:S(2)}) collective-permute-start(bf16[256,1024]{1,0:T(8,128)(2,1)S(1)} %broadcast_select_fusion), channel_id=1, source_target_pairs={{0,2},{1,3},{2,0},{3,1},{4,6},{5,7},{6,4},{7,5},{8,10},{9,11},{10,... | collective-permute-start | bytes 1572872 | tf_op jit(solution)/shard_map/ppermute | solution.py:387
  5.4 26.3 %collective-permute-start.8 = (bf16[256,1024]{1,0:T(8,128)(2,1)}, bf16[256,1024]{1,0:T(8,128)(2,1)S(1)}, u32[]{:S(2)}, u32[]{:S(2)}) collective-permute-start(bf16[256,1024]{1,0:T(8,128)(2,1)} %refs_4_.1), channel_id=1, source_target_pairs={{0,2},{1,3},{2,0},{3,1},{4,6},{5,7},{6,4},{7,5},{8,10},{9,11},{10,... | collective-permute-start | bytes 1572872 | tf_op jit(solution)/shard_map/ppermute | solution.py:387
  5.5 38.1 %copy-start.2 = (bf16[256,1024]{1,0:T(8,128)(2,1)S(1)}, bf16[256,1024]{1,0:T(8,128)(2,1)}, u32[]{:S(2)}) copy-start(bf16[256,1024]{1,0:T(8,128)(2,1)} %refs_4_.1) | copy-start | bytes 1572868
  5.5 39.2 %copy-start = (bf16[256,1024]{1,0:T(8,128)(2,1)S(1)}, bf16[256,1024]{1,0:T(8,128)(2,1)}, u32[]{:S(2)}) copy-start(bf16[256,1024]{1,0:T(8,128)(2,1)} %refs_0_.1) | copy-start | bytes 1572868
  5.5 39.2 %copy-start.1 = (bf16[256,1024]{1,0:T(8,128)(2,1)S(1)}, bf16[256,1024]{1,0:T(8,128)(2,1)}, u32[]{:S(2)}) copy-start(bf16[256,1024]{1,0:T(8,128)(2,1)} %refs_1_.1) | copy-start | bytes 1572868
  16.8 6.4 %collective-permute-start.5 = (bf16[1,16,1280]{2,1,0:T(8,128)(2,1)}, bf16[1,16,1280]{2,1,0:T(8,128)(2,1)S(1)}, u32[]{:S(2)}, u32[]{:S(2)}) collective-permute-start(bf16[1,16,1280]{2,1,0:T(8,128)(2,1)} %bitcast.2), channel_id=1, source_target_pairs={{0,24},{4,28},{8,16},{12,20},{16,8},{20,12},{24,0},{28,4},{1,25},{... | collective-permute-start | bytes 122888 | tf_op jit(solution)/shard_map/ppermute | solution.py:387
  21.0 5.1 %collective-permute-start.4 = (bf16[1,16,1280]{2,1,0:T(8,128)(2,1)}, bf16[1,16,1280]{2,1,0:T(8,128)(2,1)S(1)}, u32[]{:S(2)}, u32[]{:S(2)}) collective-permute-start(bf16[1,16,1280]{2,1,0:T(8,128)(2,1)} %bitcast.3), channel_id=1, source_target_pairs={{0,16},{4,20},{8,24},{12,28},{16,0},{20,4},{24,8},{28,12},{1,17},{... | collective-permute-start | bytes 122888 | tf_op jit(solution)/shard_map/ppermute | solution.py:387
  21.0 5.1 %collective-permute-start.3 = (bf16[1,16,1280]{2,1,0:T(8,128)(2,1)}, bf16[1,16,1280]{2,1,0:T(8,128)(2,1)S(1)}, u32[]{:S(2)}, u32[]{:S(2)}) collective-permute-start(bf16[1,16,1280]{2,1,0:T(8,128)(2,1)} %bitcast.4), channel_id=1, source_target_pairs={{0,8},{4,12},{8,0},{12,4},{16,24},{20,28},{24,16},{28,20},{1,9},{5... | collective-permute-start | bytes 122888 | tf_op jit(solution)/shard_map/ppermute | solution.py:387
  21.6 0.8 %copy-start.3 = (bf16[16,1280]{1,0:T(8,128)(2,1)S(1)}, bf16[16,1280]{1,0:T(8,128)(2,1)}, u32[]{:S(2)}) copy-start(bf16[16,1280]{1,0:T(8,128)(2,1)} %shard_map.110) | copy-start | bytes 122884
  26.1 12.3 %collective-permute-start.9 = (bf16[256,1024]{1,0:T(8,128)(2,1)S(1)}, bf16[256,1024]{1,0:T(8,128)(2,1)S(1)}, u32[]{:S(2)}, u32[]{:S(2)}) collective-permute-start(bf16[256,1024]{1,0:T(8,128)(2,1)S(1)} %collective-permute-done.6.refs_4_), channel_id=1, source_target_pairs={{0,8},{4,12},{8,0},{12,4},{16,24},{20,28},{24,16},{28,20},{1,9},{5... | collective-permute-start | bytes 1572872 | tf_op jit(solution)/shard_map/ppermute | solution.py:387
  26.3 5.4 %collective-permute-start.7 = (bf16[4,16,1280]{2,1,0:T(8,128)(2,1)S(1)}, bf16[4,16,1280]{2,1,0:T(8,128)(2,1)S(1)}, u32[]{:S(2)}, u32[]{:S(2)}) collective-permute-start(bf16[4,16,1280]{2,1,0:T(8,128)(2,1)S(1)} %shard_map.112.refs_0_), channel_id=1, source_target_pairs={{0,4},{4,0},{8,12},{12,8},{16,20},{20,16},{24,28},{28,24},{1,5},{5... | collective-permute-start | bytes 491528 | tf_op jit(solution)/shard_map/ppermute | solution.py:387
  31.7 2.2 %collective-permute-start.10 = (bf16[8,16,1280]{2,1,0:T(8,128)(2,1)S(1)}, bf16[8,16,1280]{2,1,0:T(8,128)(2,1)S(1)}, u32[]{:S(2)}, u32[]{:S(2)}) collective-permute-start(bf16[8,16,1280]{2,1,0:T(8,128)(2,1)S(1)} %shard_map.113.refs_0_), channel_id=1, source_target_pairs={{0,1},{1,0},{2,3},{3,2},{4,5},{5,4},{6,7},{7,6},{8,9},{9,8},{10,11... | collective-permute-start | bytes 983048 | tf_op jit(solution)/shard_map/ppermute | solution.py:387
  31.8 10.1 %collective-permute-start.11 = (bf16[8,16,1280]{2,1,0:T(8,128)(2,1)S(1)}, bf16[8,16,1280]{2,1,0:T(8,128)(2,1)S(1)}, u32[]{:S(2)}, u32[]{:S(2)}) collective-permute-start(bf16[8,16,1280]{2,1,0:T(8,128)(2,1)S(1)} %shard_map.113.refs_0_), channel_id=1, source_target_pairs={{0,2},{1,3},{2,0},{3,1},{4,6},{5,7},{6,4},{7,5},{8,10},{9,11},{10,... | collective-permute-start | bytes 983048 | tf_op jit(solution)/shard_map/ppermute | solution.py:387
  33.4 8.6 %collective-permute-start.13 = (bf16[256,1024]{1,0:T(8,128)(2,1)S(1)}, bf16[256,1024]{1,0:T(8,128)(2,1)S(1)}, u32[]{:S(2)}, u32[]{:S(2)}) collective-permute-start(bf16[256,1024]{1,0:T(8,128)(2,1)S(1)} %collective-permute-done.8.refs_6_), channel_id=1, source_target_pairs={{0,1},{1,0},{2,3},{3,2},{4,5},{5,4},{6,7},{7,6},{8,9},{9,8},{10,11... | collective-permute-start | bytes 1572872 | tf_op jit(solution)/shard_map/ppermute | solution.py:387
  33.5 11.1 %collective-permute-start.14 = (bf16[256,1024]{1,0:T(8,128)(2,1)S(1)}, bf16[256,1024]{1,0:T(8,128)(2,1)S(1)}, u32[]{:S(2)}, u32[]{:S(2)}) collective-permute-start(bf16[256,1024]{1,0:T(8,128)(2,1)S(1)} %collective-permute-done.6.refs_4_), channel_id=1, source_target_pairs={{0,1},{1,0},{2,3},{3,2},{4,5},{5,4},{6,7},{7,6},{8,9},{9,8},{10,11... | collective-permute-start | bytes 1572872 | tf_op jit(solution)/shard_map/ppermute | solution.py:387
  38.4 6.3 %collective-permute-start.15 = (bf16[256,1024]{1,0:T(8,128)(2,1)S(1)}, bf16[256,1024]{1,0:T(8,128)(2,1)S(1)}, u32[]{:S(2)}, u32[]{:S(2)}) collective-permute-start(bf16[256,1024]{1,0:T(8,128)(2,1)S(1)} %collective-permute-done.9.refs_5_), channel_id=1, source_target_pairs={{0,1},{1,0},{2,3},{3,2},{4,5},{5,4},{6,7},{7,6},{8,9},{9,8},{10,11... | collective-permute-start | bytes 1572872 | tf_op jit(solution)/shard_map/ppermute | solution.py:387
  41.9 1.6 %collective-permute-start.12 = (bf16[8,16,1280]{2,1,0:T(8,128)(2,1)S(1)}, bf16[8,16,1280]{2,1,0:T(8,128)(2,1)S(1)}, u32[]{:S(2)}, u32[]{:S(2)}) collective-permute-start(bf16[8,16,1280]{2,1,0:T(8,128)(2,1)S(1)} %collective-permute-done.11.refs_2_), channel_id=1, source_target_pairs={{0,1},{1,0},{2,3},{3,2},{4,5},{5,4},{6,7},{7,6},{8,9},{9,8},{10,11... | collective-permute-start | bytes 983048 | tf_op jit(solution)/shard_map/ppermute | solution.py:387

commit v18 on v16

--- a/solution.py
+++ b/solution.py
@@ -281,32 +281,29 @@
     cols, width = weights[0][0].shape
     nodes = got[0].shape[0] * node_dev
     vmem = pl.BlockSpec(memory_space=pltpu.VMEM)
-    known = pl.pallas_call(
-        functools.partial(embed_kernel, order, fan, node_dev),
-        out_shape=(
-            jax.ShapeDtypeStruct((2, nodes, width), BF),
-            jax.ShapeDtypeStruct((nodes, width), BF),
-            jax.ShapeDtypeStruct((nodes, cols), BF),
-            jax.ShapeDtypeStruct((nodes, nodes), BF),
-            jax.ShapeDtypeStruct((nodes, 128), F32),
-        ),
-        in_specs=[vmem] * (2 * parts),
-        out_specs=(vmem,) * 5,
-        scratch_shapes=[pltpu.VMEM((nodes, width), F32)],
-        compiler_params=pltpu.CompilerParams(vmem_limit_bytes=24 * MIB),
-        cost_estimate=pl.CostEstimate(
-            flops=2 * nodes * width * width * 2, bytes_accessed=4 * MIB, transcendentals=0
-        ),
-    )(*got, *[group[0] for group in weights])
+    anywhere = pl.BlockSpec(memory_space=pl.ANY)
     slab = jax.ShapeDtypeStruct((node_dev, cols), BF)
     big = jax.ShapeDtypeStruct((cols, width), F32)
-    anywhere = pl.BlockSpec(memory_space=pl.ANY)
+
+    def kernel(*refs):
+        first, rest = refs[: 2 * parts], refs[2 * parts : 4 * parts]
+        outs, known = refs[4 * parts : 4 * parts + 5], refs[4 * parts + 5 : 4 * parts + 10]
+        mean, *own = refs[4 * parts + 10 :]
+        embed_kernel(order, fan, node_dev, *first, *known, mean)
+        graph_kernel(node_dev, *known, *rest, *outs, *own)
+
     return pl.pallas_call(
-        functools.partial(graph_kernel, node_dev),
+        kernel,
         out_shape=(slab, slab, big, big, big),
-        in_specs=[vmem] * (5 + 2 * parts),
+        in_specs=[vmem] * (4 * parts),
         out_specs=(vmem, vmem, anywhere, anywhere, anywhere),
         scratch_shapes=[
+            pltpu.VMEM((2, nodes, width), BF),
+            pltpu.VMEM((nodes, width), BF),
+            pltpu.VMEM((nodes, cols), BF),
+            pltpu.VMEM((nodes, nodes), BF),
+            pltpu.VMEM((nodes, 128), F32),
+            pltpu.VMEM((nodes, width), F32),
             pltpu.VMEM((nodes, width), BF),
             pltpu.VMEM((node_dev, width), F32),
             pltpu.VMEM((3, cols, width), F32),
@@ -314,9 +311,9 @@
         ],
         compiler_params=pltpu.CompilerParams(vmem_limit_bytes=36 * MIB),
         cost_estimate=pl.CostEstimate(
-            flops=2 * nodes * width * width * 5, bytes_accessed=8 * MIB, transcendentals=nodes * width
+            flops=2 * nodes * width * width * 6, bytes_accessed=10 * MIB, transcendentals=nodes * width
         ),
-    )(*known, *sum((group[1:] for group in weights), ()))
+    )(*got, *[group[0] for group in weights], *sum((group[1:] for group in weights), ()))
 
 
 def graph_wide(order, fan, node_dev, got, weights):

time: 48.8 us -> 48.7 us (level)
    pallas_call x2 -> x1, Pallas kernels: 7.29 us -> 7.16 us  [graph(): pl.pallas_call(kernel, out_shape=(slab, slab, big, big, big), in_specs=[v...]
  transfers between devices with their start and end apart: 16 -> 16, of which waited for: 7 -> 7; matrix products, arithmetic and copies ran while one was open for 2% -> 2% of each run, Pallas kernels for 26% -> 23%
where the time goes in v18:
time: 48.7 us; the launch traced here: 48.4 us
  Pallas kernels  18.5 us (38%)
  waiting for transfers between devices  14.4 us (30%)
  starting transfers between devices  12.9 us (26%)
  other arithmetic  1.1 us (2%)
  local copies, waits for them, and re-layouts  0.82 us (2%)
  between operations  0.71 us (1%)
    ppermute x16, waiting for transfers between devices, hop(): lax.ppermute(x, axis, [(i, i ^ bit) for i in range(lax.axis_size(axis))])  14.4 us
    ppermute x16, starting transfers between devices, hop(): lax.ppermute(x, axis, [(i, i ^ bit) for i in range(lax.axis_size(axis))])  12.9 us
    pallas_call x1, Pallas kernels, attention(): pl.pallas_call(functools.partial(attention_kernel, heads), out_shape=jax....  11.3 us
    pallas_call x1, Pallas kernels, graph(): pl.pallas_call(kernel, out_shape=(slab, slab, big, big, big), in_specs=[v...  7.16 us
    select_n x1, other arithmetic, per_device(): jnp.where(even, w_self, w_neigh)  1.1 us
  transfers between devices with their start and end apart: 16, of which 7 were waited for; matrix products, arithmetic and copies ran while one was open for 2% of the time, Pallas kernels for 23%

profile of v18, /device:TPU:0, one launch (start us, length us, event | category | flops | bytes accessed | tf_op | source)
XLA Modules:
  0.0 48.4 jit_solution(11488207636372884449)
XLA Ops:
  0.6 0.5 %collective-permute-start = (bf16[256,1024]{1,0:T(8,128)(2,1)}, bf16[256,1024]{1,0:T(8,128)(2,1)S(1)}, u32[]{:S(2)}, u32[]{:S(2)}) collective-permute-start(bf16[256,1024]{1,0:T(8,128)(2,1)} %refs_4_.1), channel_id=1, source_target_pairs={{0,1},{1,0},{2,3},{3,2},{4,5},{5,4},{6,7},{7,6},{8,9},{9,8},{10,11... | collective-permute-start | bytes 1572872 | tf_op jit(solution)/shard_map/ppermute | solution.py:384
  1.1 0.1 collective-permute-start.1
  1.2 0.4 collective-permute-start.2
  1.7 1.1 %broadcast_select_fusion = bf16[256,1024]{1,0:T(8,128)(2,1)S(1)} fusion(bf16[256,1024]{1,0:T(8,128)(2,1)} %refs_8_.1, bf16[256,1024]{1,0:T(8,128)(2,1)} %refs_9_.1, pred[]{:T(512)S(6)} %eq.5), kind=kLoop, calls=%fused_computation | loop fusion | flops 262144 | bytes 1572865 | tf_op jit(solution)/shard_map/jit(_where)/select_n | solution.py:409
  2.8 2.6 %collective-permute-start.6 = (bf16[256,1024]{1,0:T(8,128)(2,1)S(1)}, bf16[256,1024]{1,0:T(8,128)(2,1)S(1)}, u32[]{:S(2)}, u32[]{:S(2)}) collective-permute-start(bf16[256,1024]{1,0:T(8,128)(2,1)S(1)} %broadcast_select_fusion), channel_id=1, source_target_pairs={{0,2},{1,3},{2,0},{3,1},{4,6},{5,7},{6,4},{7,5},{8,10},{9,11},{10,... | collective-permute-start | bytes 1572872 | tf_op jit(solution)/shard_map/ppermute | solution.py:384
  5.4 0.1 collective-permute-start.8
  5.5 11.3 %shard_map.110 = bf16[16,1280]{1,0:T(8,128)(2,1)} custom-call(bf16[24,128,1024]{2,1,0:T(8,128)(2,1)} %texts_ref.1, bf16[1024,768]{1,0:T(8,128)(2,1)} %w_hbm.1, bf16[24,256]{1,0:T(8,128)(2,1)} %cot_ref.1, s32[16,24]{1,0:T(8,128)} %bitcast.6), custom_call_target="tpu_custom_call" | custom-call | flops 5637144576 | bytes 7864320 | tf_op jit(solution)/shard_map/pallas_call | solution.py:149
  16.8 0.0 collective-permute-done.1.refs_10_
  16.8 0.0 collective-permute-done.2.refs_11_
  16.8 4.1 %collective-permute-start.5 = (bf16[1,16,1280]{2,1,0:T(8,128)(2,1)}, bf16[1,16,1280]{2,1,0:T(8,128)(2,1)S(1)}, u32[]{:S(2)}, u32[]{:S(2)}) collective-permute-start(bf16[1,16,1280]{2,1,0:T(8,128)(2,1)} %bitcast.2), channel_id=1, source_target_pairs={{0,24},{4,28},{8,16},{12,20},{16,8},{20,12},{24,0},{28,4},{1,25},{... | collective-permute-start | bytes 122888 | tf_op jit(solution)/shard_map/ppermute | solution.py:384
  21.0 0.0 collective-permute-start.4
  21.0 0.6 %collective-permute-start.3 = (bf16[1,16,1280]{2,1,0:T(8,128)(2,1)}, bf16[1,16,1280]{2,1,0:T(8,128)(2,1)S(1)}, u32[]{:S(2)}, u32[]{:S(2)}) collective-permute-start(bf16[1,16,1280]{2,1,0:T(8,128)(2,1)} %bitcast.4), channel_id=1, source_target_pairs={{0,8},{4,12},{8,0},{12,4},{16,24},{20,28},{24,16},{28,20},{1,9},{5... | collective-permute-start | bytes 122888 | tf_op jit(solution)/shard_map/ppermute | solution.py:384
  21.6 0.8 %copy-done.2 = bf16[16,1280]{1,0:T(8,128)(2,1)S(1)} copy-done((bf16[16,1280]{1,0:T(8,128)(2,1)S(1)}, bf16[16,1280]{1,0:T(8,128)(2,1)}, u32[]{:S(2)}) %copy-start.2) | copy-done | bytes 40984
  22.4 0.8 %collective-permute-done.5.refs_3_ = bf16[1,16,1280]{2,1,0:T(8,128)(2,1)S(1)} collective-permute-done((bf16[1,16,1280]{2,1,0:T(8,128)(2,1)}, bf16[1,16,1280]{2,1,0:T(8,128)(2,1)S(1)}, u32[]{:S(2)}, u32[]{:S(2)}) %collective-permute-start.5) | collective-permute-done | bytes 40992 | tf_op jit(solution)/shard_map/ppermute | solution.py:384
  23.2 2.9 %collective-permute-done.4.refs_2_ = bf16[1,16,1280]{2,1,0:T(8,128)(2,1)S(1)} collective-permute-done((bf16[1,16,1280]{2,1,0:T(8,128)(2,1)}, bf16[1,16,1280]{2,1,0:T(8,128)(2,1)S(1)}, u32[]{:S(2)}, u32[]{:S(2)}) %collective-permute-start.4) | collective-permute-done | bytes 40992 | tf_op jit(solution)/shard_map/ppermute | solution.py:384
  26.1 0.0 collective-permute-done.3.refs_1_
  26.1 0.2 collective-permute-start.13
  26.3 1.6 %collective-permute-start.7 = (bf16[4,16,1280]{2,1,0:T(8,128)(2,1)S(1)}, bf16[4,16,1280]{2,1,0:T(8,128)(2,1)S(1)}, u32[]{:S(2)}, u32[]{:S(2)}) collective-permute-start(bf16[4,16,1280]{2,1,0:T(8,128)(2,1)S(1)} %shard_map.112.refs_0_), channel_id=1, source_target_pairs={{0,4},{4,0},{8,12},{12,8},{16,20},{20,16},{24,28},{28,24},{1,5},{5... | collective-permute-start | bytes 491528 | tf_op jit(solution)/shard_map/ppermute | solution.py:384
  27.9 3.8 %collective-permute-done.7.refs_1_ = bf16[4,16,1280]{2,1,0:T(8,128)(2,1)S(1)} collective-permute-done((bf16[4,16,1280]{2,1,0:T(8,128)(2,1)S(1)}, bf16[4,16,1280]{2,1,0:T(8,128)(2,1)S(1)}, u32[]{:S(2)}, u32[]{:S(2)}) %collective-permute-start.7) | collective-permute-done | bytes 163872 | tf_op jit(solution)/shard_map/ppermute | solution.py:384
  31.7 1.6 %collective-permute-start.10 = (bf16[8,16,1280]{2,1,0:T(8,128)(2,1)S(1)}, bf16[8,16,1280]{2,1,0:T(8,128)(2,1)S(1)}, u32[]{:S(2)}, u32[]{:S(2)}) collective-permute-start(bf16[8,16,1280]{2,1,0:T(8,128)(2,1)S(1)} %shard_map.113.refs_0_), channel_id=1, source_target_pairs={{0,2},{1,3},{2,0},{3,1},{4,6},{5,7},{6,4},{7,5},{8,10},{9,11},{10,... | collective-permute-start | bytes 983048 | tf_op jit(solution)/shard_map/ppermute | solution.py:384
  33.3 0.0 collective-permute-start.14
  33.3 0.5 %collective-permute-start.12 = (bf16[256,1024]{1,0:T(8,128)(2,1)S(1)}, bf16[256,1024]{1,0:T(8,128)(2,1)S(1)}, u32[]{:S(2)}, u32[]{:S(2)}) collective-permute-start(bf16[256,1024]{1,0:T(8,128)(2,1)S(1)} %collective-permute-done.8.refs_6_), channel_id=1, source_target_pairs={{0,1},{1,0},{2,3},{3,2},{4,5},{5,4},{6,7},{7,6},{8,9},{9,8},{10,11... | collective-permute-start | bytes 1572872 | tf_op jit(solution)/shard_map/ppermute | solution.py:384
  33.8 4.6 %collective-permute-done.13.refs_13_ = bf16[256,1024]{1,0:T(8,128)(2,1)S(1)} collective-permute-done((bf16[256,1024]{1,0:T(8,128)(2,1)S(1)}, bf16[256,1024]{1,0:T(8,128)(2,1)S(1)}, u32[]{:S(2)}, u32[]{:S(2)}) %collective-permute-start.13) | collective-permute-done | bytes 524320 | tf_op jit(solution)/shard_map/ppermute | solution.py:384
  38.4 0.0 collective-permute-start.15
  38.4 0.5 %collective-permute-start.9 = (bf16[8,16,1280]{2,1,0:T(8,128)(2,1)S(1)}, bf16[8,16,1280]{2,1,0:T(8,128)(2,1)S(1)}, u32[]{:S(2)}, u32[]{:S(2)}) collective-permute-start(bf16[8,16,1280]{2,1,0:T(8,128)(2,1)S(1)} %shard_map.113.refs_0_), channel_id=1, source_target_pairs={{0,1},{1,0},{2,3},{3,2},{4,5},{5,4},{6,7},{7,6},{8,9},{9,8},{10,11... | collective-permute-start | bytes 983048 | tf_op jit(solution)/shard_map/ppermute | solution.py:384
  38.9 0.1 collective-permute-done.10.refs_2_
  39.0 0.0 collective-permute-start.11
  39.0 1.7 %collective-permute-done.9.refs_1_ = bf16[8,16,1280]{2,1,0:T(8,128)(2,1)S(1)} collective-permute-done((bf16[8,16,1280]{2,1,0:T(8,128)(2,1)S(1)}, bf16[8,16,1280]{2,1,0:T(8,128)(2,1)S(1)}, u32[]{:S(2)}, u32[]{:S(2)}) %collective-permute-start.9) | collective-permute-done | bytes 327712 | tf_op jit(solution)/shard_map/ppermute | solution.py:384
  40.8 0.0 collective-permute-done.14.refs_14_
  40.8 0.0 collective-permute-done.12.refs_7_
  40.8 0.5 collective-permute-done.11.refs_3_
  41.2 7.2 %shard_map.114 = (bf16[24,256]{1,0:T(8,128)(2,1)}, bf16[24,256]{1,0:T(8,128)(2,1)}, f32[256,1024]{1,0:T(8,128)}, f32[256,1024]{1,0:T(8,128)}, f32[256,1024]{1,0:T(8,128)}) custom-call(bf16[8,16,1280]{2,1,0:T(8,128)(2,1)S(1)} %shard_map.113.refs_0_, bf16[8,16,1280]{2,1,0:T(8,128)(2,1)S(1)} %collective-permute-done.9.refs_1_, ...), custom_call_target="tpu_custom_call" | custom-call | flops 2415919104 | bytes 10485760 | tf_op jit(solution)/shard_map/pallas_call | solution.py:295
  (14 shorter events, 0.1 us)
Async XLA Ops:
  0.6 16.2 %collective-permute-start = (bf16[256,1024]{1,0:T(8,128)(2,1)}, bf16[256,1024]{1,0:T(8,128)(2,1)S(1)}, u32[]{:S(2)}, u32[]{:S(2)}) collective-permute-start(bf16[256,1024]{1,0:T(8,128)(2,1)} %refs_4_.1), channel_id=1, source_target_pairs={{0,1},{1,0},{2,3},{3,2},{4,5},{5,4},{6,7},{7,6},{8,9},{9,8},{10,11... | collective-permute-start | bytes 1572872 | tf_op jit(solution)/shard_map/ppermute | solution.py:384
  1.1 15.7 %collective-permute-start.1 = (bf16[256,1024]{1,0:T(8,128)(2,1)}, bf16[256,1024]{1,0:T(8,128)(2,1)S(1)}, u32[]{:S(2)}, u32[]{:S(2)}) collective-permute-start(bf16[256,1024]{1,0:T(8,128)(2,1)} %refs_8_.1), channel_id=1, source_target_pairs={{0,1},{1,0},{2,3},{3,2},{4,5},{5,4},{6,7},{7,6},{8,9},{9,8},{10,11... | collective-permute-start | bytes 1572872 | tf_op jit(solution)/shard_map/ppermute | solution.py:384
  1.2 15.6 %collective-permute-start.2 = (bf16[256,1024]{1,0:T(8,128)(2,1)}, bf16[256,1024]{1,0:T(8,128)(2,1)S(1)}, u32[]{:S(2)}, u32[]{:S(2)}) collective-permute-start(bf16[256,1024]{1,0:T(8,128)(2,1)} %refs_9_.1), channel_id=1, source_target_pairs={{0,1},{1,0},{2,3},{3,2},{4,5},{5,4},{6,7},{7,6},{8,9},{9,8},{10,11... | collective-permute-start | bytes 1572872 | tf_op jit(solution)/shard_map/ppermute | solution.py:384
  2.8 19.6 %collective-permute-start.6 = (bf16[256,1024]{1,0:T(8,128)(2,1)S(1)}, bf16[256,1024]{1,0:T(8,128)(2,1)S(1)}, u32[]{:S(2)}, u32[]{:S(2)}) collective-permute-start(bf16[256,1024]{1,0:T(8,128)(2,1)S(1)} %broadcast_select_fusion), channel_id=1, source_target_pairs={{0,2},{1,3},{2,0},{3,1},{4,6},{5,7},{6,4},{7,5},{8,10},{9,11},{10,... | collective-permute-start | bytes 1572872 | tf_op jit(solution)/shard_map/ppermute | solution.py:384
  5.4 26.3 %collective-permute-start.8 = (bf16[256,1024]{1,0:T(8,128)(2,1)}, bf16[256,1024]{1,0:T(8,128)(2,1)S(1)}, u32[]{:S(2)}, u32[]{:S(2)}) collective-permute-start(bf16[256,1024]{1,0:T(8,128)(2,1)} %refs_4_.1), channel_id=1, source_target_pairs={{0,2},{1,3},{2,0},{3,1},{4,6},{5,7},{6,4},{7,5},{8,10},{9,11},{10,... | collective-permute-start | bytes 1572872 | tf_op jit(solution)/shard_map/ppermute | solution.py:384
  5.5 35.8 %copy-start = (bf16[256,1024]{1,0:T(8,128)(2,1)S(1)}, bf16[256,1024]{1,0:T(8,128)(2,1)}, u32[]{:S(2)}) copy-start(bf16[256,1024]{1,0:T(8,128)(2,1)} %refs_8_.1) | copy-start | bytes 1572868
  5.5 35.8 %copy-start.1 = (bf16[256,1024]{1,0:T(8,128)(2,1)S(1)}, bf16[256,1024]{1,0:T(8,128)(2,1)}, u32[]{:S(2)}) copy-start(bf16[256,1024]{1,0:T(8,128)(2,1)} %refs_9_.1) | copy-start | bytes 1572868
  5.5 35.8 %copy-start.3 = (bf16[256,1024]{1,0:T(8,128)(2,1)S(1)}, bf16[256,1024]{1,0:T(8,128)(2,1)}, u32[]{:S(2)}) copy-start(bf16[256,1024]{1,0:T(8,128)(2,1)} %refs_4_.1) | copy-start | bytes 1572868
  16.8 6.4 %collective-permute-start.5 = (bf16[1,16,1280]{2,1,0:T(8,128)(2,1)}, bf16[1,16,1280]{2,1,0:T(8,128)(2,1)S(1)}, u32[]{:S(2)}, u32[]{:S(2)}) collective-permute-start(bf16[1,16,1280]{2,1,0:T(8,128)(2,1)} %bitcast.2), channel_id=1, source_target_pairs={{0,24},{4,28},{8,16},{12,20},{16,8},{20,12},{24,0},{28,4},{1,25},{... | collective-permute-start | bytes 122888 | tf_op jit(solution)/shard_map/ppermute | solution.py:384
  21.0 5.1 %collective-permute-start.4 = (bf16[1,16,1280]{2,1,0:T(8,128)(2,1)}, bf16[1,16,1280]{2,1,0:T(8,128)(2,1)S(1)}, u32[]{:S(2)}, u32[]{:S(2)}) collective-permute-start(bf16[1,16,1280]{2,1,0:T(8,128)(2,1)} %bitcast.3), channel_id=1, source_target_pairs={{0,16},{4,20},{8,24},{12,28},{16,0},{20,4},{24,8},{28,12},{1,17},{... | collective-permute-start | bytes 122888 | tf_op jit(solution)/shard_map/ppermute | solution.py:384
  21.0 5.1 %collective-permute-start.3 = (bf16[1,16,1280]{2,1,0:T(8,128)(2,1)}, bf16[1,16,1280]{2,1,0:T(8,128)(2,1)S(1)}, u32[]{:S(2)}, u32[]{:S(2)}) collective-permute-start(bf16[1,16,1280]{2,1,0:T(8,128)(2,1)} %bitcast.4), channel_id=1, source_target_pairs={{0,8},{4,12},{8,0},{12,4},{16,24},{20,28},{24,16},{28,20},{1,9},{5... | collective-permute-start | bytes 122888 | tf_op jit(solution)/shard_map/ppermute | solution.py:384
  21.6 0.8 %copy-start.2 = (bf16[16,1280]{1,0:T(8,128)(2,1)S(1)}, bf16[16,1280]{1,0:T(8,128)(2,1)}, u32[]{:S(2)}) copy-start(bf16[16,1280]{1,0:T(8,128)(2,1)} %shard_map.110) | copy-start | bytes 122884
  26.1 12.3 %collective-permute-start.13 = (bf16[256,1024]{1,0:T(8,128)(2,1)S(1)}, bf16[256,1024]{1,0:T(8,128)(2,1)S(1)}, u32[]{:S(2)}, u32[]{:S(2)}) collective-permute-start(bf16[256,1024]{1,0:T(8,128)(2,1)S(1)} %collective-permute-done.6.refs_12_), channel_id=1, source_target_pairs={{0,8},{4,12},{8,0},{12,4},{16,24},{20,28},{24,16},{28,20},{1,9},{5... | collective-permute-start | bytes 1572872 | tf_op jit(solution)/shard_map/ppermute | solution.py:384
  26.3 5.4 %collective-permute-start.7 = (bf16[4,16,1280]{2,1,0:T(8,128)(2,1)S(1)}, bf16[4,16,1280]{2,1,0:T(8,128)(2,1)S(1)}, u32[]{:S(2)}, u32[]{:S(2)}) collective-permute-start(bf16[4,16,1280]{2,1,0:T(8,128)(2,1)S(1)} %shard_map.112.refs_0_), channel_id=1, source_target_pairs={{0,4},{4,0},{8,12},{12,8},{16,20},{20,16},{24,28},{28,24},{1,5},{5... | collective-permute-start | bytes 491528 | tf_op jit(solution)/shard_map/ppermute | solution.py:384
  31.7 7.3 %collective-permute-start.10 = (bf16[8,16,1280]{2,1,0:T(8,128)(2,1)S(1)}, bf16[8,16,1280]{2,1,0:T(8,128)(2,1)S(1)}, u32[]{:S(2)}, u32[]{:S(2)}) collective-permute-start(bf16[8,16,1280]{2,1,0:T(8,128)(2,1)S(1)} %shard_map.113.refs_0_), channel_id=1, source_target_pairs={{0,2},{1,3},{2,0},{3,1},{4,6},{5,7},{6,4},{7,5},{8,10},{9,11},{10,... | collective-permute-start | bytes 983048 | tf_op jit(solution)/shard_map/ppermute | solution.py:384
  33.3 7.5 %collective-permute-start.14 = (bf16[256,1024]{1,0:T(8,128)(2,1)S(1)}, bf16[256,1024]{1,0:T(8,128)(2,1)S(1)}, u32[]{:S(2)}, u32[]{:S(2)}) collective-permute-start(bf16[256,1024]{1,0:T(8,128)(2,1)S(1)} %collective-permute-done.6.refs_12_), channel_id=1, source_target_pairs={{0,1},{1,0},{2,3},{3,2},{4,5},{5,4},{6,7},{7,6},{8,9},{9,8},{10,11... | collective-permute-start | bytes 1572872 | tf_op jit(solution)/shard_map/ppermute | solution.py:384
  33.3 7.5 %collective-permute-start.12 = (bf16[256,1024]{1,0:T(8,128)(2,1)S(1)}, bf16[256,1024]{1,0:T(8,128)(2,1)S(1)}, u32[]{:S(2)}, u32[]{:S(2)}) collective-permute-start(bf16[256,1024]{1,0:T(8,128)(2,1)S(1)} %collective-permute-done.8.refs_6_), channel_id=1, source_target_pairs={{0,1},{1,0},{2,3},{3,2},{4,5},{5,4},{6,7},{7,6},{8,9},{9,8},{10,11... | collective-permute-start | bytes 1572872 | tf_op jit(solution)/shard_map/ppermute | solution.py:384
  38.4 2.9 %collective-permute-start.15 = (bf16[256,1024]{1,0:T(8,128)(2,1)S(1)}, bf16[256,1024]{1,0:T(8,128)(2,1)S(1)}, u32[]{:S(2)}, u32[]{:S(2)}) collective-permute-start(bf16[256,1024]{1,0:T(8,128)(2,1)S(1)} %collective-permute-done.13.refs_13_), channel_id=1, source_target_pairs={{0,1},{1,0},{2,3},{3,2},{4,5},{5,4},{6,7},{7,6},{8,9},{9,8},{10,11... | collective-permute-start | bytes 1572872 | tf_op jit(solution)/shard_map/ppermute | solution.py:384
  38.4 2.4 %collective-permute-start.9 = (bf16[8,16,1280]{2,1,0:T(8,128)(2,1)S(1)}, bf16[8,16,1280]{2,1,0:T(8,128)(2,1)S(1)}, u32[]{:S(2)}, u32[]{:S(2)}) collective-permute-start(bf16[8,16,1280]{2,1,0:T(8,128)(2,1)S(1)} %shard_map.113.refs_0_), channel_id=1, source_target_pairs={{0,1},{1,0},{2,3},{3,2},{4,5},{5,4},{6,7},{7,6},{8,9},{9,8},{10,11... | collective-permute-start | bytes 983048 | tf_op jit(solution)/shard_map/ppermute | solution.py:384
  39.0 2.2 %collective-permute-start.11 = (bf16[8,16,1280]{2,1,0:T(8,128)(2,1)S(1)}, bf16[8,16,1280]{2,1,0:T(8,128)(2,1)S(1)}, u32[]{:S(2)}, u32[]{:S(2)}) collective-permute-start(bf16[8,16,1280]{2,1,0:T(8,128)(2,1)S(1)} %collective-permute-done.10.refs_2_), channel_id=1, source_target_pairs={{0,1},{1,0},{2,3},{3,2},{4,5},{5,4},{6,7},{7,6},{8,9},{9,8},{10,11... | collective-permute-start | bytes 983048 | tf_op jit(solution)/shard_map/ppermute | solution.py:384

commit v19 on v18

--- a/solution.py
+++ b/solution.py
@@ -10,7 +10,7 @@
 HD = 64
 BF = jnp.bfloat16
 F32 = jnp.float32
-NODES_STEP = 8
+NODES_STEP = 12
 WIDE_LIMIT = 256
 IDS_COLS = 128
 IDS_AT = 32

time: 48.7 us -> 49.2 us (1.010)
  transfers between devices with their start and end apart: 16 -> 16, of which waited for: 7 -> 6; matrix products, arithmetic and copies ran while one was open for 2% -> 2% of each run, Pallas kernels for 23% -> 23%
where the time goes in v19:
time: 49.2 us; the launch traced here: 48.9 us
  Pallas kernels  18.6 us (38%)
  waiting for transfers between devices  14.8 us (30%)
  starting transfers between devices  12.9 us (26%)
  other arithmetic  1.1 us (2%)
  local copies, waits for them, and re-layouts  0.82 us (2%)
  between operations  0.71 us (1%)
    ppermute x16, waiting for transfers between devices, hop(): lax.ppermute(x, axis, [(i, i ^ bit) for i in range(lax.axis_size(axis))])  14.8 us
    ppermute x16, starting transfers between devices, hop(): lax.ppermute(x, axis, [(i, i ^ bit) for i in range(lax.axis_size(axis))])  12.9 us
    pallas_call x1, Pallas kernels, attention(): pl.pallas_call(functools.partial(attention_kernel, heads), out_shape=jax....  11.4 us
    pallas_call x1, Pallas kernels, graph(): pl.pallas_call(kernel, out_shape=(slab, slab, big, big, big), in_specs=[v...  7.16 us
    select_n x1, other arithmetic, per_device(): jnp.where(even, w_self, w_neigh)  1.1 us
  transfers between devices with their start and end apart: 16, of which 6 were waited for; matrix products, arithmetic and copies ran while one was open for 2% of the time, Pallas kernels for 23%

profile of v19, /device:TPU:0, one launch (start us, length us, event | category | flops | bytes accessed | tf_op | source)
XLA Modules:
  0.0 48.9 jit_solution(88837195930133343)
XLA Ops:
  0.6 0.5 %collective-permute-start = (bf16[256,1024]{1,0:T(8,128)(2,1)}, bf16[256,1024]{1,0:T(8,128)(2,1)S(1)}, u32[]{:S(2)}, u32[]{:S(2)}) collective-permute-start(bf16[256,1024]{1,0:T(8,128)(2,1)} %refs_4_.1), channel_id=1, source_target_pairs={{0,1},{1,0},{2,3},{3,2},{4,5},{5,4},{6,7},{7,6},{8,9},{9,8},{10,11... | collective-permute-start | bytes 1572872 | tf_op jit(solution)/shard_map/ppermute | solution.py:384
  1.1 0.1 collective-permute-start.1
  1.2 0.4 collective-permute-start.2
  1.7 1.1 %broadcast_select_fusion = bf16[256,1024]{1,0:T(8,128)(2,1)S(1)} fusion(bf16[256,1024]{1,0:T(8,128)(2,1)} %refs_8_.1, bf16[256,1024]{1,0:T(8,128)(2,1)} %refs_9_.1, pred[]{:T(512)S(6)} %eq.5), kind=kLoop, calls=%fused_computation | loop fusion | flops 262144 | bytes 1572865 | tf_op jit(solution)/shard_map/jit(_where)/select_n | solution.py:409
  2.8 2.6 %collective-permute-start.6 = (bf16[256,1024]{1,0:T(8,128)(2,1)S(1)}, bf16[256,1024]{1,0:T(8,128)(2,1)S(1)}, u32[]{:S(2)}, u32[]{:S(2)}) collective-permute-start(bf16[256,1024]{1,0:T(8,128)(2,1)S(1)} %broadcast_select_fusion), channel_id=1, source_target_pairs={{0,2},{1,3},{2,0},{3,1},{4,6},{5,7},{6,4},{7,5},{8,10},{9,11},{10,... | collective-permute-start | bytes 1572872 | tf_op jit(solution)/shard_map/ppermute | solution.py:384
  5.4 0.1 collective-permute-start.8
  5.5 11.4 %shard_map.110 = bf16[16,1280]{1,0:T(8,128)(2,1)} custom-call(bf16[24,128,1024]{2,1,0:T(8,128)(2,1)} %texts_ref.1, bf16[1024,768]{1,0:T(8,128)(2,1)} %w_hbm.1, bf16[24,256]{1,0:T(8,128)(2,1)} %cot_ref.1, s32[16,24]{1,0:T(8,128)} %bitcast.6), custom_call_target="tpu_custom_call" | custom-call | flops 5637144576 | bytes 7864320 | tf_op jit(solution)/shard_map/pallas_call | solution.py:149
  16.9 0.0 collective-permute-done.refs_5_
  16.9 0.0 collective-permute-done.1.refs_10_
  16.9 0.0 collective-permute-done.2.refs_11_
  16.9 4.1 %collective-permute-start.5 = (bf16[1,16,1280]{2,1,0:T(8,128)(2,1)}, bf16[1,16,1280]{2,1,0:T(8,128)(2,1)S(1)}, u32[]{:S(2)}, u32[]{:S(2)}) collective-permute-start(bf16[1,16,1280]{2,1,0:T(8,128)(2,1)} %bitcast.2), channel_id=1, source_target_pairs={{0,24},{4,28},{8,16},{12,20},{16,8},{20,12},{24,0},{28,4},{1,25},{... | collective-permute-start | bytes 122888 | tf_op jit(solution)/shard_map/ppermute | solution.py:384
  21.0 0.0 collective-permute-start.4
  21.0 0.6 %collective-permute-start.3 = (bf16[1,16,1280]{2,1,0:T(8,128)(2,1)}, bf16[1,16,1280]{2,1,0:T(8,128)(2,1)S(1)}, u32[]{:S(2)}, u32[]{:S(2)}) collective-permute-start(bf16[1,16,1280]{2,1,0:T(8,128)(2,1)} %bitcast.4), channel_id=1, source_target_pairs={{0,8},{4,12},{8,0},{12,4},{16,24},{20,28},{24,16},{28,20},{1,9},{5... | collective-permute-start | bytes 122888 | tf_op jit(solution)/shard_map/ppermute | solution.py:384
  21.7 0.8 %copy-done.2 = bf16[16,1280]{1,0:T(8,128)(2,1)S(1)} copy-done((bf16[16,1280]{1,0:T(8,128)(2,1)S(1)}, bf16[16,1280]{1,0:T(8,128)(2,1)}, u32[]{:S(2)}) %copy-start.2) | copy-done | bytes 40984
  22.5 0.0 collective-permute-done.6.refs_12_
  22.5 0.8 %collective-permute-done.5.refs_3_ = bf16[1,16,1280]{2,1,0:T(8,128)(2,1)S(1)} collective-permute-done((bf16[1,16,1280]{2,1,0:T(8,128)(2,1)}, bf16[1,16,1280]{2,1,0:T(8,128)(2,1)S(1)}, u32[]{:S(2)}, u32[]{:S(2)}) %collective-permute-start.5) | collective-permute-done | bytes 40992 | tf_op jit(solution)/shard_map/ppermute | solution.py:384
  23.2 2.9 %collective-permute-done.4.refs_2_ = bf16[1,16,1280]{2,1,0:T(8,128)(2,1)S(1)} collective-permute-done((bf16[1,16,1280]{2,1,0:T(8,128)(2,1)}, bf16[1,16,1280]{2,1,0:T(8,128)(2,1)S(1)}, u32[]{:S(2)}, u32[]{:S(2)}) %collective-permute-start.4) | collective-permute-done | bytes 40992 | tf_op jit(solution)/shard_map/ppermute | solution.py:384
  26.1 0.0 collective-permute-done.3.refs_1_
  26.1 0.3 collective-permute-start.13
  26.4 1.6 %collective-permute-start.7 = (bf16[4,16,1280]{2,1,0:T(8,128)(2,1)S(1)}, bf16[4,16,1280]{2,1,0:T(8,128)(2,1)S(1)}, u32[]{:S(2)}, u32[]{:S(2)}) collective-permute-start(bf16[4,16,1280]{2,1,0:T(8,128)(2,1)S(1)} %shard_map.112.refs_0_), channel_id=1, source_target_pairs={{0,4},{4,0},{8,12},{12,8},{16,20},{20,16},{24,28},{28,24},{1,5},{5... | collective-permute-start | bytes 491528 | tf_op jit(solution)/shard_map/ppermute | solution.py:384
  28.0 3.8 %collective-permute-done.7.refs_1_ = bf16[4,16,1280]{2,1,0:T(8,128)(2,1)S(1)} collective-permute-done((bf16[4,16,1280]{2,1,0:T(8,128)(2,1)S(1)}, bf16[4,16,1280]{2,1,0:T(8,128)(2,1)S(1)}, u32[]{:S(2)}, u32[]{:S(2)}) %collective-permute-start.7) | collective-permute-done | bytes 163872 | tf_op jit(solution)/shard_map/ppermute | solution.py:384
  31.8 0.0 collective-permute-done.8.refs_6_
  31.8 1.5 %collective-permute-start.10 = (bf16[8,16,1280]{2,1,0:T(8,128)(2,1)S(1)}, bf16[8,16,1280]{2,1,0:T(8,128)(2,1)S(1)}, u32[]{:S(2)}, u32[]{:S(2)}) collective-permute-start(bf16[8,16,1280]{2,1,0:T(8,128)(2,1)S(1)} %shard_map.113.refs_0_), channel_id=1, source_target_pairs={{0,2},{1,3},{2,0},{3,1},{4,6},{5,7},{6,4},{7,5},{8,10},{9,11},{10,... | collective-permute-start | bytes 983048 | tf_op jit(solution)/shard_map/ppermute | solution.py:384
  33.4 0.0 collective-permute-start.14
  33.4 0.5 %collective-permute-start.12 = (bf16[256,1024]{1,0:T(8,128)(2,1)S(1)}, bf16[256,1024]{1,0:T(8,128)(2,1)S(1)}, u32[]{:S(2)}, u32[]{:S(2)}) collective-permute-start(bf16[256,1024]{1,0:T(8,128)(2,1)S(1)} %collective-permute-done.8.refs_6_), channel_id=1, source_target_pairs={{0,1},{1,0},{2,3},{3,2},{4,5},{5,4},{6,7},{7,6},{8,9},{9,8},{10,11... | collective-permute-start | bytes 1572872 | tf_op jit(solution)/shard_map/ppermute | solution.py:384
  33.9 5.0 %collective-permute-done.13.refs_13_ = bf16[256,1024]{1,0:T(8,128)(2,1)S(1)} collective-permute-done((bf16[256,1024]{1,0:T(8,128)(2,1)S(1)}, bf16[256,1024]{1,0:T(8,128)(2,1)S(1)}, u32[]{:S(2)}, u32[]{:S(2)}) %collective-permute-start.13) | collective-permute-done | bytes 524320 | tf_op jit(solution)/shard_map/ppermute | solution.py:384
  38.9 0.5 %collective-permute-start.9 = (bf16[8,16,1280]{2,1,0:T(8,128)(2,1)S(1)}, bf16[8,16,1280]{2,1,0:T(8,128)(2,1)S(1)}, u32[]{:S(2)}, u32[]{:S(2)}) collective-permute-start(bf16[8,16,1280]{2,1,0:T(8,128)(2,1)S(1)} %shard_map.113.refs_0_), channel_id=1, source_target_pairs={{0,1},{1,0},{2,3},{3,2},{4,5},{5,4},{6,7},{7,6},{8,9},{9,8},{10,11... | collective-permute-start | bytes 983048 | tf_op jit(solution)/shard_map/ppermute | solution.py:384
  39.4 0.0 collective-permute-done.10.refs_2_
  39.4 0.0 collective-permute-start.11
  39.4 1.9 %collective-permute-done.9.refs_1_ = bf16[8,16,1280]{2,1,0:T(8,128)(2,1)S(1)} collective-permute-done((bf16[8,16,1280]{2,1,0:T(8,128)(2,1)S(1)}, bf16[8,16,1280]{2,1,0:T(8,128)(2,1)S(1)}, u32[]{:S(2)}, u32[]{:S(2)}) %collective-permute-start.9) | collective-permute-done | bytes 327712 | tf_op jit(solution)/shard_map/ppermute | solution.py:384
  41.3 0.5 collective-permute-done.11.refs_3_
  41.8 7.2 %shard_map.114 = (bf16[24,256]{1,0:T(8,128)(2,1)}, bf16[24,256]{1,0:T(8,128)(2,1)}, f32[256,1024]{1,0:T(8,128)}, f32[256,1024]{1,0:T(8,128)}, f32[256,1024]{1,0:T(8,128)}) custom-call(bf16[8,16,1280]{2,1,0:T(8,128)(2,1)S(1)} %shard_map.113.refs_0_, bf16[8,16,1280]{2,1,0:T(8,128)(2,1)S(1)} %collective-permute-done.9.refs_1_, ...), custom_call_target="tpu_custom_call" | custom-call | flops 2415919104 | bytes 10485760 | tf_op jit(solution)/shard_map/pallas_call | solution.py:295
  (14 shorter events, 0.1 us)
Async XLA Ops:
  0.6 16.2 %collective-permute-start = (bf16[256,1024]{1,0:T(8,128)(2,1)}, bf16[256,1024]{1,0:T(8,128)(2,1)S(1)}, u32[]{:S(2)}, u32[]{:S(2)}) collective-permute-start(bf16[256,1024]{1,0:T(8,128)(2,1)} %refs_4_.1), channel_id=1, source_target_pairs={{0,1},{1,0},{2,3},{3,2},{4,5},{5,4},{6,7},{7,6},{8,9},{9,8},{10,11... | collective-permute-start | bytes 1572872 | tf_op jit(solution)/shard_map/ppermute | solution.py:384
  1.1 15.7 %collective-permute-start.1 = (bf16[256,1024]{1,0:T(8,128)(2,1)}, bf16[256,1024]{1,0:T(8,128)(2,1)S(1)}, u32[]{:S(2)}, u32[]{:S(2)}) collective-permute-start(bf16[256,1024]{1,0:T(8,128)(2,1)} %refs_8_.1), channel_id=1, source_target_pairs={{0,1},{1,0},{2,3},{3,2},{4,5},{5,4},{6,7},{7,6},{8,9},{9,8},{10,11... | collective-permute-start | bytes 1572872 | tf_op jit(solution)/shard_map/ppermute | solution.py:384
  1.2 15.7 %collective-permute-start.2 = (bf16[256,1024]{1,0:T(8,128)(2,1)}, bf16[256,1024]{1,0:T(8,128)(2,1)S(1)}, u32[]{:S(2)}, u32[]{:S(2)}) collective-permute-start(bf16[256,1024]{1,0:T(8,128)(2,1)} %refs_9_.1), channel_id=1, source_target_pairs={{0,1},{1,0},{2,3},{3,2},{4,5},{5,4},{6,7},{7,6},{8,9},{9,8},{10,11... | collective-permute-start | bytes 1572872 | tf_op jit(solution)/shard_map/ppermute | solution.py:384
  2.8 19.7 %collective-permute-start.6 = (bf16[256,1024]{1,0:T(8,128)(2,1)S(1)}, bf16[256,1024]{1,0:T(8,128)(2,1)S(1)}, u32[]{:S(2)}, u32[]{:S(2)}) collective-permute-start(bf16[256,1024]{1,0:T(8,128)(2,1)S(1)} %broadcast_select_fusion), channel_id=1, source_target_pairs={{0,2},{1,3},{2,0},{3,1},{4,6},{5,7},{6,4},{7,5},{8,10},{9,11},{10,... | collective-permute-start | bytes 1572872 | tf_op jit(solution)/shard_map/ppermute | solution.py:384
  5.4 26.4 %collective-permute-start.8 = (bf16[256,1024]{1,0:T(8,128)(2,1)}, bf16[256,1024]{1,0:T(8,128)(2,1)S(1)}, u32[]{:S(2)}, u32[]{:S(2)}) collective-permute-start(bf16[256,1024]{1,0:T(8,128)(2,1)} %refs_4_.1), channel_id=1, source_target_pairs={{0,2},{1,3},{2,0},{3,1},{4,6},{5,7},{6,4},{7,5},{8,10},{9,11},{10,... | collective-permute-start | bytes 1572872 | tf_op jit(solution)/shard_map/ppermute | solution.py:384
  5.5 36.3 %copy-start = (bf16[256,1024]{1,0:T(8,128)(2,1)S(1)}, bf16[256,1024]{1,0:T(8,128)(2,1)}, u32[]{:S(2)}) copy-start(bf16[256,1024]{1,0:T(8,128)(2,1)} %refs_8_.1) | copy-start | bytes 1572868
  5.5 36.3 %copy-start.1 = (bf16[256,1024]{1,0:T(8,128)(2,1)S(1)}, bf16[256,1024]{1,0:T(8,128)(2,1)}, u32[]{:S(2)}) copy-start(bf16[256,1024]{1,0:T(8,128)(2,1)} %refs_9_.1) | copy-start | bytes 1572868
  5.5 36.3 %copy-start.3 = (bf16[256,1024]{1,0:T(8,128)(2,1)S(1)}, bf16[256,1024]{1,0:T(8,128)(2,1)}, u32[]{:S(2)}) copy-start(bf16[256,1024]{1,0:T(8,128)(2,1)} %refs_4_.1) | copy-start | bytes 1572868
  16.9 6.4 %collective-permute-start.5 = (bf16[1,16,1280]{2,1,0:T(8,128)(2,1)}, bf16[1,16,1280]{2,1,0:T(8,128)(2,1)S(1)}, u32[]{:S(2)}, u32[]{:S(2)}) collective-permute-start(bf16[1,16,1280]{2,1,0:T(8,128)(2,1)} %bitcast.2), channel_id=1, source_target_pairs={{0,24},{4,28},{8,16},{12,20},{16,8},{20,12},{24,0},{28,4},{1,25},{... | collective-permute-start | bytes 122888 | tf_op jit(solution)/shard_map/ppermute | solution.py:384
  21.0 5.1 %collective-permute-start.4 = (bf16[1,16,1280]{2,1,0:T(8,128)(2,1)}, bf16[1,16,1280]{2,1,0:T(8,128)(2,1)S(1)}, u32[]{:S(2)}, u32[]{:S(2)}) collective-permute-start(bf16[1,16,1280]{2,1,0:T(8,128)(2,1)} %bitcast.3), channel_id=1, source_target_pairs={{0,16},{4,20},{8,24},{12,28},{16,0},{20,4},{24,8},{28,12},{1,17},{... | collective-permute-start | bytes 122888 | tf_op jit(solution)/shard_map/ppermute | solution.py:384
  21.0 5.1 %collective-permute-start.3 = (bf16[1,16,1280]{2,1,0:T(8,128)(2,1)}, bf16[1,16,1280]{2,1,0:T(8,128)(2,1)S(1)}, u32[]{:S(2)}, u32[]{:S(2)}) collective-permute-start(bf16[1,16,1280]{2,1,0:T(8,128)(2,1)} %bitcast.4), channel_id=1, source_target_pairs={{0,8},{4,12},{8,0},{12,4},{16,24},{20,28},{24,16},{28,20},{1,9},{5... | collective-permute-start | bytes 122888 | tf_op jit(solution)/shard_map/ppermute | solution.py:384
  21.7 0.8 %copy-start.2 = (bf16[16,1280]{1,0:T(8,128)(2,1)S(1)}, bf16[16,1280]{1,0:T(8,128)(2,1)}, u32[]{:S(2)}) copy-start(bf16[16,1280]{1,0:T(8,128)(2,1)} %shard_map.110) | copy-start | bytes 122884
  26.1 12.8 %collective-permute-start.13 = (bf16[256,1024]{1,0:T(8,128)(2,1)S(1)}, bf16[256,1024]{1,0:T(8,128)(2,1)S(1)}, u32[]{:S(2)}, u32[]{:S(2)}) collective-permute-start(bf16[256,1024]{1,0:T(8,128)(2,1)S(1)} %collective-permute-done.6.refs_12_), channel_id=1, source_target_pairs={{0,8},{4,12},{8,0},{12,4},{16,24},{20,28},{24,16},{28,20},{1,9},{5... | collective-permute-start | bytes 1572872 | tf_op jit(solution)/shard_map/ppermute | solution.py:384
  26.4 5.4 %collective-permute-start.7 = (bf16[4,16,1280]{2,1,0:T(8,128)(2,1)S(1)}, bf16[4,16,1280]{2,1,0:T(8,128)(2,1)S(1)}, u32[]{:S(2)}, u32[]{:S(2)}) collective-permute-start(bf16[4,16,1280]{2,1,0:T(8,128)(2,1)S(1)} %shard_map.112.refs_0_), channel_id=1, source_target_pairs={{0,4},{4,0},{8,12},{12,8},{16,20},{20,16},{24,28},{28,24},{1,5},{5... | collective-permute-start | bytes 491528 | tf_op jit(solution)/shard_map/ppermute | solution.py:384
  31.8 7.6 %collective-permute-start.10 = (bf16[8,16,1280]{2,1,0:T(8,128)(2,1)S(1)}, bf16[8,16,1280]{2,1,0:T(8,128)(2,1)S(1)}, u32[]{:S(2)}, u32[]{:S(2)}) collective-permute-start(bf16[8,16,1280]{2,1,0:T(8,128)(2,1)S(1)} %shard_map.113.refs_0_), channel_id=1, source_target_pairs={{0,2},{1,3},{2,0},{3,1},{4,6},{5,7},{6,4},{7,5},{8,10},{9,11},{10,... | collective-permute-start | bytes 983048 | tf_op jit(solution)/shard_map/ppermute | solution.py:384
  33.4 7.9 %collective-permute-start.14 = (bf16[256,1024]{1,0:T(8,128)(2,1)S(1)}, bf16[256,1024]{1,0:T(8,128)(2,1)S(1)}, u32[]{:S(2)}, u32[]{:S(2)}) collective-permute-start(bf16[256,1024]{1,0:T(8,128)(2,1)S(1)} %collective-permute-done.6.refs_12_), channel_id=1, source_target_pairs={{0,1},{1,0},{2,3},{3,2},{4,5},{5,4},{6,7},{7,6},{8,9},{9,8},{10,11... | collective-permute-start | bytes 1572872 | tf_op jit(solution)/shard_map/ppermute | solution.py:384
  33.4 7.9 %collective-permute-start.12 = (bf16[256,1024]{1,0:T(8,128)(2,1)S(1)}, bf16[256,1024]{1,0:T(8,128)(2,1)S(1)}, u32[]{:S(2)}, u32[]{:S(2)}) collective-permute-start(bf16[256,1024]{1,0:T(8,128)(2,1)S(1)} %collective-permute-done.8.refs_6_), channel_id=1, source_target_pairs={{0,1},{1,0},{2,3},{3,2},{4,5},{5,4},{6,7},{7,6},{8,9},{9,8},{10,11... | collective-permute-start | bytes 1572872 | tf_op jit(solution)/shard_map/ppermute | solution.py:384
  38.9 2.9 %collective-permute-start.15 = (bf16[256,1024]{1,0:T(8,128)(2,1)S(1)}, bf16[256,1024]{1,0:T(8,128)(2,1)S(1)}, u32[]{:S(2)}, u32[]{:S(2)}) collective-permute-start(bf16[256,1024]{1,0:T(8,128)(2,1)S(1)} %collective-permute-done.13.refs_13_), channel_id=1, source_target_pairs={{0,1},{1,0},{2,3},{3,2},{4,5},{5,4},{6,7},{7,6},{8,9},{9,8},{10,11... | collective-permute-start | bytes 1572872 | tf_op jit(solution)/shard_map/ppermute | solution.py:384
  38.9 2.4 %collective-permute-start.9 = (bf16[8,16,1280]{2,1,0:T(8,128)(2,1)S(1)}, bf16[8,16,1280]{2,1,0:T(8,128)(2,1)S(1)}, u32[]{:S(2)}, u32[]{:S(2)}) collective-permute-start(bf16[8,16,1280]{2,1,0:T(8,128)(2,1)S(1)} %shard_map.113.refs_0_), channel_id=1, source_target_pairs={{0,1},{1,0},{2,3},{3,2},{4,5},{5,4},{6,7},{7,6},{8,9},{9,8},{10,11... | collective-permute-start | bytes 983048 | tf_op jit(solution)/shard_map/ppermute | solution.py:384
  39.4 2.3 %collective-permute-start.11 = (bf16[8,16,1280]{2,1,0:T(8,128)(2,1)S(1)}, bf16[8,16,1280]{2,1,0:T(8,128)(2,1)S(1)}, u32[]{:S(2)}, u32[]{:S(2)}) collective-permute-start(bf16[8,16,1280]{2,1,0:T(8,128)(2,1)S(1)} %collective-permute-done.10.refs_2_), channel_id=1, source_target_pairs={{0,1},{1,0},{2,3},{3,2},{4,5},{5,4},{6,7},{7,6},{8,9},{9,8},{10,11... | collective-permute-start | bytes 983048 | tf_op jit(solution)/shard_map/ppermute | solution.py:384

commit v20 on v19

--- a/solution.py
+++ b/solution.py
@@ -10,14 +10,14 @@
 HD = 64
 BF = jnp.bfloat16
 F32 = jnp.float32
-NODES_STEP = 12
+NODES_STEP = 6
 WIDE_LIMIT = 256
 IDS_COLS = 128
 IDS_AT = 32
 TOP = 16
 LOG2E = 1.4426950408889634
 ATTENTION_VMEM = 58
-COPIES = 4
+COPIES = 2
 MIB = 1 << 20
 
 

time: 49.2 us -> 48.8 us (level)
  transfers between devices with their start and end apart: 16 -> 16, of which waited for: 6 -> 7; matrix products, arithmetic and copies ran while one was open for 2% -> 2% of each run, Pallas kernels for 23% -> 24%
where the time goes in v20:
time: 48.8 us; the launch traced here: 48.5 us
  Pallas kernels  18.6 us (38%)
  waiting for transfers between devices  14.4 us (30%)
  starting transfers between devices  12.9 us (26%)
  other arithmetic  1.1 us (2%)
  local copies, waits for them, and re-layouts  0.82 us (2%)
  between operations  0.71 us (1%)
    ppermute x16, waiting for transfers between devices, hop(): lax.ppermute(x, axis, [(i, i ^ bit) for i in range(lax.axis_size(axis))])  14.4 us
    ppermute x16, starting transfers between devices, hop(): lax.ppermute(x, axis, [(i, i ^ bit) for i in range(lax.axis_size(axis))])  12.9 us
    pallas_call x1, Pallas kernels, attention(): pl.pallas_call(functools.partial(attention_kernel, heads), out_shape=jax....  11.4 us
    pallas_call x1, Pallas kernels, graph(): pl.pallas_call(kernel, out_shape=(slab, slab, big, big, big), in_specs=[v...  7.16 us
    select_n x1, other arithmetic, per_device(): jnp.where(even, w_self, w_neigh)  1.1 us
  transfers between devices with their start and end apart: 16, of which 7 were waited for; matrix products, arithmetic and copies ran while one was open for 2% of the time, Pallas kernels for 24%

profile of v20, /device:TPU:0, one launch (start us, length us, event | category | flops | bytes accessed | tf_op | source)
XLA Modules:
  0.0 48.5 jit_solution(12338786633926546266)
XLA Ops:
  0.6 0.5 %collective-permute-start = (bf16[256,1024]{1,0:T(8,128)(2,1)}, bf16[256,1024]{1,0:T(8,128)(2,1)S(1)}, u32[]{:S(2)}, u32[]{:S(2)}) collective-permute-start(bf16[256,1024]{1,0:T(8,128)(2,1)} %refs_4_.1), channel_id=1, source_target_pairs={{0,1},{1,0},{2,3},{3,2},{4,5},{5,4},{6,7},{7,6},{8,9},{9,8},{10,11... | collective-permute-start | bytes 1572872 | tf_op jit(solution)/shard_map/ppermute | solution.py:384
  1.1 0.1 collective-permute-start.1
  1.2 0.4 collective-permute-start.2
  1.7 1.1 %broadcast_select_fusion = bf16[256,1024]{1,0:T(8,128)(2,1)S(1)} fusion(bf16[256,1024]{1,0:T(8,128)(2,1)} %refs_8_.1, bf16[256,1024]{1,0:T(8,128)(2,1)} %refs_9_.1, pred[]{:T(512)S(6)} %eq.5), kind=kLoop, calls=%fused_computation | loop fusion | flops 262144 | bytes 1572865 | tf_op jit(solution)/shard_map/jit(_where)/select_n | solution.py:409
  2.8 2.6 %collective-permute-start.6 = (bf16[256,1024]{1,0:T(8,128)(2,1)S(1)}, bf16[256,1024]{1,0:T(8,128)(2,1)S(1)}, u32[]{:S(2)}, u32[]{:S(2)}) collective-permute-start(bf16[256,1024]{1,0:T(8,128)(2,1)S(1)} %broadcast_select_fusion), channel_id=1, source_target_pairs={{0,2},{1,3},{2,0},{3,1},{4,6},{5,7},{6,4},{7,5},{8,10},{9,11},{10,... | collective-permute-start | bytes 1572872 | tf_op jit(solution)/shard_map/ppermute | solution.py:384
  5.4 0.1 collective-permute-start.8
  5.5 11.4 %shard_map.110 = bf16[16,1280]{1,0:T(8,128)(2,1)} custom-call(bf16[24,128,1024]{2,1,0:T(8,128)(2,1)} %texts_ref.1, bf16[1024,768]{1,0:T(8,128)(2,1)} %w_hbm.1, bf16[24,256]{1,0:T(8,128)(2,1)} %cot_ref.1, s32[16,24]{1,0:T(8,128)} %bitcast.6), custom_call_target="tpu_custom_call" | custom-call | flops 5637144576 | bytes 7864320 | tf_op jit(solution)/shard_map/pallas_call | solution.py:149
  16.9 0.0 collective-permute-done.refs_5_
  16.9 0.0 collective-permute-done.2.refs_11_
  16.9 4.1 %collective-permute-start.5 = (bf16[1,16,1280]{2,1,0:T(8,128)(2,1)}, bf16[1,16,1280]{2,1,0:T(8,128)(2,1)S(1)}, u32[]{:S(2)}, u32[]{:S(2)}) collective-permute-start(bf16[1,16,1280]{2,1,0:T(8,128)(2,1)} %bitcast.2), channel_id=1, source_target_pairs={{0,24},{4,28},{8,16},{12,20},{16,8},{20,12},{24,0},{28,4},{1,25},{... | collective-permute-start | bytes 122888 | tf_op jit(solution)/shard_map/ppermute | solution.py:384
  21.1 0.0 collective-permute-start.4
  21.1 0.6 %collective-permute-start.3 = (bf16[1,16,1280]{2,1,0:T(8,128)(2,1)}, bf16[1,16,1280]{2,1,0:T(8,128)(2,1)S(1)}, u32[]{:S(2)}, u32[]{:S(2)}) collective-permute-start(bf16[1,16,1280]{2,1,0:T(8,128)(2,1)} %bitcast.4), channel_id=1, source_target_pairs={{0,8},{4,12},{8,0},{12,4},{16,24},{20,28},{24,16},{28,20},{1,9},{5... | collective-permute-start | bytes 122888 | tf_op jit(solution)/shard_map/ppermute | solution.py:384
  21.7 0.8 %copy-done.2 = bf16[16,1280]{1,0:T(8,128)(2,1)S(1)} copy-done((bf16[16,1280]{1,0:T(8,128)(2,1)S(1)}, bf16[16,1280]{1,0:T(8,128)(2,1)}, u32[]{:S(2)}) %copy-start.2) | copy-done | bytes 40984
  22.5 0.0 collective-permute-done.6.refs_12_
  22.5 0.8 %collective-permute-done.5.refs_3_ = bf16[1,16,1280]{2,1,0:T(8,128)(2,1)S(1)} collective-permute-done((bf16[1,16,1280]{2,1,0:T(8,128)(2,1)}, bf16[1,16,1280]{2,1,0:T(8,128)(2,1)S(1)}, u32[]{:S(2)}, u32[]{:S(2)}) %collective-permute-start.5) | collective-permute-done | bytes 40992 | tf_op jit(solution)/shard_map/ppermute | solution.py:384
  23.3 2.9 %collective-permute-done.4.refs_2_ = bf16[1,16,1280]{2,1,0:T(8,128)(2,1)S(1)} collective-permute-done((bf16[1,16,1280]{2,1,0:T(8,128)(2,1)}, bf16[1,16,1280]{2,1,0:T(8,128)(2,1)S(1)}, u32[]{:S(2)}, u32[]{:S(2)}) %collective-permute-start.4) | collective-permute-done | bytes 40992 | tf_op jit(solution)/shard_map/ppermute | solution.py:384
  26.2 0.2 collective-permute-start.13
  26.4 1.6 %collective-permute-start.7 = (bf16[4,16,1280]{2,1,0:T(8,128)(2,1)S(1)}, bf16[4,16,1280]{2,1,0:T(8,128)(2,1)S(1)}, u32[]{:S(2)}, u32[]{:S(2)}) collective-permute-start(bf16[4,16,1280]{2,1,0:T(8,128)(2,1)S(1)} %shard_map.112.refs_0_), channel_id=1, source_target_pairs={{0,4},{4,0},{8,12},{12,8},{16,20},{20,16},{24,28},{28,24},{1,5},{5... | collective-permute-start | bytes 491528 | tf_op jit(solution)/shard_map/ppermute | solution.py:384
  28.0 3.8 %collective-permute-done.7.refs_1_ = bf16[4,16,1280]{2,1,0:T(8,128)(2,1)S(1)} collective-permute-done((bf16[4,16,1280]{2,1,0:T(8,128)(2,1)S(1)}, bf16[4,16,1280]{2,1,0:T(8,128)(2,1)S(1)}, u32[]{:S(2)}, u32[]{:S(2)}) %collective-permute-start.7) | collective-permute-done | bytes 163872 | tf_op jit(solution)/shard_map/ppermute | solution.py:384
  31.8 1.6 %collective-permute-start.10 = (bf16[8,16,1280]{2,1,0:T(8,128)(2,1)S(1)}, bf16[8,16,1280]{2,1,0:T(8,128)(2,1)S(1)}, u32[]{:S(2)}, u32[]{:S(2)}) collective-permute-start(bf16[8,16,1280]{2,1,0:T(8,128)(2,1)S(1)} %shard_map.113.refs_0_), channel_id=1, source_target_pairs={{0,2},{1,3},{2,0},{3,1},{4,6},{5,7},{6,4},{7,5},{8,10},{9,11},{10,... | collective-permute-start | bytes 983048 | tf_op jit(solution)/shard_map/ppermute | solution.py:384
  33.4 0.5 %collective-permute-start.12 = (bf16[256,1024]{1,0:T(8,128)(2,1)S(1)}, bf16[256,1024]{1,0:T(8,128)(2,1)S(1)}, u32[]{:S(2)}, u32[]{:S(2)}) collective-permute-start(bf16[256,1024]{1,0:T(8,128)(2,1)S(1)} %collective-permute-done.8.refs_6_), channel_id=1, source_target_pairs={{0,1},{1,0},{2,3},{3,2},{4,5},{5,4},{6,7},{7,6},{8,9},{9,8},{10,11... | collective-permute-start | bytes 1572872 | tf_op jit(solution)/shard_map/ppermute | solution.py:384
  33.9 4.6 %collective-permute-done.13.refs_13_ = bf16[256,1024]{1,0:T(8,128)(2,1)S(1)} collective-permute-done((bf16[256,1024]{1,0:T(8,128)(2,1)S(1)}, bf16[256,1024]{1,0:T(8,128)(2,1)S(1)}, u32[]{:S(2)}, u32[]{:S(2)}) %collective-permute-start.13) | collective-permute-done | bytes 524320 | tf_op jit(solution)/shard_map/ppermute | solution.py:384
  38.5 0.0 collective-permute-start.15
  38.5 0.5 %collective-permute-start.9 = (bf16[8,16,1280]{2,1,0:T(8,128)(2,1)S(1)}, bf16[8,16,1280]{2,1,0:T(8,128)(2,1)S(1)}, u32[]{:S(2)}, u32[]{:S(2)}) collective-permute-start(bf16[8,16,1280]{2,1,0:T(8,128)(2,1)S(1)} %shard_map.113.refs_0_), channel_id=1, source_target_pairs={{0,1},{1,0},{2,3},{3,2},{4,5},{5,4},{6,7},{7,6},{8,9},{9,8},{10,11... | collective-permute-start | bytes 983048 | tf_op jit(solution)/shard_map/ppermute | solution.py:384
  39.0 0.1 collective-permute-done.10.refs_2_
  39.1 0.0 collective-permute-start.11
  39.1 1.8 %collective-permute-done.9.refs_1_ = bf16[8,16,1280]{2,1,0:T(8,128)(2,1)S(1)} collective-permute-done((bf16[8,16,1280]{2,1,0:T(8,128)(2,1)S(1)}, bf16[8,16,1280]{2,1,0:T(8,128)(2,1)S(1)}, u32[]{:S(2)}, u32[]{:S(2)}) %collective-permute-start.9) | collective-permute-done | bytes 327712 | tf_op jit(solution)/shard_map/ppermute | solution.py:384
  40.9 0.0 collective-permute-done.14.refs_14_
  40.9 0.0 collective-permute-done.12.refs_7_
  40.9 0.5 collective-permute-done.11.refs_3_
  41.3 0.0 collective-permute-done.15.refs_15_
  41.3 7.2 %shard_map.114 = (bf16[24,256]{1,0:T(8,128)(2,1)}, bf16[24,256]{1,0:T(8,128)(2,1)}, f32[256,1024]{1,0:T(8,128)}, f32[256,1024]{1,0:T(8,128)}, f32[256,1024]{1,0:T(8,128)}) custom-call(bf16[8,16,1280]{2,1,0:T(8,128)(2,1)S(1)} %shard_map.113.refs_0_, bf16[8,16,1280]{2,1,0:T(8,128)(2,1)S(1)} %collective-permute-done.9.refs_1_, ...), custom_call_target="tpu_custom_call" | custom-call | flops 2415919104 | bytes 10485760 | tf_op jit(solution)/shard_map/pallas_call | solution.py:295
  (14 shorter events, 0.1 us)
Async XLA Ops:
  0.6 16.3 %collective-permute-start = (bf16[256,1024]{1,0:T(8,128)(2,1)}, bf16[256,1024]{1,0:T(8,128)(2,1)S(1)}, u32[]{:S(2)}, u32[]{:S(2)}) collective-permute-start(bf16[256,1024]{1,0:T(8,128)(2,1)} %refs_4_.1), channel_id=1, source_target_pairs={{0,1},{1,0},{2,3},{3,2},{4,5},{5,4},{6,7},{7,6},{8,9},{9,8},{10,11... | collective-permute-start | bytes 1572872 | tf_op jit(solution)/shard_map/ppermute | solution.py:384
  1.1 15.8 %collective-permute-start.1 = (bf16[256,1024]{1,0:T(8,128)(2,1)}, bf16[256,1024]{1,0:T(8,128)(2,1)S(1)}, u32[]{:S(2)}, u32[]{:S(2)}) collective-permute-start(bf16[256,1024]{1,0:T(8,128)(2,1)} %refs_8_.1), channel_id=1, source_target_pairs={{0,1},{1,0},{2,3},{3,2},{4,5},{5,4},{6,7},{7,6},{8,9},{9,8},{10,11... | collective-permute-start | bytes 1572872 | tf_op jit(solution)/shard_map/ppermute | solution.py:384
  1.2 15.7 %collective-permute-start.2 = (bf16[256,1024]{1,0:T(8,128)(2,1)}, bf16[256,1024]{1,0:T(8,128)(2,1)S(1)}, u32[]{:S(2)}, u32[]{:S(2)}) collective-permute-start(bf16[256,1024]{1,0:T(8,128)(2,1)} %refs_9_.1), channel_id=1, source_target_pairs={{0,1},{1,0},{2,3},{3,2},{4,5},{5,4},{6,7},{7,6},{8,9},{9,8},{10,11... | collective-permute-start | bytes 1572872 | tf_op jit(solution)/shard_map/ppermute | solution.py:384
  2.8 19.8 %collective-permute-start.6 = (bf16[256,1024]{1,0:T(8,128)(2,1)S(1)}, bf16[256,1024]{1,0:T(8,128)(2,1)S(1)}, u32[]{:S(2)}, u32[]{:S(2)}) collective-permute-start(bf16[256,1024]{1,0:T(8,128)(2,1)S(1)} %broadcast_select_fusion), channel_id=1, source_target_pairs={{0,2},{1,3},{2,0},{3,1},{4,6},{5,7},{6,4},{7,5},{8,10},{9,11},{10,... | collective-permute-start | bytes 1572872 | tf_op jit(solution)/shard_map/ppermute | solution.py:384
  5.4 26.4 %collective-permute-start.8 = (bf16[256,1024]{1,0:T(8,128)(2,1)}, bf16[256,1024]{1,0:T(8,128)(2,1)S(1)}, u32[]{:S(2)}, u32[]{:S(2)}) collective-permute-start(bf16[256,1024]{1,0:T(8,128)(2,1)} %refs_4_.1), channel_id=1, source_target_pairs={{0,2},{1,3},{2,0},{3,1},{4,6},{5,7},{6,4},{7,5},{8,10},{9,11},{10,... | collective-permute-start | bytes 1572872 | tf_op jit(solution)/shard_map/ppermute | solution.py:384
  5.5 35.9 %copy-start = (bf16[256,1024]{1,0:T(8,128)(2,1)S(1)}, bf16[256,1024]{1,0:T(8,128)(2,1)}, u32[]{:S(2)}) copy-start(bf16[256,1024]{1,0:T(8,128)(2,1)} %refs_8_.1) | copy-start | bytes 1572868
  5.5 35.9 %copy-start.1 = (bf16[256,1024]{1,0:T(8,128)(2,1)S(1)}, bf16[256,1024]{1,0:T(8,128)(2,1)}, u32[]{:S(2)}) copy-start(bf16[256,1024]{1,0:T(8,128)(2,1)} %refs_9_.1) | copy-start | bytes 1572868
  5.5 35.9 %copy-start.3 = (bf16[256,1024]{1,0:T(8,128)(2,1)S(1)}, bf16[256,1024]{1,0:T(8,128)(2,1)}, u32[]{:S(2)}) copy-start(bf16[256,1024]{1,0:T(8,128)(2,1)} %refs_4_.1) | copy-start | bytes 1572868
  16.9 6.4 %collective-permute-start.5 = (bf16[1,16,1280]{2,1,0:T(8,128)(2,1)}, bf16[1,16,1280]{2,1,0:T(8,128)(2,1)S(1)}, u32[]{:S(2)}, u32[]{:S(2)}) collective-permute-start(bf16[1,16,1280]{2,1,0:T(8,128)(2,1)} %bitcast.2), channel_id=1, source_target_pairs={{0,24},{4,28},{8,16},{12,20},{16,8},{20,12},{24,0},{28,4},{1,25},{... | collective-permute-start | bytes 122888 | tf_op jit(solution)/shard_map/ppermute | solution.py:384
  21.1 5.1 %collective-permute-start.4 = (bf16[1,16,1280]{2,1,0:T(8,128)(2,1)}, bf16[1,16,1280]{2,1,0:T(8,128)(2,1)S(1)}, u32[]{:S(2)}, u32[]{:S(2)}) collective-permute-start(bf16[1,16,1280]{2,1,0:T(8,128)(2,1)} %bitcast.3), channel_id=1, source_target_pairs={{0,16},{4,20},{8,24},{12,28},{16,0},{20,4},{24,8},{28,12},{1,17},{... | collective-permute-start | bytes 122888 | tf_op jit(solution)/shard_map/ppermute | solution.py:384
  21.1 5.1 %collective-permute-start.3 = (bf16[1,16,1280]{2,1,0:T(8,128)(2,1)}, bf16[1,16,1280]{2,1,0:T(8,128)(2,1)S(1)}, u32[]{:S(2)}, u32[]{:S(2)}) collective-permute-start(bf16[1,16,1280]{2,1,0:T(8,128)(2,1)} %bitcast.4), channel_id=1, source_target_pairs={{0,8},{4,12},{8,0},{12,4},{16,24},{20,28},{24,16},{28,20},{1,9},{5... | collective-permute-start | bytes 122888 | tf_op jit(solution)/shard_map/ppermute | solution.py:384
  21.7 0.8 %copy-start.2 = (bf16[16,1280]{1,0:T(8,128)(2,1)S(1)}, bf16[16,1280]{1,0:T(8,128)(2,1)}, u32[]{:S(2)}) copy-start(bf16[16,1280]{1,0:T(8,128)(2,1)} %shard_map.110) | copy-start | bytes 122884
  26.2 12.3 %collective-permute-start.13 = (bf16[256,1024]{1,0:T(8,128)(2,1)S(1)}, bf16[256,1024]{1,0:T(8,128)(2,1)S(1)}, u32[]{:S(2)}, u32[]{:S(2)}) collective-permute-start(bf16[256,1024]{1,0:T(8,128)(2,1)S(1)} %collective-permute-done.6.refs_12_), channel_id=1, source_target_pairs={{0,8},{4,12},{8,0},{12,4},{16,24},{20,28},{24,16},{28,20},{1,9},{5... | collective-permute-start | bytes 1572872 | tf_op jit(solution)/shard_map/ppermute | solution.py:384
  26.4 5.4 %collective-permute-start.7 = (bf16[4,16,1280]{2,1,0:T(8,128)(2,1)S(1)}, bf16[4,16,1280]{2,1,0:T(8,128)(2,1)S(1)}, u32[]{:S(2)}, u32[]{:S(2)}) collective-permute-start(bf16[4,16,1280]{2,1,0:T(8,128)(2,1)S(1)} %shard_map.112.refs_0_), channel_id=1, source_target_pairs={{0,4},{4,0},{8,12},{12,8},{16,20},{20,16},{24,28},{28,24},{1,5},{5... | collective-permute-start | bytes 491528 | tf_op jit(solution)/shard_map/ppermute | solution.py:384
  31.8 7.3 %collective-permute-start.10 = (bf16[8,16,1280]{2,1,0:T(8,128)(2,1)S(1)}, bf16[8,16,1280]{2,1,0:T(8,128)(2,1)S(1)}, u32[]{:S(2)}, u32[]{:S(2)}) collective-permute-start(bf16[8,16,1280]{2,1,0:T(8,128)(2,1)S(1)} %shard_map.113.refs_0_), channel_id=1, source_target_pairs={{0,2},{1,3},{2,0},{3,1},{4,6},{5,7},{6,4},{7,5},{8,10},{9,11},{10,... | collective-permute-start | bytes 983048 | tf_op jit(solution)/shard_map/ppermute | solution.py:384
  33.4 7.5 %collective-permute-start.14 = (bf16[256,1024]{1,0:T(8,128)(2,1)S(1)}, bf16[256,1024]{1,0:T(8,128)(2,1)S(1)}, u32[]{:S(2)}, u32[]{:S(2)}) collective-permute-start(bf16[256,1024]{1,0:T(8,128)(2,1)S(1)} %collective-permute-done.6.refs_12_), channel_id=1, source_target_pairs={{0,1},{1,0},{2,3},{3,2},{4,5},{5,4},{6,7},{7,6},{8,9},{9,8},{10,11... | collective-permute-start | bytes 1572872 | tf_op jit(solution)/shard_map/ppermute | solution.py:384
  33.4 7.5 %collective-permute-start.12 = (bf16[256,1024]{1,0:T(8,128)(2,1)S(1)}, bf16[256,1024]{1,0:T(8,128)(2,1)S(1)}, u32[]{:S(2)}, u32[]{:S(2)}) collective-permute-start(bf16[256,1024]{1,0:T(8,128)(2,1)S(1)} %collective-permute-done.8.refs_6_), channel_id=1, source_target_pairs={{0,1},{1,0},{2,3},{3,2},{4,5},{5,4},{6,7},{7,6},{8,9},{9,8},{10,11... | collective-permute-start | bytes 1572872 | tf_op jit(solution)/shard_map/ppermute | solution.py:384
  38.5 2.9 %collective-permute-start.15 = (bf16[256,1024]{1,0:T(8,128)(2,1)S(1)}, bf16[256,1024]{1,0:T(8,128)(2,1)S(1)}, u32[]{:S(2)}, u32[]{:S(2)}) collective-permute-start(bf16[256,1024]{1,0:T(8,128)(2,1)S(1)} %collective-permute-done.13.refs_13_), channel_id=1, source_target_pairs={{0,1},{1,0},{2,3},{3,2},{4,5},{5,4},{6,7},{7,6},{8,9},{9,8},{10,11... | collective-permute-start | bytes 1572872 | tf_op jit(solution)/shard_map/ppermute | solution.py:384
  38.5 2.4 %collective-permute-start.9 = (bf16[8,16,1280]{2,1,0:T(8,128)(2,1)S(1)}, bf16[8,16,1280]{2,1,0:T(8,128)(2,1)S(1)}, u32[]{:S(2)}, u32[]{:S(2)}) collective-permute-start(bf16[8,16,1280]{2,1,0:T(8,128)(2,1)S(1)} %shard_map.113.refs_0_), channel_id=1, source_target_pairs={{0,1},{1,0},{2,3},{3,2},{4,5},{5,4},{6,7},{7,6},{8,9},{9,8},{10,11... | collective-permute-start | bytes 983048 | tf_op jit(solution)/shard_map/ppermute | solution.py:384
  39.1 2.2 %collective-permute-start.11 = (bf16[8,16,1280]{2,1,0:T(8,128)(2,1)S(1)}, bf16[8,16,1280]{2,1,0:T(8,128)(2,1)S(1)}, u32[]{:S(2)}, u32[]{:S(2)}) collective-permute-start(bf16[8,16,1280]{2,1,0:T(8,128)(2,1)S(1)} %collective-permute-done.10.refs_2_), channel_id=1, source_target_pairs={{0,1},{1,0},{2,3},{3,2},{4,5},{5,4},{6,7},{7,6},{8,9},{9,8},{10,11... | collective-permute-start | bytes 983048 | tf_op jit(solution)/shard_map/ppermute | solution.py:384
